TPU v7x, 32 devices: a whole 2x2x4 slice. The times are simulated.
32 devices in a mesh: dp: 8 (over y, x, core), tensor: 4 (over z).
Axes of the slice: x: 2, y: 2, z: 4, core: 2. Of those that a mesh axis runs over, the one named last changes fastest.
Arguments:
- inputs: bfloat16 [1024, 8192], P('dp', 'tensor'), may hold values from -6 to 6
- out_grad: bfloat16 [1024, 8192], P('dp', 'tensor'), may hold values from -6 to 6
- weights: bfloat16 [3, 384, 128, 128], P(None, 'tensor'), may hold values from -0.1875 to 0.1875
- block_index: int32 [3, 384, 2], P(None, 'tensor'), may hold values from 0 to 63, as said below
- block_counts: int32 [4, 3], P('tensor'), may hold values from 38 to 96, as said below
- first_moment: float32 [3, 384, 128, 128], P(None, ('tensor', 'dp')), may hold values from -120 to 120
- second_moment: float32 [3, 384, 128, 128], P(None, ('tensor', 'dp')), may hold values from 100 to 10000
Outputs:
- outputs: bfloat16 [1024, 8192], P('dp', 'tensor')
- input_grad: bfloat16 [1024, 8192], P('dp', 'tensor')
- update: float32 [3, 384, 128, 128], P(None, ('tensor', 'dp'))
Inputs may be any that keep to these rules, and one draw needn't show every extreme that they name: block_index[k, t * 96 + j, 0] is a feature block (below 64) and block_index[k, t * 96 + j, 1] a hidden block of tensor index t (below 14); the 96 slots of one matrix on one tensor index name distinct blocks. block_counts[t, k] live slots of matrix k on tensor index t; for each matrix some tensor index has exactly 96.
All inputs are finite; a program needn't handle non-finite values.
Results may differ from a plain program's by a relative error of at most 0.013.
Values may be sent and summed in bfloat16 or wider, within the bound.
No kernel may reach another device: no remote copies, remote signals or barrier semaphores. Data moves between devices by JAX's collectives and lax.ppermute only.
A program may use at most 128 MiB of HBM per device.

v0:
```python
import jax
import jax.numpy as jnp
from jax import lax
from jax.sharding import PartitionSpec as P

HB_DEV = 14


EPSILON = 1e-08


def block_rows(rows_in, blocks):
    return jnp.einsum("tsk,skn->tsn", rows_in, blocks, preferred_element_type=jnp.float32)


def block_rows_back(rows_in, blocks):
    return jnp.einsum("tsn,skn->tsk", rows_in, blocks, preferred_element_type=jnp.float32)


def place(products, target_ids, live_row, segments):
    segment_ids = jnp.arange(segments, dtype=jnp.int32)
    select = (target_ids[:, None] == segment_ids[None, :]).astype(jnp.float32) * live_row[:, None]
    return jnp.einsum(
        "tsn,sh->thn",
        products,
        select,
        preferred_element_type=jnp.float32,
        precision=lax.Precision.HIGHEST,
    )


def block_grad(left_rows, right_rows, live_row):
    return (
        jnp.einsum("tsk,tsn->skn", left_rows, right_rows, preferred_element_type=jnp.float32)
        * live_row[:, None, None]
    )


def local(inputs, out_grad, weights, block_index, block_counts, first_moment, second_moment):
    token_rows = inputs.shape[0]
    capacity = weights.shape[1]
    block_size = weights.shape[2]
    inputs_full = lax.all_gather(inputs, "tensor", axis=1, tiled=True)
    model_width = inputs_full.shape[1]
    feature_blocks = model_width // block_size
    input_blocks = inputs_full.reshape(token_rows, feature_blocks, block_size)
    counts_here = block_counts[0]
    slot_ids = jnp.arange(capacity, dtype=jnp.int32)
    live_slots = (slot_ids[None, :] < counts_here[:, None]).astype(jnp.float32)
    gate_inputs = input_blocks[:, block_index[0, :, 0], :]
    up_inputs = input_blocks[:, block_index[1, :, 0], :]
    gate_proj = place(
        block_rows(gate_inputs, weights[0]), block_index[0, :, 1], live_slots[0], HB_DEV
    )
    up_proj = place(block_rows(up_inputs, weights[1]), block_index[1, :, 1], live_slots[1], HB_DEV)
    sigmoid_gate = jax.nn.sigmoid(gate_proj)
    activated = gate_proj * sigmoid_gate
    hidden = (activated * up_proj).astype(jnp.bfloat16)
    down_inputs = hidden[:, block_index[2, :, 1], :]
    out_partial = place(
        block_rows(down_inputs, weights[2]), block_index[2, :, 0], live_slots[2], feature_blocks
    ).reshape(token_rows, model_width)
    outputs = lax.psum_scatter(
        out_partial.astype(jnp.bfloat16), "tensor", scatter_dimension=1, tiled=True
    )
    cotangent_full = lax.all_gather(out_grad, "tensor", axis=1, tiled=True)
    cotangent_blocks = cotangent_full.reshape(token_rows, feature_blocks, block_size)
    down_cotangents = cotangent_blocks[:, block_index[2, :, 0], :]
    hidden_grad = place(
        block_rows_back(down_cotangents, weights[2]), block_index[2, :, 1], live_slots[2], HB_DEV
    )
    down_grad = block_grad(down_inputs, down_cotangents, live_slots[2])
    gate_grad_rows = (
        hidden_grad * up_proj * sigmoid_gate * (1.0 + gate_proj * (1.0 - sigmoid_gate))
    ).astype(jnp.bfloat16)
    up_grad_rows = (hidden_grad * activated).astype(jnp.bfloat16)
    gate_back = gate_grad_rows[:, block_index[0, :, 1], :]
    up_back = up_grad_rows[:, block_index[1, :, 1], :]
    input_partial = place(
        block_rows_back(gate_back, weights[0]), block_index[0, :, 0], live_slots[0], feature_blocks
    )
    input_partial = (
        input_partial
        + place(
            block_rows_back(up_back, weights[1]),
            block_index[1, :, 0],
            live_slots[1],
            feature_blocks,
        )
    ).reshape(token_rows, model_width)
    gate_grad = block_grad(gate_inputs, gate_back, live_slots[0])
    up_grad = block_grad(up_inputs, up_back, live_slots[1])
    shares = lax.psum_scatter(
        jnp.stack([gate_grad, up_grad, down_grad]).astype(jnp.bfloat16),
        "dp",
        scatter_dimension=1,
        tiled=True,
    ).astype(jnp.float32)
    input_grad = lax.psum_scatter(
        input_partial.astype(jnp.bfloat16), "tensor", scatter_dimension=1, tiled=True
    )
    share_rows = shares.shape[1]
    share_start = lax.axis_index("dp") * share_rows
    share_ids = share_start + jnp.arange(share_rows, dtype=jnp.int32)
    share_live = (share_ids[None, :] < counts_here[:, None]).astype(jnp.float32)
    first_new = 0.9 * first_moment + 0.1 * shares
    second_new = 0.95 * second_moment + 0.05 * shares * shares
    update = share_live[:, :, None, None] * first_new / (jnp.sqrt(second_new) + EPSILON)
    return (outputs, input_grad, update)


def solution(mesh):
    in_specs = (
        P("dp", "tensor"),
        P("dp", "tensor"),
        P(None, "tensor", None, None),
        P(None, "tensor", None),
        P("tensor", None),
        P(None, ("tensor", "dp"), None, None),
        P(None, ("tensor", "dp"), None, None),
    )
    out_specs = (P("dp", "tensor"), P("dp", "tensor"), P(None, ("tensor", "dp"), None, None))
    return jax.shard_map(local, mesh=mesh, in_specs=in_specs, out_specs=out_specs, check_vma=False)
```

profile of v0, /device:TPU:0, one launch (start us, length us, event | category | flops | bytes accessed | tf_op | source)
XLA Modules:
  0.0 419.9 jit_solution(13693562674650971753)
XLA Ops:
  11.6 47.2 %all-gather.3.cloned.1.call-done = bf16[128,8192]{0,1:T(8,128)(2,1)} async-done(((bf16[128,2048]{0,1:T(8,128)(2,1)}), bf16[128,8192]{0,1:T(8,128)(2,1)}) %all-gather.3.cloned.1.call-update) | async-done | bytes 2097168 | tf_op jit(solution)/shard_map/all_gather | solution.py:43
  58.8 3.2 copy.54
  62.1 2.8 gather_fusion
  64.8 2.7 gather_fusion.1
  67.6 6.7 %fusion.48 = f32[128,96,128]{2,0,1:T(8,128)} fusion(bf16[3,96,128,128]{3,2,1,0:T(8,128)(2,1)} %param.9, bf16[96,128,128]{2,1,0:T(8,128)(2,1)} %gather_fusion), kind=kOutput, calls=%fused_computation.61 | convolution fusion | flops 402653184 | bytes 12582912 | tf_op jit(solution)/shard_map/tsk,skn->tsn/dot_general | solution.py:13
  74.3 5.6 %fusion.53 = f32[128,96,128]{2,0,1:T(8,128)} fusion(bf16[3,96,128,128]{3,2,1,0:T(8,128)(2,1)} %param.9, bf16[96,128,128]{2,1,0:T(8,128)(2,1)S(1)} %copy-done.1), kind=kOutput, calls=%fused_computation.62 | convolution fusion | flops 402653184 | bytes 12582912 | tf_op jit(solution)/shard_map/tsk,skn->tsn/dot_general | solution.py:13
  79.8 25.8 %all-gather.5.cloned.1.call-done = bf16[128,8192]{0,1:T(8,128)(2,1)} async-done(((bf16[128,2048]{0,1:T(8,128)(2,1)}), bf16[128,8192]{0,1:T(8,128)(2,1)}) %all-gather.5.cloned.1.call-update) | async-done | bytes 2097168 | tf_op jit(solution)/shard_map/all_gather | solution.py:66
  105.7 4.1 copy.62
  109.7 2.7 gather_fusion.3
  112.5 5.3 %fusion.63 = f32[128,96,128]{2,0,1:T(8,128)S(1)} fusion(bf16[3,96,128,128]{3,2,1,0:T(8,128)(2,1)} %param.9, bf16[96,128,128]{2,1,0:T(8,128)(2,1)S(1)} %gather_fusion.3), kind=kOutput, calls=%fused_computation.64 | convolution fusion | flops 402653184 | bytes 12582912 | tf_op jit(solution)/shard_map/tsn,skn->tsk/dot_general | solution.py:17
  117.8 9.5 %fusion.10 = f32[14,128,128]{2,0,1:T(8,128)S(1)} fusion(f32[128,96,128]{2,0,1:T(8,128)} %fusion.48, f32[96]{0:T(128)S(1)} %get-tuple-element.20, s32[96]{0:T(128)S(1)} %get-tuple-element.10), kind=kOutput, calls=%fused_computation.17 | convolution fusion | flops 264243840 | bytes 7209728 | tf_op jit(solution)/shard_map/tsn,sh->thn/dot_general | solution.py:23
  127.4 9.8 %fusion.8 = f32[14,128,128]{2,0,1:T(8,128)S(1)} fusion(f32[128,96,128]{2,0,1:T(8,128)} %fusion.53, f32[96]{0:T(128)S(1)} %get-tuple-element.19, s32[96]{0:T(128)S(1)} %get-tuple-element.9), kind=kOutput, calls=%fused_computation.15 | convolution fusion | flops 264243840 | bytes 7209728 | tf_op jit(solution)/shard_map/tsn,sh->thn/dot_general | solution.py:23
  137.2 6.5 %fusion.4 = f32[14,128,128]{2,0,1:T(8,128)S(1)} fusion(f32[128,96,128]{2,0,1:T(8,128)S(1)} %fusion.63, f32[96]{0:T(128)S(1)} %get-tuple-element.18, s32[96]{0:T(128)S(1)} %get-tuple-element.8), kind=kOutput, calls=%fused_computation.11 | convolution fusion | flops 264243840 | bytes 7209728 | tf_op jit(solution)/shard_map/tsn,sh->thn/dot_general | solution.py:23
  144.7 2.7 gather_fusion.4
  147.4 6.1 %fusion.12 = bf16[1,96,128,128]{3,2,1,0:T(8,128)(2,1)} fusion(f32[96]{0:T(128)S(1)} %get-tuple-element.20, bf16[96,128,128]{2,1,0:T(8,128)(2,1)} %gather_fusion.4, bf16[96,128,128]{2,1,0:T(8,128)(2,1)} %gather_fusion), kind=kOutput, calls=%fused_computation.24 | convolution fusion | flops 405798912 | bytes 9437568 | tf_op jit(solution)/shard_map/tsk,tsn->skn/dot_general | solution.py:34
  153.5 2.8 gather_fusion.5
  156.2 15.5 %fusion.13 = bf16[1,96,128,128]{3,2,1,0:T(8,128)(2,1)} fusion(f32[96]{0:T(128)S(1)} %get-tuple-element.19, bf16[96,128,128]{2,1,0:T(8,128)(2,1)} %gather_fusion.5, bf16[96,128,128]{2,1,0:T(8,128)(2,1)} %gather_fusion.1), kind=kOutput, calls=%fused_computation.25 | convolution fusion | flops 405798912 | bytes 9437568 | tf_op jit(solution)/shard_map/tsk,tsn->skn/dot_general | solution.py:34
  171.7 2.7 gather_fusion.2
  174.5 4.6 %fusion.14 = bf16[1,96,128,128]{3,2,1,0:T(8,128)(2,1)S(1)} fusion(f32[96]{0:T(128)S(1)} %get-tuple-element.18, bf16[96,128,128]{2,1,0:T(8,128)(2,1)} %copy-done.3, bf16[96,128,128]{2,1,0:T(8,128)(2,1)} %gather_fusion.2), kind=kOutput, calls=%fused_computation.26 | convolution fusion | flops 405798912 | bytes 9437568 | tf_op jit(solution)/shard_map/tsk,tsn->skn/dot_general | solution.py:34
  179.2 4.2 %pad_maximum_fusion = bf16[3,96,128,128]{3,2,1,0:T(8,128)(2,1)} fusion(bf16[1,96,128,128]{3,2,1,0:T(8,128)(2,1)S(1)} %fusion.14, bf16[1,96,128,128]{3,2,1,0:T(8,128)(2,1)S(1)} %copy-done.6, bf16[1,96,128,128]{3,2,1,0:T(8,128)(2,1)S(1)} %copy-done.5), kind=kLoop, calls=%fused_computation.6 | loop fusion | flops 9437184 | bytes 18874368 | tf_op jit(solution)/shard_map/stack | solution.py:94
  185.3 4.2 fusion.73
  189.5 8.0 %fusion = f32[64,128,128]{2,0,1:T(8,128)S(1)} fusion(f32[128,96,128]{2,0,1:T(8,128)S(1)} %fusion.73, f32[96]{0:T(128)S(1)} %get-tuple-element.19, s32[96]{0:T(128)S(1)} %get-tuple-element.7), kind=kOutput, calls=%fused_computation.7 | convolution fusion | flops 1207971840 | bytes 10486528 | tf_op jit(solution)/shard_map/tsn,sh->thn/dot_general | solution.py:23
  197.4 4.3 %fusion.68 = f32[128,96,128]{2,0,1:T(8,128)S(1)} fusion(bf16[3,96,128,128]{3,2,1,0:T(8,128)(2,1)} %param.9, bf16[96,128,128]{2,1,0:T(8,128)(2,1)S(1)} %copy-done.2), kind=kOutput, calls=%fused_computation.65 | convolution fusion | flops 402653184 | bytes 12582912 | tf_op jit(solution)/shard_map/tsn,skn->tsk/dot_general | solution.py:17
  201.7 10.5 %add_convert_fusion = bf16[64,128,128]{2,0,1:T(8,128)(2,1)S(1)} fusion(f32[64,128,128]{2,0,1:T(8,128)S(1)} %fusion, f32[128,96,128]{2,0,1:T(8,128)S(1)} %fusion.68, f32[96]{0:T(128)S(1)} %get-tuple-element.20, s32[96]{0:T(128)S(1)} %get-tuple-element.6), kind=kOutput, calls=%fused_computation.22 | convolution fusion | flops 1210068992 | bytes 12583680 | tf_op jit(solution)/shard_map/tsn,sh->thn/dot_general | solution.py:23
  212.2 3.2 copy.105
  215.5 2.9 fusion.58
  218.4 10.2 %fusion.98 = bf16[64,128,128]{2,0,1:T(8,128)(2,1)S(1)} fusion(f32[128,96,128]{2,0,1:T(8,128)S(1)} %fusion.58, f32[96]{0:T(128)S(1)} %get-tuple-element.18, s32[96]{0:T(128)S(1)} %get-tuple-element.11), kind=kOutput, calls=%fused_computation.75 | convolution fusion | flops 1209020416 | bytes 8389376 | tf_op jit(solution)/shard_map/tsn,sh->thn/dot_general | solution.py:23
  228.7 3.1 copy.106
  233.2 87.0 %all-reduce.3.cloned.1.call-done = bf16[3,96,128,128]{3,2,1,0:T(8,128)(2,1)} async-done(((bf16[3,96,128,128]{3,2,1,0:T(8,128)(2,1)}), bf16[3,96,128,128]{3,2,1,0:T(8,128)(2,1)}) %all-reduce.3.cloned.1.call-update) | async-done | bytes 9437200
  320.2 4.8 %fusion.80 = f32[3,12,128,128]{3,2,1,0:T(8,128)} fusion(f32[3,12,128,128]{3,2,1,0:T(8,128)S(1)} %copy-done.7, f32[3,12,128,128]{3,2,1,0:T(8,128)} %param.12, bf16[3,96,128,128]{3,2,1,0:T(8,128)(2,1)} %all-reduce.3.cloned.1.call-done, u32[]{:T(128)S(6)} %multiply.1, f32[3,12]{1,0:T(4,128)S(1)} %compare_convert_fusion), kind=kLoop, calls=%fused_computation.69 | loop fusion | flops 6488064 | bytes 8257684 | tf_op jit(solution)/shard_map/div | solution.py:108
  325.0 42.0 %reduce-scatter.8.cloned.1.call-done = bf16[128,2048]{1,0:T(8,128)(2,1)} async-done(((bf16[128,8192]{1,0:T(8,128)(2,1)}), bf16[128,2048]{1,0:T(8,128)(2,1)}) %reduce-scatter.8.cloned.1.call-update) | async-done | bytes 524304 | tf_op jit(solution)/shard_map/reduce_scatter | solution.py:99
  367.0 45.9 %reduce-scatter.6.cloned.1.call-done = bf16[128,2048]{1,0:T(8,128)(2,1)} async-done(((bf16[128,8192]{1,0:T(8,128)(2,1)}), bf16[128,2048]{1,0:T(8,128)(2,1)}) %reduce-scatter.6.cloned.1.call-update) | async-done | bytes 524304 | tf_op jit(solution)/shard_map/reduce_scatter | solution.py:63
  (45 shorter events, 8.1 us)
Async XLA Ops:
  7.2 4.3 %copy-start.8 = (s32[3,96,2]{1,2,0:T(2,128)S(1)}, s32[3,96,2]{1,2,0:T(2,128)}, u32[]{:S(2)}) copy-start(s32[3,96,2]{1,2,0:T(2,128)} %param.10) | copy-start | bytes 6916
  7.2 4.4 %copy-start.9 = (s32[1,3]{1,0:T(1,128)S(1)}, s32[1,3]{1,0:T(1,128)}, u32[]{:S(2)}) copy-start(s32[1,3]{1,0:T(1,128)} %param.11) | copy-start | bytes 40
  7.2 51.6 %all-gather.3.cloned.1.call-start = ((), (), s32[]{:S(2)}) async-start(), calls=%async_computation.2 | async-start | bytes 2621440 | tf_op jit(solution)/shard_map/all_gather | solution.py:43
  9.3 96.4 %all-gather.5.cloned.1.call-start = ((), (), s32[]{:S(2)}) async-start(), calls=%async_computation.4 | async-start | bytes 2621440 | tf_op jit(solution)/shard_map/all_gather | solution.py:66
  11.4 308.8 %all-reduce.3.cloned.1.call-start = ((), (), s32[]{:S(2)}) async-start(), calls=%async_computation.6 | async-start | bytes 18874368
  67.6 6.7 %copy-start.1 = (bf16[96,128,128]{2,1,0:T(8,128)(2,1)S(1)}, bf16[96,128,128]{2,1,0:T(8,128)(2,1)}, u32[]{:S(2)}) copy-start(bf16[96,128,128]{2,1,0:T(8,128)(2,1)} %gather_fusion.1) | copy-start | bytes 9437188
  112.5 5.3 %copy-start.3 = (bf16[96,128,128]{2,1,0:T(8,128)(2,1)}, bf16[96,128,128]{2,1,0:T(8,128)(2,1)S(1)}, u32[]{:S(2)}) copy-start(bf16[96,128,128]{2,1,0:T(8,128)(2,1)S(1)} %gather_fusion.3) | copy-start | bytes 9437188
  174.5 4.6 %copy-start.5 = (bf16[1,96,128,128]{3,2,1,0:T(8,128)(2,1)S(1)}, bf16[1,96,128,128]{3,2,1,0:T(8,128)(2,1)}, u32[]{:S(2)}) copy-start(bf16[1,96,128,128]{3,2,1,0:T(8,128)(2,1)} %fusion.12) | copy-start | bytes 9437188
  174.5 4.7 %copy-start.6 = (bf16[1,96,128,128]{3,2,1,0:T(8,128)(2,1)S(1)}, bf16[1,96,128,128]{3,2,1,0:T(8,128)(2,1)}, u32[]{:S(2)}) copy-start(bf16[1,96,128,128]{3,2,1,0:T(8,128)(2,1)} %fusion.13) | copy-start | bytes 9437188
  183.4 1.9 copy-start.4
  183.4 183.6 %reduce-scatter.8.cloned.1.call-start = ((), (), s32[]{:S(2)}) async-start(), calls=%async_computation.5 | async-start | bytes 2621440 | tf_op jit(solution)/shard_map/reduce_scatter | solution.py:99
  189.4 8.0 %copy-start.2 = (bf16[96,128,128]{2,1,0:T(8,128)(2,1)S(1)}, bf16[96,128,128]{2,1,0:T(8,128)(2,1)}, u32[]{:S(2)}) copy-start(bf16[96,128,128]{2,1,0:T(8,128)(2,1)} %gather_fusion.4) | copy-start | bytes 9437188
  212.2 3.3 copy-start
  215.4 197.5 %reduce-scatter.6.cloned.1.call-start = ((), (), s32[]{:S(2)}) async-start(), calls=%async_computation.3 | async-start | bytes 2621440 | tf_op jit(solution)/shard_map/reduce_scatter | solution.py:63
  228.7 3.2 copy-start.10
  228.7 91.5 %copy-start.7 = (f32[3,12,128,128]{3,2,1,0:T(8,128)S(1)}, f32[3,12,128,128]{3,2,1,0:T(8,128)}, u32[]{:S(2)}) copy-start(f32[3,12,128,128]{3,2,1,0:T(8,128)} %param.13) | copy-start | bytes 7077892
Sparse Core Ops, SparseCore 0:
  10.2 48.6 all-gather.2
  61.0 44.6 all-gather.4
  183.5 136.6 all-reduce.2
  323.0 43.9 reduce-scatter.7
  369.7 43.1 reduce-scatter.5
where the time goes:
time: 428 us; the launch traced here: 420 us
  waiting for transfers between devices  248 us (58%)
  matrix products  110 us (26%)
  local copies, waits for them, and re-layouts  36.7 us (9%)
  between operations  15.1 us (4%)
  other arithmetic  10.3 us (2%)
    unnamed x6, waiting for transfers between devices  87.1 us
    dot_general x6, matrix products, place(): jnp.einsum('tsn,sh->thn', products, select, preferred_element_type=jnp.fl...  54.5 us
    all_gather x1, waiting for transfers between devices, local(): inputs_full = lax.all_gather(inputs, 'tensor', axis=1, tiled=True)  47.2 us
    reduce_scatter x1, waiting for transfers between devices, local(): lax.psum_scatter(out_partial.astype(jnp.bfloat16), 'tensor', scatter_dime...  45.9 us
    reduce_scatter x1, waiting for transfers between devices, local(): lax.psum_scatter(input_partial.astype(jnp.bfloat16), 'tensor', scatter_di...  42 us
    dot_general x3, matrix products, block_grad(): jnp.einsum('tsk,tsn->skn', left_rows, right_rows, preferred_element_type=...  26.1 us
    all_gather x1, waiting for transfers between devices, local(): cotangent_full = lax.all_gather(out_grad, 'tensor', axis=1, tiled=True)  25.8 us
    dot_general x3, matrix products, block_rows(): jnp.einsum('tsk,skn->tsn', rows_in, blocks, preferred_element_type=jnp.fl...  15.2 us
  transfers between devices with their start and end apart: 5, of which 5 were waited for; matrix products, arithmetic and copies ran while one was open for 18% of the time, Pallas kernels for 0%

commit v1 on v0

v1 whole, which is shorter than its diff:
```python
import functools
import jax
import jax.numpy as jnp
from jax import lax
from jax.experimental import pallas as pl
from jax.experimental.pallas import tpu as pltpu
from jax.sharding import PartitionSpec as P

HB_DEV = 14
EPSILON = 1e-08
GROUP = 8
VMEM_LIMIT = 56 * 1024 * 1024


def group_of(capacity):
    return next(g for g in (GROUP, 4, 2, 1) if capacity % g == 0)


def feature_block(ref, block, size):
    per_shard = ref.shape[2] // size
    start = pl.multiple_of(lax.rem(block, per_shard) * size, size)
    return ref.at[lax.div(block, per_shard), :, pl.ds(start, size)]


def slot_pair(index_ref, matrix, slot, capacity):
    at = (matrix * capacity + slot) * 2
    return index_ref[at], index_ref[at + 1]


def each_group(count, group, body):
    def step(i, carry):
        body([i * group + u for u in range(group)])
        return carry

    lax.fori_loop(0, lax.div(count + (group - 1), group), step, 0)


def dot(a, b, contract):
    return lax.dot_general(a, b, ((contract[0], contract[1]), ((), ())), preferred_element_type=jnp.float32)


def forward_kernel(index_ref, count_ref, x_ref, w_ref, hidden_ref, act_ref, slope_ref, out_ref, gate, up, total):
    capacity, size = w_ref.shape[1], w_ref.shape[2]
    group = group_of(capacity)
    hidden_blocks = hidden_ref.shape[0]
    feature_blocks = x_ref.shape[0] * (x_ref.shape[2] // size)
    gate[...] = jnp.zeros_like(gate)
    up[...] = jnp.zeros_like(up)
    total[...] = jnp.zeros_like(total)
    for matrix, acc in ((0, gate), (1, up)):
        count = count_ref[matrix]

        def project(slots, matrix=matrix, acc=acc, count=count):
            products, targets = [], []
            for s in slots:
                f, h = slot_pair(index_ref, matrix, s, capacity)
                targets.append(jnp.where(s < count, h, hidden_blocks))
                products.append(dot(feature_block(x_ref, f, size)[...], w_ref[matrix, s], ((1,), (0,))))
            for h, p in zip(targets, products):
                acc[h] += p

        each_group(count, group, project)
    for h in range(hidden_blocks):
        g, u = gate[h], up[h]
        sig = 1.0 / (1.0 + jnp.exp(-g))
        act = g * sig
        act_ref[h] = act
        slope_ref[h] = u * sig * (1.0 + g * (1.0 - sig))
        hidden_ref[h] = (act * u).astype(hidden_ref.dtype)
    count = count_ref[2]

    def down(slots):
        products, targets = [], []
        for s in slots:
            f, h = slot_pair(index_ref, 2, s, capacity)
            targets.append(jnp.where(s < count, f, feature_blocks))
            products.append(dot(hidden_ref[h], w_ref[2, s], ((1,), (0,))))
        for f, p in zip(targets, products):
            total[f] += p

    each_group(count, group, down)
    for f in range(feature_blocks):
        feature_block(out_ref, f, size)[...] = total[f].astype(out_ref.dtype)


def rows_kernel(index_ref, count_ref, og_ref, w_ref, act_ref, slope_ref, gate_rows_ref, up_rows_ref, acc):
    capacity, size = w_ref.shape[1], w_ref.shape[2]
    group = group_of(capacity)
    hidden_blocks = act_ref.shape[0]
    acc[...] = jnp.zeros_like(acc)
    count = count_ref[2]

    def back(slots):
        products, targets = [], []
        for s in slots:
            f, h = slot_pair(index_ref, 2, s, capacity)
            targets.append(jnp.where(s < count, h, hidden_blocks))
            products.append(dot(feature_block(og_ref, f, size)[...], w_ref[2, s], ((1,), (1,))))
        for h, p in zip(targets, products):
            acc[h] += p

    each_group(count, group, back)
    for h in range(hidden_blocks):
        gate_rows_ref[h] = (acc[h] * slope_ref[h]).astype(gate_rows_ref.dtype)
        up_rows_ref[h] = (acc[h] * act_ref[h]).astype(up_rows_ref.dtype)


def grad_kernel(index_ref, count_ref, x_ref, og_ref, hidden_ref, gate_rows_ref, up_rows_ref, grad_ref):
    size = grad_ref.shape[2]
    share = grad_ref.shape[1]
    group = group_of(share)
    matrix, part = pl.program_id(0), pl.program_id(1)
    capacity = share * pl.num_programs(1)
    first = part * share
    live = jnp.clip(count_ref[matrix] - first, 0, share)

    def run(left, right):
        def body(slots):
            for s in slots:
                f, h = slot_pair(index_ref, matrix, first + s, capacity)
                grad_ref[0, s] = dot(left(f, h), right(f, h), ((0,), (0,))).astype(grad_ref.dtype)

        each_group(live, group, body)

    @pl.when(matrix == 0)
    def _():
        run(lambda f, h: feature_block(x_ref, f, size)[...], lambda f, h: gate_rows_ref[h])

    @pl.when(matrix == 1)
    def _():
        run(lambda f, h: feature_block(x_ref, f, size)[...], lambda f, h: up_rows_ref[h])

    @pl.when(matrix == 2)
    def _():
        run(lambda f, h: hidden_ref[h], lambda f, h: feature_block(og_ref, f, size)[...])


def input_kernel(index_ref, count_ref, gate_rows_ref, up_rows_ref, w_ref, out_ref, total):
    capacity, size = w_ref.shape[1], w_ref.shape[2]
    group = group_of(capacity)
    feature_blocks = out_ref.shape[0] * (out_ref.shape[2] // size)
    total[...] = jnp.zeros_like(total)
    for matrix, rows in ((0, gate_rows_ref), (1, up_rows_ref)):
        count = count_ref[matrix]

        def back(slots, matrix=matrix, rows=rows, count=count):
            products, targets = [], []
            for s in slots:
                f, h = slot_pair(index_ref, matrix, s, capacity)
                targets.append(jnp.where(s < count, f, feature_blocks))
                products.append(dot(rows[h], w_ref[matrix, s], ((1,), (1,))))
            for f, p in zip(targets, products):
                total[f] += p

        each_group(count, group, back)
    for f in range(feature_blocks):
        feature_block(out_ref, f, size)[...] = total[f].astype(out_ref.dtype)


SMEM = pl.BlockSpec(memory_space=pltpu.SMEM)
VMEM = pl.BlockSpec(memory_space=pltpu.VMEM)


def call(kernel, name, outs, scratch, *operands):
    return pl.pallas_call(
        kernel,
        name=name,
        out_shape=outs,
        in_specs=[SMEM, SMEM] + [VMEM] * (len(operands) - 2),
        out_specs=jax.tree.map(lambda _: VMEM, outs),
        scratch_shapes=scratch,
        compiler_params=pltpu.CompilerParams(vmem_limit_bytes=VMEM_LIMIT),
    )(*operands)


def forward(index, counts, x, w):
    shards, rows, width = x.shape
    size = w.shape[2]
    f32, bf16 = jnp.float32, jnp.bfloat16
    wide = jax.ShapeDtypeStruct((HB_DEV, rows, size), f32)
    outs = (
        jax.ShapeDtypeStruct((HB_DEV, rows, size), bf16),
        wide,
        wide,
        jax.ShapeDtypeStruct(x.shape, bf16),
    )
    acc = pltpu.VMEM((HB_DEV + 1, rows, size), f32)
    total = pltpu.VMEM((shards * width // size + 1, rows, size), f32)
    return call(forward_kernel, "forward", outs, [acc, acc, total], index, counts, x, w)


def row_grads(index, counts, og, w, act, slope):
    rows = og.shape[1]
    size = w.shape[2]
    out = jax.ShapeDtypeStruct((HB_DEV, rows, size), jnp.bfloat16)
    acc = pltpu.VMEM((HB_DEV + 1, rows, size), jnp.float32)
    return call(rows_kernel, "row_grads", (out, out), [acc], index, counts, og, w, act, slope)


def block_grads(index, counts, x, og, hidden, gate_rows, up_rows, capacity):
    size = hidden.shape[2]
    parts = next(p for p in (4, 3, 2, 1) if capacity % p == 0)
    return pl.pallas_call(
        grad_kernel,
        name="block_grads",
        grid=(3, parts),
        out_shape=jax.ShapeDtypeStruct((3, capacity, size, size), jnp.bfloat16),
        in_specs=[SMEM, SMEM] + [VMEM] * 5,
        out_specs=pl.BlockSpec((1, capacity // parts, size, size), lambda k, p: (k, p, 0, 0)),
        compiler_params=pltpu.CompilerParams(vmem_limit_bytes=VMEM_LIMIT),
    )(index, counts, x, og, hidden, gate_rows, up_rows)


def input_grads(index, counts, gate_rows, up_rows, w, like):
    rows, size = gate_rows.shape[1], w.shape[2]
    total = pltpu.VMEM((like.shape[0] * like.shape[2] // size + 1, rows, size), jnp.float32)
    return call(
        input_kernel, "input_grads", jax.ShapeDtypeStruct(like.shape, jnp.bfloat16), [total],
        index, counts, gate_rows, up_rows, w,
    )


def local(inputs, out_grad, weights, block_index, block_counts, first_moment, second_moment):
    capacity = weights.shape[1]
    index = block_index.reshape(-1)
    counts = block_counts[0]
    x = lax.all_gather(inputs, "tensor", axis=0)
    og = lax.all_gather(out_grad, "tensor", axis=0)
    hidden, act, slope, out_partial = forward(index, counts, x, weights)
    outputs = lax.psum_scatter(out_partial, "tensor", scatter_dimension=0)
    gate_rows, up_rows = row_grads(index, counts, og, weights, act, slope)
    grads = block_grads(index, counts, x, og, hidden, gate_rows, up_rows, capacity)
    shares = lax.psum_scatter(grads, "dp", scatter_dimension=1, tiled=True).astype(jnp.float32)
    input_partial = input_grads(index, counts, gate_rows, up_rows, weights, x)
    input_grad = lax.psum_scatter(input_partial, "tensor", scatter_dimension=0)
    share_rows = shares.shape[1]
    share_ids = lax.axis_index("dp") * share_rows + jnp.arange(share_rows, dtype=jnp.int32)
    live = (share_ids[None, :] < counts[:, None])[:, :, None, None]
    first_new = 0.9 * first_moment + 0.1 * shares
    second_new = 0.95 * second_moment + 0.05 * shares * shares
    update = jnp.where(live, first_new / (jnp.sqrt(second_new) + EPSILON), 0.0)
    return (outputs, input_grad, update)


def solution(mesh):
    in_specs = (
        P("dp", "tensor"),
        P("dp", "tensor"),
        P(None, "tensor", None, None),
        P(None, "tensor", None),
        P("tensor", None),
        P(None, ("tensor", "dp"), None, None),
        P(None, ("tensor", "dp"), None, None),
    )
    out_specs = (P("dp", "tensor"), P("dp", "tensor"), P(None, ("tensor", "dp"), None, None))
    return jax.shard_map(local, mesh=mesh, in_specs=in_specs, out_specs=out_specs, check_vma=False)
```

time: 428 us -> 364 us (0.85); the launches traced: 420 us -> 363 us
  matrix products: 110 us -> 0 us
  Pallas kernels: 0 us -> 50.1 us
  waiting for transfers between devices: 248 us -> 292 us
  local copies, waits for them, and re-layouts: 36.7 us -> 2.14 us
  other arithmetic: 10.3 us -> 4.97 us
    dot_general x15 -> x0, matrix products: 110 us -> none  [the longest x6 54.5 us: place(): jnp.einsum('tsn,sh->thn', products, select, preferred_element_type=jnp.fl...]
    pallas_call x0 -> x4, Pallas kernels: none -> 50.1 us  [the longest x3 36.4 us: call(): pl.pallas_call(kernel, name=name, out_shape=outs, in_specs=[SMEM, SMEM] +...]
    unnamed x6, waiting for transfers between devices: 87.1 us -> 124 us
    gather x6 -> x0, local copies, waits for them, and re-layouts: 16.4 us -> none  [the longest x1 2.76 us: local(): gate_inputs = input_blocks[:, block_index[0, :, 0], :]]
    unnamed x27 -> x8, local copies, waits for them, and re-layouts: 12.9 us -> 1.4 us
    all_gather x2, waiting for transfers between devices: 73 us -> 80 us  [the longest x1 48 us: local(): x = lax.all_gather(inputs, 'tensor', axis=0)]
    reshape x2 -> x1, local copies, waits for them, and re-layouts: 7.28 us -> 0.74 us  [local(): index = block_index.reshape(-1)]
    select_n x1, other arithmetic: 0.01 us -> 4.89 us  [local(): update = jnp.where(live, first_new / (jnp.sqrt(second_new) + EPSILON), 0.0)]
  transfers between devices with their start and end apart: 5 -> 5, of which waited for: 5 -> 5; matrix products, arithmetic and copies ran while one was open for 18% -> 2% of each run, Pallas kernels for 0% -> 7%
where the time goes in v1:
time: 364 us; the launch traced here: 363 us
  waiting for transfers between devices  292 us (80%)
  Pallas kernels  50.1 us (14%)
  between operations  14.5 us (4%)
  other arithmetic  4.97 us (1%)
    unnamed x6, waiting for transfers between devices  124 us
    all_gather x1, waiting for transfers between devices, local(): x = lax.all_gather(inputs, 'tensor', axis=0)  48 us
    reduce_scatter x1, waiting for transfers between devices, local(): input_grad = lax.psum_scatter(input_partial, 'tensor', scatter_dimension=0)  45.9 us
    reduce_scatter x1, waiting for transfers between devices, local(): outputs = lax.psum_scatter(out_partial, 'tensor', scatter_dimension=0)  41.9 us
    pallas_call x3, Pallas kernels, call(): pl.pallas_call(kernel, name=name, out_shape=outs, in_specs=[SMEM, SMEM] +...  36.4 us
    all_gather x1, waiting for transfers between devices, local(): og = lax.all_gather(out_grad, 'tensor', axis=0)  32 us
    pallas_call x1, Pallas kernels, block_grads(): pl.pallas_call(grad_kernel, name='block_grads', grid=(3, parts), out_shap...  13.6 us
  transfers between devices with their start and end apart: 5, of which 5 were waited for; matrix products, arithmetic and copies ran while one was open for 2% of the time, Pallas kernels for 7%

profile of v1, /device:TPU:0, one launch (start us, length us, event | category | flops | bytes accessed | tf_op | source)
XLA Modules:
  0.0 363.5 jit_solution(2182668403721249229)
XLA Ops:
  7.2 0.0 all-gather.5.cloned.1.call-start
  7.2 0.7 all-gather.5.cloned.1.call-update
  7.9 0.0 all-gather.7.cloned.1.call-start
  7.9 0.7 all-gather.7.cloned.1.call-update
  8.6 0.0 all-reduce.3.cloned.1.call-start
  8.7 0.8 copy.11
  9.5 0.7 reshape.44.index_ref
  10.2 48.0 %all-gather.5.cloned.1.call-done = bf16[512,2048]{1,0:T(8,128)(2,1)} async-done(((bf16[128,2048]{1,0:T(8,128)(2,1)}), bf16[512,2048]{1,0:T(8,128)(2,1)}) %all-gather.5.cloned.1.call-update) | async-done | bytes 2097168 | tf_op jit(solution)/shard_map/all_gather | solution.py:227
  58.2 14.2 %forward.1 = (bf16[14,128,128]{2,1,0:T(8,128)(2,1)}, f32[14,128,128]{2,1,0:T(8,128)}, f32[14,128,128]{2,1,0:T(8,128)}, bf16[4,128,2048]{2,1,0:T(8,128)(2,1)}) custom-call(s32[576]{0:T(1024)} %reshape.44.index_ref, s32[3]{0:T(128)} %bitcast.16, bf16[4,128,2048]{2,1,0:T(8,128)(2,1)} %bitcast.14, bf16[3,96,128,128]{3,2,1,0:T(8,128)(2,1)} %w_ref.5), custom_call_target="tpu_custom_call" | custom-call | tf_op jit(solution)/shard_map/forward/pallas_call | solution.py:165
  72.5 32.0 %all-gather.7.cloned.1.call-done = bf16[512,2048]{1,0:T(8,128)(2,1)} async-done(((bf16[128,2048]{1,0:T(8,128)(2,1)}), bf16[512,2048]{1,0:T(8,128)(2,1)}) %all-gather.7.cloned.1.call-update) | async-done | bytes 2097168 | tf_op jit(solution)/shard_map/all_gather | solution.py:228
  104.5 9.7 %row_grads.1 = (bf16[14,128,128]{2,1,0:T(8,128)(2,1)}, bf16[14,128,128]{2,1,0:T(8,128)(2,1)}) custom-call(s32[576]{0:T(1024)} %reshape.44.index_ref, s32[3]{0:T(128)} %bitcast.17, bf16[4,128,2048]{2,1,0:T(8,128)(2,1)} %bitcast.12, bf16[3,96,128,128]{3,2,1,0:T(8,128)(2,1)} %w_ref.5, f32[14,128,128]{2,1,0:T(8,128)} %get-tuple-element.10.act_ref, ...), custom_call_target="tpu_custom_call" | custom-call | tf_op jit(solution)/shard_map/row_grads/pallas_call | solution.py:165
  114.2 13.6 %block_grads.1 = bf16[3,96,128,128]{3,2,1,0:T(8,128)(2,1)} custom-call(s32[576]{0:T(1024)} %reshape.44.index_ref, s32[3]{0:T(128)} %bitcast.18, bf16[4,128,2048]{2,1,0:T(8,128)(2,1)} %bitcast.15, bf16[4,128,2048]{2,1,0:T(8,128)(2,1)} %bitcast.13, bf16[14,128,128]{2,1,0:T(8,128)(2,1)} %get-tuple-element.14.hidden_ref, ...), custom_call_target="tpu_custom_call" | custom-call | tf_op jit(solution)/shard_map/block_grads/pallas_call | solution.py:203
  127.8 0.0 all-reduce.3.cloned.1.call-update
  127.8 0.0 reduce-scatter.6.cloned.1.call-start
  127.9 0.5 reduce-scatter.6.cloned.1.call-update
  128.4 0.0 copy-start.2
  128.4 0.0 copy-start.1
  128.4 0.0 reduce-scatter.8.cloned.1.call-start
  128.5 0.0 copy-start
  128.5 12.5 %input_grads.1 = bf16[4,128,2048]{2,1,0:T(8,128)(2,1)} custom-call(s32[576]{0:T(1024)} %reshape.44.index_ref, s32[3]{0:T(128)} %bitcast.19, bf16[14,128,128]{2,1,0:T(8,128)(2,1)} %get-tuple-element.12.gate_rows_ref, bf16[14,128,128]{2,1,0:T(8,128)(2,1)} %get-tuple-element.13.up_rows_ref, bf16[3,96,128,128]{3,2,1,0:T(8,128)(2,1)} %w_ref.5), custom_call_target="tpu_custom_call" | custom-call | tf_op jit(solution)/shard_map/input_grads/pallas_call | solution.py:165
  141.0 0.0 reduce-scatter.8.cloned.1.call-update
  141.0 0.0 copy-done.2
  141.0 0.6 dynamic-slice
  142.3 0.0 copy-done.1
  142.3 0.1 broadcast_compare_fusion
  142.4 121.8 %all-reduce.3.cloned.1.call-done = bf16[3,96,128,128]{3,2,1,0:T(8,128)(2,1)} async-done(((bf16[3,96,128,128]{3,2,1,0:T(8,128)(2,1)}), bf16[3,96,128,128]{3,2,1,0:T(8,128)(2,1)}) %all-reduce.3.cloned.1.call-update) | async-done | bytes 9437200
  264.2 0.0 copy-done
  264.2 4.9 %fusion.2 = f32[3,12,128,128]{3,2,1,0:T(8,128)} fusion(f32[3,12,128,128]{3,2,1,0:T(8,128)S(1)} %copy-done, f32[3,12,128,128]{3,2,1,0:T(8,128)} %param.12, bf16[3,96,128,128]{3,2,1,0:T(8,128)(2,1)} %all-reduce.3.cloned.1.call-done, u32[]{:T(128)S(6)} %multiply.1, pred[3,12]{1,0:T(4,128)(4,1)S(1)} %broadcast_compare_fusion), kind=kLoop, calls=%fused_computation.4 | loop fusion | flops 6488064 | bytes 8257576 | tf_op jit(solution)/shard_map/jit(_where)/select_n | solution.py:241
  269.1 41.9 %reduce-scatter.6.cloned.1.call-done = bf16[1,128,2048]{2,1,0:T(8,128)(2,1)} async-done(((bf16[4,128,2048]{2,1,0:T(8,128)(2,1)}), bf16[1,128,2048]{2,1,0:T(8,128)(2,1)}) %reduce-scatter.6.cloned.1.call-update) | async-done | bytes 524304 | tf_op jit(solution)/shard_map/reduce_scatter | solution.py:230
  311.0 45.9 %reduce-scatter.8.cloned.1.call-done = bf16[1,128,2048]{2,1,0:T(8,128)(2,1)} async-done(((bf16[4,128,2048]{2,1,0:T(8,128)(2,1)}), bf16[1,128,2048]{2,1,0:T(8,128)(2,1)}) %reduce-scatter.8.cloned.1.call-update) | async-done | bytes 524304 | tf_op jit(solution)/shard_map/reduce_scatter | solution.py:235
  (1 shorter events, 0.0 us)
Async XLA Ops:
  7.2 51.1 %all-gather.5.cloned.1.call-start = ((), (), s32[]{:S(2)}) async-start(), calls=%async_computation.4 | async-start | bytes 2621440 | tf_op jit(solution)/shard_map/all_gather | solution.py:227
  7.9 96.6 %all-gather.7.cloned.1.call-start = ((), (), s32[]{:S(2)}) async-start(), calls=%async_computation.5 | async-start | bytes 2621440 | tf_op jit(solution)/shard_map/all_gather | solution.py:228
  8.6 255.6 %all-reduce.3.cloned.1.call-start = ((), (), s32[]{:S(2)}) async-start(), calls=%async_computation.6 | async-start | bytes 18874368
  127.8 183.2 %reduce-scatter.6.cloned.1.call-start = ((), (), s32[]{:S(2)}) async-start(), calls=%async_computation.2 | async-start | bytes 2621440 | tf_op jit(solution)/shard_map/reduce_scatter | solution.py:230
  128.4 12.6 %copy-start.2 = (u32[32]{0:T(128)S(1)}, u32[32]{0:T(128)}, u32[]{:S(2)}) copy-start(u32[32]{0:T(128)} %constant.25) | copy-start | bytes 388
  128.4 13.9 %copy-start.1 = (s32[1,3]{1,0:T(1,128)S(1)}, s32[1,3]{1,0:T(1,128)}, u32[]{:S(2)}) copy-start(s32[1,3]{1,0:T(1,128)} %param.11) | copy-start | bytes 40
  128.4 228.5 %reduce-scatter.8.cloned.1.call-start = ((), (), s32[]{:S(2)}) async-start(), calls=%async_computation.3 | async-start | bytes 2621440 | tf_op jit(solution)/shard_map/reduce_scatter | solution.py:235
  128.5 135.7 %copy-start = (f32[3,12,128,128]{3,2,1,0:T(8,128)S(1)}, f32[3,12,128,128]{3,2,1,0:T(8,128)}, u32[]{:S(2)}) copy-start(f32[3,12,128,128]{3,2,1,0:T(8,128)} %param.13) | copy-start | bytes 7077892
Sparse Core Ops, SparseCore 0:
  9.6 48.6 all-gather.4
  59.8 44.6 all-gather.6
  127.9 136.2 all-reduce.2
  267.0 43.9 reduce-scatter.5
  313.7 43.1 reduce-scatter.7

commit v2 on v1

v2 whole, which is shorter than its diff:
```python
import functools
import jax
import jax.numpy as jnp
from jax import lax
from jax.experimental import pallas as pl
from jax.experimental.pallas import tpu as pltpu
from jax.sharding import PartitionSpec as P

HB_DEV = 14
EPSILON = 1e-08
GROUP = 8
VMEM_LIMIT = 32 * 1024 * 1024


def group_of(capacity):
    return next(g for g in (GROUP, 4, 2, 1) if capacity % g == 0)


def feature_block(ref, block, size):
    per_shard = ref.shape[2] // size
    start = pl.multiple_of(lax.rem(block, per_shard) * size, size)
    return ref.at[lax.div(block, per_shard), :, pl.ds(start, size)]


def slot_pair(index_ref, matrix, slot, capacity):
    at = (matrix * capacity + slot) * 2
    return index_ref[at], index_ref[at + 1]


def each_group(count, group, body):
    def step(i, carry):
        body([i * group + u for u in range(group)])
        return carry

    lax.fori_loop(0, lax.div(count + (group - 1), group), step, 0)


def dot(a, b, contract):
    return lax.dot_general(a, b, ((contract[0], contract[1]), ((), ())), preferred_element_type=jnp.float32)


def load_shards(pieces, held, me):
    if len(pieces) == 1:
        return pieces[0]
    own, below, above, across, far = pieces
    last = held.shape[0] - 1
    held[me] = own[...]
    held[lax.bitwise_xor(me, 2)] = across[...]

    @pl.when(me > 0)
    def _():
        held[me - 1] = below[...]

    @pl.when(me < last)
    def _():
        held[me + 1] = above[...]

    @pl.when((me == 0) | (me == last))
    def _():
        held[last - me] = far[...]

    return held


def load_matrices(weights, held, sems, matrices):
    copies = [pltpu.make_async_copy(weights.at[k], held.at[i], sems.at[i]) for i, k in enumerate(matrices)]
    for copy in copies:
        copy.start()
    return [copy.wait for copy in copies]


def store_shards(total, outs, me, per_shard, size):
    if len(outs) == 1:
        shards = range(outs[0].shape[0])
        places = [(outs[0].at[t], t) for t in shards]
    else:
        last = len(outs) - 2
        own, below, above, across, far = outs
        places = [
            (own, me),
            (below, jnp.maximum(me - 1, 0)),
            (above, jnp.minimum(me + 1, last)),
            (across, lax.bitwise_xor(me, 2)),
            (far, last - me),
        ]
    for out, t in places:
        for c in range(per_shard):
            out[:, c * size : (c + 1) * size] = total[t * per_shard + c].astype(out.dtype)


def forward_kernel(n_pieces, n_outs, me_ref, index_ref, count_ref, *refs):
    pieces, refs = refs[:n_pieces], refs[n_pieces:]
    weights, hidden_ref, act_ref, slope_ref = refs[:4]
    outs, (held, w_ref, sems, gate, up, total) = refs[4 : 4 + n_outs], refs[4 + n_outs :]
    me = me_ref[0]
    ready = load_matrices(weights, w_ref, sems, (0, 1, 2))
    x_ref = load_shards(pieces, held, me)
    capacity, size = w_ref.shape[1], w_ref.shape[2]
    group = group_of(capacity)
    hidden_blocks = hidden_ref.shape[0]
    per_shard = x_ref.shape[2] // size
    feature_blocks = x_ref.shape[0] * per_shard
    gate[...] = jnp.zeros_like(gate)
    up[...] = jnp.zeros_like(up)
    total[...] = jnp.zeros_like(total)
    for matrix, acc in ((0, gate), (1, up)):
        count = count_ref[matrix]
        ready[matrix]()

        def project(slots, matrix=matrix, acc=acc, count=count):
            products, targets = [], []
            for s in slots:
                f, h = slot_pair(index_ref, matrix, s, capacity)
                targets.append(jnp.where(s < count, h, hidden_blocks))
                products.append(dot(feature_block(x_ref, f, size)[...], w_ref[matrix, s], ((1,), (0,))))
            for h, p in zip(targets, products):
                acc[h] += p

        each_group(count, group, project)
    for h in range(hidden_blocks):
        g, u = gate[h], up[h]
        sig = 1.0 / (1.0 + jnp.exp(-g))
        act = g * sig
        act_ref[h] = act
        slope_ref[h] = u * sig * (1.0 + g * (1.0 - sig))
        hidden_ref[h] = (act * u).astype(hidden_ref.dtype)
    count = count_ref[2]
    ready[2]()

    def down(slots):
        products, targets = [], []
        for s in slots:
            f, h = slot_pair(index_ref, 2, s, capacity)
            targets.append(jnp.where(s < count, f, feature_blocks))
            products.append(dot(hidden_ref[h], w_ref[2, s], ((1,), (0,))))
        for f, p in zip(targets, products):
            total[f] += p

    each_group(count, group, down)
    store_shards(total, outs, me, per_shard, size)


def rows_kernel(n_pieces, me_ref, index_ref, count_ref, *refs):
    pieces, refs = refs[:n_pieces], refs[n_pieces:]
    act_ref, slope_ref, weights, gate_rows_ref, up_rows_ref, held, w_ref, sems, acc = refs
    (ready,) = load_matrices(weights, w_ref, sems, (2,))
    og_ref = load_shards(pieces, held, me_ref[0])
    capacity, size = w_ref.shape[1], w_ref.shape[2]
    group = group_of(capacity)
    hidden_blocks = act_ref.shape[0]
    acc[...] = jnp.zeros_like(acc)
    count = count_ref[2]
    ready()

    def back(slots):
        products, targets = [], []
        for s in slots:
            f, h = slot_pair(index_ref, 2, s, capacity)
            targets.append(jnp.where(s < count, h, hidden_blocks))
            products.append(dot(feature_block(og_ref, f, size)[...], w_ref[0, s], ((1,), (1,))))
        for h, p in zip(targets, products):
            acc[h] += p

    each_group(count, group, back)
    for h in range(hidden_blocks):
        gate_rows_ref[h] = (acc[h] * slope_ref[h]).astype(gate_rows_ref.dtype)
        up_rows_ref[h] = (acc[h] * act_ref[h]).astype(up_rows_ref.dtype)


def grads_kernel(matrix, n_pieces, me_ref, index_ref, count_ref, *refs):
    pieces, refs = refs[:n_pieces], refs[n_pieces:]
    rows_ref, keep_ref, send_ref, held = refs
    size, share = keep_ref.shape[2], keep_ref.shape[1]
    places = keep_ref.shape[0]
    replica = me_ref[1]
    tok_ref = load_shards(pieces, held, me_ref[0])
    capacity = 2 * places * share
    count = count_ref[matrix]
    for out, bit in ((send_ref, 1), (keep_ref, 0)):

        def one_place(q, carry, out=out, bit=bit):
            first = lax.bitwise_xor(replica, 2 * q + bit) * share

            @pl.when(first < count)
            def _():
                for s in range(share):
                    f, h = slot_pair(index_ref, matrix, first + s, capacity)
                    tok = feature_block(tok_ref, f, size)[...]
                    row = rows_ref[h]
                    left, right = (row, tok) if matrix == 2 else (tok, row)
                    out[q, s] = dot(left, right, ((0,), (0,))).astype(out.dtype)

            return carry

        lax.fori_loop(0, places, one_place, 0)


def input_kernel(n_outs, me_ref, index_ref, count_ref, gate_rows_ref, up_rows_ref, weights, *refs):
    outs, (w_ref, sems, total) = refs[:n_outs], refs[n_outs:]
    ready = load_matrices(weights, w_ref, sems, (0, 1))
    capacity, size = w_ref.shape[1], w_ref.shape[2]
    group = group_of(capacity)
    feature_blocks = total.shape[0] - 1
    per_shard = outs[0].shape[-1] // size
    total[...] = jnp.zeros_like(total)
    for matrix, rows in ((0, gate_rows_ref), (1, up_rows_ref)):
        count = count_ref[matrix]
        ready[matrix]()

        def back(slots, matrix=matrix, rows=rows, count=count):
            products, targets = [], []
            for s in slots:
                f, h = slot_pair(index_ref, matrix, s, capacity)
                targets.append(jnp.where(s < count, f, feature_blocks))
                products.append(dot(rows[h], w_ref[matrix, s], ((1,), (1,))))
            for f, p in zip(targets, products):
                total[f] += p

        each_group(count, group, back)
    store_shards(total, outs, me_ref[0], per_shard, size)


SMEM = pl.BlockSpec(memory_space=pltpu.SMEM)
VMEM = pl.BlockSpec(memory_space=pltpu.VMEM)
ANY = pl.BlockSpec(memory_space=pl.ANY)


def call(kernel, name, outs, scratch, scalars, operands, weights=()):
    return pl.pallas_call(
        kernel,
        name=name,
        out_shape=outs,
        in_specs=[SMEM] * len(scalars) + [VMEM] * len(operands) + [ANY] * len(weights),
        out_specs=jax.tree.map(lambda _: VMEM, outs),
        scratch_shapes=scratch,
        compiler_params=pltpu.CompilerParams(vmem_limit_bytes=VMEM_LIMIT),
    )(*scalars, *operands, *weights)


def matrices_held(count, weights):
    return [pltpu.VMEM((count, *weights.shape[1:]), weights.dtype), pltpu.SemaphoreType.DMA((count,))]


def parts_of(shards, rows, width):
    if shards == 4:
        return [jax.ShapeDtypeStruct((rows, width), jnp.bfloat16)] * 5
    return [jax.ShapeDtypeStruct((shards, rows, width), jnp.bfloat16)]


def gather_line(v, shards):
    if shards != 4:
        return [lax.all_gather(v, "tensor", axis=0)]
    across = lax.ppermute(v, "tensor", [(a, a ^ 2) for a in range(4)])
    below = lax.ppermute(v, "tensor", [(a, a + 1) for a in range(3)])
    above = lax.ppermute(v, "tensor", [(a + 1, a) for a in range(3)])
    far = lax.ppermute(across, "tensor", [(2, 3), (1, 0)])
    return [v, below, above, across, far]


def scatter_line(parts):
    if len(parts) == 1:
        return lax.psum_scatter(parts[0], "tensor", scatter_dimension=0)
    own, below, above, across, far = parts
    far = lax.ppermute(far, "tensor", [(3, 2), (0, 1)])
    below = lax.ppermute(below, "tensor", [(a + 1, a) for a in range(3)])
    above = lax.ppermute(above, "tensor", [(a, a + 1) for a in range(3)])
    across = lax.ppermute(across + far, "tensor", [(a, a ^ 2) for a in range(4)])
    wide = [p.astype(jnp.float32) for p in (own, below, above, across)]
    return (wide[0] + wide[1] + wide[2] + wide[3]).astype(jnp.bfloat16)


def swap(v, replicas, bit):
    return lax.ppermute(v, "dp", [(a, a ^ bit) for a in range(replicas)])


def replica_sum(keep, send, replicas):
    total = keep + swap(send, replicas, 1)
    levels = (replicas // 2).bit_length() - 1
    share = keep.shape[1]
    cut = share // 2
    rest = keep.shape[1:]
    total = total.reshape((2,) * levels + rest)
    halves = []
    for part, order in ((total[..., :cut, :, :], range(levels)), (total[..., cut:, :, :], reversed(range(levels)))):
        done = []
        for level in order:
            axis = levels - 1 - level
            axis -= sum(1 for d in done if d > level)
            mine = lax.index_in_dim(part, 0, axis, keepdims=False)
            theirs = lax.index_in_dim(part, 1, axis, keepdims=False)
            got = swap(theirs, replicas, 2 << level)
            done.append(level)
            if len(done) == levels:
                part = mine.astype(jnp.float32) + got.astype(jnp.float32)
            else:
                part = mine + got
        halves.append(part)
    return jnp.concatenate(halves, axis=0)


def local(replicas, shards, inputs, out_grad, weights, block_index, block_counts, first_moment, second_moment):
    capacity, size = weights.shape[1], weights.shape[2]
    rows, width = inputs.shape
    f32, bf16 = jnp.float32, jnp.bfloat16
    shape = jax.ShapeDtypeStruct
    counts = block_counts[0]
    me = jnp.stack([lax.axis_index("tensor"), lax.axis_index("dp")]).astype(jnp.int32)
    scalars = (me, block_index.reshape(-1), counts)
    features = shards * width // size
    x = gather_line(inputs, shards)
    og = gather_line(out_grad, shards)
    parts = parts_of(shards, rows, width)
    held = pltpu.VMEM((shards, rows, width), bf16)
    wide = shape((HB_DEV, rows, size), f32)
    narrow = shape((HB_DEV, rows, size), bf16)
    acc = pltpu.VMEM((HB_DEV + 1, rows, size), f32)
    total = pltpu.VMEM((features + 1, rows, size), f32)
    hidden, act, slope, *out_parts = call(
        functools.partial(forward_kernel, len(x), len(parts)),
        "forward",
        [narrow, wide, wide, *parts],
        [held, *matrices_held(3, weights), acc, acc, total],
        scalars,
        x,
        [weights],
    )
    outputs = scatter_line(out_parts)
    places, share = replicas // 2, capacity // replicas
    half = shape((places, share, size, size), bf16)

    def grads(matrix, tok, row):
        keep, send = call(
            functools.partial(grads_kernel, matrix, len(tok)), ("gate_grads", "up_grads", "down_grads")[matrix],
            [half, half], [held], scalars, [*tok, row],
        )
        return replica_sum(keep, send, replicas)

    down_grad = grads(2, og, hidden)
    gate_rows, up_rows = call(
        functools.partial(rows_kernel, len(og)), "row_grads", [narrow, narrow],
        [held, *matrices_held(1, weights), acc], scalars, [*og, act, slope], [weights],
    )
    gate_grad = grads(0, x, gate_rows)
    in_parts = call(
        functools.partial(input_kernel, len(parts)), "input_grads", parts, [*matrices_held(2, weights), total],
        scalars, [gate_rows, up_rows], [weights],
    )
    input_grad = scatter_line(in_parts)
    up_grad = grads(1, x, up_rows)
    share_ids = lax.axis_index("dp") * share + jnp.arange(share, dtype=jnp.int32)
    updates = []
    for matrix, g in enumerate((gate_grad, up_grad, down_grad)):
        live = (share_ids < counts[matrix])[:, None, None]
        first_new = 0.9 * first_moment[matrix] + 0.1 * g
        second_new = 0.95 * second_moment[matrix] + 0.05 * g * g
        updates.append(jnp.where(live, first_new / (jnp.sqrt(second_new) + EPSILON), 0.0))
    return (outputs, input_grad, jnp.stack(updates))


def solution(mesh):
    in_specs = (
        P("dp", "tensor"),
        P("dp", "tensor"),
        P(None, "tensor", None, None),
        P(None, "tensor", None),
        P("tensor", None),
        P(None, ("tensor", "dp"), None, None),
        P(None, ("tensor", "dp"), None, None),
    )
    out_specs = (P("dp", "tensor"), P("dp", "tensor"), P(None, ("tensor", "dp"), None, None))
    body = functools.partial(local, mesh.shape["dp"], mesh.shape["tensor"])
    return jax.shard_map(body, mesh=mesh, in_specs=in_specs, out_specs=out_specs, check_vma=False)
```

time: 364 us -> 226 us (0.62); the launches traced: 363 us -> 221 us
  waiting for transfers between devices: 292 us -> 104 us
  starting transfers between devices: 0.19 us -> 53.4 us
  between operations: 14.5 us -> 1.23 us
  Pallas kernels: 50.1 us -> 38.8 us
  other arithmetic: 4.97 us -> 14.4 us
  local copies, waits for them, and re-layouts: 2.14 us -> 9.19 us
    unnamed x6 -> x0, waiting for transfers between devices: 124 us -> none
    ppermute x0 -> x31, waiting for transfers between devices: none -> 104 us  [the longest x2 38.2 us: gather_line(): across = lax.ppermute(v, 'tensor', [(a, a ^ 2) for a in range(4)])]
    reduce_scatter x2 -> x0, waiting for transfers between devices: 87.8 us -> none  [the longest x1 45.9 us: local(): input_grad = lax.psum_scatter(input_partial, 'tensor', scatter_dimension=0)]
    all_gather x2 -> x0, waiting for transfers between devices: 80 us -> none  [the longest x1 48 us: local(): x = lax.all_gather(inputs, 'tensor', axis=0)]
    ppermute x0 -> x31, starting transfers between devices: none -> 53.4 us  [the longest x15 16.4 us: swap(): return lax.ppermute(v, 'dp', [(a, a ^ bit) for a in range(replicas)])]
    pallas_call x4 -> x6, Pallas kernels: 50.1 us -> 38.8 us  [call(): pl.pallas_call(kernel, name=name, out_shape=outs, in_specs=[SMEM] * len(s...]
    unnamed x8 -> x55, local copies, waits for them, and re-layouts: 1.4 us -> 8.23 us
    convert_element_type x0 -> x2, other arithmetic: none -> 4.65 us  [scatter_line(): return (wide[0] + wide[1] + wide[2] + wide[3]).astype(jnp.bfloat16)]
  transfers between devices with their start and end apart: 5 -> 31, of which waited for: 5 -> 18; matrix products, arithmetic and copies ran while one was open for 2% -> 6% of each run, Pallas kernels for 7% -> 18%
where the time goes in v2:
time: 226 us; the launch traced here: 221 us
  waiting for transfers between devices  104 us (46%)
  starting transfers between devices  53.4 us (24%)
  Pallas kernels  38.8 us (17%)
  other arithmetic  14.4 us (6%)
  local copies, waits for them, and re-layouts  9.19 us (4%)
    pallas_call x6, Pallas kernels, call(): pl.pallas_call(kernel, name=name, out_shape=outs, in_specs=[SMEM] * len(s...  38.8 us
    ppermute x2, waiting for transfers between devices, gather_line(): across = lax.ppermute(v, 'tensor', [(a, a ^ 2) for a in range(4)])  38.2 us
    ppermute x2, waiting for transfers between devices, scatter_line(): lax.ppermute(across + far, 'tensor', [(a, a ^ 2) for a in range(4)])  25.8 us
    ppermute x15, waiting for transfers between devices, swap(): return lax.ppermute(v, 'dp', [(a, a ^ bit) for a in range(replicas)])  23.2 us
    ppermute x15, starting transfers between devices, swap(): return lax.ppermute(v, 'dp', [(a, a ^ bit) for a in range(replicas)])  16.4 us
    ppermute x2, waiting for transfers between devices, scatter_line(): below = lax.ppermute(below, 'tensor', [(a + 1, a) for a in range(3)])  11.5 us
    ppermute x2, starting transfers between devices, scatter_line(): above = lax.ppermute(above, 'tensor', [(a, a + 1) for a in range(3)])  8.99 us
    unnamed x55, local copies, waits for them, and re-layouts  8.23 us
  transfers between devices with their start and end apart: 31, of which 18 were waited for; matrix products, arithmetic and copies ran while one was open for 6% of the time, Pallas kernels for 18%

profile of v2, /device:TPU:0, one launch (start us, length us, event | category | flops | bytes accessed | tf_op | source)
XLA Modules:
  0.0 221.1 jit_solution(14395457848428801686)
XLA Ops:
  0.6 4.1 %collective-permute-start.2 = (bf16[128,2048]{1,0:T(8,128)(2,1)}, bf16[128,2048]{1,0:T(8,128)(2,1)S(1)}, u32[]{:S(2)}, u32[]{:S(2)}) collective-permute-start(bf16[128,2048]{1,0:T(8,128)(2,1)} %refs_0_.8), channel_id=1, source_target_pairs={{0,2},{1,3},{2,0},{3,1},{4,6},{5,7},{6,4},{7,5},{8,10},{9,11},{10,... | collective-permute-start | bytes 1572872 | tf_op jit(solution)/shard_map/ppermute | solution.py:253
  6.1 4.6 %collective-permute-start = (bf16[128,2048]{1,0:T(8,128)(2,1)}, bf16[128,2048]{1,0:T(8,128)(2,1)S(1)}, u32[]{:S(2)}, u32[]{:S(2)}) collective-permute-start(bf16[128,2048]{1,0:T(8,128)(2,1)} %refs_0_.8), channel_id=1, source_target_pairs={{0,1},{1,2},{2,3},{4,5},{5,6},{6,7},{8,9},{9,10},{10,11},{12,13},{... | collective-permute-start | bytes 1572872 | tf_op jit(solution)/shard_map/ppermute | solution.py:254
  10.7 29.5 %collective-permute-done.2.refs_3_ = bf16[128,2048]{1,0:T(8,128)(2,1)S(1)} collective-permute-done((bf16[128,2048]{1,0:T(8,128)(2,1)}, bf16[128,2048]{1,0:T(8,128)(2,1)S(1)}, u32[]{:S(2)}, u32[]{:S(2)}) %collective-permute-start.2) | collective-permute-done | bytes 524320 | tf_op jit(solution)/shard_map/ppermute | solution.py:253
  42.8 8.7 %collective-permute-done.10.refs_3_ = bf16[128,2048]{1,0:T(8,128)(2,1)S(1)} collective-permute-done((bf16[128,2048]{1,0:T(8,128)(2,1)}, bf16[128,2048]{1,0:T(8,128)(2,1)S(1)}, u32[]{:S(2)}, u32[]{:S(2)}) %collective-permute-start.10) | collective-permute-done | bytes 524320 | tf_op jit(solution)/shard_map/ppermute | solution.py:253
  51.4 2.8 %collective-permute-start.8 = (bf16[128,2048]{1,0:T(8,128)(2,1)}, bf16[128,2048]{1,0:T(8,128)(2,1)}, u32[]{:S(2)}, u32[]{:S(2)}) collective-permute-start(bf16[128,2048]{1,0:T(8,128)(2,1)} %refs_0_.9), channel_id=1, source_target_pairs={{0,1},{1,2},{2,3},{4,5},{5,6},{6,7},{8,9},{9,10},{10,11},{12,13},{... | collective-permute-start | bytes 1572872 | tf_op jit(solution)/shard_map/ppermute | solution.py:254
  56.6 5.3 %collective-permute-done.3.refs_4_ = bf16[128,2048]{1,0:T(8,128)(2,1)S(1)} collective-permute-done((bf16[128,2048]{1,0:T(8,128)(2,1)S(1)}, bf16[128,2048]{1,0:T(8,128)(2,1)S(1)}, u32[]{:S(2)}, u32[]{:S(2)}) %collective-permute-start.3) | collective-permute-done | bytes 524320 | tf_op jit(solution)/shard_map/ppermute | solution.py:256
  61.9 3.7 %copy-done = bf16[3,96,128,128]{3,2,1,0:T(8,128)(2,1)S(1)} copy-done((bf16[3,96,128,128]{3,2,1,0:T(8,128)(2,1)S(1)}, bf16[3,96,128,128]{3,2,1,0:T(8,128)(2,1)}, u32[]{:S(2)}) %copy-start) | copy-done | bytes 9437208
  67.3 11.7 %forward.1 = (bf16[14,128,128]{2,1,0:T(8,128)(2,1)S(1)}, f32[14,128,128]{2,1,0:T(8,128)S(1)}, f32[14,128,128]{2,1,0:T(8,128)S(1)}, bf16[128,2048]{1,0:T(8,128)(2...) custom-call(s32[2]{0:T(128)S(1)} %pad_add_fusion.me_ref, ...), custom_call_target="tpu_custom_call" | custom-call | tf_op jit(solution)/shard_map/forward/pallas_call | solution.py:229
  79.0 5.2 %collective-permute-start.6 = (bf16[128,2048]{1,0:T(8,128)(2,1)S(1)}, bf16[128,2048]{1,0:T(8,128)(2,1)S(1)}, u32[]{:S(2)}, u32[]{:S(2)}) collective-permute-start(bf16[128,2048]{1,0:T(8,128)(2,1)S(1)} %get-tuple-element.28), channel_id=1, source_target_pairs={{3,2},{0,1},{7,6},{4,5},{11,10},{8,9},{15,14},{12,13},{19,18},{16,... | collective-permute-start | bytes 1572872 | tf_op jit(solution)/shard_map/ppermute | solution.py:264
  84.4 5.2 %row_grads.1 = (bf16[14,128,128]{2,1,0:T(8,128)(2,1)S(1)}, bf16[14,128,128]{2,1,0:T(8,128)(2,1)S(1)}) custom-call(s32[2]{0:T(128)S(1)} %pad_add_fusion.me_ref, s32[576]{0:T(1024)S(1)} %reshape.296.index_ref, s32[3]{0:T(128)S(1)} %bitcast.106, bf16[128,2048]{1,0:T(8,128)(2,1)S(1)} %copy-done.4, bf16[128,2048]{1,0:T(8,128)(2,1)} %collective-permute-done.8.refs_1_, ...), custom_call_target="tpu_custom_call" | custom-call | tf_op jit(solution)/shard_map/row_grads/pallas_call | solution.py:229
  89.7 9.9 %input_grads.1 = (bf16[128,2048]{1,0:T(8,128)(2,1)S(1)}, bf16[128,2048]{1,0:T(8,128)(2,1)}, bf16[128,2048]{1,0:T(8,128)(2,1)S(1)}, bf16[128,2048]{1,0:T(8,128)(2,1)S(1)}, bf16[128,2048]{1,0:T(8,128)(2,1)S(1)}) custom-call(s32[2]{0:T(128)S(1)} %pad_add_fusion.me_ref, s32[576]{0:T(1024)S(1)} %reshape.296.index_ref, s32[3]{0:T(128)S(1)} %bitcast.107, ...), custom_call_target="tpu_custom_call" | custom-call | tf_op jit(solution)/shard_map/input_grads/pallas_call | solution.py:229
  102.2 5.3 %collective-permute-start.5 = (bf16[128,2048]{1,0:T(8,128)(2,1)}, bf16[128,2048]{1,0:T(8,128)(2,1)}, u32[]{:S(2)}, u32[]{:S(2)}) collective-permute-start(bf16[128,2048]{1,0:T(8,128)(2,1)} %get-tuple-element.26), channel_id=1, source_target_pairs={{0,1},{1,2},{2,3},{4,5},{5,6},{6,7},{8,9},{9,10},{10,11},{12,13},{... | collective-permute-start | bytes 1572872 | tf_op jit(solution)/shard_map/ppermute | solution.py:266
  108.9 5.1 %down_grads.1 = (bf16[4,12,128,128]{3,2,1,0:T(8,128)(2,1)S(1)}, bf16[4,12,128,128]{3,2,1,0:T(8,128)(2,1)}) custom-call(s32[2]{0:T(128)S(1)} %pad_add_fusion.me_ref, s32[576]{0:T(1024)S(1)} %reshape.296.index_ref, s32[3]{0:T(128)S(1)} %bitcast.108, bf16[128,2048]{1,0:T(8,128)(2,1)S(1)} %copy-done.4, bf16[128,2048]{1,0:T(8,128)(2,1)} %collective-permute-done.8.refs_1_, ...), custom_call_target="tpu_custom_call" | custom-call | tf_op jit(solution)/shard_map/down_grads/pallas_call | solution.py:229
  120.2 3.4 %gate_grads.1 = (bf16[4,12,128,128]{3,2,1,0:T(8,128)(2,1)S(1)}, bf16[4,12,128,128]{3,2,1,0:T(8,128)(2,1)S(1)}) custom-call(s32[2]{0:T(128)S(1)} %pad_add_fusion.me_ref, s32[576]{0:T(1024)S(1)} %reshape.296.index_ref, s32[3]{0:T(128)S(1)} %bitcast.109, bf16[128,2048]{1,0:T(8,128)(2,1)S(1)} %copy-done.3, bf16[128,2048]{1,0:T(8,128)(2,1)S(1)} %collective-permute-done.refs_1_, ...), custom_call_target="tpu_custom_call" | custom-call | tf_op jit(solution)/shard_map/gate_grads/pallas_call | solution.py:229
  123.8 3.7 %collective-permute-start.13 = (bf16[128,2048]{1,0:T(8,128)(2,1)S(1)}, bf16[128,2048]{1,0:T(8,128)(2,1)S(1)}, u32[]{:S(2)}, u32[]{:S(2)}) collective-permute-start(bf16[128,2048]{1,0:T(8,128)(2,1)S(1)} %copy-done.22), channel_id=1, source_target_pairs={{0,1},{1,2},{2,3},{4,5},{5,6},{6,7},{8,9},{9,10},{10,11},{12,13},{... | collective-permute-start | bytes 1572872 | tf_op jit(solution)/shard_map/ppermute | solution.py:266
  127.5 11.4 %collective-permute-done.12 = bf16[128,2048]{1,0:T(8,128)(2,1)} collective-permute-done((bf16[128,2048]{1,0:T(8,128)(2,1)}, bf16[128,2048]{1,0:T(8,128)(2,1)}, u32[]{:S(2)}, u32[]{:S(2)}) %collective-permute-start.12) | collective-permute-done | bytes 524320 | tf_op jit(solution)/shard_map/ppermute | solution.py:265
  140.4 3.6 %up_grads.1 = (bf16[4,12,128,128]{3,2,1,0:T(8,128)(2,1)S(1)}, bf16[4,12,128,128]{3,2,1,0:T(8,128)(2,1)S(1)}) custom-call(s32[2]{0:T(128)S(1)} %pad_add_fusion.me_ref, s32[576]{0:T(1024)S(1)} %reshape.296.index_ref, s32[3]{0:T(128)S(1)} %bitcast.110, bf16[128,2048]{1,0:T(8,128)(2,1)S(1)} %copy-done.3, bf16[128,2048]{1,0:T(8,128)(2,1)S(1)} %collective-permute-done.refs_1_, ...), custom_call_target="tpu_custom_call" | custom-call | tf_op jit(solution)/shard_map/up_grads/pallas_call | solution.py:229
  143.9 17.6 %collective-permute-done.7 = bf16[128,2048]{1,0:T(8,128)(2,1)} collective-permute-done((bf16[128,2048]{1,0:T(8,128)(2,1)}, bf16[128,2048]{1,0:T(8,128)(2,1)}, u32[]{:S(2)}, u32[]{:S(2)}) %collective-permute-start.7) | collective-permute-done | bytes 524320 | tf_op jit(solution)/shard_map/ppermute | solution.py:267
  161.5 2.5 %add_convert_fusion.1 = bf16[128,2048]{1,0:T(8,128)(2,1)} fusion(bf16[128,2048]{1,0:T(8,128)(2,1)} %collective-permute-done.7, bf16[128,2048]{1,0:T(8,128)(2,1)} %collective-permute-done.5, bf16[128,2048]{1,0:T(8,128)(2,1)} %collective-permute-done.4, bf16[128,2048]{1,0:T(8,128)(2,1)S(1)} %copy-done.14), kind=kLoop, calls=%fused_computation.5 | loop fusion | flops 2097152 | bytes 2621440 | tf_op jit(solution)/shard_map/convert_element_type | solution.py:269
  164.0 8.2 %collective-permute-done.15 = bf16[128,2048]{1,0:T(8,128)(2,1)S(1)} collective-permute-done((bf16[128,2048]{1,0:T(8,128)(2,1)S(1)}, bf16[128,2048]{1,0:T(8,128)(2,1)S(1)}, u32[]{:S(2)}, u32[]{:S(2)}) %collective-permute-start.15) | collective-permute-done | bytes 524320 | tf_op jit(solution)/shard_map/ppermute | solution.py:267
  172.2 2.2 add_convert_fusion
  174.4 2.0 add.147
  176.4 1.5 collective-permute-start.27
  178.0 1.6 collective-permute-start.29
  182.0 1.5 collective-permute-start.22
  183.6 4.9 %collective-permute-done.27 = bf16[2,6,128,128]{3,2,1,0:T(8,128)(2,1)S(1)} collective-permute-done((bf16[2,6,128,128]{3,2,1,0:T(8,128)(2,1)S(1)}, bf16[2,6,128,128]{3,2,1,0:T(8,128)(2,1)S(1)}, u32[]{:S(2)}, u32[]{:S(2)}) %collective-permute-start.27) | collective-permute-done | bytes 393248 | tf_op jit(solution)/shard_map/ppermute | solution.py:273
  191.7 5.2 %collective-permute-done.17 = bf16[2,6,128,128]{3,2,1,0:T(8,128)(2,1)S(1)} collective-permute-done((bf16[2,6,128,128]{3,2,1,0:T(8,128)(2,1)S(1)}, bf16[2,6,128,128]{3,2,1,0:T(8,128)(2,1)S(1)}, u32[]{:S(2)}, u32[]{:S(2)}) %collective-permute-start.17) | collective-permute-done | bytes 393248 | tf_op jit(solution)/shard_map/ppermute | solution.py:273
  196.9 1.5 collective-permute-start.28
  200.1 5.2 %collective-permute-done.22 = bf16[2,6,128,128]{3,2,1,0:T(8,128)(2,1)S(1)} collective-permute-done((bf16[2,6,128,128]{3,2,1,0:T(8,128)(2,1)S(1)}, bf16[2,6,128,128]{3,2,1,0:T(8,128)(2,1)S(1)}, u32[]{:S(2)}, u32[]{:S(2)}) %collective-permute-start.22) | collective-permute-done | bytes 393248 | tf_op jit(solution)/shard_map/ppermute | solution.py:273
  211.2 2.6 %collective-permute-done.20 = bf16[6,128,128]{2,1,0:T(8,128)(2,1)S(1)} collective-permute-done((bf16[6,128,128]{2,1,0:T(8,128)(2,1)S(1)}, bf16[6,128,128]{2,1,0:T(8,128)(2,1)S(1)}, u32[]{:S(2)}, u32[]{:S(2)}) %collective-permute-start.20) | collective-permute-done | bytes 196640 | tf_op jit(solution)/shard_map/ppermute | solution.py:273
  213.8 1.5 collective-permute-done.18
  219.4 1.7 pad_maximum_fusion
  (126 shorter events, 37.0 us)
Async XLA Ops:
  0.6 39.5 %collective-permute-start.2 = (bf16[128,2048]{1,0:T(8,128)(2,1)}, bf16[128,2048]{1,0:T(8,128)(2,1)S(1)}, u32[]{:S(2)}, u32[]{:S(2)}) collective-permute-start(bf16[128,2048]{1,0:T(8,128)(2,1)} %refs_0_.8), channel_id=1, source_target_pairs={{0,2},{1,3},{2,0},{3,1},{4,6},{5,7},{6,4},{7,5},{8,10},{9,11},{10,... | collective-permute-start | bytes 1572872 | tf_op jit(solution)/shard_map/ppermute | solution.py:253
  4.7 46.7 %collective-permute-start.10 = (bf16[128,2048]{1,0:T(8,128)(2,1)}, bf16[128,2048]{1,0:T(8,128)(2,1)S(1)}, u32[]{:S(2)}, u32[]{:S(2)}) collective-permute-start(bf16[128,2048]{1,0:T(8,128)(2,1)} %refs_0_.9), channel_id=1, source_target_pairs={{0,2},{1,3},{2,0},{3,1},{4,6},{5,7},{6,4},{7,5},{8,10},{9,11},{10,... | collective-permute-start | bytes 1572872 | tf_op jit(solution)/shard_map/ppermute | solution.py:253
  4.8 49.4 %collective-permute-start.1 = (bf16[128,2048]{1,0:T(8,128)(2,1)}, bf16[128,2048]{1,0:T(8,128)(2,1)S(1)}, u32[]{:S(2)}, u32[]{:S(2)}) collective-permute-start(bf16[128,2048]{1,0:T(8,128)(2,1)} %refs_0_.8), channel_id=1, source_target_pairs={{1,0},{2,1},{3,2},{5,4},{6,5},{7,6},{9,8},{10,9},{11,10},{13,12},{... | collective-permute-start | bytes 1572872 | tf_op jit(solution)/shard_map/ppermute | solution.py:255
  6.1 50.5 %collective-permute-start = (bf16[128,2048]{1,0:T(8,128)(2,1)}, bf16[128,2048]{1,0:T(8,128)(2,1)S(1)}, u32[]{:S(2)}, u32[]{:S(2)}) collective-permute-start(bf16[128,2048]{1,0:T(8,128)(2,1)} %refs_0_.8), channel_id=1, source_target_pairs={{0,1},{1,2},{2,3},{4,5},{5,6},{6,7},{8,9},{9,10},{10,11},{12,13},{... | collective-permute-start | bytes 1572872 | tf_op jit(solution)/shard_map/ppermute | solution.py:254
  40.2 21.7 %collective-permute-start.3 = (bf16[128,2048]{1,0:T(8,128)(2,1)S(1)}, bf16[128,2048]{1,0:T(8,128)(2,1)S(1)}, u32[]{:S(2)}, u32[]{:S(2)}) collective-permute-start(bf16[128,2048]{1,0:T(8,128)(2,1)S(1)} %collective-permute-done.2.refs_3_), channel_id=1, source_target_pairs={{2,3},{1,0},{6,7},{5,4},{10,11},{9,8},{14,15},{13,12},{18,19},{17,... | collective-permute-start | bytes 1572872 | tf_op jit(solution)/shard_map/ppermute | solution.py:256
  41.5 42.8 %collective-permute-start.9 = (bf16[128,2048]{1,0:T(8,128)(2,1)}, bf16[128,2048]{1,0:T(8,128)(2,1)S(1)}, u32[]{:S(2)}, u32[]{:S(2)}) collective-permute-start(bf16[128,2048]{1,0:T(8,128)(2,1)} %refs_0_.9), channel_id=1, source_target_pairs={{1,0},{2,1},{3,2},{5,4},{6,5},{7,6},{9,8},{10,9},{11,10},{13,12},{... | collective-permute-start | bytes 1572872 | tf_op jit(solution)/shard_map/ppermute | solution.py:255
  51.4 32.8 %collective-permute-start.8 = (bf16[128,2048]{1,0:T(8,128)(2,1)}, bf16[128,2048]{1,0:T(8,128)(2,1)}, u32[]{:S(2)}, u32[]{:S(2)}) collective-permute-start(bf16[128,2048]{1,0:T(8,128)(2,1)} %refs_0_.9), channel_id=1, source_target_pairs={{0,1},{1,2},{2,3},{4,5},{5,6},{6,7},{8,9},{9,10},{10,11},{12,13},{... | collective-permute-start | bytes 1572872 | tf_op jit(solution)/shard_map/ppermute | solution.py:254
  54.2 30.1 %collective-permute-start.11 = (bf16[128,2048]{1,0:T(8,128)(2,1)S(1)}, bf16[128,2048]{1,0:T(8,128)(2,1)}, u32[]{:S(2)}, u32[]{:S(2)}) collective-permute-start(bf16[128,2048]{1,0:T(8,128)(2,1)S(1)} %collective-permute-done.10.refs_3_), channel_id=1, source_target_pairs={{2,3},{1,0},{6,7},{5,4},{10,11},{9,8},{14,15},{13,12},{18,19},{17,... | collective-permute-start | bytes 1572872 | tf_op jit(solution)/shard_map/ppermute | solution.py:256
  79.0 36.2 %collective-permute-start.6 = (bf16[128,2048]{1,0:T(8,128)(2,1)S(1)}, bf16[128,2048]{1,0:T(8,128)(2,1)S(1)}, u32[]{:S(2)}, u32[]{:S(2)}) collective-permute-start(bf16[128,2048]{1,0:T(8,128)(2,1)S(1)} %get-tuple-element.28), channel_id=1, source_target_pairs={{3,2},{0,1},{7,6},{4,5},{11,10},{8,9},{15,14},{12,13},{19,18},{16,... | collective-permute-start | bytes 1572872 | tf_op jit(solution)/shard_map/ppermute | solution.py:264
  99.6 16.5 %collective-permute-start.14 = (bf16[128,2048]{1,0:T(8,128)(2,1)S(1)}, bf16[128,2048]{1,0:T(8,128)(2,1)S(1)}, u32[]{:S(2)}, u32[]{:S(2)}) collective-permute-start(bf16[128,2048]{1,0:T(8,128)(2,1)S(1)} %get-tuple-element.37), channel_id=1, source_target_pairs={{3,2},{0,1},{7,6},{4,5},{11,10},{8,9},{15,14},{12,13},{19,18},{16,... | collective-permute-start | bytes 1572872 | tf_op jit(solution)/shard_map/ppermute | solution.py:264
  101.0 22.8 %collective-permute-start.4 = (bf16[128,2048]{1,0:T(8,128)(2,1)}, bf16[128,2048]{1,0:T(8,128)(2,1)}, u32[]{:S(2)}, u32[]{:S(2)}) collective-permute-start(bf16[128,2048]{1,0:T(8,128)(2,1)} %get-tuple-element.25), channel_id=1, source_target_pairs={{1,0},{2,1},{3,2},{5,4},{6,5},{7,6},{9,8},{10,9},{11,10},{13,12},{... | collective-permute-start | bytes 1572872 | tf_op jit(solution)/shard_map/ppermute | solution.py:265
  102.2 25.2 %collective-permute-start.5 = (bf16[128,2048]{1,0:T(8,128)(2,1)}, bf16[128,2048]{1,0:T(8,128)(2,1)}, u32[]{:S(2)}, u32[]{:S(2)}) collective-permute-start(bf16[128,2048]{1,0:T(8,128)(2,1)} %get-tuple-element.26), channel_id=1, source_target_pairs={{0,1},{1,2},{2,3},{4,5},{5,6},{6,7},{8,9},{9,10},{10,11},{12,13},{... | collective-permute-start | bytes 1572872 | tf_op jit(solution)/shard_map/ppermute | solution.py:266
  107.6 31.4 %collective-permute-start.12 = (bf16[128,2048]{1,0:T(8,128)(2,1)}, bf16[128,2048]{1,0:T(8,128)(2,1)}, u32[]{:S(2)}, u32[]{:S(2)}) collective-permute-start(bf16[128,2048]{1,0:T(8,128)(2,1)} %get-tuple-element.34), channel_id=1, source_target_pairs={{1,0},{2,1},{3,2},{5,4},{6,5},{7,6},{9,8},{10,9},{11,10},{13,12},{... | collective-permute-start | bytes 1572872 | tf_op jit(solution)/shard_map/ppermute | solution.py:265
  115.2 59.2 %collective-permute-start.26 = (bf16[4,12,128,128]{3,2,1,0:T(8,128)(2,1)}, bf16[4,12,128,128]{3,2,1,0:T(8,128)(2,1)}, u32[]{:S(2)}, u32[]{:S(2)}) collective-permute-start(bf16[4,12,128,128]{3,2,1,0:T(8,128)(2,1)} %get-tuple-element.44), channel_id=1, source_target_pairs={{0,4},{4,0},{8,12},{12,8},{16,20},{20,16},{24,28},{28,24},{1,5},{5... | collective-permute-start | bytes 4718600 | tf_op jit(solution)/shard_map/ppermute | solution.py:273
  117.0 44.6 %collective-permute-start.7 = (bf16[128,2048]{1,0:T(8,128)(2,1)}, bf16[128,2048]{1,0:T(8,128)(2,1)}, u32[]{:S(2)}, u32[]{:S(2)}) collective-permute-start(bf16[128,2048]{1,0:T(8,128)(2,1)} %add.123), channel_id=1, source_target_pairs={{0,2},{1,3},{2,0},{3,1},{4,6},{5,7},{6,4},{7,5},{8,10},{9,11},{10,... | collective-permute-start | bytes 1572872 | tf_op jit(solution)/shard_map/ppermute | solution.py:267
  123.7 37.8 %copy-start.14 = (bf16[128,2048]{1,0:T(8,128)(2,1)S(1)}, bf16[128,2048]{1,0:T(8,128)(2,1)}, u32[]{:S(2)}) copy-start(bf16[128,2048]{1,0:T(8,128)(2,1)} %copy-done.13) | copy-start | bytes 1572868
  123.8 40.2 %collective-permute-start.13 = (bf16[128,2048]{1,0:T(8,128)(2,1)S(1)}, bf16[128,2048]{1,0:T(8,128)(2,1)S(1)}, u32[]{:S(2)}, u32[]{:S(2)}) collective-permute-start(bf16[128,2048]{1,0:T(8,128)(2,1)S(1)} %copy-done.22), channel_id=1, source_target_pairs={{0,1},{1,2},{2,3},{4,5},{5,6},{6,7},{8,9},{9,10},{10,11},{12,13},{... | collective-permute-start | bytes 1572872 | tf_op jit(solution)/shard_map/ppermute | solution.py:266
  127.4 52.1 %collective-permute-start.16 = (bf16[4,12,128,128]{3,2,1,0:T(8,128)(2,1)S(1)}, bf16[4,12,128,128]{3,2,1,0:T(8,128)(2,1)S(1)}, u32[]{:S(2)}, u32[]{:S(2)}) collective-permute-start(bf16[4,12,128,128]{3,2,1,0:T(8,128)(2,1)S(1)} %get-tuple-element.39), channel_id=1, source_target_pairs={{0,4},{4,0},{8,12},{12,8},{16,20},{20,16},{24,28},{28,24},{1,5},{5... | collective-permute-start | bytes 4718600 | tf_op jit(solution)/shard_map/ppermute | solution.py:273
  139.0 33.2 %collective-permute-start.15 = (bf16[128,2048]{1,0:T(8,128)(2,1)S(1)}, bf16[128,2048]{1,0:T(8,128)(2,1)S(1)}, u32[]{:S(2)}, u32[]{:S(2)}) collective-permute-start(bf16[128,2048]{1,0:T(8,128)(2,1)S(1)} %add.127), channel_id=1, source_target_pairs={{0,2},{1,3},{2,0},{3,1},{4,6},{5,7},{6,4},{7,5},{8,10},{9,11},{10,... | collective-permute-start | bytes 1572872 | tf_op jit(solution)/shard_map/ppermute | solution.py:267
  161.5 19.9 %collective-permute-start.21 = (bf16[4,12,128,128]{3,2,1,0:T(8,128)(2,1)S(1)}, bf16[4,12,128,128]{3,2,1,0:T(8,128)(2,1)S(1)}, u32[]{:S(2)}, u32[]{:S(2)}) collective-permute-start(bf16[4,12,128,128]{3,2,1,0:T(8,128)(2,1)S(1)} %get-tuple-element.41), channel_id=1, source_target_pairs={{0,4},{4,0},{8,12},{12,8},{16,20},{20,16},{24,28},{28,24},{1,5},{5... | collective-permute-start | bytes 4718600 | tf_op jit(solution)/shard_map/ppermute | solution.py:273
  176.4 12.1 %collective-permute-start.27 = (bf16[2,6,128,128]{3,2,1,0:T(8,128)(2,1)S(1)}, bf16[2,6,128,128]{3,2,1,0:T(8,128)(2,1)S(1)}, u32[]{:S(2)}, u32[]{:S(2)}) collective-permute-start(bf16[2,6,128,128]{3,2,1,0:T(8,128)(2,1)S(1)} %slice_bitcast_fusion.2), channel_id=1, source_target_pairs={{0,8},{4,12},{8,0},{12,4},{16,24},{20,28},{24,16},{28,20},{1,9},{5... | collective-permute-start | bytes 1179656 | tf_op jit(solution)/shard_map/ppermute | solution.py:273
  178.0 12.1 %collective-permute-start.29 = (bf16[2,6,128,128]{3,2,1,0:T(8,128)(2,1)S(1)}, bf16[2,6,128,128]{3,2,1,0:T(8,128)(2,1)S(1)}, u32[]{:S(2)}, u32[]{:S(2)}) collective-permute-start(bf16[2,6,128,128]{3,2,1,0:T(8,128)(2,1)S(1)} %slice_bitcast_fusion), channel_id=1, source_target_pairs={{0,16},{4,20},{8,24},{12,28},{16,0},{20,4},{24,8},{28,12},{1,17},{... | collective-permute-start | bytes 1179656 | tf_op jit(solution)/shard_map/ppermute | solution.py:273
  180.2 16.8 %collective-permute-start.17 = (bf16[2,6,128,128]{3,2,1,0:T(8,128)(2,1)S(1)}, bf16[2,6,128,128]{3,2,1,0:T(8,128)(2,1)S(1)}, u32[]{:S(2)}, u32[]{:S(2)}) collective-permute-start(bf16[2,6,128,128]{3,2,1,0:T(8,128)(2,1)S(1)} %slice_bitcast_fusion.10), channel_id=1, source_target_pairs={{0,8},{4,12},{8,0},{12,4},{16,24},{20,28},{24,16},{28,20},{1,9},{5... | collective-permute-start | bytes 1179656 | tf_op jit(solution)/shard_map/ppermute | solution.py:273
  180.8 17.7 %collective-permute-start.19 = (bf16[2,6,128,128]{3,2,1,0:T(8,128)(2,1)S(1)}, bf16[2,6,128,128]{3,2,1,0:T(8,128)(2,1)S(1)}, u32[]{:S(2)}, u32[]{:S(2)}) collective-permute-start(bf16[2,6,128,128]{3,2,1,0:T(8,128)(2,1)S(1)} %slice_bitcast_fusion.8), channel_id=1, source_target_pairs={{0,16},{4,20},{8,24},{12,28},{16,0},{20,4},{24,8},{28,12},{1,17},{... | collective-permute-start | bytes 1179656 | tf_op jit(solution)/shard_map/ppermute | solution.py:273
  182.0 23.4 %collective-permute-start.22 = (bf16[2,6,128,128]{3,2,1,0:T(8,128)(2,1)S(1)}, bf16[2,6,128,128]{3,2,1,0:T(8,128)(2,1)S(1)}, u32[]{:S(2)}, u32[]{:S(2)}) collective-permute-start(bf16[2,6,128,128]{3,2,1,0:T(8,128)(2,1)S(1)} %slice_bitcast_fusion.6), channel_id=1, source_target_pairs={{0,8},{4,12},{8,0},{12,4},{16,24},{20,28},{24,16},{28,20},{1,9},{5... | collective-permute-start | bytes 1179656 | tf_op jit(solution)/shard_map/ppermute | solution.py:273
  188.5 18.4 %collective-permute-start.24 = (bf16[2,6,128,128]{3,2,1,0:T(8,128)(2,1)S(1)}, bf16[2,6,128,128]{3,2,1,0:T(8,128)(2,1)S(1)}, u32[]{:S(2)}, u32[]{:S(2)}) collective-permute-start(bf16[2,6,128,128]{3,2,1,0:T(8,128)(2,1)S(1)} %slice_bitcast_fusion.4), channel_id=1, source_target_pairs={{0,16},{4,20},{8,24},{12,28},{16,0},{20,4},{24,8},{28,12},{1,17},{... | collective-permute-start | bytes 1179656 | tf_op jit(solution)/shard_map/ppermute | solution.py:273
  190.2 19.4 %collective-permute-start.30 = (bf16[6,128,128]{2,1,0:T(8,128)(2,1)S(1)}, bf16[6,128,128]{2,1,0:T(8,128)(2,1)S(1)}, u32[]{:S(2)}, u32[]{:S(2)}) collective-permute-start(bf16[6,128,128]{2,1,0:T(8,128)(2,1)S(1)} %slice_bitcast_fusion.12), channel_id=1, source_target_pairs={{0,8},{4,12},{8,0},{12,4},{16,24},{20,28},{24,16},{28,20},{1,9},{5... | collective-permute-start | bytes 589832 | tf_op jit(solution)/shard_map/ppermute | solution.py:273
  196.9 14.2 %collective-permute-start.28 = (bf16[6,128,128]{2,1,0:T(8,128)(2,1)S(1)}, bf16[6,128,128]{2,1,0:T(8,128)(2,1)S(1)}, u32[]{:S(2)}, u32[]{:S(2)}) collective-permute-start(bf16[6,128,128]{2,1,0:T(8,128)(2,1)S(1)} %slice_bitcast_fusion.14), channel_id=1, source_target_pairs={{0,16},{4,20},{8,24},{12,28},{16,0},{20,4},{24,8},{28,12},{1,17},{... | collective-permute-start | bytes 589832 | tf_op jit(solution)/shard_map/ppermute | solution.py:273
  198.6 15.1 %collective-permute-start.20 = (bf16[6,128,128]{2,1,0:T(8,128)(2,1)S(1)}, bf16[6,128,128]{2,1,0:T(8,128)(2,1)S(1)}, u32[]{:S(2)}, u32[]{:S(2)}) collective-permute-start(bf16[6,128,128]{2,1,0:T(8,128)(2,1)S(1)} %slice_bitcast_fusion.20), channel_id=1, source_target_pairs={{0,8},{4,12},{8,0},{12,4},{16,24},{20,28},{24,16},{28,20},{1,9},{5... | collective-permute-start | bytes 589832 | tf_op jit(solution)/shard_map/ppermute | solution.py:273
  205.4 10.0 %collective-permute-start.18 = (bf16[6,128,128]{2,1,0:T(8,128)(2,1)S(1)}, bf16[6,128,128]{2,1,0:T(8,128)(2,1)S(1)}, u32[]{:S(2)}, u32[]{:S(2)}) collective-permute-start(bf16[6,128,128]{2,1,0:T(8,128)(2,1)S(1)} %slice_bitcast_fusion.22), channel_id=1, source_target_pairs={{0,16},{4,20},{8,24},{12,28},{16,0},{20,4},{24,8},{28,12},{1,17},{... | collective-permute-start | bytes 589832 | tf_op jit(solution)/shard_map/ppermute | solution.py:273
  207.1 9.6 %collective-permute-start.25 = (bf16[6,128,128]{2,1,0:T(8,128)(2,1)S(1)}, bf16[6,128,128]{2,1,0:T(8,128)(2,1)S(1)}, u32[]{:S(2)}, u32[]{:S(2)}) collective-permute-start(bf16[6,128,128]{2,1,0:T(8,128)(2,1)S(1)} %slice_bitcast_fusion.16), channel_id=1, source_target_pairs={{0,8},{4,12},{8,0},{12,4},{16,24},{20,28},{24,16},{28,20},{1,9},{5... | collective-permute-start | bytes 589832 | tf_op jit(solution)/shard_map/ppermute | solution.py:273
  209.6 8.3 %collective-permute-start.23 = (bf16[6,128,128]{2,1,0:T(8,128)(2,1)S(1)}, bf16[6,128,128]{2,1,0:T(8,128)(2,1)S(1)}, u32[]{:S(2)}, u32[]{:S(2)}) collective-permute-start(bf16[6,128,128]{2,1,0:T(8,128)(2,1)S(1)} %slice_bitcast_fusion.18), channel_id=1, source_target_pairs={{0,16},{4,20},{8,24},{12,28},{16,0},{20,4},{24,8},{28,12},{1,17},{... | collective-permute-start | bytes 589832 | tf_op jit(solution)/shard_map/ppermute | solution.py:273
  (26 other events, 258.5 us)

commit v3 on v2

v3 whole, which is shorter than its diff:
```python
import functools
import jax
import jax.numpy as jnp
from jax import lax
from jax.experimental import pallas as pl
from jax.experimental.pallas import tpu as pltpu
from jax.sharding import PartitionSpec as P

HB_DEV = 14
EPSILON = 1e-08
GROUP = 8
VMEM_LIMIT = 32 * 1024 * 1024
F32, BF16 = jnp.float32, jnp.bfloat16
SHAPE = jax.ShapeDtypeStruct
SMEM = pl.BlockSpec(memory_space=pltpu.SMEM)
VMEM = pl.BlockSpec(memory_space=pltpu.VMEM)
ANY = pl.BlockSpec(memory_space=pl.ANY)
TOKEN = SHAPE((1,), jnp.int32)


def group_of(capacity):
    return next(g for g in (GROUP, 4, 2, 1) if capacity % g == 0)


def feature_block(ref, block, size):
    per_shard = ref.shape[2] // size
    start = pl.multiple_of(lax.rem(block, per_shard) * size, size)
    return ref.at[lax.div(block, per_shard), :, pl.ds(start, size)]


def slot_pair(index_ref, matrix, slot, capacity):
    at = (matrix * capacity + slot) * 2
    return index_ref[at], index_ref[at + 1]


def each_group(count, group, body):
    def step(i, carry):
        body([i * group + u for u in range(group)])
        return carry

    lax.fori_loop(0, lax.div(count + (group - 1), group), step, 0)


def dot(a, b, contract):
    return lax.dot_general(a, b, (contract, ((), ())), preferred_element_type=F32)


def accumulate(index_ref, matrix, count, capacity, acc, into, product):
    trash = acc.shape[0] - 1

    def body(slots):
        products, targets = [], []
        for s in slots:
            pair = slot_pair(index_ref, matrix, s, capacity)
            targets.append(jnp.where(s < count, pair[into], trash))
            products.append(product(s, *pair))
        for t, p in zip(targets, products):
            acc[t] += p

    each_group(count, group_of(capacity), body)


def load_shards(pieces, held, me):
    if len(pieces) == 1:
        return pieces[0]
    if len(pieces) == 4:
        for offset, piece in enumerate(pieces):
            held[lax.bitwise_xor(me, offset)] = piece[...]
        return held
    own, below, above, across, far = pieces
    last = held.shape[0] - 1
    held[me] = own[...]
    held[lax.bitwise_xor(me, 2)] = across[...]

    @pl.when(me > 0)
    def _():
        held[me - 1] = below[...]

    @pl.when(me < last)
    def _():
        held[me + 1] = above[...]

    @pl.when((me == 0) | (me == last))
    def _():
        held[last - me] = far[...]

    return held


def store_shards(total, outs, me, per_shard, size):
    if len(outs) == 1:
        places = [(outs[0].at[t], t) for t in range(outs[0].shape[0])]
    elif len(outs) == 4:
        places = [(out, lax.bitwise_xor(me, offset)) for offset, out in enumerate(outs)]
    else:
        last = len(outs) - 2
        own, below, above, across, far = outs
        places = [
            (own, me),
            (below, jnp.maximum(me - 1, 0)),
            (above, jnp.minimum(me + 1, last)),
            (across, lax.bitwise_xor(me, 2)),
            (far, last - me),
        ]
    for out, t in places:
        for c in range(per_shard):
            out[:, c * size : (c + 1) * size] = total[t * per_shard + c].astype(out.dtype)


def forward_kernel(n_pieces, n_outs, me_ref, index_ref, count_ref, *refs):
    pieces, refs = refs[:n_pieces], refs[n_pieces:]
    w_ref, hidden_ref, turned_ref, act_ref, slope_ref = refs[:5]
    outs, (held, gate, up, total) = refs[5 : 5 + n_outs], refs[5 + n_outs :]
    me = me_ref[0]
    x_ref = load_shards(pieces, held, me)
    capacity, size = w_ref.shape[1], w_ref.shape[2]
    gate[...] = jnp.zeros_like(gate)
    up[...] = jnp.zeros_like(up)
    total[...] = jnp.zeros_like(total)
    for matrix, acc in ((0, gate), (1, up)):
        accumulate(
            index_ref, matrix, count_ref[matrix], capacity, acc, 1,
            lambda s, f, h, matrix=matrix: dot(feature_block(x_ref, f, size)[...], w_ref[matrix, s], ((1,), (0,))),
        )
    for h in range(hidden_ref.shape[0]):
        g, u = gate[h], up[h]
        sig = 1.0 / (1.0 + jnp.exp(-g))
        act = g * sig
        act_ref[h] = act
        slope_ref[h] = u * sig * (1.0 + g * (1.0 - sig))
        hidden = (act * u).astype(hidden_ref.dtype)
        hidden_ref[h] = hidden
        turned_ref[h] = hidden.T
    accumulate(
        index_ref, 2, count_ref[2], capacity, total, 0,
        lambda s, f, h: dot(hidden_ref[h], w_ref[2, s], ((1,), (0,))),
    )
    store_shards(total, outs, me, x_ref.shape[2] // size, size)


def turn_kernel(n_pieces, me_ref, *refs):
    pieces, (turned_ref, held) = refs[:n_pieces], refs[n_pieces:]
    x_ref = load_shards(pieces, held, me_ref[0])
    size = turned_ref.shape[1]
    per_shard = x_ref.shape[2] // size
    for f in range(turned_ref.shape[0]):
        c = f % per_shard
        turned_ref[f] = x_ref[f // per_shard, :, c * size : (c + 1) * size].T


def rows_kernel(n_pieces, me_ref, index_ref, count_ref, *refs):
    pieces, refs = refs[:n_pieces], refs[n_pieces:]
    w_ref, act_ref, slope_ref, gate_rows_ref, up_rows_ref, held, acc = refs
    og_ref = load_shards(pieces, held, me_ref[0])
    capacity, size = w_ref.shape[1], w_ref.shape[2]
    acc[...] = jnp.zeros_like(acc)
    accumulate(
        index_ref, 2, count_ref[2], capacity, acc, 1,
        lambda s, f, h: dot(feature_block(og_ref, f, size)[...], w_ref[2, s], ((1,), (1,))),
    )
    for h in range(act_ref.shape[0]):
        gate_rows_ref[h] = (acc[h] * slope_ref[h]).astype(gate_rows_ref.dtype)
        up_rows_ref[h] = (acc[h] * act_ref[h]).astype(up_rows_ref.dtype)


def spread(place, core, places):
    levels = places.bit_length() - 1
    turned = sum(lax.shift_left(lax.bitwise_and(lax.shift_right_logical(place, b), 1), levels - 1 - b) for b in range(levels))
    return 2 * jnp.where(core == 0, place, turned)


def grads_kernel(matrix, n_pieces, me_ref, index_ref, count_ref, *refs):
    pieces, refs = refs[:n_pieces], refs[n_pieces:]
    turned_ref, keep_ref, send_ref, held = refs
    size, share = keep_ref.shape[2], keep_ref.shape[1]
    places = keep_ref.shape[0]
    replica = me_ref[1]
    right_ref = load_shards(pieces, held, me_ref[0])
    capacity = 2 * places * share
    count = count_ref[matrix]
    for out, bit in ((send_ref, 1), (keep_ref, 0)):

        def one_place(q, carry, out=out, bit=bit):
            owner = lax.bitwise_xor(replica, bit)
            first = lax.bitwise_xor(owner, spread(q, lax.bitwise_and(owner, 1), places)) * share

            @pl.when(first < count)
            def _():
                for s in range(share):
                    f, h = slot_pair(index_ref, matrix, first + s, capacity)
                    if matrix == 2:
                        left, right = turned_ref[h], feature_block(right_ref, f, size)[...]
                    else:
                        left, right = turned_ref[f], right_ref[h]
                    out[q, s] = dot(left, right, ((1,), (0,))).astype(out.dtype)

            return carry

        lax.fori_loop(0, places, one_place, 0)


def input_kernel(n_outs, me_ref, index_ref, count_ref, gate_rows_ref, up_rows_ref, w_ref, *refs):
    outs, (total,) = refs[:n_outs], refs[n_outs:]
    capacity, size = w_ref.shape[1], w_ref.shape[2]
    total[...] = jnp.zeros_like(total)
    for matrix, rows in ((0, gate_rows_ref), (1, up_rows_ref)):
        accumulate(
            index_ref, matrix, count_ref[matrix], capacity, total, 0,
            lambda s, f, h, matrix=matrix, rows=rows: dot(rows[h], w_ref[matrix, s], ((1,), (1,))),
        )
    store_shards(total, outs, me_ref[0], outs[0].shape[-1] // size, size)


def fold_kernel(keep_ref, got_ref, keep_out, send_out):
    half = keep_out.shape[0]
    keep_out[...] = keep_ref[:half] + got_ref[:half]
    send_out[...] = keep_ref[half:] + got_ref[half:]


def add_kernel(a_ref, b_ref, out_ref):
    out_ref[...] = a_ref[...] + b_ref[...]


def sum_kernel(*refs):
    *parts, out_ref = refs
    total = parts[0][...].astype(F32)
    for part in parts[1:]:
        total += part[...].astype(F32)
    out_ref[...] = total.astype(out_ref.dtype)


def update_kernel(matrix, me_ref, count_ref, keep_ref, got_ref, m1_ref, m2_ref, *refs):
    out_ref = refs[-1]
    share = keep_ref.shape[1]
    first = me_ref[1] * share
    for s in range(share):
        g = keep_ref[0, s].astype(F32) + got_ref[0, s].astype(F32)
        first_new = 0.9 * m1_ref[0, s] + 0.1 * g
        second_new = 0.95 * m2_ref[0, s] + 0.05 * g * g
        live = first + s < count_ref[matrix]
        out_ref[0, s] = jnp.where(live, first_new / (jnp.sqrt(second_new) + EPSILON), 0.0)


def hold_kernel(v_ref, _, out_ref):
    out_ref[...] = v_ref[...]


class Line:
    token = None

    def __call__(self, kernel, name, outs, scratch, operands, scalars=(), specs=None, out_specs=None, aliases=None, **more):
        tokens = [] if self.token is None else [self.token]
        n_in, n_out = len(scalars) + len(operands), len(outs)

        def body(*refs):
            ins, rest = refs[:n_in], refs[n_in + len(tokens) :]
            results, token, scratches = rest[:n_out], rest[n_out], rest[n_out + 1 :]
            token[0] = 0
            kernel(*ins, *results, *scratches)

        *results, self.token = pl.pallas_call(
            body,
            name=name,
            out_shape=[*outs, TOKEN],
            in_specs=[SMEM] * len(scalars) + (specs or [VMEM] * len(operands)) + [SMEM] * len(tokens),
            out_specs=[*(out_specs or [VMEM] * n_out), SMEM],
            scratch_shapes=scratch,
            input_output_aliases=aliases or {},
            compiler_params=pltpu.CompilerParams(vmem_limit_bytes=VMEM_LIMIT),
            **more,
        )(*scalars, *operands, *tokens)
        return results


def flip(v, shards, bit):
    return lax.ppermute(v, "tensor", [(a, a ^ bit) for a in range(shards)])


def gather_near(v):
    across, beside = flip(v, 4, 2), flip(v, 4, 1)
    return [v, beside, across, flip(across, 4, 1)]


def gather_line(v):
    across = flip(v, 4, 2)
    below = lax.ppermute(v, "tensor", [(a, a + 1) for a in range(3)])
    above = lax.ppermute(v, "tensor", [(a + 1, a) for a in range(3)])
    far = lax.ppermute(across, "tensor", [(2, 3), (1, 0)])
    return [v, below, above, across, far]


def scatter_first(parts):
    if len(parts) == 4:
        own, beside, across, far = parts
        return [own, flip(beside, 4, 1)], across, flip(far, 4, 1)
    own, below, above, across, far = parts
    far = lax.ppermute(far, "tensor", [(3, 2), (0, 1)])
    below = lax.ppermute(below, "tensor", [(a + 1, a) for a in range(3)])
    above = lax.ppermute(above, "tensor", [(a, a + 1) for a in range(3)])
    return [own, below, above], across, far


def core_swap(v, replicas):
    return lax.ppermute(v, "dp", [(a, a ^ 1) for a in range(replicas)])


def axis_swap(v, replicas, step):
    levels = replicas.bit_length() - 2
    pairs = [(a, a ^ (1 << (1 + step if a & 1 else levels - step))) for a in range(replicas)]
    return lax.ppermute(v, "dp", pairs)


def local(replicas, shards, inputs, out_grad, weights, block_index, block_counts, first_moment, second_moment):
    capacity, size = weights.shape[1], weights.shape[2]
    rows, width = inputs.shape
    me = jnp.stack([lax.axis_index("tensor"), lax.axis_index("dp")]).astype(jnp.int32)
    scalars = (me, block_index.reshape(-1), block_counts[0])
    features = shards * width // size
    places, share = replicas // 2, capacity // replicas
    levels = places.bit_length() - 1
    held = pltpu.VMEM((shards, rows, width), BF16)
    acc = pltpu.VMEM((HB_DEV + 1, rows, size), F32)
    total = pltpu.VMEM((features + 1, rows, size), F32)
    wide = SHAPE((HB_DEV, rows, size), F32)
    narrow = SHAPE((HB_DEV, rows, size), BF16)
    turned = SHAPE((HB_DEV, size, rows), BF16)
    piece = SHAPE((rows, width), BF16)
    line = Line()
    lined = shards == 4

    def gather(v, form):
        return form(v) if lined else [lax.all_gather(v, "tensor", axis=0)]

    def parts_of(count):
        return [piece] * count if lined else [SHAPE((shards, rows, width), BF16)]

    def grads(matrix, right, left):
        half = SHAPE((places, share, size, size), BF16)
        name = ("gate_grads", "up_grads", "down_grads")[matrix]
        kernel = functools.partial(grads_kernel, matrix, len(right))
        keep, send = line(kernel, name, [half, half], [held], [*right, left], scalars)
        return keep, core_swap(send, replicas)

    def fold(keep, got, step):
        half = SHAPE((keep.shape[0] // 2, *keep.shape[1:]), BF16)
        keep, send = line(fold_kernel, "fold", [half, half], [], [keep, got])
        return keep, axis_swap(send, replicas, step)

    def update(matrix, keep, got, buffer):
        block = pl.BlockSpec((1, share, size, size), lambda i: (matrix, 0, 0, 0))
        extra = [] if buffer is None else [buffer]
        return line(
            functools.partial(update_kernel, matrix),
            "update",
            [SHAPE(first_moment.shape, F32)],
            [],
            [keep, got, first_moment, second_moment, *extra],
            (me, scalars[2]),
            specs=[VMEM, VMEM, block, block] + [ANY] * len(extra),
            out_specs=[block],
            aliases={6: 0} if extra else {},
            grid=(1,),
        )[0]

    def join(across, far):
        return flip(line(add_kernel, "join", [piece], [], [across, far])[0], 4, 2)

    def finish(held_parts, across):
        return line(sum_kernel, "finish", [piece], [], [*held_parts, across])[0]

    x = gather(inputs, gather_near)
    if lined:
        (out_grad,) = line(hold_kernel, "hold", [piece], [], [out_grad, x[2]])
    og = gather(out_grad, gather_line)
    out_parts, in_parts = parts_of(5), parts_of(4)
    hidden, hidden_turned, act, slope, *out_parts = line(
        functools.partial(forward_kernel, len(x), len(out_parts)),
        "forward",
        [narrow, turned, wide, wide, *out_parts],
        [held, acc, acc, total],
        [*x, weights],
        scalars,
    )
    if lined:
        out_held, across, far = scatter_first(out_parts)
    else:
        outputs = lax.psum_scatter(out_parts[0], "tensor", scatter_dimension=0)
    (x_turned,) = line(
        functools.partial(turn_kernel, len(x)), "turn", [SHAPE((features, size, rows), BF16)], [held], x, (me,)
    )
    if lined:
        across = join(across, far)
    gate_rows, up_rows = line(
        functools.partial(rows_kernel, len(og)),
        "row_grads",
        [narrow, narrow],
        [held, acc],
        [*og, weights, act, slope],
        scalars,
    )
    in_parts = line(
        functools.partial(input_kernel, len(in_parts)),
        "input_grads",
        in_parts,
        [total],
        [gate_rows, up_rows, weights],
        scalars,
    )
    if lined:
        in_held, in_across, in_far = scatter_first(in_parts)
    else:
        input_grad = lax.psum_scatter(in_parts[0], "tensor", scatter_dimension=0)
    down = grads(2, og, hidden_turned)
    gate = grads(0, [gate_rows], x_turned)
    down = fold(*down, 0)
    if lined:
        in_across = join(in_across, in_far)
    up = grads(1, [up_rows], x_turned)
    gate = fold(*gate, 0)
    if lined:
        outputs = finish(out_held, across)
    for step in range(1, levels):
        down = fold(*down, step)
        if step == 1:
            up = fold(*up, 0)
        gate = fold(*gate, step)
    buffer = update(2, *down, None)
    for step in range(1, levels):
        up = fold(*up, step)
    buffer = update(0, *gate, buffer)
    if lined:
        input_grad = finish(in_held, in_across)
    buffer = update(1, *up, buffer)
    return (outputs, input_grad, buffer)


def solution(mesh):
    in_specs = (
        P("dp", "tensor"),
        P("dp", "tensor"),
        P(None, "tensor", None, None),
        P(None, "tensor", None),
        P("tensor", None),
        P(None, ("tensor", "dp"), None, None),
        P(None, ("tensor", "dp"), None, None),
    )
    out_specs = (P("dp", "tensor"), P("dp", "tensor"), P(None, ("tensor", "dp"), None, None))
    body = functools.partial(local, mesh.shape["dp"], mesh.shape["tensor"])
    return jax.shard_map(body, mesh=mesh, in_specs=in_specs, out_specs=out_specs, check_vma=False)
```

time: 226 us -> 217 us (0.960); the launches traced: 221 us -> 216 us
  Pallas kernels: 38.8 us -> 64.7 us
  starting transfers between devices: 53.4 us -> 38.2 us
  other arithmetic: 14.4 us -> 0.08 us
    pallas_call x6 -> x21, Pallas kernels: 38.8 us -> 64.7 us  [__call__(): pl.pallas_call(body, name=name, out_shape=[*outs, TOKEN], in_specs=[SMEM]...]
    ppermute x25 -> x20, starting transfers between devices: 40.9 us -> 31 us  [the longest x8 15.2 us: flip(): return lax.ppermute(v, 'tensor', [(a, a ^ bit) for a in range(shards)])]
    ppermute x25 -> x20, waiting for transfers between devices: 98.6 us -> 93.1 us  [the longest x8 74.5 us: flip(): return lax.ppermute(v, 'tensor', [(a, a ^ bit) for a in range(shards)])]
    convert_element_type x2 -> x0, other arithmetic: 4.65 us -> none  [scatter_line(): return (wide[0] + wide[1] + wide[2] + wide[3]).astype(jnp.bfloat16)]
    add x8 -> x0, other arithmetic: 4.52 us -> none  [the longest x3 3.11 us: replica_sum(): total = keep + swap(send, replicas, 1)]
    ppermute x2 -> x1, waiting for transfers between devices: 0.01 us -> 4.35 us  [gather_line(): below = lax.ppermute(v, 'tensor', [(a, a + 1) for a in range(3)])]
    ppermute x2 -> x1, waiting for transfers between devices: 0.01 us -> 3.2 us  [gather_line(): above = lax.ppermute(v, 'tensor', [(a + 1, a) for a in range(3)])]
    ppermute x2 -> x1, starting transfers between devices: 7.38 us -> 4.58 us  [gather_line(): below = lax.ppermute(v, 'tensor', [(a, a + 1) for a in range(3)])]
  transfers between devices with their start and end apart: 31 -> 23, of which waited for: 18 -> 14; matrix products, arithmetic and copies ran while one was open for 6% -> 0% of each run, Pallas kernels for 18% -> 20%
where the time goes in v3:
time: 217 us; the launch traced here: 216 us
  waiting for transfers between devices  105 us (48%)
  Pallas kernels  64.7 us (30%)
  starting transfers between devices  38.2 us (18%)
  local copies, waits for them, and re-layouts  7.15 us (3%)
    ppermute x8, waiting for transfers between devices, flip(): return lax.ppermute(v, 'tensor', [(a, a ^ bit) for a in range(shards)])  74.5 us
    pallas_call x21, Pallas kernels, __call__(): pl.pallas_call(body, name=name, out_shape=[*outs, TOKEN], in_specs=[SMEM]...  64.7 us
    ppermute x8, starting transfers between devices, flip(): return lax.ppermute(v, 'tensor', [(a, a ^ bit) for a in range(shards)])  15.2 us
    ppermute x1, waiting for transfers between devices, scatter_first(): below = lax.ppermute(below, 'tensor', [(a + 1, a) for a in range(3)])  8.43 us
    ppermute x6, starting transfers between devices, axis_swap(): return lax.ppermute(v, 'dp', pairs)  7.78 us
    unnamed x29, local copies, waits for them, and re-layouts  7.01 us
    ppermute x6, waiting for transfers between devices, axis_swap(): return lax.ppermute(v, 'dp', pairs)  6.11 us
    ppermute x1, starting transfers between devices, scatter_first(): above = lax.ppermute(above, 'tensor', [(a, a + 1) for a in range(3)])  4.76 us
  transfers between devices with their start and end apart: 23, of which 14 were waited for; matrix products, arithmetic and copies ran while one was open for 0% of the time, Pallas kernels for 20%

profile of v3, /device:TPU:0, one launch (start us, length us, event | category | flops | bytes accessed | tf_op | source)
XLA Modules:
  0.0 216.1 jit_solution(10775335763870282324)
XLA Ops:
  0.6 4.1 %collective-permute-start.1 = (bf16[128,2048]{1,0:T(8,128)(2,1)}, bf16[128,2048]{1,0:T(8,128)(2,1)S(1)}, u32[]{:S(2)}, u32[]{:S(2)}) collective-permute-start(bf16[128,2048]{1,0:T(8,128)(2,1)} %refs_1_.1), channel_id=1, source_target_pairs={{0,2},{1,3},{2,0},{3,1},{4,6},{5,7},{6,4},{7,5},{8,10},{9,11},{10,... | collective-permute-start | bytes 1572872 | tf_op jit(solution)/shard_map/ppermute | solution.py:276
  6.3 21.9 %collective-permute-done.1.refs_1_.refs_5_.refs_3_ = bf16[128,2048]{1,0:T(8,128)(2,1)S(1)} collective-permute-done((bf16[128,2048]{1,0:T(8,128)(2,1)}, bf16[128,2048]{1,0:T(8,128)(2,1)S(1)}, u32[]{:S(2)}, u32[]{:S(2)}) %collective-permute-start.1) | collective-permute-done | bytes 524320 | tf_op jit(solution)/shard_map/ppermute | solution.py:276
  30.5 3.3 %collective-permute-start.9 = (bf16[128,2048]{1,0:T(8,128)(2,1)S(1)}, bf16[128,2048]{1,0:T(8,128)(2,1)S(1)}, u32[]{:S(2)}, u32[]{:S(2)}) collective-permute-start(bf16[128,2048]{1,0:T(8,128)(2,1)S(1)} %get-tuple-element.73.refs_3_), channel_id=1, source_target_pairs={{0,2},{1,3},{2,0},{3,1},{4,6},{5,7},{6,4},{7,5},{8,10},{9,11},{10,... | collective-permute-start | bytes 1572872 | tf_op jit(solution)/shard_map/ppermute | solution.py:276
  34.9 15.7 %collective-permute-done.2.refs_6_.refs_4_ = bf16[128,2048]{1,0:T(8,128)(2,1)S(1)} collective-permute-done((bf16[128,2048]{1,0:T(8,128)(2,1)S(1)}, bf16[128,2048]{1,0:T(8,128)(2,1)S(1)}, u32[]{:S(2)}, u32[]{:S(2)}) %collective-permute-start.2) | collective-permute-done | bytes 524320 | tf_op jit(solution)/shard_map/ppermute | solution.py:276
  50.6 3.7 %copy-done = bf16[3,96,128,128]{3,2,1,0:T(8,128)(2,1)S(1)} copy-done((bf16[3,96,128,128]{3,2,1,0:T(8,128)(2,1)S(1)}, bf16[3,96,128,128]{3,2,1,0:T(8,128)(2,1)}, u32[]{:S(2)}) %copy-start) | copy-done | bytes 9437208
  55.0 12.1 %forward.1 = (bf16[14,128,128]{2,1,0:T(8,128)(2,1)}, bf16[14,128,128]{2,1,0:T(8,128)(2,1)S(1)}, f32[14,128,128]{2,1,0:T(8,128)S(1)}, f32[14,128,128]{2,1,0:T(8,1...) custom-call(s32[2]{0:T(128)S(1)} %pad_add_fusion.refs_0_, ...), custom_call_target="tpu_custom_call" | custom-call | tf_op jit(solution)/shard_map/forward/pallas_call | solution.py:261
  70.5 4.6 %collective-permute-start.7 = (bf16[128,2048]{1,0:T(8,128)(2,1)S(1)}, bf16[128,2048]{1,0:T(8,128)(2,1)S(1)}, u32[]{:S(2)}, u32[]{:S(2)}) collective-permute-start(bf16[128,2048]{1,0:T(8,128)(2,1)S(1)} %get-tuple-element.73.refs_3_), channel_id=1, source_target_pairs={{0,1},{1,2},{2,3},{4,5},{5,6},{6,7},{8,9},{9,10},{10,11},{12,13},{... | collective-permute-start | bytes 1572872 | tf_op jit(solution)/shard_map/ppermute | solution.py:286
  76.4 1.9 turn.1
  78.3 3.2 %collective-permute-done.5.refs_1_ = bf16[128,2048]{1,0:T(8,128)(2,1)S(1)} collective-permute-done((bf16[128,2048]{1,0:T(8,128)(2,1)S(1)}, bf16[128,2048]{1,0:T(8,128)(2,1)S(1)}, u32[]{:S(2)}, u32[]{:S(2)}) %collective-permute-start.5) | collective-permute-done | bytes 524320 | tf_op jit(solution)/shard_map/ppermute | solution.py:297
  82.8 3.2 %collective-permute-done.8.refs_5_ = bf16[128,2048]{1,0:T(8,128)(2,1)S(1)} collective-permute-done((bf16[128,2048]{1,0:T(8,128)(2,1)S(1)}, bf16[128,2048]{1,0:T(8,128)(2,1)S(1)}, u32[]{:S(2)}, u32[]{:S(2)}) %collective-permute-start.8) | collective-permute-done | bytes 524320 | tf_op jit(solution)/shard_map/ppermute | solution.py:287
  86.0 4.4 %collective-permute-done.7.refs_4_ = bf16[128,2048]{1,0:T(8,128)(2,1)S(1)} collective-permute-done((bf16[128,2048]{1,0:T(8,128)(2,1)S(1)}, bf16[128,2048]{1,0:T(8,128)(2,1)S(1)}, u32[]{:S(2)}, u32[]{:S(2)}) %collective-permute-start.7) | collective-permute-done | bytes 524320 | tf_op jit(solution)/shard_map/ppermute | solution.py:286
  90.3 4.1 %collective-permute-done.10.refs_7_ = bf16[128,2048]{1,0:T(8,128)(2,1)S(1)} collective-permute-done((bf16[128,2048]{1,0:T(8,128)(2,1)S(1)}, bf16[128,2048]{1,0:T(8,128)(2,1)S(1)}, u32[]{:S(2)}, u32[]{:S(2)}) %collective-permute-start.10) | collective-permute-done | bytes 524320 | tf_op jit(solution)/shard_map/ppermute | solution.py:288
  94.5 5.6 %row_grads.1 = (bf16[14,128,128]{2,1,0:T(8,128)(2,1)S(1)}, bf16[14,128,128]{2,1,0:T(8,128)(2,1)S(1)}, s32[1]{0:T(128)}) custom-call(s32[2]{0:T(128)S(1)} %pad_add_fusion.refs_0_, s32[576]{0:T(1024)S(1)} %reshape.9.refs_1_, s32[3]{0:T(128)S(1)} %bitcast.4, bf16[128,2048]{1,0:T(8,128)(2,1)S(1)} %get-tuple-element.73.refs_3_, ...), custom_call_target="tpu_custom_call" | custom-call | tf_op jit(solution)/shard_map/row_grads/pallas_call | solution.py:261
  100.1 9.9 %input_grads.1 = (bf16[128,2048]{1,0:T(8,128)(2,1)S(1)}, bf16[128,2048]{1,0:T(8,128)(2,1)S(1)}, bf16[128,2048]{1,0:T(8,128)(2,1)S(1)}, bf16[128,2048]{1,0:T(8,128)(2,1)S(1)}, s32[1]{0:T(128)}) custom-call(s32[2]{0:T(128)S(1)} %pad_add_fusion.refs_0_, s32[576]{0:T(1024)S(1)} %reshape.9.refs_1_, s32[3]{0:T(128)S(1)} %bitcast.5, ...), custom_call_target="tpu_custom_call" | custom-call | tf_op jit(solution)/shard_map/input_grads/pallas_call | solution.py:261
  110.0 4.2 %down_grads.1 = (bf16[4,12,128,128]{3,2,1,0:T(8,128)(2,1)S(1)}, bf16[4,12,128,128]{3,2,1,0:T(8,128)(2,1)S(1)}, s32[1]{0:T(128)}) custom-call(s32[2]{0:T(128)S(1)} %pad_add_fusion.refs_0_, s32[576]{0:T(1024)S(1)} %reshape.9.refs_1_, s32[3]{0:T(128)S(1)} %bitcast.6, bf16[128,2048]{1,0:T(8,128)(2,1)S(1)} %get-tuple-element.73.refs_3_, ...), custom_call_target="tpu_custom_call" | custom-call | tf_op jit(solution)/shard_map/down_grads/pallas_call | solution.py:261
  114.4 4.0 %gate_grads.1 = (bf16[4,12,128,128]{3,2,1,0:T(8,128)(2,1)S(1)}, bf16[4,12,128,128]{3,2,1,0:T(8,128)(2,1)S(1)}, s32[1]{0:T(128)}) custom-call(s32[2]{0:T(128)S(1)} %pad_add_fusion.refs_0_, s32[576]{0:T(1024)S(1)} %reshape.9.refs_1_, s32[3]{0:T(128)S(1)} %bitcast.7, bf16[14,128,128]{2,1,0:T(8,128)(2,1)S(1)} %get-tuple-element.77.refs_3_, ...), custom_call_target="tpu_custom_call" | custom-call | tf_op jit(solution)/shard_map/gate_grads/pallas_call | solution.py:261
  120.5 12.4 %collective-permute-done.12.refs_1_ = bf16[128,2048]{1,0:T(8,128)(2,1)S(1)} collective-permute-done((bf16[128,2048]{1,0:T(8,128)(2,1)S(1)}, bf16[128,2048]{1,0:T(8,128)(2,1)S(1)}, u32[]{:S(2)}, u32[]{:S(2)}) %collective-permute-start.12) | collective-permute-done | bytes 524320 | tf_op jit(solution)/shard_map/ppermute | solution.py:276
  134.2 3.9 %up_grads.1 = (bf16[4,12,128,128]{3,2,1,0:T(8,128)(2,1)S(1)}, bf16[4,12,128,128]{3,2,1,0:T(8,128)(2,1)S(1)}, s32[1]{0:T(128)}) custom-call(s32[2]{0:T(128)S(1)} %pad_add_fusion.refs_0_, s32[576]{0:T(1024)S(1)} %reshape.9.refs_1_, s32[3]{0:T(128)S(1)} %bitcast.8, bf16[14,128,128]{2,1,0:T(8,128)(2,1)S(1)} %get-tuple-element.80.refs_4_.refs_3_, ...), custom_call_target="tpu_custom_call" | custom-call | tf_op jit(solution)/shard_map/up_grads/pallas_call | solution.py:261
  140.6 4.8 %collective-permute-start.4 = (bf16[128,2048]{1,0:T(8,128)(2,1)S(1)}, bf16[128,2048]{1,0:T(8,128)(2,1)S(1)}, u32[]{:S(2)}, u32[]{:S(2)}) collective-permute-start(bf16[128,2048]{1,0:T(8,128)(2,1)S(1)} %copy-done.11), channel_id=1, source_target_pairs={{0,1},{1,2},{2,3},{4,5},{5,6},{6,7},{8,9},{9,10},{10,11},{12,13},{... | collective-permute-start | bytes 1572872 | tf_op jit(solution)/shard_map/ppermute | solution.py:299
  146.9 8.4 %collective-permute-done.3.refs_1_ = bf16[128,2048]{1,0:T(8,128)(2,1)S(1)} collective-permute-done((bf16[128,2048]{1,0:T(8,128)(2,1)S(1)}, bf16[128,2048]{1,0:T(8,128)(2,1)S(1)}, u32[]{:S(2)}, u32[]{:S(2)}) %collective-permute-start.3) | collective-permute-done | bytes 524320 | tf_op jit(solution)/shard_map/ppermute | solution.py:298
  157.4 19.6 %collective-permute-done.6.refs_3_ = bf16[128,2048]{1,0:T(8,128)(2,1)S(1)} collective-permute-done((bf16[128,2048]{1,0:T(8,128)(2,1)S(1)}, bf16[128,2048]{1,0:T(8,128)(2,1)S(1)}, u32[]{:S(2)}, u32[]{:S(2)}) %collective-permute-start.6) | collective-permute-done | bytes 524320 | tf_op jit(solution)/shard_map/ppermute | solution.py:276
  177.0 1.7 finish.2
  180.3 1.7 fold.9
  184.1 2.0 collective-permute-start.14
  186.1 3.4 %collective-permute-start.15 = (bf16[128,2048]{1,0:T(8,128)(2,1)S(1)}, bf16[128,2048]{1,0:T(8,128)(2,1)S(1)}, u32[]{:S(2)}, u32[]{:S(2)}) collective-permute-start(bf16[128,2048]{1,0:T(8,128)(2,1)S(1)} %get-tuple-element.98), channel_id=1, source_target_pairs={{0,2},{1,3},{2,0},{3,1},{4,6},{5,7},{6,4},{7,5},{8,10},{9,11},{10,... | collective-permute-start | bytes 1572872 | tf_op jit(solution)/shard_map/ppermute | solution.py:276
  192.3 3.2 %collective-permute-done.20.refs_3_ = bf16[1,12,128,128]{3,2,1,0:T(8,128)(2,1)S(1)} collective-permute-done((bf16[1,12,128,128]{3,2,1,0:T(8,128)(2,1)S(1)}, bf16[1,12,128,128]{3,2,1,0:T(8,128)(2,1)S(1)}, u32[]{:S(2)}, u32[]{:S(2)}) %collective-permute-start.20) | collective-permute-done | bytes 393248 | tf_op jit(solution)/shard_map/ppermute | solution.py:310
  195.6 2.6 %update.3 = (f32[3,12,128,128]{3,2,1,0:T(8,128)}, s32[1]{0:T(128)}) custom-call(s32[2]{0:T(128)S(1)} %pad_add_fusion.refs_0_, s32[3]{0:T(128)S(1)} %bitcast.9, bf16[1,12,128,128]{3,2,1,0:T(8,128)(2,1)S(1)} %get-tuple-element.110.refs_2_, bf16[1,12,128,128]{3,2,1,0:T(8,128)(2,1)S(1)} %collective-permute-done.20.refs_3_, f32[3,12,128,128]{3,2,1,0:T(8,128)S(1)} %copy-done.2, ...), custom_call_target="tpu_custom_call" | custom-call | tf_op jit(solution)/shard_map/update/pallas_call | solution.py:261
  198.2 2.9 %collective-permute-done.21.refs_1_ = bf16[2,12,128,128]{3,2,1,0:T(8,128)(2,1)S(1)} collective-permute-done((bf16[2,12,128,128]{3,2,1,0:T(8,128)(2,1)S(1)}, bf16[2,12,128,128]{3,2,1,0:T(8,128)(2,1)S(1)}, u32[]{:S(2)}, u32[]{:S(2)}) %collective-permute-start.21) | collective-permute-done | bytes 786464 | tf_op jit(solution)/shard_map/ppermute | solution.py:310
  202.4 1.7 collective-permute-start.22
  204.1 2.6 %update.4 = (f32[3,12,128,128]{3,2,1,0:T(8,128)}, s32[1]{0:T(128)}) custom-call(s32[2]{0:T(128)S(1)} %pad_add_fusion.refs_0_, s32[3]{0:T(128)S(1)} %bitcast.10, bf16[1,12,128,128]{3,2,1,0:T(8,128)(2,1)S(1)} %get-tuple-element.108.refs_2_, bf16[1,12,128,128]{3,2,1,0:T(8,128)(2,1)S(1)} %collective-permute-done.19.refs_3_, ...), custom_call_target="tpu_custom_call", output_to_operand_aliasing={{0}: (6, {})} | custom-call | tf_op jit(solution)/shard_map/update/pallas_call | solution.py:261
  208.3 3.4 %collective-permute-done.15.refs_2_ = bf16[128,2048]{1,0:T(8,128)(2,1)S(1)} collective-permute-done((bf16[128,2048]{1,0:T(8,128)(2,1)S(1)}, bf16[128,2048]{1,0:T(8,128)(2,1)S(1)}, u32[]{:S(2)}, u32[]{:S(2)}) %collective-permute-start.15) | collective-permute-done | bytes 524320 | tf_op jit(solution)/shard_map/ppermute | solution.py:276
  213.3 2.6 %update.5 = (f32[3,12,128,128]{3,2,1,0:T(8,128)}, s32[1]{0:T(128)}) custom-call(s32[2]{0:T(128)S(1)} %pad_add_fusion.refs_0_, s32[3]{0:T(128)S(1)} %bitcast.11, bf16[1,12,128,128]{3,2,1,0:T(8,128)(2,1)S(1)} %get-tuple-element.120.refs_2_, bf16[1,12,128,128]{3,2,1,0:T(8,128)(2,1)S(1)} %collective-permute-done.22.refs_3_, ...), custom_call_target="tpu_custom_call", output_to_operand_aliasing={{0}: (6, {})} | custom-call | tf_op jit(solution)/shard_map/update/pallas_call | solution.py:261
  (66 shorter events, 31.9 us)
Async XLA Ops:
  0.6 50.0 %copy-start.4 = (bf16[128,2048]{1,0:T(8,128)(2,1)S(1)}, bf16[128,2048]{1,0:T(8,128)(2,1)}, u32[]{:S(2)}) copy-start(bf16[128,2048]{1,0:T(8,128)(2,1)} %refs_1_.1) | copy-start | bytes 1572868
  0.6 27.6 %collective-permute-start.1 = (bf16[128,2048]{1,0:T(8,128)(2,1)}, bf16[128,2048]{1,0:T(8,128)(2,1)S(1)}, u32[]{:S(2)}, u32[]{:S(2)}) collective-permute-start(bf16[128,2048]{1,0:T(8,128)(2,1)} %refs_1_.1), channel_id=1, source_target_pairs={{0,2},{1,3},{2,0},{3,1},{4,6},{5,7},{6,4},{7,5},{8,10},{9,11},{10,... | collective-permute-start | bytes 1572872 | tf_op jit(solution)/shard_map/ppermute | solution.py:276
  4.7 30.2 %collective-permute-start = (bf16[128,2048]{1,0:T(8,128)(2,1)}, bf16[128,2048]{1,0:T(8,128)(2,1)S(1)}, u32[]{:S(2)}, u32[]{:S(2)}) collective-permute-start(bf16[128,2048]{1,0:T(8,128)(2,1)} %refs_1_.1), channel_id=1, source_target_pairs={{0,1},{1,0},{2,3},{3,2},{4,5},{5,4},{6,7},{7,6},{8,9},{9,8},{10,11... | collective-permute-start | bytes 1572872 | tf_op jit(solution)/shard_map/ppermute | solution.py:276
  28.2 22.4 %collective-permute-start.2 = (bf16[128,2048]{1,0:T(8,128)(2,1)S(1)}, bf16[128,2048]{1,0:T(8,128)(2,1)S(1)}, u32[]{:S(2)}, u32[]{:S(2)}) collective-permute-start(bf16[128,2048]{1,0:T(8,128)(2,1)S(1)} %collective-permute-done.1.refs_1_.refs_5_.refs_3_), channel_id=1, source_target_pairs={{0,1},{1,0},{2,3},{3,2},{4,5},{5,4},{6,7},{7,6},{8,9},{9,8},{10,11... | collective-permute-start | bytes 1572872 | tf_op jit(solution)/shard_map/ppermute | solution.py:276
  30.5 44.6 %collective-permute-start.9 = (bf16[128,2048]{1,0:T(8,128)(2,1)S(1)}, bf16[128,2048]{1,0:T(8,128)(2,1)S(1)}, u32[]{:S(2)}, u32[]{:S(2)}) collective-permute-start(bf16[128,2048]{1,0:T(8,128)(2,1)S(1)} %get-tuple-element.73.refs_3_), channel_id=1, source_target_pairs={{0,2},{1,3},{2,0},{3,1},{4,6},{5,7},{6,4},{7,5},{8,10},{9,11},{10,... | collective-permute-start | bytes 1572872 | tf_op jit(solution)/shard_map/ppermute | solution.py:276
  54.9 39.5 %copy-start.1 = (bf16[3,96,128,128]{3,2,1,0:T(8,128)(2,1)S(1)}, bf16[3,96,128,128]{3,2,1,0:T(8,128)(2,1)}, u32[]{:S(2)}) copy-start(bf16[3,96,128,128]{3,2,1,0:T(8,128)(2,1)} %refs_5_.4) | copy-start | bytes 28311556
  67.9 13.7 %copy-start.12 = (bf16[128,2048]{1,0:T(8,128)(2,1)}, bf16[128,2048]{1,0:T(8,128)(2,1)S(1)}, u32[]{:S(2)}) copy-start(bf16[128,2048]{1,0:T(8,128)(2,1)S(1)} %get-tuple-element.66) | copy-start | bytes 1572868
  67.9 13.6 %collective-permute-start.5 = (bf16[128,2048]{1,0:T(8,128)(2,1)S(1)}, bf16[128,2048]{1,0:T(8,128)(2,1)S(1)}, u32[]{:S(2)}, u32[]{:S(2)}) collective-permute-start(bf16[128,2048]{1,0:T(8,128)(2,1)S(1)} %get-tuple-element.69), channel_id=1, source_target_pairs={{3,2},{0,1},{7,6},{4,5},{11,10},{8,9},{15,14},{12,13},{19,18},{16,... | collective-permute-start | bytes 1572872 | tf_op jit(solution)/shard_map/ppermute | solution.py:297
  69.2 16.8 %collective-permute-start.8 = (bf16[128,2048]{1,0:T(8,128)(2,1)S(1)}, bf16[128,2048]{1,0:T(8,128)(2,1)S(1)}, u32[]{:S(2)}, u32[]{:S(2)}) collective-permute-start(bf16[128,2048]{1,0:T(8,128)(2,1)S(1)} %get-tuple-element.73.refs_3_), channel_id=1, source_target_pairs={{1,0},{2,1},{3,2},{5,4},{6,5},{7,6},{9,8},{10,9},{11,10},{13,12},{... | collective-permute-start | bytes 1572872 | tf_op jit(solution)/shard_map/ppermute | solution.py:287
  70.5 19.8 %collective-permute-start.7 = (bf16[128,2048]{1,0:T(8,128)(2,1)S(1)}, bf16[128,2048]{1,0:T(8,128)(2,1)S(1)}, u32[]{:S(2)}, u32[]{:S(2)}) collective-permute-start(bf16[128,2048]{1,0:T(8,128)(2,1)S(1)} %get-tuple-element.73.refs_3_), channel_id=1, source_target_pairs={{0,1},{1,2},{2,3},{4,5},{5,6},{6,7},{8,9},{9,10},{10,11},{12,13},{... | collective-permute-start | bytes 1572872 | tf_op jit(solution)/shard_map/ppermute | solution.py:286
  75.1 19.4 %collective-permute-start.10 = (bf16[128,2048]{1,0:T(8,128)(2,1)S(1)}, bf16[128,2048]{1,0:T(8,128)(2,1)S(1)}, u32[]{:S(2)}, u32[]{:S(2)}) collective-permute-start(bf16[128,2048]{1,0:T(8,128)(2,1)S(1)} %collective-permute-done.9.refs_6_), channel_id=1, source_target_pairs={{2,3},{1,0},{6,7},{5,4},{10,11},{9,8},{14,15},{13,12},{18,19},{17,... | collective-permute-start | bytes 1572872 | tf_op jit(solution)/shard_map/ppermute | solution.py:288
  110.0 8.4 %copy-start.8 = (bf16[128,2048]{1,0:T(8,128)(2,1)}, bf16[128,2048]{1,0:T(8,128)(2,1)S(1)}, u32[]{:S(2)}) copy-start(bf16[128,2048]{1,0:T(8,128)(2,1)S(1)} %get-tuple-element.97) | copy-start | bytes 1572868
  114.3 4.7 %collective-permute-start.13 = (bf16[4,12,128,128]{3,2,1,0:T(8,128)(2,1)S(1)}, bf16[4,12,128,128]{3,2,1,0:T(8,128)(2,1)S(1)}, u32[]{:S(2)}, u32[]{:S(2)}) collective-permute-start(bf16[4,12,128,128]{3,2,1,0:T(8,128)(2,1)S(1)} %get-tuple-element.89), channel_id=1, source_target_pairs={{0,4},{4,0},{8,12},{12,8},{16,20},{20,16},{24,28},{28,24},{1,5},{5... | collective-permute-start | bytes 4718600 | tf_op jit(solution)/shard_map/ppermute | solution.py:304
  118.4 26.9 %collective-permute-start.11 = (bf16[4,12,128,128]{3,2,1,0:T(8,128)(2,1)S(1)}, bf16[4,12,128,128]{3,2,1,0:T(8,128)(2,1)S(1)}, u32[]{:S(2)}, u32[]{:S(2)}) collective-permute-start(bf16[4,12,128,128]{3,2,1,0:T(8,128)(2,1)S(1)} %get-tuple-element.85), channel_id=1, source_target_pairs={{0,4},{4,0},{8,12},{12,8},{16,20},{20,16},{24,28},{28,24},{1,5},{5... | collective-permute-start | bytes 4718600 | tf_op jit(solution)/shard_map/ppermute | solution.py:304
  119.0 13.9 %collective-permute-start.12 = (bf16[128,2048]{1,0:T(8,128)(2,1)S(1)}, bf16[128,2048]{1,0:T(8,128)(2,1)S(1)}, u32[]{:S(2)}, u32[]{:S(2)}) collective-permute-start(bf16[128,2048]{1,0:T(8,128)(2,1)S(1)} %get-tuple-element.87), channel_id=1, source_target_pairs={{0,1},{1,0},{2,3},{3,2},{4,5},{5,4},{6,7},{7,6},{8,9},{9,8},{10,11... | collective-permute-start | bytes 1572872 | tf_op jit(solution)/shard_map/ppermute | solution.py:276
  132.9 6.4 %copy-start.13 = (bf16[128,2048]{1,0:T(8,128)(2,1)S(1)}, bf16[128,2048]{1,0:T(8,128)(2,1)}, u32[]{:S(2)}) copy-start(bf16[128,2048]{1,0:T(8,128)(2,1)} %copy-done.12) | copy-start | bytes 1572868
  132.9 7.7 %copy-start.11 = (bf16[128,2048]{1,0:T(8,128)(2,1)S(1)}, bf16[128,2048]{1,0:T(8,128)(2,1)}, u32[]{:S(2)}) copy-start(bf16[128,2048]{1,0:T(8,128)(2,1)} %copy-done.10) | copy-start | bytes 1572868
  138.1 42.1 %collective-permute-start.17 = (bf16[4,12,128,128]{3,2,1,0:T(8,128)(2,1)S(1)}, bf16[4,12,128,128]{3,2,1,0:T(8,128)(2,1)S(1)}, u32[]{:S(2)}, u32[]{:S(2)}) collective-permute-start(bf16[4,12,128,128]{3,2,1,0:T(8,128)(2,1)S(1)} %get-tuple-element.102), channel_id=1, source_target_pairs={{0,4},{4,0},{8,12},{12,8},{16,20},{20,16},{24,28},{28,24},{1,5},{5... | collective-permute-start | bytes 4718600 | tf_op jit(solution)/shard_map/ppermute | solution.py:304
  138.2 40.6 %collective-permute-start.18 = (bf16[2,12,128,128]{3,2,1,0:T(8,128)(2,1)S(1)}, bf16[2,12,128,128]{3,2,1,0:T(8,128)(2,1)S(1)}, u32[]{:S(2)}, u32[]{:S(2)}) collective-permute-start(bf16[2,12,128,128]{3,2,1,0:T(8,128)(2,1)S(1)} %get-tuple-element.104), channel_id=1, source_target_pairs={{0,16},{4,12},{8,24},{12,4},{16,0},{20,28},{24,8},{28,20},{1,17},{... | collective-permute-start | bytes 2359304 | tf_op jit(solution)/shard_map/ppermute | solution.py:310
  139.3 16.1 %collective-permute-start.3 = (bf16[128,2048]{1,0:T(8,128)(2,1)S(1)}, bf16[128,2048]{1,0:T(8,128)(2,1)S(1)}, u32[]{:S(2)}, u32[]{:S(2)}) collective-permute-start(bf16[128,2048]{1,0:T(8,128)(2,1)S(1)} %copy-done.13), channel_id=1, source_target_pairs={{1,0},{2,1},{3,2},{5,4},{6,5},{7,6},{9,8},{10,9},{11,10},{13,12},{... | collective-permute-start | bytes 1572872 | tf_op jit(solution)/shard_map/ppermute | solution.py:298
  140.6 16.9 %collective-permute-start.4 = (bf16[128,2048]{1,0:T(8,128)(2,1)S(1)}, bf16[128,2048]{1,0:T(8,128)(2,1)S(1)}, u32[]{:S(2)}, u32[]{:S(2)}) collective-permute-start(bf16[128,2048]{1,0:T(8,128)(2,1)S(1)} %copy-done.11), channel_id=1, source_target_pairs={{0,1},{1,2},{2,3},{4,5},{5,6},{6,7},{8,9},{9,10},{10,11},{12,13},{... | collective-permute-start | bytes 1572872 | tf_op jit(solution)/shard_map/ppermute | solution.py:299
  145.3 31.7 %collective-permute-start.6 = (bf16[128,2048]{1,0:T(8,128)(2,1)S(1)}, bf16[128,2048]{1,0:T(8,128)(2,1)S(1)}, u32[]{:S(2)}, u32[]{:S(2)}) collective-permute-start(bf16[128,2048]{1,0:T(8,128)(2,1)S(1)} %get-tuple-element.72), channel_id=1, source_target_pairs={{0,2},{1,3},{2,0},{3,1},{4,6},{5,7},{6,4},{7,5},{8,10},{9,11},{10,... | collective-permute-start | bytes 1572872 | tf_op jit(solution)/shard_map/ppermute | solution.py:276
  155.3 34.1 %collective-permute-start.16 = (bf16[2,12,128,128]{3,2,1,0:T(8,128)(2,1)S(1)}, bf16[2,12,128,128]{3,2,1,0:T(8,128)(2,1)S(1)}, u32[]{:S(2)}, u32[]{:S(2)}) collective-permute-start(bf16[2,12,128,128]{3,2,1,0:T(8,128)(2,1)S(1)} %get-tuple-element.100), channel_id=1, source_target_pairs={{0,16},{4,12},{8,24},{12,4},{16,0},{20,28},{24,8},{28,20},{1,17},{... | collective-permute-start | bytes 2359304 | tf_op jit(solution)/shard_map/ppermute | solution.py:310
  180.2 15.3 %copy-start.2 = (f32[3,12,128,128]{3,2,1,0:T(8,128)S(1)}, f32[3,12,128,128]{3,2,1,0:T(8,128)}, u32[]{:S(2)}) copy-start(f32[3,12,128,128]{3,2,1,0:T(8,128)} %refs_4_.5) | copy-start | bytes 7077892
  180.3 15.3 %copy-start.3 = (f32[3,12,128,128]{3,2,1,0:T(8,128)S(1)}, f32[3,12,128,128]{3,2,1,0:T(8,128)}, u32[]{:S(2)}) copy-start(f32[3,12,128,128]{3,2,1,0:T(8,128)} %refs_5_.7) | copy-start | bytes 7077892
  181.9 13.7 %copy-start.7 = (s32[1,3]{1,0:T(1,128)S(1)}, s32[1,3]{1,0:T(1,128)}, u32[]{:S(2)}) copy-start(s32[1,3]{1,0:T(1,128)} %param.11) | copy-start | bytes 40
  181.9 19.1 %collective-permute-start.21 = (bf16[2,12,128,128]{3,2,1,0:T(8,128)(2,1)S(1)}, bf16[2,12,128,128]{3,2,1,0:T(8,128)(2,1)S(1)}, u32[]{:S(2)}, u32[]{:S(2)}) collective-permute-start(bf16[2,12,128,128]{3,2,1,0:T(8,128)(2,1)S(1)} %get-tuple-element.115), channel_id=1, source_target_pairs={{0,16},{4,12},{8,24},{12,4},{16,0},{20,28},{24,8},{28,20},{1,17},{... | collective-permute-start | bytes 2359304 | tf_op jit(solution)/shard_map/ppermute | solution.py:310
  183.5 12.1 %collective-permute-start.20 = (bf16[1,12,128,128]{3,2,1,0:T(8,128)(2,1)S(1)}, bf16[1,12,128,128]{3,2,1,0:T(8,128)(2,1)S(1)}, u32[]{:S(2)}, u32[]{:S(2)}) collective-permute-start(bf16[1,12,128,128]{3,2,1,0:T(8,128)(2,1)S(1)} %get-tuple-element.111), channel_id=1, source_target_pairs={{0,8},{4,20},{8,0},{12,28},{16,24},{20,4},{24,16},{28,12},{1,9},{5... | collective-permute-start | bytes 1179656 | tf_op jit(solution)/shard_map/ppermute | solution.py:310
  184.1 24.2 %collective-permute-start.14 = (bf16[128,2048]{1,0:T(8,128)(2,1)S(1)}, bf16[128,2048]{1,0:T(8,128)(2,1)S(1)}, u32[]{:S(2)}, u32[]{:S(2)}) collective-permute-start(bf16[128,2048]{1,0:T(8,128)(2,1)S(1)} %copy-done.9), channel_id=1, source_target_pairs={{0,1},{1,0},{2,3},{3,2},{4,5},{5,4},{6,7},{7,6},{8,9},{9,8},{10,11... | collective-permute-start | bytes 1572872 | tf_op jit(solution)/shard_map/ppermute | solution.py:276
  186.1 25.6 %collective-permute-start.15 = (bf16[128,2048]{1,0:T(8,128)(2,1)S(1)}, bf16[128,2048]{1,0:T(8,128)(2,1)S(1)}, u32[]{:S(2)}, u32[]{:S(2)}) collective-permute-start(bf16[128,2048]{1,0:T(8,128)(2,1)S(1)} %get-tuple-element.98), channel_id=1, source_target_pairs={{0,2},{1,3},{2,0},{3,1},{4,6},{5,7},{6,4},{7,5},{8,10},{9,11},{10,... | collective-permute-start | bytes 1572872 | tf_op jit(solution)/shard_map/ppermute | solution.py:276
  190.8 13.4 %collective-permute-start.19 = (bf16[1,12,128,128]{3,2,1,0:T(8,128)(2,1)S(1)}, bf16[1,12,128,128]{3,2,1,0:T(8,128)(2,1)S(1)}, u32[]{:S(2)}, u32[]{:S(2)}) collective-permute-start(bf16[1,12,128,128]{3,2,1,0:T(8,128)(2,1)S(1)} %get-tuple-element.109), channel_id=1, source_target_pairs={{0,8},{4,20},{8,0},{12,28},{16,24},{20,4},{24,16},{28,12},{1,9},{5... | collective-permute-start | bytes 1179656 | tf_op jit(solution)/shard_map/ppermute | solution.py:310
  202.4 10.9 %collective-permute-start.22 = (bf16[1,12,128,128]{3,2,1,0:T(8,128)(2,1)S(1)}, bf16[1,12,128,128]{3,2,1,0:T(8,128)(2,1)S(1)}, u32[]{:S(2)}, u32[]{:S(2)}) collective-permute-start(bf16[1,12,128,128]{3,2,1,0:T(8,128)(2,1)S(1)} %get-tuple-element.121), channel_id=1, source_target_pairs={{0,8},{4,20},{8,0},{12,28},{16,24},{20,4},{24,16},{28,12},{1,9},{5... | collective-permute-start | bytes 1179656 | tf_op jit(solution)/shard_map/ppermute | solution.py:310
  (5 other events, 11.5 us)

commit v4 on v3

--- a/solution.py
+++ b/solution.py
@@ -267,6 +267,7 @@
             scratch_shapes=scratch,
             input_output_aliases=aliases or {},
             compiler_params=pltpu.CompilerParams(vmem_limit_bytes=VMEM_LIMIT),
+            cost_estimate=pl.CostEstimate(flops=10**15, bytes_accessed=10**12, transcendentals=0),
             **more,
         )(*scalars, *operands, *tokens)
         return results

time: 217 us -> 202 us (0.931)
  waiting for transfers between devices: 105 us -> 59.1 us
  Pallas kernels: 64.7 us -> 84.2 us
  starting transfers between devices: 38.2 us -> 53.3 us
  local copies, waits for them, and re-layouts: 7.15 us -> 2.05 us
    ppermute x8, waiting for transfers between devices: 74.5 us -> 31.9 us  [flip(): return lax.ppermute(v, 'tensor', [(a, a ^ bit) for a in range(shards)])]
    pallas_call x21, Pallas kernels: 64.7 us -> 84.2 us  [__call__(): pl.pallas_call(body, name=name, out_shape=[*outs, TOKEN], in_specs=[SMEM]...]
    ppermute x6, waiting for transfers between devices: 6.11 us -> 20.3 us  [axis_swap(): return lax.ppermute(v, 'dp', pairs)]
    ppermute x8, starting transfers between devices: 15.2 us -> 28.6 us  [flip(): return lax.ppermute(v, 'tensor', [(a, a ^ bit) for a in range(shards)])]
    ppermute x1, waiting for transfers between devices: 8.43 us -> 0.01 us  [scatter_first(): below = lax.ppermute(below, 'tensor', [(a + 1, a) for a in range(3)])]
    unnamed x29 -> x37, local copies, waits for them, and re-layouts: 7.01 us -> 1.91 us
    ppermute x1, waiting for transfers between devices: 4.35 us -> 0.01 us  [gather_line(): below = lax.ppermute(v, 'tensor', [(a, a + 1) for a in range(3)])]
    ppermute x1, waiting for transfers between devices: 4.15 us -> 0.01 us  [gather_line(): far = lax.ppermute(across, 'tensor', [(2, 3), (1, 0)])]
  transfers between devices with their start and end apart: 23 -> 23, of which waited for: 14 -> 8; matrix products, arithmetic and copies ran while one was open for 0% -> 1% of each run, Pallas kernels for 20% -> 41%
where the time goes in v4:
time: 202 us; the launch traced here: 200 us
  Pallas kernels  84.2 us (42%)
  waiting for transfers between devices  59.1 us (29%)
  starting transfers between devices  53.3 us (26%)
  local copies, waits for them, and re-layouts  2.05 us (1%)
    pallas_call x21, Pallas kernels, __call__(): pl.pallas_call(body, name=name, out_shape=[*outs, TOKEN], in_specs=[SMEM]...  84.2 us
    ppermute x8, waiting for transfers between devices, flip(): return lax.ppermute(v, 'tensor', [(a, a ^ bit) for a in range(shards)])  31.9 us
    ppermute x8, starting transfers between devices, flip(): return lax.ppermute(v, 'tensor', [(a, a ^ bit) for a in range(shards)])  28.6 us
    ppermute x6, waiting for transfers between devices, axis_swap(): return lax.ppermute(v, 'dp', pairs)  20.3 us
    ppermute x6, starting transfers between devices, axis_swap(): return lax.ppermute(v, 'dp', pairs)  7.87 us
    ppermute x1, waiting for transfers between devices, scatter_first(): far = lax.ppermute(far, 'tensor', [(3, 2), (0, 1)])  6.9 us
    ppermute x1, starting transfers between devices, scatter_first(): far = lax.ppermute(far, 'tensor', [(3, 2), (0, 1)])  5.42 us
    ppermute x1, starting transfers between devices, gather_line(): below = lax.ppermute(v, 'tensor', [(a, a + 1) for a in range(3)])  5.36 us
  transfers between devices with their start and end apart: 23, of which 8 were waited for; matrix products, arithmetic and copies ran while one was open for 1% of the time, Pallas kernels for 41%

profile of v4, /device:TPU:0, one launch (start us, length us, event | category | flops | bytes accessed | tf_op | source)
XLA Modules:
  0.0 200.0 jit_solution(15794361121556184944)
XLA Ops:
  0.6 4.1 %collective-permute-start.1 = (bf16[128,2048]{1,0:T(8,128)(2,1)}, bf16[128,2048]{1,0:T(8,128)(2,1)}, u32[]{:S(2)}, u32[]{:S(2)}) collective-permute-start(bf16[128,2048]{1,0:T(8,128)(2,1)} %refs_1_.1), channel_id=1, source_target_pairs={{0,2},{1,3},{2,0},{3,1},{4,6},{5,7},{6,4},{7,5},{8,10},{9,11},{10,... | collective-permute-start | bytes 1572872 | tf_op jit(solution)/shard_map/ppermute | solution.py:277
  7.3 21.0 %collective-permute-done.1.refs_1_.refs_5_.refs_3_ = bf16[128,2048]{1,0:T(8,128)(2,1)} collective-permute-done((bf16[128,2048]{1,0:T(8,128)(2,1)}, bf16[128,2048]{1,0:T(8,128)(2,1)}, u32[]{:S(2)}, u32[]{:S(2)}) %collective-permute-start.1) | collective-permute-done | bytes 524320 | tf_op jit(solution)/shard_map/ppermute | solution.py:277
  32.0 3.4 %collective-permute-start.9 = (bf16[128,2048]{1,0:T(8,128)(2,1)}, bf16[128,2048]{1,0:T(8,128)(2,1)}, u32[]{:S(2)}, u32[]{:S(2)}) collective-permute-start(bf16[128,2048]{1,0:T(8,128)(2,1)} %get-tuple-element.73.refs_3_), channel_id=1, source_target_pairs={{0,2},{1,3},{2,0},{3,1},{4,6},{5,7},{6,4},{7,5},{8,10},{9,11},{10,... | collective-permute-start | bytes 1572872 | tf_op jit(solution)/shard_map/ppermute | solution.py:277
  36.7 5.4 %collective-permute-start.7 = (bf16[128,2048]{1,0:T(8,128)(2,1)}, bf16[128,2048]{1,0:T(8,128)(2,1)}, u32[]{:S(2)}, u32[]{:S(2)}) collective-permute-start(bf16[128,2048]{1,0:T(8,128)(2,1)} %get-tuple-element.73.refs_3_), channel_id=1, source_target_pairs={{0,1},{1,2},{2,3},{4,5},{5,6},{6,7},{8,9},{9,10},{10,11},{12,13},{... | collective-permute-start | bytes 1572872 | tf_op jit(solution)/shard_map/ppermute | solution.py:287
  42.1 9.2 %collective-permute-done.2.refs_6_.refs_4_ = bf16[128,2048]{1,0:T(8,128)(2,1)} collective-permute-done((bf16[128,2048]{1,0:T(8,128)(2,1)}, bf16[128,2048]{1,0:T(8,128)(2,1)}, u32[]{:S(2)}, u32[]{:S(2)}) %collective-permute-start.2) | collective-permute-done | bytes 524320 | tf_op jit(solution)/shard_map/ppermute | solution.py:277
  51.4 11.0 %forward.1 = (bf16[14,128,128]{2,1,0:T(8,128)(2,1)}, bf16[14,128,128]{2,1,0:T(8,128)(2,1)S(1)}, f32[14,128,128]{2,1,0:T(8,128)S(1)}, f32[14,128,128]{2,1,0:T(8,1...) custom-call(s32[2]{0:T(128)S(1)} %pad_add_fusion.refs_0_, ...), custom_call_target="tpu_custom_call" | custom-call | flops 999999986991104 | bytes 999999995904 | tf_op jit(solution)/shard_map/forward/pallas_call | solution.py:261
  63.6 5.4 %collective-permute-start.5 = (bf16[128,2048]{1,0:T(8,128)(2,1)}, bf16[128,2048]{1,0:T(8,128)(2,1)}, u32[]{:S(2)}, u32[]{:S(2)}) collective-permute-start(bf16[128,2048]{1,0:T(8,128)(2,1)} %get-tuple-element.69), channel_id=1, source_target_pairs={{3,2},{0,1},{7,6},{4,5},{11,10},{8,9},{15,14},{12,13},{19,18},{16,... | collective-permute-start | bytes 1572872 | tf_op jit(solution)/shard_map/ppermute | solution.py:298
  69.1 2.8 %turn.1 = (bf16[64,128,128]{2,1,0:T(8,128)(2,1)S(1)}, s32[1]{0:T(128)}) custom-call(s32[2]{0:T(128)S(1)} %pad_add_fusion.refs_0_, bf16[128,2048]{1,0:T(8,128)(2,1)S(1)} %copy-done.5, bf16[128,2048]{1,0:T(8,128)(2,1)} %collective-permute-done.refs_4_.refs_2_, bf16[128,2048]{1,0:T(8,128)(2,1)} %collective-permute-done.1.refs_1_.refs_5_.refs_3_, ...), custom_call_target="tpu_custom_call" | custom-call | flops 999999986991104 | bytes 999999995904 | tf_op jit(solution)/shard_map/turn/pallas_call | solution.py:261
  74.0 6.9 %collective-permute-done.5.refs_1_ = bf16[128,2048]{1,0:T(8,128)(2,1)} collective-permute-done((bf16[128,2048]{1,0:T(8,128)(2,1)}, bf16[128,2048]{1,0:T(8,128)(2,1)}, u32[]{:S(2)}, u32[]{:S(2)}) %collective-permute-start.5) | collective-permute-done | bytes 524320 | tf_op jit(solution)/shard_map/ppermute | solution.py:298
  82.2 3.0 %join.2 = (bf16[128,2048]{1,0:T(8,128)(2,1)}, s32[1]{0:T(128)}) custom-call(bf16[128,2048]{1,0:T(8,128)(2,1)S(1)} %get-tuple-element.68.refs_0_, bf16[128,2048]{1,0:T(8,128)(2,1)} %collective-permute-done.5.refs_1_, s32[1]{0:T(128)} %get-tuple-element.71.refs_2_), custom_call_target="tpu_custom_call" | custom-call | flops 999999986991104 | bytes 999999995904 | tf_op jit(solution)/shard_map/join/pallas_call | solution.py:261
  85.2 9.8 %collective-permute-start.6 = (bf16[128,2048]{1,0:T(8,128)(2,1)}, bf16[128,2048]{1,0:T(8,128)(2,1)}, u32[]{:S(2)}, u32[]{:S(2)}) collective-permute-start(bf16[128,2048]{1,0:T(8,128)(2,1)} %get-tuple-element.72), channel_id=1, source_target_pairs={{0,2},{1,3},{2,0},{3,1},{4,6},{5,7},{6,4},{7,5},{8,10},{9,11},{10,... | collective-permute-start | bytes 1572872 | tf_op jit(solution)/shard_map/ppermute | solution.py:277
  95.1 6.7 %row_grads.1 = (bf16[14,128,128]{2,1,0:T(8,128)(2,1)S(1)}, bf16[14,128,128]{2,1,0:T(8,128)(2,1)S(1)}, s32[1]{0:T(128)}) custom-call(s32[2]{0:T(128)S(1)} %copy-done.11, s32[576]{0:T(1024)S(1)} %reshape.9.refs_1_, s32[3]{0:T(128)S(1)} %bitcast.4, bf16[128,2048]{1,0:T(8,128)(2,1)} %get-tuple-element.73.refs_3_, ...), custom_call_target="tpu_custom_call" | custom-call | flops 999999986991104 | bytes 999999995904 | tf_op jit(solution)/shard_map/row_grads/pallas_call | solution.py:261
  101.8 7.7 %input_grads.1 = (bf16[128,2048]{1,0:T(8,128)(2,1)S(1)}, bf16[128,2048]{1,0:T(8,128)(2,1)}, bf16[128,2048]{1,0:T(8,128)(2,1)S(1)}, bf16[128,2048]{1,0:T(8,128)(2,1)}, s32[1]{0:T(128)}) custom-call(s32[2]{0:T(128)S(1)} %copy-done.11, s32[576]{0:T(1024)S(1)} %reshape.9.refs_1_, s32[3]{0:T(128)S(1)} %bitcast.5, ...), custom_call_target="tpu_custom_call" | custom-call | flops 999999986991104 | bytes 999999995904 | tf_op jit(solution)/shard_map/input_grads/pallas_call | solution.py:261
  109.6 6.2 %down_grads.1 = (bf16[4,12,128,128]{3,2,1,0:T(8,128)(2,1)S(1)}, bf16[4,12,128,128]{3,2,1,0:T(8,128)(2,1)}, s32[1]{0:T(128)}) custom-call(s32[2]{0:T(128)S(1)} %copy-done.11, s32[576]{0:T(1024)S(1)} %reshape.9.refs_1_, s32[3]{0:T(128)S(1)} %bitcast.6, bf16[128,2048]{1,0:T(8,128)(2,1)} %get-tuple-element.73.refs_3_, ...), custom_call_target="tpu_custom_call" | custom-call | flops 999999986991104 | bytes 999999995904 | tf_op jit(solution)/shard_map/down_grads/pallas_call | solution.py:261
  115.9 3.9 %gate_grads.1 = (bf16[4,12,128,128]{3,2,1,0:T(8,128)(2,1)S(1)}, bf16[4,12,128,128]{3,2,1,0:T(8,128)(2,1)}, s32[1]{0:T(128)}) custom-call(s32[2]{0:T(128)S(1)} %copy-done.11, s32[576]{0:T(1024)S(1)} %reshape.9.refs_1_, s32[3]{0:T(128)S(1)} %bitcast.7, bf16[14,128,128]{2,1,0:T(8,128)(2,1)S(1)} %copy-done.17, ...), custom_call_target="tpu_custom_call" | custom-call | flops 999999986991104 | bytes 999999995904 | tf_op jit(solution)/shard_map/gate_grads/pallas_call | solution.py:261
  119.8 2.6 %collective-permute-start.14 = (bf16[128,2048]{1,0:T(8,128)(2,1)}, bf16[128,2048]{1,0:T(8,128)(2,1)}, u32[]{:S(2)}, u32[]{:S(2)}) collective-permute-start(bf16[128,2048]{1,0:T(8,128)(2,1)} %get-tuple-element.97), channel_id=1, source_target_pairs={{0,1},{1,0},{2,3},{3,2},{4,5},{5,4},{6,7},{7,6},{8,9},{9,8},{10,11... | collective-permute-start | bytes 1572872 | tf_op jit(solution)/shard_map/ppermute | solution.py:277
  122.4 3.5 %fold.6 = (bf16[2,12,128,128]{3,2,1,0:T(8,128)(2,1)S(1)}, bf16[2,12,128,128]{3,2,1,0:T(8,128)(2,1)}, s32[1]{0:T(128)}) custom-call(bf16[4,12,128,128]{3,2,1,0:T(8,128)(2,1)S(1)} %get-tuple-element.88.refs_0_, bf16[4,12,128,128]{3,2,1,0:T(8,128)(2,1)} %collective-permute-done.13.refs_1_, s32[1]{0:T(128)} %get-tuple-element.90.refs_2_), custom_call_target="tpu_custom_call" | custom-call | flops 999999986991104 | bytes 999999995904 | tf_op jit(solution)/shard_map/fold/pallas_call | solution.py:261
  130.2 4.2 %up_grads.1 = (bf16[4,12,128,128]{3,2,1,0:T(8,128)(2,1)S(1)}, bf16[4,12,128,128]{3,2,1,0:T(8,128)(2,1)}, s32[1]{0:T(128)}) custom-call(s32[2]{0:T(128)S(1)} %copy-done.11, s32[576]{0:T(1024)S(1)} %reshape.9.refs_1_, s32[3]{0:T(128)S(1)} %bitcast.8, bf16[14,128,128]{2,1,0:T(8,128)(2,1)S(1)} %copy-done.15, ...), custom_call_target="tpu_custom_call" | custom-call | flops 999999986991104 | bytes 999999995904 | tf_op jit(solution)/shard_map/up_grads/pallas_call | solution.py:261
  134.3 6.4 %collective-permute-start.15 = (bf16[128,2048]{1,0:T(8,128)(2,1)}, bf16[128,2048]{1,0:T(8,128)(2,1)}, u32[]{:S(2)}, u32[]{:S(2)}) collective-permute-start(bf16[128,2048]{1,0:T(8,128)(2,1)} %get-tuple-element.98), channel_id=1, source_target_pairs={{0,2},{1,3},{2,0},{3,1},{4,6},{5,7},{6,4},{7,5},{8,10},{9,11},{10,... | collective-permute-start | bytes 1572872 | tf_op jit(solution)/shard_map/ppermute | solution.py:277
  140.7 3.5 %fold.7 = (bf16[2,12,128,128]{3,2,1,0:T(8,128)(2,1)S(1)}, bf16[2,12,128,128]{3,2,1,0:T(8,128)(2,1)}, s32[1]{0:T(128)}) custom-call(bf16[4,12,128,128]{3,2,1,0:T(8,128)(2,1)S(1)} %get-tuple-element.84.refs_0_, bf16[4,12,128,128]{3,2,1,0:T(8,128)(2,1)} %collective-permute-done.11.refs_1_, s32[1]{0:T(128)} %get-tuple-element.93.refs_2_), custom_call_target="tpu_custom_call" | custom-call | flops 999999986991104 | bytes 999999995904 | tf_op jit(solution)/shard_map/fold/pallas_call | solution.py:261
  146.8 3.0 %finish.2 = (bf16[128,2048]{1,0:T(8,128)(2,1)}, s32[1]{0:T(128)}) custom-call(bf16[128,2048]{1,0:T(8,128)(2,1)S(1)} %get-tuple-element.65.refs_0_, bf16[128,2048]{1,0:T(8,128)(2,1)} %collective-permute-done.3.refs_1_, bf16[128,2048]{1,0:T(8,128)(2,1)} %collective-permute-done.4.refs_2_, bf16[128,2048]{1,0:T(8,128)(2,1)} %collective-permute-done.6.refs_3_, ...), custom_call_target="tpu_custom_call" | custom-call | flops 999999986991104 | bytes 999999995904 | tf_op jit(solution)/shard_map/finish/pallas_call | solution.py:261
  149.9 6.7 %collective-permute-done.18.refs_1_ = bf16[2,12,128,128]{3,2,1,0:T(8,128)(2,1)} collective-permute-done((bf16[2,12,128,128]{3,2,1,0:T(8,128)(2,1)}, bf16[2,12,128,128]{3,2,1,0:T(8,128)(2,1)}, u32[]{:S(2)}, u32[]{:S(2)}) %collective-permute-start.18) | collective-permute-done | bytes 786464 | tf_op jit(solution)/shard_map/ppermute | solution.py:311
  156.6 2.8 %fold.8 = (bf16[1,12,128,128]{3,2,1,0:T(8,128)(2,1)S(1)}, bf16[1,12,128,128]{3,2,1,0:T(8,128)(2,1)}, s32[1]{0:T(128)}) custom-call(bf16[2,12,128,128]{3,2,1,0:T(8,128)(2,1)S(1)} %get-tuple-element.103.refs_0_, bf16[2,12,128,128]{3,2,1,0:T(8,128)(2,1)} %collective-permute-done.18.refs_1_, s32[1]{0:T(128)} %get-tuple-element.105.refs_2_), custom_call_target="tpu_custom_call" | custom-call | flops 999999986991104 | bytes 999999995904 | tf_op jit(solution)/shard_map/fold/pallas_call | solution.py:261
  160.9 3.5 %fold.9 = (bf16[2,12,128,128]{3,2,1,0:T(8,128)(2,1)S(1)}, bf16[2,12,128,128]{3,2,1,0:T(8,128)(2,1)}, s32[1]{0:T(128)}) custom-call(bf16[4,12,128,128]{3,2,1,0:T(8,128)(2,1)S(1)} %get-tuple-element.101.refs_0_, bf16[4,12,128,128]{3,2,1,0:T(8,128)(2,1)} %collective-permute-done.17.refs_1_, s32[1]{0:T(128)} %get-tuple-element.106.refs_2_), custom_call_target="tpu_custom_call" | custom-call | flops 999999986991104 | bytes 999999995904 | tf_op jit(solution)/shard_map/fold/pallas_call | solution.py:261
  164.4 4.3 %collective-permute-done.16.refs_1_ = bf16[2,12,128,128]{3,2,1,0:T(8,128)(2,1)} collective-permute-done((bf16[2,12,128,128]{3,2,1,0:T(8,128)(2,1)}, bf16[2,12,128,128]{3,2,1,0:T(8,128)(2,1)}, u32[]{:S(2)}, u32[]{:S(2)}) %collective-permute-start.16) | collective-permute-done | bytes 786464 | tf_op jit(solution)/shard_map/ppermute | solution.py:311
  168.7 3.3 %fold.10 = (bf16[1,12,128,128]{3,2,1,0:T(8,128)(2,1)S(1)}, bf16[1,12,128,128]{3,2,1,0:T(8,128)(2,1)}, s32[1]{0:T(128)}) custom-call(bf16[2,12,128,128]{3,2,1,0:T(8,128)(2,1)S(1)} %get-tuple-element.99.refs_0_, bf16[2,12,128,128]{3,2,1,0:T(8,128)(2,1)} %collective-permute-done.16.refs_1_, s32[1]{0:T(128)} %get-tuple-element.107.refs_2_), custom_call_target="tpu_custom_call" | custom-call | flops 999999986991104 | bytes 999999995904 | tf_op jit(solution)/shard_map/fold/pallas_call | solution.py:261
  175.1 3.1 %update.3 = (f32[3,12,128,128]{3,2,1,0:T(8,128)}, s32[1]{0:T(128)}) custom-call(s32[2]{0:T(128)S(1)} %copy-done.12, s32[3]{0:T(128)S(1)} %bitcast.9, bf16[1,12,128,128]{3,2,1,0:T(8,128)(2,1)S(1)} %get-tuple-element.110.refs_2_, bf16[1,12,128,128]{3,2,1,0:T(8,128)(2,1)} %collective-permute-done.20.refs_3_, f32[3,12,128,128]{3,2,1,0:T(8,128)S(1)} %copy-done.2, ...), custom_call_target="tpu_custom_call" | custom-call | flops 999999986991104 | bytes 999999995904 | tf_op jit(solution)/shard_map/update/pallas_call | solution.py:261
  178.2 7.6 %collective-permute-done.21.refs_1_ = bf16[2,12,128,128]{3,2,1,0:T(8,128)(2,1)} collective-permute-done((bf16[2,12,128,128]{3,2,1,0:T(8,128)(2,1)}, bf16[2,12,128,128]{3,2,1,0:T(8,128)(2,1)}, u32[]{:S(2)}, u32[]{:S(2)}) %collective-permute-start.21) | collective-permute-done | bytes 786464 | tf_op jit(solution)/shard_map/ppermute | solution.py:311
  185.8 2.8 %fold.11 = (bf16[1,12,128,128]{3,2,1,0:T(8,128)(2,1)S(1)}, bf16[1,12,128,128]{3,2,1,0:T(8,128)(2,1)}, s32[1]{0:T(128)}) custom-call(bf16[2,12,128,128]{3,2,1,0:T(8,128)(2,1)S(1)} %get-tuple-element.114.refs_0_, bf16[2,12,128,128]{3,2,1,0:T(8,128)(2,1)} %collective-permute-done.21.refs_1_, s32[1]{0:T(128)} %get-tuple-element.116.refs_2_), custom_call_target="tpu_custom_call" | custom-call | flops 999999986991104 | bytes 999999995904 | tf_op jit(solution)/shard_map/fold/pallas_call | solution.py:261
  189.2 3.1 %update.4 = (f32[3,12,128,128]{3,2,1,0:T(8,128)}, s32[1]{0:T(128)}) custom-call(s32[2]{0:T(128)S(1)} %copy-done.12, s32[3]{0:T(128)S(1)} %bitcast.10, bf16[1,12,128,128]{3,2,1,0:T(8,128)(2,1)S(1)} %get-tuple-element.108.refs_2_, bf16[1,12,128,128]{3,2,1,0:T(8,128)(2,1)} %collective-permute-done.19.refs_3_, ...), custom_call_target="tpu_custom_call", output_to_operand_aliasing={{0}: (6, {})} | custom-call | flops 999999986991104 | bytes 999999995904 | tf_op jit(solution)/shard_map/update/pallas_call | solution.py:261
  192.3 2.7 %finish.3 = (bf16[128,2048]{1,0:T(8,128)(2,1)}, s32[1]{0:T(128)}) custom-call(bf16[128,2048]{1,0:T(8,128)(2,1)S(1)} %get-tuple-element.96.refs_0_, bf16[128,2048]{1,0:T(8,128)(2,1)} %collective-permute-done.14.refs_1_, bf16[128,2048]{1,0:T(8,128)(2,1)} %collective-permute-done.15.refs_2_, s32[1]{0:T(128)} %get-tuple-element.118.refs_3_), custom_call_target="tpu_custom_call" | custom-call | flops 999999986991104 | bytes 999999995904 | tf_op jit(solution)/shard_map/finish/pallas_call | solution.py:261
  196.8 3.1 %update.5 = (f32[3,12,128,128]{3,2,1,0:T(8,128)}, s32[1]{0:T(128)}) custom-call(s32[2]{0:T(128)S(1)} %copy-done.13, s32[3]{0:T(128)S(1)} %bitcast.11, bf16[1,12,128,128]{3,2,1,0:T(8,128)(2,1)S(1)} %get-tuple-element.120.refs_2_, bf16[1,12,128,128]{3,2,1,0:T(8,128)(2,1)} %collective-permute-done.22.refs_3_, ...), custom_call_target="tpu_custom_call", output_to_operand_aliasing={{0}: (6, {})} | custom-call | flops 999999986991104 | bytes 999999995904 | tf_op jit(solution)/shard_map/update/pallas_call | solution.py:261
  (74 shorter events, 26.3 us)
Async XLA Ops:
  0.6 27.7 %collective-permute-start.1 = (bf16[128,2048]{1,0:T(8,128)(2,1)}, bf16[128,2048]{1,0:T(8,128)(2,1)}, u32[]{:S(2)}, u32[]{:S(2)}) collective-permute-start(bf16[128,2048]{1,0:T(8,128)(2,1)} %refs_1_.1), channel_id=1, source_target_pairs={{0,2},{1,3},{2,0},{3,1},{4,6},{5,7},{6,4},{7,5},{8,10},{9,11},{10,... | collective-permute-start | bytes 1572872 | tf_op jit(solution)/shard_map/ppermute | solution.py:277
  4.7 37.4 %collective-permute-start = (bf16[128,2048]{1,0:T(8,128)(2,1)}, bf16[128,2048]{1,0:T(8,128)(2,1)}, u32[]{:S(2)}, u32[]{:S(2)}) collective-permute-start(bf16[128,2048]{1,0:T(8,128)(2,1)} %refs_1_.1), channel_id=1, source_target_pairs={{0,1},{1,0},{2,3},{3,2},{4,5},{5,4},{6,7},{7,6},{8,9},{9,8},{10,11... | collective-permute-start | bytes 1572872 | tf_op jit(solution)/shard_map/ppermute | solution.py:277
  7.3 61.7 %copy-start.10 = (s32[2]{0:T(128)}, s32[2]{0:T(128)S(1)}, u32[]{:S(2)}) copy-start(s32[2]{0:T(128)S(1)} %pad_add_fusion.refs_0_) | copy-start | bytes 28
  28.3 23.0 %collective-permute-start.2 = (bf16[128,2048]{1,0:T(8,128)(2,1)}, bf16[128,2048]{1,0:T(8,128)(2,1)}, u32[]{:S(2)}, u32[]{:S(2)}) collective-permute-start(bf16[128,2048]{1,0:T(8,128)(2,1)} %collective-permute-done.1.refs_1_.refs_5_.refs_3_), channel_id=1, source_target_pairs={{0,1},{1,0},{2,3},{3,2},{4,5},{5,4},{6,7},{7,6},{8,9},{9,8},{10,11... | collective-permute-start | bytes 1572872 | tf_op jit(solution)/shard_map/ppermute | solution.py:277
  30.0 21.4 %copy-start = (bf16[3,96,128,128]{3,2,1,0:T(8,128)(2,1)S(1)}, bf16[3,96,128,128]{3,2,1,0:T(8,128)(2,1)}, u32[]{:S(2)}) copy-start(bf16[3,96,128,128]{3,2,1,0:T(8,128)(2,1)} %refs_5_.4) | copy-start | bytes 28311556
  30.0 21.4 %copy-start.5 = (bf16[128,2048]{1,0:T(8,128)(2,1)S(1)}, bf16[128,2048]{1,0:T(8,128)(2,1)}, u32[]{:S(2)}) copy-start(bf16[128,2048]{1,0:T(8,128)(2,1)} %refs_1_.1) | copy-start | bytes 1572868
  30.0 21.4 %copy-start.6 = (s32[1,3]{1,0:T(1,128)S(1)}, s32[1,3]{1,0:T(1,128)}, u32[]{:S(2)}) copy-start(s32[1,3]{1,0:T(1,128)} %param.11) | copy-start | bytes 40
  32.0 39.8 %collective-permute-start.9 = (bf16[128,2048]{1,0:T(8,128)(2,1)}, bf16[128,2048]{1,0:T(8,128)(2,1)}, u32[]{:S(2)}, u32[]{:S(2)}) collective-permute-start(bf16[128,2048]{1,0:T(8,128)(2,1)} %get-tuple-element.73.refs_3_), channel_id=1, source_target_pairs={{0,2},{1,3},{2,0},{3,1},{4,6},{5,7},{6,4},{7,5},{8,10},{9,11},{10,... | collective-permute-start | bytes 1572872 | tf_op jit(solution)/shard_map/ppermute | solution.py:277
  35.5 49.7 %collective-permute-start.8 = (bf16[128,2048]{1,0:T(8,128)(2,1)}, bf16[128,2048]{1,0:T(8,128)(2,1)}, u32[]{:S(2)}, u32[]{:S(2)}) collective-permute-start(bf16[128,2048]{1,0:T(8,128)(2,1)} %get-tuple-element.73.refs_3_), channel_id=1, source_target_pairs={{1,0},{2,1},{3,2},{5,4},{6,5},{7,6},{9,8},{10,9},{11,10},{13,12},{... | collective-permute-start | bytes 1572872 | tf_op jit(solution)/shard_map/ppermute | solution.py:288
  36.7 58.3 %collective-permute-start.7 = (bf16[128,2048]{1,0:T(8,128)(2,1)}, bf16[128,2048]{1,0:T(8,128)(2,1)}, u32[]{:S(2)}, u32[]{:S(2)}) collective-permute-start(bf16[128,2048]{1,0:T(8,128)(2,1)} %get-tuple-element.73.refs_3_), channel_id=1, source_target_pairs={{0,1},{1,2},{2,3},{4,5},{5,6},{6,7},{8,9},{9,10},{10,11},{12,13},{... | collective-permute-start | bytes 1572872 | tf_op jit(solution)/shard_map/ppermute | solution.py:287
  62.3 81.9 %collective-permute-start.3 = (bf16[128,2048]{1,0:T(8,128)(2,1)}, bf16[128,2048]{1,0:T(8,128)(2,1)}, u32[]{:S(2)}, u32[]{:S(2)}) collective-permute-start(bf16[128,2048]{1,0:T(8,128)(2,1)} %get-tuple-element.66), channel_id=1, source_target_pairs={{1,0},{2,1},{3,2},{5,4},{6,5},{7,6},{9,8},{10,9},{11,10},{13,12},{... | collective-permute-start | bytes 1572872 | tf_op jit(solution)/shard_map/ppermute | solution.py:299
  63.6 17.2 %collective-permute-start.5 = (bf16[128,2048]{1,0:T(8,128)(2,1)}, bf16[128,2048]{1,0:T(8,128)(2,1)}, u32[]{:S(2)}, u32[]{:S(2)}) collective-permute-start(bf16[128,2048]{1,0:T(8,128)(2,1)} %get-tuple-element.69), channel_id=1, source_target_pairs={{3,2},{0,1},{7,6},{4,5},{11,10},{8,9},{15,14},{12,13},{19,18},{16,... | collective-permute-start | bytes 1572872 | tf_op jit(solution)/shard_map/ppermute | solution.py:298
  71.9 74.0 %collective-permute-start.4 = (bf16[128,2048]{1,0:T(8,128)(2,1)}, bf16[128,2048]{1,0:T(8,128)(2,1)}, u32[]{:S(2)}, u32[]{:S(2)}) collective-permute-start(bf16[128,2048]{1,0:T(8,128)(2,1)} %get-tuple-element.67), channel_id=1, source_target_pairs={{0,1},{1,2},{2,3},{4,5},{5,6},{6,7},{8,9},{9,10},{10,11},{12,13},{... | collective-permute-start | bytes 1572872 | tf_op jit(solution)/shard_map/ppermute | solution.py:300
  80.9 14.2 %collective-permute-start.10 = (bf16[128,2048]{1,0:T(8,128)(2,1)}, bf16[128,2048]{1,0:T(8,128)(2,1)}, u32[]{:S(2)}, u32[]{:S(2)}) collective-permute-start(bf16[128,2048]{1,0:T(8,128)(2,1)} %collective-permute-done.9.refs_6_), channel_id=1, source_target_pairs={{2,3},{1,0},{6,7},{5,4},{10,11},{9,8},{14,15},{13,12},{18,19},{17,... | collective-permute-start | bytes 1572872 | tf_op jit(solution)/shard_map/ppermute | solution.py:289
  82.2 12.9 %copy-start.1 = (bf16[3,96,128,128]{3,2,1,0:T(8,128)(2,1)S(1)}, bf16[3,96,128,128]{3,2,1,0:T(8,128)(2,1)}, u32[]{:S(2)}) copy-start(bf16[3,96,128,128]{3,2,1,0:T(8,128)(2,1)} %refs_5_.4) | copy-start | bytes 28311556
  82.2 12.9 %copy-start.7 = (s32[1,3]{1,0:T(1,128)S(1)}, s32[1,3]{1,0:T(1,128)}, u32[]{:S(2)}) copy-start(s32[1,3]{1,0:T(1,128)} %param.11) | copy-start | bytes 40
  82.2 12.9 %copy-start.11 = (s32[2]{0:T(128)S(1)}, s32[2]{0:T(128)}, u32[]{:S(2)}) copy-start(s32[2]{0:T(128)} %copy-done.10) | copy-start | bytes 28
  85.2 60.6 %collective-permute-start.6 = (bf16[128,2048]{1,0:T(8,128)(2,1)}, bf16[128,2048]{1,0:T(8,128)(2,1)}, u32[]{:S(2)}, u32[]{:S(2)}) collective-permute-start(bf16[128,2048]{1,0:T(8,128)(2,1)} %get-tuple-element.72), channel_id=1, source_target_pairs={{0,2},{1,3},{2,0},{3,1},{4,6},{5,7},{6,4},{7,5},{8,10},{9,11},{10,... | collective-permute-start | bytes 1572872 | tf_op jit(solution)/shard_map/ppermute | solution.py:277
  101.8 7.7 %copy-start.14 = (bf16[14,128,128]{2,1,0:T(8,128)(2,1)}, bf16[14,128,128]{2,1,0:T(8,128)(2,1)S(1)}, u32[]{:S(2)}) copy-start(bf16[14,128,128]{2,1,0:T(8,128)(2,1)S(1)} %get-tuple-element.80.refs_4_.refs_3_) | copy-start | bytes 1376260
  101.8 7.7 %copy-start.16 = (bf16[14,128,128]{2,1,0:T(8,128)(2,1)}, bf16[14,128,128]{2,1,0:T(8,128)(2,1)S(1)}, u32[]{:S(2)}) copy-start(bf16[14,128,128]{2,1,0:T(8,128)(2,1)S(1)} %get-tuple-element.77.refs_3_) | copy-start | bytes 1376260
  109.5 18.0 %collective-permute-start.12 = (bf16[128,2048]{1,0:T(8,128)(2,1)}, bf16[128,2048]{1,0:T(8,128)(2,1)}, u32[]{:S(2)}, u32[]{:S(2)}) collective-permute-start(bf16[128,2048]{1,0:T(8,128)(2,1)} %get-tuple-element.87), channel_id=1, source_target_pairs={{0,1},{1,0},{2,3},{3,2},{4,5},{5,4},{6,7},{7,6},{8,9},{9,8},{10,11... | collective-permute-start | bytes 1572872 | tf_op jit(solution)/shard_map/ppermute | solution.py:277
  115.8 4.0 %collective-permute-start.13 = (bf16[4,12,128,128]{3,2,1,0:T(8,128)(2,1)}, bf16[4,12,128,128]{3,2,1,0:T(8,128)(2,1)}, u32[]{:S(2)}, u32[]{:S(2)}) collective-permute-start(bf16[4,12,128,128]{3,2,1,0:T(8,128)(2,1)} %get-tuple-element.89), channel_id=1, source_target_pairs={{0,4},{4,0},{8,12},{12,8},{16,20},{20,16},{24,28},{28,24},{1,5},{5... | collective-permute-start | bytes 4718600 | tf_op jit(solution)/shard_map/ppermute | solution.py:305
  119.8 72.5 %collective-permute-start.14 = (bf16[128,2048]{1,0:T(8,128)(2,1)}, bf16[128,2048]{1,0:T(8,128)(2,1)}, u32[]{:S(2)}, u32[]{:S(2)}) collective-permute-start(bf16[128,2048]{1,0:T(8,128)(2,1)} %get-tuple-element.97), channel_id=1, source_target_pairs={{0,1},{1,0},{2,3},{3,2},{4,5},{5,4},{6,7},{7,6},{8,9},{9,8},{10,11... | collective-permute-start | bytes 1572872 | tf_op jit(solution)/shard_map/ppermute | solution.py:277
  127.6 6.8 %collective-permute-start.11 = (bf16[4,12,128,128]{3,2,1,0:T(8,128)(2,1)}, bf16[4,12,128,128]{3,2,1,0:T(8,128)(2,1)}, u32[]{:S(2)}, u32[]{:S(2)}) collective-permute-start(bf16[4,12,128,128]{3,2,1,0:T(8,128)(2,1)} %get-tuple-element.85), channel_id=1, source_target_pairs={{0,4},{4,0},{8,12},{12,8},{16,20},{20,16},{24,28},{28,24},{1,5},{5... | collective-permute-start | bytes 4718600 | tf_op jit(solution)/shard_map/ppermute | solution.py:305
  134.3 57.9 %collective-permute-start.15 = (bf16[128,2048]{1,0:T(8,128)(2,1)}, bf16[128,2048]{1,0:T(8,128)(2,1)}, u32[]{:S(2)}, u32[]{:S(2)}) collective-permute-start(bf16[128,2048]{1,0:T(8,128)(2,1)} %get-tuple-element.98), channel_id=1, source_target_pairs={{0,2},{1,3},{2,0},{3,1},{4,6},{5,7},{6,4},{7,5},{8,10},{9,11},{10,... | collective-permute-start | bytes 1572872 | tf_op jit(solution)/shard_map/ppermute | solution.py:277
  144.2 12.4 %collective-permute-start.18 = (bf16[2,12,128,128]{3,2,1,0:T(8,128)(2,1)}, bf16[2,12,128,128]{3,2,1,0:T(8,128)(2,1)}, u32[]{:S(2)}, u32[]{:S(2)}) collective-permute-start(bf16[2,12,128,128]{3,2,1,0:T(8,128)(2,1)} %get-tuple-element.104), channel_id=1, source_target_pairs={{0,16},{4,12},{8,24},{12,4},{16,0},{20,28},{24,8},{28,20},{1,17},{... | collective-permute-start | bytes 2359304 | tf_op jit(solution)/shard_map/ppermute | solution.py:311
  145.8 15.1 %collective-permute-start.17 = (bf16[4,12,128,128]{3,2,1,0:T(8,128)(2,1)}, bf16[4,12,128,128]{3,2,1,0:T(8,128)(2,1)}, u32[]{:S(2)}, u32[]{:S(2)}) collective-permute-start(bf16[4,12,128,128]{3,2,1,0:T(8,128)(2,1)} %get-tuple-element.102), channel_id=1, source_target_pairs={{0,4},{4,0},{8,12},{12,8},{16,20},{20,16},{24,28},{28,24},{1,5},{5... | collective-permute-start | bytes 4718600 | tf_op jit(solution)/shard_map/ppermute | solution.py:305
  145.9 22.8 %collective-permute-start.16 = (bf16[2,12,128,128]{3,2,1,0:T(8,128)(2,1)}, bf16[2,12,128,128]{3,2,1,0:T(8,128)(2,1)}, u32[]{:S(2)}, u32[]{:S(2)}) collective-permute-start(bf16[2,12,128,128]{3,2,1,0:T(8,128)(2,1)} %get-tuple-element.100), channel_id=1, source_target_pairs={{0,16},{4,12},{8,24},{12,4},{16,0},{20,28},{24,8},{28,20},{1,17},{... | collective-permute-start | bytes 2359304 | tf_op jit(solution)/shard_map/ppermute | solution.py:311
  159.4 15.7 %collective-permute-start.20 = (bf16[1,12,128,128]{3,2,1,0:T(8,128)(2,1)}, bf16[1,12,128,128]{3,2,1,0:T(8,128)(2,1)}, u32[]{:S(2)}, u32[]{:S(2)}) collective-permute-start(bf16[1,12,128,128]{3,2,1,0:T(8,128)(2,1)} %get-tuple-element.111), channel_id=1, source_target_pairs={{0,8},{4,20},{8,0},{12,28},{16,24},{20,4},{24,16},{28,12},{1,9},{5... | collective-permute-start | bytes 1179656 | tf_op jit(solution)/shard_map/ppermute | solution.py:311
  172.0 17.3 %collective-permute-start.19 = (bf16[1,12,128,128]{3,2,1,0:T(8,128)(2,1)}, bf16[1,12,128,128]{3,2,1,0:T(8,128)(2,1)}, u32[]{:S(2)}, u32[]{:S(2)}) collective-permute-start(bf16[1,12,128,128]{3,2,1,0:T(8,128)(2,1)} %get-tuple-element.109), channel_id=1, source_target_pairs={{0,8},{4,20},{8,0},{12,28},{16,24},{20,4},{24,16},{28,12},{1,9},{5... | collective-permute-start | bytes 1179656 | tf_op jit(solution)/shard_map/ppermute | solution.py:311
  173.5 12.3 %collective-permute-start.21 = (bf16[2,12,128,128]{3,2,1,0:T(8,128)(2,1)}, bf16[2,12,128,128]{3,2,1,0:T(8,128)(2,1)}, u32[]{:S(2)}, u32[]{:S(2)}) collective-permute-start(bf16[2,12,128,128]{3,2,1,0:T(8,128)(2,1)} %get-tuple-element.115), channel_id=1, source_target_pairs={{0,16},{4,12},{8,24},{12,4},{16,0},{20,28},{24,8},{28,20},{1,17},{... | collective-permute-start | bytes 2359304 | tf_op jit(solution)/shard_map/ppermute | solution.py:311
  188.6 8.2 %collective-permute-start.22 = (bf16[1,12,128,128]{3,2,1,0:T(8,128)(2,1)}, bf16[1,12,128,128]{3,2,1,0:T(8,128)(2,1)}, u32[]{:S(2)}, u32[]{:S(2)}) collective-permute-start(bf16[1,12,128,128]{3,2,1,0:T(8,128)(2,1)} %get-tuple-element.121), channel_id=1, source_target_pairs={{0,8},{4,20},{8,0},{12,28},{16,24},{20,4},{24,16},{28,12},{1,9},{5... | collective-permute-start | bytes 1179656 | tf_op jit(solution)/shard_map/ppermute | solution.py:311
  (9 other events, 44.5 us)

commit v5 on v3

--- a/solution.py
+++ b/solution.py
@@ -8,7 +8,8 @@
 
 HB_DEV = 14
 EPSILON = 1e-08
-GROUP = 8
+GROUP = 16
+COST = 10**10
 VMEM_LIMIT = 32 * 1024 * 1024
 F32, BF16 = jnp.float32, jnp.bfloat16
 SHAPE = jax.ShapeDtypeStruct
@@ -19,7 +20,7 @@
 
 
 def group_of(capacity):
-    return next(g for g in (GROUP, 4, 2, 1) if capacity % g == 0)
+    return next(g for g in (GROUP, 8, 4, 2, 1) if capacity % g == 0)
 
 
 def feature_block(ref, block, size):
@@ -217,8 +218,11 @@
     send_out[...] = keep_ref[half:] + got_ref[half:]
 
 
-def add_kernel(a_ref, b_ref, out_ref):
-    out_ref[...] = a_ref[...] + b_ref[...]
+def join_kernel(*refs):
+    ins, outs = refs[: len(refs) // 2 + 1], refs[len(refs) // 2 + 1 :]
+    outs[0][...] = ins[0][...] + ins[1][...]
+    for source, out in zip(ins[2:], outs[1:]):
+        out[...] = source[...]
 
 
 def sum_kernel(*refs):
@@ -248,7 +252,7 @@
 class Line:
     token = None
 
-    def __call__(self, kernel, name, outs, scratch, operands, scalars=(), specs=None, out_specs=None, aliases=None, **more):
+    def __call__(self, kernel, name, outs, scratch, operands, scalars=(), specs=None, out_specs=None, aliases=None, cost=COST, **more):
         tokens = [] if self.token is None else [self.token]
         n_in, n_out = len(scalars) + len(operands), len(outs)
 
@@ -267,6 +271,7 @@
             scratch_shapes=scratch,
             input_output_aliases=aliases or {},
             compiler_params=pltpu.CompilerParams(vmem_limit_bytes=VMEM_LIMIT),
+            cost_estimate=pl.CostEstimate(flops=cost, bytes_accessed=0, transcendentals=0),
             **more,
         )(*scalars, *operands, *tokens)
         return results
@@ -291,13 +296,21 @@
 
 def scatter_first(parts):
     if len(parts) == 4:
-        own, beside, across, far = parts
-        return [own, flip(beside, 4, 1)], across, flip(far, 4, 1)
-    own, below, above, across, far = parts
-    far = lax.ppermute(far, "tensor", [(3, 2), (0, 1)])
+        return flip(parts[3], 4, 1)
+    return lax.ppermute(parts[4], "tensor", [(3, 2), (0, 1)])
+
+
+def scatter_second(line, parts, far):
+    piece = SHAPE(far.shape, far.dtype)
+    if len(parts) == 4:
+        own, beside, across, _ = parts
+        across, beside = line(join_kernel, "join", [piece] * 2, [], [across, far, beside])
+        return [own, flip(across, 4, 2), flip(beside, 4, 1)]
+    own, below, above, across, _ = parts
+    across, below, above = line(join_kernel, "join", [piece] * 3, [], [across, far, below, above])
     below = lax.ppermute(below, "tensor", [(a + 1, a) for a in range(3)])
     above = lax.ppermute(above, "tensor", [(a, a + 1) for a in range(3)])
-    return [own, below, above], across, far
+    return [own, flip(across, 4, 2), below, above]
 
 
 def core_swap(v, replicas):
@@ -362,11 +375,8 @@
             grid=(1,),
         )[0]
 
-    def join(across, far):
-        return flip(line(add_kernel, "join", [piece], [], [across, far])[0], 4, 2)
-
-    def finish(held_parts, across):
-        return line(sum_kernel, "finish", [piece], [], [*held_parts, across])[0]
+    def finish(held_parts):
+        return line(sum_kernel, "finish", [piece], [], held_parts)[0]
 
     x = gather(inputs, gather_near)
     if lined:
@@ -382,14 +392,14 @@
         scalars,
     )
     if lined:
-        out_held, across, far = scatter_first(out_parts)
+        out_far = scatter_first(out_parts)
     else:
         outputs = lax.psum_scatter(out_parts[0], "tensor", scatter_dimension=0)
     (x_turned,) = line(
         functools.partial(turn_kernel, len(x)), "turn", [SHAPE((features, size, rows), BF16)], [held], x, (me,)
     )
     if lined:
-        across = join(across, far)
+        out_sums = scatter_second(line, out_parts, out_far)
     gate_rows, up_rows = line(
         functools.partial(rows_kernel, len(og)),
         "row_grads",
@@ -398,6 +408,7 @@
         [*og, weights, act, slope],
         scalars,
     )
+    down = grads(2, og, hidden_turned)
     in_parts = line(
         functools.partial(input_kernel, len(in_parts)),
         "input_grads",
@@ -407,18 +418,17 @@
         scalars,
     )
     if lined:
-        in_held, in_across, in_far = scatter_first(in_parts)
+        in_far = scatter_first(in_parts)
     else:
         input_grad = lax.psum_scatter(in_parts[0], "tensor", scatter_dimension=0)
-    down = grads(2, og, hidden_turned)
+    if lined:
+        outputs = finish(out_sums)
+    down = fold(*down, 0)
     gate = grads(0, [gate_rows], x_turned)
-    down = fold(*down, 0)
-    if lined:
-        in_across = join(in_across, in_far)
     up = grads(1, [up_rows], x_turned)
+    if lined:
+        in_sums = scatter_second(line, in_parts, in_far)
     gate = fold(*gate, 0)
-    if lined:
-        outputs = finish(out_held, across)
     for step in range(1, levels):
         down = fold(*down, step)
         if step == 1:
@@ -429,7 +439,7 @@
         up = fold(*up, step)
     buffer = update(0, *gate, buffer)
     if lined:
-        input_grad = finish(in_held, in_across)
+        input_grad = finish(in_sums)
     buffer = update(1, *up, buffer)
     return (outputs, input_grad, buffer)
 

time: 217 us -> 171 us (0.79)
  waiting for transfers between devices: 105 us -> 62.2 us
  starting transfers between devices: 38.2 us -> 48.7 us
  Pallas kernels: 64.7 us -> 56.3 us
  local copies, waits for them, and re-layouts: 7.15 us -> 2 us
    ppermute x8, waiting for transfers between devices: 74.5 us -> 33.5 us  [flip(): return lax.ppermute(v, 'tensor', [(a, a ^ bit) for a in range(shards)])]
    ppermute x6, waiting for transfers between devices: 6.11 us -> 17.9 us  [axis_swap(): return lax.ppermute(v, 'dp', pairs)]
    ppermute x8, starting transfers between devices: 15.2 us -> 24.1 us  [flip(): return lax.ppermute(v, 'tensor', [(a, a ^ bit) for a in range(shards)])]
    pallas_call x21, Pallas kernels: 64.7 us -> 56.3 us  [__call__(): pl.pallas_call(body, name=name, out_shape=[*outs, TOKEN], in_specs=[SMEM]...]
    unnamed x29 -> x17, local copies, waits for them, and re-layouts: 7.01 us -> 1.87 us
    ppermute x1, waiting for transfers between devices: 4.35 us -> 0.01 us  [gather_line(): below = lax.ppermute(v, 'tensor', [(a, a + 1) for a in range(3)])]
    ppermute x1, waiting for transfers between devices: 4.15 us -> 0.01 us  [gather_line(): far = lax.ppermute(across, 'tensor', [(2, 3), (1, 0)])]
    ppermute x1, waiting for transfers between devices: 3.2 us -> 0.01 us  [gather_line(): above = lax.ppermute(v, 'tensor', [(a + 1, a) for a in range(3)])]
  transfers between devices with their start and end apart: 23 -> 23, of which waited for: 14 -> 7; matrix products, arithmetic and copies ran while one was open for 0% -> 1% of each run, Pallas kernels for 20% -> 32%
where the time goes in v5:
time: 171 us; the launch traced here: 170 us
  waiting for transfers between devices  62.2 us (36%)
  Pallas kernels  56.3 us (33%)
  starting transfers between devices  48.7 us (28%)
  local copies, waits for them, and re-layouts  2 us (1%)
    pallas_call x21, Pallas kernels, __call__(): pl.pallas_call(body, name=name, out_shape=[*outs, TOKEN], in_specs=[SMEM]...  56.3 us
    ppermute x8, waiting for transfers between devices, flip(): return lax.ppermute(v, 'tensor', [(a, a ^ bit) for a in range(shards)])  33.5 us
    ppermute x8, starting transfers between devices, flip(): return lax.ppermute(v, 'tensor', [(a, a ^ bit) for a in range(shards)])  24.1 us
    ppermute x6, waiting for transfers between devices, axis_swap(): return lax.ppermute(v, 'dp', pairs)  17.9 us
    ppermute x6, starting transfers between devices, axis_swap(): return lax.ppermute(v, 'dp', pairs)  8.8 us
    ppermute x1, waiting for transfers between devices, scatter_first(): return lax.ppermute(parts[4], 'tensor', [(3, 2), (0, 1)])  7.66 us
    ppermute x1, starting transfers between devices, gather_line(): below = lax.ppermute(v, 'tensor', [(a, a + 1) for a in range(3)])  4.58 us
    ppermute x1, starting transfers between devices, scatter_second(): above = lax.ppermute(above, 'tensor', [(a, a + 1) for a in range(3)])  4.58 us
  transfers between devices with their start and end apart: 23, of which 7 were waited for; matrix products, arithmetic and copies ran while one was open for 1% of the time, Pallas kernels for 32%

profile of v5, /device:TPU:0, one launch (start us, length us, event | category | flops | bytes accessed | tf_op | source)
XLA Modules:
  0.0 170.4 jit_solution(13691674873996442418)
XLA Ops:
  0.6 4.1 %collective-permute-start.1 = (bf16[128,2048]{1,0:T(8,128)(2,1)}, bf16[128,2048]{1,0:T(8,128)(2,1)S(1)}, u32[]{:S(2)}, u32[]{:S(2)}) collective-permute-start(bf16[128,2048]{1,0:T(8,128)(2,1)} %refs_1_.1), channel_id=1, source_target_pairs={{0,2},{1,3},{2,0},{3,1},{4,6},{5,7},{6,4},{7,5},{8,10},{9,11},{10,... | collective-permute-start | bytes 1572872 | tf_op jit(solution)/shard_map/ppermute | solution.py:281
  4.7 1.6 collective-permute-start
  7.4 20.9 %collective-permute-done.1.refs_1_.refs_5_.refs_3_ = bf16[128,2048]{1,0:T(8,128)(2,1)S(1)} collective-permute-done((bf16[128,2048]{1,0:T(8,128)(2,1)}, bf16[128,2048]{1,0:T(8,128)(2,1)S(1)}, u32[]{:S(2)}, u32[]{:S(2)}) %collective-permute-start.1) | collective-permute-done | bytes 524320 | tf_op jit(solution)/shard_map/ppermute | solution.py:281
  30.5 3.3 %collective-permute-start.9 = (bf16[128,2048]{1,0:T(8,128)(2,1)S(1)}, bf16[128,2048]{1,0:T(8,128)(2,1)S(1)}, u32[]{:S(2)}, u32[]{:S(2)}) collective-permute-start(bf16[128,2048]{1,0:T(8,128)(2,1)S(1)} %get-tuple-element.78.refs_3_), channel_id=1, source_target_pairs={{0,2},{1,3},{2,0},{3,1},{4,6},{5,7},{6,4},{7,5},{8,10},{9,11},{10,... | collective-permute-start | bytes 1572872 | tf_op jit(solution)/shard_map/ppermute | solution.py:281
  35.2 4.6 %collective-permute-start.7 = (bf16[128,2048]{1,0:T(8,128)(2,1)S(1)}, bf16[128,2048]{1,0:T(8,128)(2,1)S(1)}, u32[]{:S(2)}, u32[]{:S(2)}) collective-permute-start(bf16[128,2048]{1,0:T(8,128)(2,1)S(1)} %get-tuple-element.78.refs_3_), channel_id=1, source_target_pairs={{0,1},{1,2},{2,3},{4,5},{5,6},{6,7},{8,9},{9,10},{10,11},{12,13},{... | collective-permute-start | bytes 1572872 | tf_op jit(solution)/shard_map/ppermute | solution.py:291
  39.8 12.7 %collective-permute-done.2.refs_6_.refs_4_ = bf16[128,2048]{1,0:T(8,128)(2,1)S(1)} collective-permute-done((bf16[128,2048]{1,0:T(8,128)(2,1)S(1)}, bf16[128,2048]{1,0:T(8,128)(2,1)S(1)}, u32[]{:S(2)}, u32[]{:S(2)}) %collective-permute-start.2) | collective-permute-done | bytes 524320 | tf_op jit(solution)/shard_map/ppermute | solution.py:281
  52.4 8.3 %forward.1 = (bf16[14,128,128]{2,1,0:T(8,128)(2,1)}, bf16[14,128,128]{2,1,0:T(8,128)(2,1)S(1)}, f32[14,128,128]{2,1,0:T(8,128)S(1)}, f32[14,128,128]{2,1,0:T(8,1...) custom-call(s32[2]{0:T(128)S(1)} %pad_add_fusion.refs_0_, ...), custom_call_target="tpu_custom_call" | custom-call | flops 10000000000 | tf_op jit(solution)/shard_map/forward/pallas_call | solution.py:265
  60.8 2.4 %collective-permute-start.3 = (bf16[128,2048]{1,0:T(8,128)(2,1)S(1)}, bf16[128,2048]{1,0:T(8,128)(2,1)S(1)}, u32[]{:S(2)}, u32[]{:S(2)}) collective-permute-start(bf16[128,2048]{1,0:T(8,128)(2,1)S(1)} %get-tuple-element.70), channel_id=1, source_target_pairs={{3,2},{0,1},{7,6},{4,5},{11,10},{8,9},{15,14},{12,13},{19,18},{16,... | collective-permute-start | bytes 1572872 | tf_op jit(solution)/shard_map/ppermute | solution.py:300
  64.4 1.9 %turn.1 = (bf16[64,128,128]{2,1,0:T(8,128)(2,1)S(1)}, s32[1]{0:T(128)}) custom-call(s32[2]{0:T(128)S(1)} %pad_add_fusion.refs_0_, bf16[128,2048]{1,0:T(8,128)(2,1)S(1)} %copy-done.3, bf16[128,2048]{1,0:T(8,128)(2,1)S(1)} %collective-permute-done.refs_4_.refs_2_, bf16[128,2048]{1,0:T(8,128)(2,1)S(1)} %collective-permute-done.1.refs_1_.refs_5_.refs_3_, ...), custom_call_target="tpu_custom_call" | custom-call | flops 10000000000 | tf_op jit(solution)/shard_map/turn/pallas_call | solution.py:265
  66.4 7.7 %collective-permute-done.3.refs_1_ = bf16[128,2048]{1,0:T(8,128)(2,1)S(1)} collective-permute-done((bf16[128,2048]{1,0:T(8,128)(2,1)S(1)}, bf16[128,2048]{1,0:T(8,128)(2,1)S(1)}, u32[]{:S(2)}, u32[]{:S(2)}) %collective-permute-start.3) | collective-permute-done | bytes 524320 | tf_op jit(solution)/shard_map/ppermute | solution.py:300
  75.3 4.1 %collective-permute-start.4 = (bf16[128,2048]{1,0:T(8,128)(2,1)S(1)}, bf16[128,2048]{1,0:T(8,128)(2,1)S(1)}, u32[]{:S(2)}, u32[]{:S(2)}) collective-permute-start(bf16[128,2048]{1,0:T(8,128)(2,1)S(1)} %get-tuple-element.75), channel_id=1, source_target_pairs={{0,2},{1,3},{2,0},{3,1},{4,6},{5,7},{6,4},{7,5},{8,10},{9,11},{10,... | collective-permute-start | bytes 1572872 | tf_op jit(solution)/shard_map/ppermute | solution.py:281
  80.7 4.6 %collective-permute-start.6 = (bf16[128,2048]{1,0:T(8,128)(2,1)S(1)}, bf16[128,2048]{1,0:T(8,128)(2,1)S(1)}, u32[]{:S(2)}, u32[]{:S(2)}) collective-permute-start(bf16[128,2048]{1,0:T(8,128)(2,1)S(1)} %get-tuple-element.77), channel_id=1, source_target_pairs={{0,1},{1,2},{2,3},{4,5},{5,6},{6,7},{8,9},{9,10},{10,11},{12,13},{... | collective-permute-start | bytes 1572872 | tf_op jit(solution)/shard_map/ppermute | solution.py:312
  85.3 4.9 %row_grads.1 = (bf16[14,128,128]{2,1,0:T(8,128)(2,1)S(1)}, bf16[14,128,128]{2,1,0:T(8,128)(2,1)S(1)}, s32[1]{0:T(128)}) custom-call(s32[2]{0:T(128)S(1)} %pad_add_fusion.refs_0_, s32[576]{0:T(1024)S(1)} %reshape.9.refs_1_, s32[3]{0:T(128)S(1)} %bitcast.6, bf16[128,2048]{1,0:T(8,128)(2,1)S(1)} %get-tuple-element.78.refs_3_, ...), custom_call_target="tpu_custom_call" | custom-call | flops 10000000000 | tf_op jit(solution)/shard_map/row_grads/pallas_call | solution.py:265
  90.3 4.2 %down_grads.1 = (bf16[4,12,128,128]{3,2,1,0:T(8,128)(2,1)S(1)}, bf16[4,12,128,128]{3,2,1,0:T(8,128)(2,1)S(1)}, s32[1]{0:T(128)}) custom-call(s32[2]{0:T(128)S(1)} %pad_add_fusion.refs_0_, s32[576]{0:T(1024)S(1)} %reshape.9.refs_1_, s32[3]{0:T(128)S(1)} %bitcast.7, bf16[128,2048]{1,0:T(8,128)(2,1)S(1)} %get-tuple-element.78.refs_3_, ...), custom_call_target="tpu_custom_call" | custom-call | flops 10000000000 | tf_op jit(solution)/shard_map/down_grads/pallas_call | solution.py:265
  94.6 6.9 %input_grads.1 = (bf16[128,2048]{1,0:T(8,128)(2,1)S(1)}, bf16[128,2048]{1,0:T(8,128)(2,1)S(1)}, bf16[128,2048]{1,0:T(8,128)(2,1)S(1)}, bf16[128,2048]{1,0:T(8,128)(2,1)S(1)}, s32[1]{0:T(128)}) custom-call(s32[2]{0:T(128)S(1)} %pad_add_fusion.refs_0_, s32[576]{0:T(1024)S(1)} %reshape.9.refs_1_, s32[3]{0:T(128)S(1)} %bitcast.8, ...), custom_call_target="tpu_custom_call" | custom-call | flops 10000000000 | tf_op jit(solution)/shard_map/input_grads/pallas_call | solution.py:265
  101.5 1.6 collective-permute-start.11
  103.1 3.1 %collective-permute-done.5.refs_2_ = bf16[128,2048]{1,0:T(8,128)(2,1)S(1)} collective-permute-done((bf16[128,2048]{1,0:T(8,128)(2,1)S(1)}, bf16[128,2048]{1,0:T(8,128)(2,1)S(1)}, u32[]{:S(2)}, u32[]{:S(2)}) %collective-permute-start.5) | collective-permute-done | bytes 524320 | tf_op jit(solution)/shard_map/ppermute | solution.py:311
  106.2 1.7 finish.2
  109.4 1.6 collective-permute-start.18
  111.0 3.9 %gate_grads.1 = (bf16[4,12,128,128]{3,2,1,0:T(8,128)(2,1)S(1)}, bf16[4,12,128,128]{3,2,1,0:T(8,128)(2,1)S(1)}, s32[1]{0:T(128)}) custom-call(s32[2]{0:T(128)S(1)} %pad_add_fusion.refs_0_, s32[576]{0:T(1024)S(1)} %reshape.9.refs_1_, s32[3]{0:T(128)S(1)} %bitcast.9, bf16[14,128,128]{2,1,0:T(8,128)(2,1)S(1)} %get-tuple-element.82.refs_3_, ...), custom_call_target="tpu_custom_call" | custom-call | flops 10000000000 | tf_op jit(solution)/shard_map/gate_grads/pallas_call | solution.py:265
  115.0 2.9 %up_grads.1 = (bf16[4,12,128,128]{3,2,1,0:T(8,128)(2,1)S(1)}, bf16[4,12,128,128]{3,2,1,0:T(8,128)(2,1)S(1)}, s32[1]{0:T(128)}) custom-call(s32[2]{0:T(128)S(1)} %pad_add_fusion.refs_0_, s32[576]{0:T(1024)S(1)} %reshape.9.refs_1_, s32[3]{0:T(128)S(1)} %bitcast.10, bf16[14,128,128]{2,1,0:T(8,128)(2,1)S(1)} %get-tuple-element.83.refs_4_.refs_3_, ...), custom_call_target="tpu_custom_call" | custom-call | flops 10000000000 | tf_op jit(solution)/shard_map/up_grads/pallas_call | solution.py:265
  119.2 8.4 %collective-permute-start.13 = (bf16[128,2048]{1,0:T(8,128)(2,1)S(1)}, bf16[128,2048]{1,0:T(8,128)(2,1)S(1)}, u32[]{:S(2)}, u32[]{:S(2)}) collective-permute-start(bf16[128,2048]{1,0:T(8,128)(2,1)S(1)} %get-tuple-element.100), channel_id=1, source_target_pairs={{0,2},{1,3},{2,0},{3,1},{4,6},{5,7},{6,4},{7,5},{8,10},{9,11},{10,... | collective-permute-start | bytes 1572872 | tf_op jit(solution)/shard_map/ppermute | solution.py:281
  131.0 1.6 collective-permute-start.20
  134.6 1.6 collective-permute-start.21
  136.2 10.4 %collective-permute-done.16.refs_1_ = bf16[2,12,128,128]{3,2,1,0:T(8,128)(2,1)S(1)} collective-permute-done((bf16[2,12,128,128]{3,2,1,0:T(8,128)(2,1)S(1)}, bf16[2,12,128,128]{3,2,1,0:T(8,128)(2,1)S(1)}, u32[]{:S(2)}, u32[]{:S(2)}) %collective-permute-start.16) | collective-permute-done | bytes 786464 | tf_op jit(solution)/shard_map/ppermute | solution.py:323
  146.6 1.6 fold.10
  149.8 2.7 %update.3 = (f32[3,12,128,128]{3,2,1,0:T(8,128)}, s32[1]{0:T(128)}) custom-call(s32[2]{0:T(128)S(1)} %pad_add_fusion.refs_0_, s32[3]{0:T(128)S(1)} %bitcast.11, bf16[1,12,128,128]{3,2,1,0:T(8,128)(2,1)S(1)} %get-tuple-element.116.refs_2_, bf16[1,12,128,128]{3,2,1,0:T(8,128)(2,1)S(1)} %collective-permute-done.20.refs_3_, f32[3,12,128,128]{3,2,1,0:T(8,128)S(1)} %copy-done, ...), custom_call_target="tpu_custom_call" | custom-call | flops 10000000000 | tf_op jit(solution)/shard_map/update/pallas_call | solution.py:265
  152.5 5.9 %collective-permute-done.21.refs_1_ = bf16[2,12,128,128]{3,2,1,0:T(8,128)(2,1)S(1)} collective-permute-done((bf16[2,12,128,128]{3,2,1,0:T(8,128)(2,1)S(1)}, bf16[2,12,128,128]{3,2,1,0:T(8,128)(2,1)S(1)}, u32[]{:S(2)}, u32[]{:S(2)}) %collective-permute-start.21) | collective-permute-done | bytes 786464 | tf_op jit(solution)/shard_map/ppermute | solution.py:323
  159.8 2.0 %collective-permute-start.22 = (bf16[1,12,128,128]{3,2,1,0:T(8,128)(2,1)S(1)}, bf16[1,12,128,128]{3,2,1,0:T(8,128)(2,1)S(1)}, u32[]{:S(2)}, u32[]{:S(2)}) collective-permute-start(bf16[1,12,128,128]{3,2,1,0:T(8,128)(2,1)S(1)} %get-tuple-element.127), channel_id=1, source_target_pairs={{0,8},{4,20},{8,0},{12,28},{16,24},{20,4},{24,16},{28,12},{1,9},{5... | collective-permute-start | bytes 1179656 | tf_op jit(solution)/shard_map/ppermute | solution.py:323
  161.8 2.6 %update.4 = (f32[3,12,128,128]{3,2,1,0:T(8,128)}, s32[1]{0:T(128)}) custom-call(s32[2]{0:T(128)S(1)} %pad_add_fusion.refs_0_, s32[3]{0:T(128)S(1)} %bitcast.12, bf16[1,12,128,128]{3,2,1,0:T(8,128)(2,1)S(1)} %get-tuple-element.114.refs_2_, bf16[1,12,128,128]{3,2,1,0:T(8,128)(2,1)S(1)} %collective-permute-done.19.refs_3_, ...), custom_call_target="tpu_custom_call", output_to_operand_aliasing={{0}: (6, {})} | custom-call | flops 10000000000 | tf_op jit(solution)/shard_map/update/pallas_call | solution.py:265
  164.5 1.7 finish.3
  167.7 2.6 %update.5 = (f32[3,12,128,128]{3,2,1,0:T(8,128)}, s32[1]{0:T(128)}) custom-call(s32[2]{0:T(128)S(1)} %pad_add_fusion.refs_0_, s32[3]{0:T(128)S(1)} %bitcast.13, bf16[1,12,128,128]{3,2,1,0:T(8,128)(2,1)S(1)} %get-tuple-element.126.refs_2_, bf16[1,12,128,128]{3,2,1,0:T(8,128)(2,1)S(1)} %collective-permute-done.22.refs_3_, ...), custom_call_target="tpu_custom_call", output_to_operand_aliasing={{0}: (6, {})} | custom-call | flops 10000000000 | tf_op jit(solution)/shard_map/update/pallas_call | solution.py:265
  (55 shorter events, 21.4 us)
Async XLA Ops:
  0.6 27.6 %collective-permute-start.1 = (bf16[128,2048]{1,0:T(8,128)(2,1)}, bf16[128,2048]{1,0:T(8,128)(2,1)S(1)}, u32[]{:S(2)}, u32[]{:S(2)}) collective-permute-start(bf16[128,2048]{1,0:T(8,128)(2,1)} %refs_1_.1), channel_id=1, source_target_pairs={{0,2},{1,3},{2,0},{3,1},{4,6},{5,7},{6,4},{7,5},{8,10},{9,11},{10,... | collective-permute-start | bytes 1572872 | tf_op jit(solution)/shard_map/ppermute | solution.py:281
  4.7 35.0 %collective-permute-start = (bf16[128,2048]{1,0:T(8,128)(2,1)}, bf16[128,2048]{1,0:T(8,128)(2,1)S(1)}, u32[]{:S(2)}, u32[]{:S(2)}) collective-permute-start(bf16[128,2048]{1,0:T(8,128)(2,1)} %refs_1_.1), channel_id=1, source_target_pairs={{0,1},{1,0},{2,3},{3,2},{4,5},{5,4},{6,7},{7,6},{8,9},{9,8},{10,11... | collective-permute-start | bytes 1572872 | tf_op jit(solution)/shard_map/ppermute | solution.py:281
  7.3 45.2 %slice-start = ((s8[9437184]{0:T(1024)(128)(4,1)}), s8[4194304]{0:T(1024)(128)(4,1)S(1)}, s32[]{:S(2)}) async-start(s8[9437184]{0:T(1024)(128)(4,1)} %bitcast.3), calls=%async_computation | async-start | bytes 8388608
  7.3 45.1 %slice-start.1 = ((s8[9437184]{0:T(1024)(128)(4,1)}), s8[4194304]{0:T(1024)(128)(4,1)S(1)}, s32[]{:S(2)}) async-start(s8[9437184]{0:T(1024)(128)(4,1)} %bitcast.3), calls=%async_computation.1 | async-start | bytes 8388608
  7.4 45.1 %slice-start.2 = ((s8[9437184]{0:T(1024)(128)(4,1)}), s8[1048576]{0:T(1024)(128)(4,1)S(1)}, s32[]{:S(2)}) async-start(s8[9437184]{0:T(1024)(128)(4,1)} %bitcast.3), calls=%async_computation.2 | async-start | bytes 2097152
  28.2 24.2 %collective-permute-start.2 = (bf16[128,2048]{1,0:T(8,128)(2,1)S(1)}, bf16[128,2048]{1,0:T(8,128)(2,1)S(1)}, u32[]{:S(2)}, u32[]{:S(2)}) collective-permute-start(bf16[128,2048]{1,0:T(8,128)(2,1)S(1)} %collective-permute-done.1.refs_1_.refs_5_.refs_3_), channel_id=1, source_target_pairs={{0,1},{1,0},{2,3},{3,2},{4,5},{5,4},{6,7},{7,6},{8,9},{9,8},{10,11... | collective-permute-start | bytes 1572872 | tf_op jit(solution)/shard_map/ppermute | solution.py:281
  28.9 1.0 copy-start.2
  30.0 22.5 %copy-start.3 = (bf16[128,2048]{1,0:T(8,128)(2,1)S(1)}, bf16[128,2048]{1,0:T(8,128)(2,1)}, u32[]{:S(2)}) copy-start(bf16[128,2048]{1,0:T(8,128)(2,1)} %refs_1_.1) | copy-start | bytes 1572868
  30.0 22.5 %copy-start.4 = (s32[1,3]{1,0:T(1,128)S(1)}, s32[1,3]{1,0:T(1,128)}, u32[]{:S(2)}) copy-start(s32[1,3]{1,0:T(1,128)} %param.11) | copy-start | bytes 40
  30.5 32.6 %collective-permute-start.9 = (bf16[128,2048]{1,0:T(8,128)(2,1)S(1)}, bf16[128,2048]{1,0:T(8,128)(2,1)S(1)}, u32[]{:S(2)}, u32[]{:S(2)}) collective-permute-start(bf16[128,2048]{1,0:T(8,128)(2,1)S(1)} %get-tuple-element.78.refs_3_), channel_id=1, source_target_pairs={{0,2},{1,3},{2,0},{3,1},{4,6},{5,7},{6,4},{7,5},{8,10},{9,11},{10,... | collective-permute-start | bytes 1572872 | tf_op jit(solution)/shard_map/ppermute | solution.py:281
  33.9 46.8 %collective-permute-start.8 = (bf16[128,2048]{1,0:T(8,128)(2,1)S(1)}, bf16[128,2048]{1,0:T(8,128)(2,1)S(1)}, u32[]{:S(2)}, u32[]{:S(2)}) collective-permute-start(bf16[128,2048]{1,0:T(8,128)(2,1)S(1)} %get-tuple-element.78.refs_3_), channel_id=1, source_target_pairs={{1,0},{2,1},{3,2},{5,4},{6,5},{7,6},{9,8},{10,9},{11,10},{13,12},{... | collective-permute-start | bytes 1572872 | tf_op jit(solution)/shard_map/ppermute | solution.py:292
  35.2 50.1 %collective-permute-start.7 = (bf16[128,2048]{1,0:T(8,128)(2,1)S(1)}, bf16[128,2048]{1,0:T(8,128)(2,1)S(1)}, u32[]{:S(2)}, u32[]{:S(2)}) collective-permute-start(bf16[128,2048]{1,0:T(8,128)(2,1)S(1)} %get-tuple-element.78.refs_3_), channel_id=1, source_target_pairs={{0,1},{1,2},{2,3},{4,5},{5,6},{6,7},{8,9},{9,10},{10,11},{12,13},{... | collective-permute-start | bytes 1572872 | tf_op jit(solution)/shard_map/ppermute | solution.py:291
  60.8 13.3 %collective-permute-start.3 = (bf16[128,2048]{1,0:T(8,128)(2,1)S(1)}, bf16[128,2048]{1,0:T(8,128)(2,1)S(1)}, u32[]{:S(2)}, u32[]{:S(2)}) collective-permute-start(bf16[128,2048]{1,0:T(8,128)(2,1)S(1)} %get-tuple-element.70), channel_id=1, source_target_pairs={{3,2},{0,1},{7,6},{4,5},{11,10},{8,9},{15,14},{12,13},{19,18},{16,... | collective-permute-start | bytes 1572872 | tf_op jit(solution)/shard_map/ppermute | solution.py:300
  63.1 22.2 %collective-permute-start.10 = (bf16[128,2048]{1,0:T(8,128)(2,1)S(1)}, bf16[128,2048]{1,0:T(8,128)(2,1)S(1)}, u32[]{:S(2)}, u32[]{:S(2)}) collective-permute-start(bf16[128,2048]{1,0:T(8,128)(2,1)S(1)} %collective-permute-done.9.refs_6_), channel_id=1, source_target_pairs={{2,3},{1,0},{6,7},{5,4},{10,11},{9,8},{14,15},{13,12},{18,19},{17,... | collective-permute-start | bytes 1572872 | tf_op jit(solution)/shard_map/ppermute | solution.py:293
  75.3 27.8 %collective-permute-start.4 = (bf16[128,2048]{1,0:T(8,128)(2,1)S(1)}, bf16[128,2048]{1,0:T(8,128)(2,1)S(1)}, u32[]{:S(2)}, u32[]{:S(2)}) collective-permute-start(bf16[128,2048]{1,0:T(8,128)(2,1)S(1)} %get-tuple-element.75), channel_id=1, source_target_pairs={{0,2},{1,3},{2,0},{3,1},{4,6},{5,7},{6,4},{7,5},{8,10},{9,11},{10,... | collective-permute-start | bytes 1572872 | tf_op jit(solution)/shard_map/ppermute | solution.py:281
  79.4 26.8 %collective-permute-start.5 = (bf16[128,2048]{1,0:T(8,128)(2,1)S(1)}, bf16[128,2048]{1,0:T(8,128)(2,1)S(1)}, u32[]{:S(2)}, u32[]{:S(2)}) collective-permute-start(bf16[128,2048]{1,0:T(8,128)(2,1)S(1)} %get-tuple-element.76), channel_id=1, source_target_pairs={{1,0},{2,1},{3,2},{5,4},{6,5},{7,6},{9,8},{10,9},{11,10},{13,12},{... | collective-permute-start | bytes 1572872 | tf_op jit(solution)/shard_map/ppermute | solution.py:311
  80.7 25.5 %collective-permute-start.6 = (bf16[128,2048]{1,0:T(8,128)(2,1)S(1)}, bf16[128,2048]{1,0:T(8,128)(2,1)S(1)}, u32[]{:S(2)}, u32[]{:S(2)}) collective-permute-start(bf16[128,2048]{1,0:T(8,128)(2,1)S(1)} %get-tuple-element.77), channel_id=1, source_target_pairs={{0,1},{1,2},{2,3},{4,5},{5,6},{6,7},{8,9},{9,10},{10,11},{12,13},{... | collective-permute-start | bytes 1572872 | tf_op jit(solution)/shard_map/ppermute | solution.py:312
  94.5 13.4 %collective-permute-start.12 = (bf16[4,12,128,128]{3,2,1,0:T(8,128)(2,1)S(1)}, bf16[4,12,128,128]{3,2,1,0:T(8,128)(2,1)S(1)}, u32[]{:S(2)}, u32[]{:S(2)}) collective-permute-start(bf16[4,12,128,128]{3,2,1,0:T(8,128)(2,1)S(1)} %get-tuple-element.95), channel_id=1, source_target_pairs={{0,4},{4,0},{8,12},{12,8},{16,20},{20,16},{24,28},{28,24},{1,5},{5... | collective-permute-start | bytes 4718600 | tf_op jit(solution)/shard_map/ppermute | solution.py:317
  101.5 16.4 %collective-permute-start.11 = (bf16[128,2048]{1,0:T(8,128)(2,1)S(1)}, bf16[128,2048]{1,0:T(8,128)(2,1)S(1)}, u32[]{:S(2)}, u32[]{:S(2)}) collective-permute-start(bf16[128,2048]{1,0:T(8,128)(2,1)S(1)} %get-tuple-element.91), channel_id=1, source_target_pairs={{0,1},{1,0},{2,3},{3,2},{4,5},{5,4},{6,7},{7,6},{8,9},{9,8},{10,11... | collective-permute-start | bytes 1572872 | tf_op jit(solution)/shard_map/ppermute | solution.py:281
  109.4 20.3 %collective-permute-start.18 = (bf16[2,12,128,128]{3,2,1,0:T(8,128)(2,1)S(1)}, bf16[2,12,128,128]{3,2,1,0:T(8,128)(2,1)S(1)}, u32[]{:S(2)}, u32[]{:S(2)}) collective-permute-start(bf16[2,12,128,128]{3,2,1,0:T(8,128)(2,1)S(1)} %get-tuple-element.110), channel_id=1, source_target_pairs={{0,16},{4,12},{8,24},{12,4},{16,0},{20,28},{24,8},{28,20},{1,17},{... | collective-permute-start | bytes 2359304 | tf_op jit(solution)/shard_map/ppermute | solution.py:323
  114.9 13.2 %collective-permute-start.15 = (bf16[4,12,128,128]{3,2,1,0:T(8,128)(2,1)S(1)}, bf16[4,12,128,128]{3,2,1,0:T(8,128)(2,1)S(1)}, u32[]{:S(2)}, u32[]{:S(2)}) collective-permute-start(bf16[4,12,128,128]{3,2,1,0:T(8,128)(2,1)S(1)} %get-tuple-element.103), channel_id=1, source_target_pairs={{0,4},{4,0},{8,12},{12,8},{16,20},{20,16},{24,28},{28,24},{1,5},{5... | collective-permute-start | bytes 4718600 | tf_op jit(solution)/shard_map/ppermute | solution.py:317
  119.2 45.2 %collective-permute-start.13 = (bf16[128,2048]{1,0:T(8,128)(2,1)S(1)}, bf16[128,2048]{1,0:T(8,128)(2,1)S(1)}, u32[]{:S(2)}, u32[]{:S(2)}) collective-permute-start(bf16[128,2048]{1,0:T(8,128)(2,1)S(1)} %get-tuple-element.100), channel_id=1, source_target_pairs={{0,2},{1,3},{2,0},{3,1},{4,6},{5,7},{6,4},{7,5},{8,10},{9,11},{10,... | collective-permute-start | bytes 1572872 | tf_op jit(solution)/shard_map/ppermute | solution.py:281
  127.6 36.9 %collective-permute-start.14 = (bf16[128,2048]{1,0:T(8,128)(2,1)S(1)}, bf16[128,2048]{1,0:T(8,128)(2,1)S(1)}, u32[]{:S(2)}, u32[]{:S(2)}) collective-permute-start(bf16[128,2048]{1,0:T(8,128)(2,1)S(1)} %get-tuple-element.101), channel_id=1, source_target_pairs={{0,1},{1,0},{2,3},{3,2},{4,5},{5,4},{6,7},{7,6},{8,9},{9,8},{10,11... | collective-permute-start | bytes 1572872 | tf_op jit(solution)/shard_map/ppermute | solution.py:281
  128.0 5.1 %collective-permute-start.17 = (bf16[4,12,128,128]{3,2,1,0:T(8,128)(2,1)S(1)}, bf16[4,12,128,128]{3,2,1,0:T(8,128)(2,1)S(1)}, u32[]{:S(2)}, u32[]{:S(2)}) collective-permute-start(bf16[4,12,128,128]{3,2,1,0:T(8,128)(2,1)S(1)} %get-tuple-element.108), channel_id=1, source_target_pairs={{0,4},{4,0},{8,12},{12,8},{16,20},{20,16},{24,28},{28,24},{1,5},{5... | collective-permute-start | bytes 4718600 | tf_op jit(solution)/shard_map/ppermute | solution.py:317
  131.0 18.8 %collective-permute-start.20 = (bf16[1,12,128,128]{3,2,1,0:T(8,128)(2,1)S(1)}, bf16[1,12,128,128]{3,2,1,0:T(8,128)(2,1)S(1)}, u32[]{:S(2)}, u32[]{:S(2)}) collective-permute-start(bf16[1,12,128,128]{3,2,1,0:T(8,128)(2,1)S(1)} %get-tuple-element.117), channel_id=1, source_target_pairs={{0,8},{4,20},{8,0},{12,28},{16,24},{20,4},{24,16},{28,12},{1,9},{5... | collective-permute-start | bytes 1179656 | tf_op jit(solution)/shard_map/ppermute | solution.py:323
  132.6 14.0 %collective-permute-start.16 = (bf16[2,12,128,128]{3,2,1,0:T(8,128)(2,1)S(1)}, bf16[2,12,128,128]{3,2,1,0:T(8,128)(2,1)S(1)}, u32[]{:S(2)}, u32[]{:S(2)}) collective-permute-start(bf16[2,12,128,128]{3,2,1,0:T(8,128)(2,1)S(1)} %get-tuple-element.106), channel_id=1, source_target_pairs={{0,16},{4,12},{8,24},{12,4},{16,0},{20,28},{24,8},{28,20},{1,17},{... | collective-permute-start | bytes 2359304 | tf_op jit(solution)/shard_map/ppermute | solution.py:323
  134.6 23.8 %collective-permute-start.21 = (bf16[2,12,128,128]{3,2,1,0:T(8,128)(2,1)S(1)}, bf16[2,12,128,128]{3,2,1,0:T(8,128)(2,1)S(1)}, u32[]{:S(2)}, u32[]{:S(2)}) collective-permute-start(bf16[2,12,128,128]{3,2,1,0:T(8,128)(2,1)S(1)} %get-tuple-element.121), channel_id=1, source_target_pairs={{0,16},{4,12},{8,24},{12,4},{16,0},{20,28},{24,8},{28,20},{1,17},{... | collective-permute-start | bytes 2359304 | tf_op jit(solution)/shard_map/ppermute | solution.py:323
  146.6 3.2 %copy-start = (f32[3,12,128,128]{3,2,1,0:T(8,128)S(1)}, f32[3,12,128,128]{3,2,1,0:T(8,128)}, u32[]{:S(2)}) copy-start(f32[3,12,128,128]{3,2,1,0:T(8,128)} %refs_4_.5) | copy-start | bytes 7077892
  146.6 3.2 %copy-start.1 = (f32[3,12,128,128]{3,2,1,0:T(8,128)S(1)}, f32[3,12,128,128]{3,2,1,0:T(8,128)}, u32[]{:S(2)}) copy-start(f32[3,12,128,128]{3,2,1,0:T(8,128)} %refs_5_.7) | copy-start | bytes 7077892
  148.2 13.6 %collective-permute-start.19 = (bf16[1,12,128,128]{3,2,1,0:T(8,128)(2,1)S(1)}, bf16[1,12,128,128]{3,2,1,0:T(8,128)(2,1)S(1)}, u32[]{:S(2)}, u32[]{:S(2)}) collective-permute-start(bf16[1,12,128,128]{3,2,1,0:T(8,128)(2,1)S(1)} %get-tuple-element.115), channel_id=1, source_target_pairs={{0,8},{4,20},{8,0},{12,28},{16,24},{20,4},{24,16},{28,12},{1,9},{5... | collective-permute-start | bytes 1179656 | tf_op jit(solution)/shard_map/ppermute | solution.py:323
  159.8 7.8 %collective-permute-start.22 = (bf16[1,12,128,128]{3,2,1,0:T(8,128)(2,1)S(1)}, bf16[1,12,128,128]{3,2,1,0:T(8,128)(2,1)S(1)}, u32[]{:S(2)}, u32[]{:S(2)}) collective-permute-start(bf16[1,12,128,128]{3,2,1,0:T(8,128)(2,1)S(1)} %get-tuple-element.127), channel_id=1, source_target_pairs={{0,8},{4,20},{8,0},{12,28},{16,24},{20,4},{24,16},{28,12},{1,9},{5... | collective-permute-start | bytes 1179656 | tf_op jit(solution)/shard_map/ppermute | solution.py:323

commit v6 on v5

--- a/solution.py
+++ b/solution.py
@@ -9,7 +9,7 @@
 HB_DEV = 14
 EPSILON = 1e-08
 GROUP = 16
-COST = 10**10
+COST = 2 * 10**10
 VMEM_LIMIT = 32 * 1024 * 1024
 F32, BF16 = jnp.float32, jnp.bfloat16
 SHAPE = jax.ShapeDtypeStruct
@@ -94,15 +94,10 @@
     elif len(outs) == 4:
         places = [(out, lax.bitwise_xor(me, offset)) for offset, out in enumerate(outs)]
     else:
-        last = len(outs) - 2
-        own, below, above, across, far = outs
-        places = [
-            (own, me),
-            (below, jnp.maximum(me - 1, 0)),
-            (above, jnp.minimum(me + 1, last)),
-            (across, lax.bitwise_xor(me, 2)),
-            (far, last - me),
-        ]
+        last = 3
+        own, beside, across, far, middle = outs
+        places = [(out, lax.bitwise_xor(me, offset)) for offset, out in enumerate((own, beside, across, far))]
+        places.append((middle, last - me))
     for out, t in places:
         for c in range(per_shard):
             out[:, c * size : (c + 1) * size] = total[t * per_shard + c].astype(out.dtype)
@@ -296,21 +291,15 @@
 
 def scatter_first(parts):
     if len(parts) == 4:
-        return flip(parts[3], 4, 1)
-    return lax.ppermute(parts[4], "tensor", [(3, 2), (0, 1)])
-
-
-def scatter_second(line, parts, far):
-    piece = SHAPE(far.shape, far.dtype)
-    if len(parts) == 4:
-        own, beside, across, _ = parts
-        across, beside = line(join_kernel, "join", [piece] * 2, [], [across, far, beside])
-        return [own, flip(across, 4, 2), flip(beside, 4, 1)]
-    own, below, above, across, _ = parts
-    across, below, above = line(join_kernel, "join", [piece] * 3, [], [across, far, below, above])
-    below = lax.ppermute(below, "tensor", [(a + 1, a) for a in range(3)])
-    above = lax.ppermute(above, "tensor", [(a, a + 1) for a in range(3)])
-    return [own, flip(across, 4, 2), below, above]
+        return [flip(parts[3], 4, 1)]
+    return [lax.ppermute(parts[3], "tensor", [(0, 1), (3, 2)]), lax.ppermute(parts[4], "tensor", [(1, 2), (2, 1)])]
+
+
+def scatter_second(line, parts, came):
+    piece = SHAPE(parts[0].shape, parts[0].dtype)
+    own, beside, across = parts[:3]
+    across, beside, *came = line(join_kernel, "join", [piece] * (1 + len(came)), [], [across, came[0], beside, *came[1:]])
+    return [own, flip(across, 4, 2), flip(beside, 4, 1), *came]
 
 
 def core_swap(v, replicas):
@@ -400,6 +389,7 @@
     )
     if lined:
         out_sums = scatter_second(line, out_parts, out_far)
+    down = grads(2, og, hidden_turned)
     gate_rows, up_rows = line(
         functools.partial(rows_kernel, len(og)),
         "row_grads",
@@ -408,7 +398,7 @@
         [*og, weights, act, slope],
         scalars,
     )
-    down = grads(2, og, hidden_turned)
+    down = fold(*down, 0)
     in_parts = line(
         functools.partial(input_kernel, len(in_parts)),
         "input_grads",
@@ -418,26 +408,25 @@
         scalars,
     )
     if lined:
-        in_far = scatter_first(in_parts)
+        in_came = scatter_first(in_parts)
     else:
         input_grad = lax.psum_scatter(in_parts[0], "tensor", scatter_dimension=0)
-    if lined:
-        outputs = finish(out_sums)
-    down = fold(*down, 0)
     gate = grads(0, [gate_rows], x_turned)
-    up = grads(1, [up_rows], x_turned)
-    if lined:
-        in_sums = scatter_second(line, in_parts, in_far)
-    gate = fold(*gate, 0)
     for step in range(1, levels):
         down = fold(*down, step)
-        if step == 1:
-            up = fold(*up, 0)
+    if lined:
+        outputs = finish(out_sums)
+    gate = fold(*gate, 0)
+    up = grads(1, [up_rows], x_turned)
+    if lined:
+        in_sums = scatter_second(line, in_parts, in_came)
+    for step in range(1, levels):
         gate = fold(*gate, step)
+    up = fold(*up, 0)
     buffer = update(2, *down, None)
+    buffer = update(0, *gate, buffer)
     for step in range(1, levels):
         up = fold(*up, step)
-    buffer = update(0, *gate, buffer)
     if lined:
         input_grad = finish(in_sums)
     buffer = update(1, *up, buffer)

time: 171 us -> 157 us (0.918)
  starting transfers between devices: 48.7 us -> 36.2 us
  waiting for transfers between devices: 62.2 us -> 59.1 us
    ppermute x3 -> x2, starting transfers between devices: 8.22 us -> 2.02 us  [the longest x1 1.32 us: scatter_first(): lax.ppermute(parts[3], 'tensor', [(0, 1), (3, 2)])]
    ppermute x8 -> x9, starting transfers between devices: 24.1 us -> 19.2 us  [flip(): return lax.ppermute(v, 'tensor', [(a, a ^ bit) for a in range(shards)])]
    ppermute x3 -> x2, waiting for transfers between devices: 10.8 us -> 8.03 us  [the longest x1 8.02 us: scatter_first(): lax.ppermute(parts[3], 'tensor', [(0, 1), (3, 2)])]
    ppermute x8 -> x9, waiting for transfers between devices: 33.5 us -> 34.1 us  [flip(): return lax.ppermute(v, 'tensor', [(a, a ^ bit) for a in range(shards)])]
  transfers between devices with their start and end apart: 23 -> 23, of which waited for: 7 -> 7; matrix products, arithmetic and copies ran while one was open for 1% -> 1% of each run, Pallas kernels for 32% -> 35%
where the time goes in v6:
time: 157 us; the launch traced here: 155 us
  waiting for transfers between devices  59.1 us (38%)
  Pallas kernels  56.4 us (36%)
  starting transfers between devices  36.2 us (23%)
  local copies, waits for them, and re-layouts  2 us (1%)
    pallas_call x21, Pallas kernels, __call__(): pl.pallas_call(body, name=name, out_shape=[*outs, TOKEN], in_specs=[SMEM]...  56.4 us
    ppermute x9, waiting for transfers between devices, flip(): return lax.ppermute(v, 'tensor', [(a, a ^ bit) for a in range(shards)])  34.1 us
    ppermute x9, starting transfers between devices, flip(): return lax.ppermute(v, 'tensor', [(a, a ^ bit) for a in range(shards)])  19.2 us
    ppermute x6, waiting for transfers between devices, axis_swap(): return lax.ppermute(v, 'dp', pairs)  17 us
    ppermute x1, waiting for transfers between devices, scatter_first(): lax.ppermute(parts[3], 'tensor', [(0, 1), (3, 2)])  8.02 us
    ppermute x6, starting transfers between devices, axis_swap(): return lax.ppermute(v, 'dp', pairs)  7.5 us
    ppermute x1, starting transfers between devices, gather_line(): below = lax.ppermute(v, 'tensor', [(a, a + 1) for a in range(3)])  4.58 us
  transfers between devices with their start and end apart: 23, of which 7 were waited for; matrix products, arithmetic and copies ran while one was open for 1% of the time, Pallas kernels for 35%

profile of v6, /device:TPU:0, one launch (start us, length us, event | category | flops | bytes accessed | tf_op | source)
XLA Modules:
  0.0 154.9 jit_solution(12936843742503928446)
XLA Ops:
  0.6 4.1 %collective-permute-start.1 = (bf16[128,2048]{1,0:T(8,128)(2,1)}, bf16[128,2048]{1,0:T(8,128)(2,1)S(1)}, u32[]{:S(2)}, u32[]{:S(2)}) collective-permute-start(bf16[128,2048]{1,0:T(8,128)(2,1)} %refs_1_.1), channel_id=1, source_target_pairs={{0,2},{1,3},{2,0},{3,1},{4,6},{5,7},{6,4},{7,5},{8,10},{9,11},{10,... | collective-permute-start | bytes 1572872 | tf_op jit(solution)/shard_map/ppermute | solution.py:276
  4.7 1.6 %collective-permute-start = (bf16[128,2048]{1,0:T(8,128)(2,1)}, bf16[128,2048]{1,0:T(8,128)(2,1)S(1)}, u32[]{:S(2)}, u32[]{:S(2)}) collective-permute-start(bf16[128,2048]{1,0:T(8,128)(2,1)} %refs_1_.1), channel_id=1, source_target_pairs={{0,1},{1,0},{2,3},{3,2},{4,5},{5,4},{6,7},{7,6},{8,9},{9,8},{10,11... | collective-permute-start | bytes 1572872 | tf_op jit(solution)/shard_map/ppermute | solution.py:276
  7.4 20.9 %collective-permute-done.1.refs_1_.refs_5_.refs_3_ = bf16[128,2048]{1,0:T(8,128)(2,1)S(1)} collective-permute-done((bf16[128,2048]{1,0:T(8,128)(2,1)}, bf16[128,2048]{1,0:T(8,128)(2,1)S(1)}, u32[]{:S(2)}, u32[]{:S(2)}) %collective-permute-start.1) | collective-permute-done | bytes 524320 | tf_op jit(solution)/shard_map/ppermute | solution.py:276
  30.5 3.3 %collective-permute-start.9 = (bf16[128,2048]{1,0:T(8,128)(2,1)S(1)}, bf16[128,2048]{1,0:T(8,128)(2,1)S(1)}, u32[]{:S(2)}, u32[]{:S(2)}) collective-permute-start(bf16[128,2048]{1,0:T(8,128)(2,1)S(1)} %get-tuple-element.78.refs_3_), channel_id=1, source_target_pairs={{0,2},{1,3},{2,0},{3,1},{4,6},{5,7},{6,4},{7,5},{8,10},{9,11},{10,... | collective-permute-start | bytes 1572872 | tf_op jit(solution)/shard_map/ppermute | solution.py:276
  35.2 4.6 %collective-permute-start.7 = (bf16[128,2048]{1,0:T(8,128)(2,1)S(1)}, bf16[128,2048]{1,0:T(8,128)(2,1)S(1)}, u32[]{:S(2)}, u32[]{:S(2)}) collective-permute-start(bf16[128,2048]{1,0:T(8,128)(2,1)S(1)} %get-tuple-element.78.refs_3_), channel_id=1, source_target_pairs={{0,1},{1,2},{2,3},{4,5},{5,6},{6,7},{8,9},{9,10},{10,11},{12,13},{... | collective-permute-start | bytes 1572872 | tf_op jit(solution)/shard_map/ppermute | solution.py:286
  39.8 12.7 %collective-permute-done.2.refs_6_.refs_4_ = bf16[128,2048]{1,0:T(8,128)(2,1)S(1)} collective-permute-done((bf16[128,2048]{1,0:T(8,128)(2,1)S(1)}, bf16[128,2048]{1,0:T(8,128)(2,1)S(1)}, u32[]{:S(2)}, u32[]{:S(2)}) %collective-permute-start.2) | collective-permute-done | bytes 524320 | tf_op jit(solution)/shard_map/ppermute | solution.py:276
  52.4 8.3 %forward.1 = (bf16[14,128,128]{2,1,0:T(8,128)(2,1)}, bf16[14,128,128]{2,1,0:T(8,128)(2,1)S(1)}, f32[14,128,128]{2,1,0:T(8,128)S(1)}, f32[14,128,128]{2,1,0:T(8,1...) custom-call(s32[2]{0:T(128)S(1)} %pad_add_fusion.refs_0_, ...), custom_call_target="tpu_custom_call" | custom-call | flops 20000000000 | tf_op jit(solution)/shard_map/forward/pallas_call | solution.py:260
  64.1 1.9 %turn.1 = (bf16[64,128,128]{2,1,0:T(8,128)(2,1)S(1)}, s32[1]{0:T(128)}) custom-call(s32[2]{0:T(128)S(1)} %pad_add_fusion.refs_0_, bf16[128,2048]{1,0:T(8,128)(2,1)S(1)} %copy-done.3, bf16[128,2048]{1,0:T(8,128)(2,1)S(1)} %collective-permute-done.refs_4_.refs_2_, bf16[128,2048]{1,0:T(8,128)(2,1)S(1)} %collective-permute-done.1.refs_1_.refs_5_.refs_3_, ...), custom_call_target="tpu_custom_call" | custom-call | flops 20000000000 | tf_op jit(solution)/shard_map/turn/pallas_call | solution.py:260
  66.0 8.0 %collective-permute-done.3.refs_1_ = bf16[128,2048]{1,0:T(8,128)(2,1)S(1)} collective-permute-done((bf16[128,2048]{1,0:T(8,128)(2,1)S(1)}, bf16[128,2048]{1,0:T(8,128)(2,1)S(1)}, u32[]{:S(2)}, u32[]{:S(2)}) %collective-permute-start.3) | collective-permute-done | bytes 524320 | tf_op jit(solution)/shard_map/ppermute | solution.py:295
  75.4 7.0 %collective-permute-start.5 = (bf16[128,2048]{1,0:T(8,128)(2,1)S(1)}, bf16[128,2048]{1,0:T(8,128)(2,1)S(1)}, u32[]{:S(2)}, u32[]{:S(2)}) collective-permute-start(bf16[128,2048]{1,0:T(8,128)(2,1)S(1)} %get-tuple-element.75), channel_id=1, source_target_pairs={{0,2},{1,3},{2,0},{3,1},{4,6},{5,7},{6,4},{7,5},{8,10},{9,11},{10,... | collective-permute-start | bytes 1572872 | tf_op jit(solution)/shard_map/ppermute | solution.py:276
  82.4 4.0 %down_grads.1 = (bf16[4,12,128,128]{3,2,1,0:T(8,128)(2,1)S(1)}, bf16[4,12,128,128]{3,2,1,0:T(8,128)(2,1)S(1)}, s32[1]{0:T(128)}) custom-call(s32[2]{0:T(128)S(1)} %pad_add_fusion.refs_0_, s32[576]{0:T(1024)S(1)} %reshape.9.refs_1_, s32[3]{0:T(128)S(1)} %bitcast.6, bf16[128,2048]{1,0:T(8,128)(2,1)S(1)} %get-tuple-element.78.refs_3_, ...), custom_call_target="tpu_custom_call" | custom-call | flops 20000000000 | tf_op jit(solution)/shard_map/down_grads/pallas_call | solution.py:260
  86.4 4.5 %row_grads.1 = (bf16[14,128,128]{2,1,0:T(8,128)(2,1)S(1)}, bf16[14,128,128]{2,1,0:T(8,128)(2,1)S(1)}, s32[1]{0:T(128)}) custom-call(s32[2]{0:T(128)S(1)} %pad_add_fusion.refs_0_, s32[576]{0:T(1024)S(1)} %reshape.9.refs_1_, s32[3]{0:T(128)S(1)} %bitcast.7, bf16[128,2048]{1,0:T(8,128)(2,1)S(1)} %get-tuple-element.78.refs_3_, ...), custom_call_target="tpu_custom_call" | custom-call | flops 20000000000 | tf_op jit(solution)/shard_map/row_grads/pallas_call | solution.py:260
  90.9 1.5 fold.6
  92.4 1.6 %collective-permute-start.12 = (bf16[2,12,128,128]{3,2,1,0:T(8,128)(2,1)S(1)}, bf16[2,12,128,128]{3,2,1,0:T(8,128)(2,1)S(1)}, u32[]{:S(2)}, u32[]{:S(2)}) collective-permute-start(bf16[2,12,128,128]{3,2,1,0:T(8,128)(2,1)S(1)} %get-tuple-element.88), channel_id=1, source_target_pairs={{0,16},{4,12},{8,24},{12,4},{16,0},{20,28},{24,8},{28,20},{1,17},{... | collective-permute-start | bytes 2359304 | tf_op jit(solution)/shard_map/ppermute | solution.py:312
  94.0 7.4 %input_grads.1 = (bf16[128,2048]{1,0:T(8,128)(2,1)S(1)}, bf16[128,2048]{1,0:T(8,128)(2,1)S(1)}, bf16[128,2048]{1,0:T(8,128)(2,1)S(1)}, bf16[128,2048]{1,0:T(8,128)(2,1)S(1)}, s32[1]{0:T(128)}) custom-call(s32[2]{0:T(128)S(1)} %pad_add_fusion.refs_0_, s32[576]{0:T(1024)S(1)} %reshape.9.refs_1_, s32[3]{0:T(128)S(1)} %bitcast.8, ...), custom_call_target="tpu_custom_call" | custom-call | flops 20000000000 | tf_op jit(solution)/shard_map/input_grads/pallas_call | solution.py:260
  101.5 4.0 %gate_grads.1 = (bf16[4,12,128,128]{3,2,1,0:T(8,128)(2,1)S(1)}, bf16[4,12,128,128]{3,2,1,0:T(8,128)(2,1)S(1)}, s32[1]{0:T(128)}) custom-call(s32[2]{0:T(128)S(1)} %pad_add_fusion.refs_0_, s32[576]{0:T(1024)S(1)} %reshape.9.refs_1_, s32[3]{0:T(128)S(1)} %bitcast.9, bf16[14,128,128]{2,1,0:T(8,128)(2,1)S(1)} %get-tuple-element.89.refs_3_, ...), custom_call_target="tpu_custom_call" | custom-call | flops 20000000000 | tf_op jit(solution)/shard_map/gate_grads/pallas_call | solution.py:260
  107.1 1.4 collective-permute-start.21
  108.5 1.7 %finish.2 = (bf16[128,2048]{1,0:T(8,128)(2,1)}, s32[1]{0:T(128)}) custom-call(bf16[128,2048]{1,0:T(8,128)(2,1)S(1)} %get-tuple-element.68.refs_0_, bf16[128,2048]{1,0:T(8,128)(2,1)S(1)} %collective-permute-done.5.refs_1_, bf16[128,2048]{1,0:T(8,128)(2,1)S(1)} %collective-permute-done.6.refs_2_, bf16[128,2048]{1,0:T(8,128)(2,1)S(1)} %get-tuple-element.77.refs_3_, ...), custom_call_target="tpu_custom_call" | custom-call | flops 20000000000 | tf_op jit(solution)/shard_map/finish/pallas_call | solution.py:260
  110.3 1.5 fold.8
  111.8 3.2 %up_grads.1 = (bf16[4,12,128,128]{3,2,1,0:T(8,128)(2,1)S(1)}, bf16[4,12,128,128]{3,2,1,0:T(8,128)(2,1)S(1)}, s32[1]{0:T(128)}) custom-call(s32[2]{0:T(128)S(1)} %pad_add_fusion.refs_0_, s32[576]{0:T(1024)S(1)} %reshape.9.refs_1_, s32[3]{0:T(128)S(1)} %bitcast.10, bf16[14,128,128]{2,1,0:T(8,128)(2,1)S(1)} %get-tuple-element.91.refs_4_.refs_3_, ...), custom_call_target="tpu_custom_call" | custom-call | flops 20000000000 | tf_op jit(solution)/shard_map/up_grads/pallas_call | solution.py:260
  117.6 1.6 %collective-permute-start.15 = (bf16[128,2048]{1,0:T(8,128)(2,1)S(1)}, bf16[128,2048]{1,0:T(8,128)(2,1)S(1)}, u32[]{:S(2)}, u32[]{:S(2)}) collective-permute-start(bf16[128,2048]{1,0:T(8,128)(2,1)S(1)} %get-tuple-element.106), channel_id=1, source_target_pairs={{0,2},{1,3},{2,0},{3,1},{4,6},{5,7},{6,4},{7,5},{8,10},{9,11},{10,... | collective-permute-start | bytes 1572872 | tf_op jit(solution)/shard_map/ppermute | solution.py:276
  119.9 7.1 %collective-permute-done.18.refs_1_ = bf16[2,12,128,128]{3,2,1,0:T(8,128)(2,1)S(1)} collective-permute-done((bf16[2,12,128,128]{3,2,1,0:T(8,128)(2,1)S(1)}, bf16[2,12,128,128]{3,2,1,0:T(8,128)(2,1)S(1)}, u32[]{:S(2)}, u32[]{:S(2)}) %collective-permute-start.18) | collective-permute-done | bytes 786464 | tf_op jit(solution)/shard_map/ppermute | solution.py:312
  127.0 1.4 fold.9
  129.2 1.6 %fold.10 = (bf16[2,12,128,128]{3,2,1,0:T(8,128)(2,1)S(1)}, bf16[2,12,128,128]{3,2,1,0:T(8,128)(2,1)S(1)}, s32[1]{0:T(128)}) custom-call(bf16[4,12,128,128]{3,2,1,0:T(8,128)(2,1)S(1)} %get-tuple-element.108.refs_0_, bf16[4,12,128,128]{3,2,1,0:T(8,128)(2,1)S(1)} %collective-permute-done.17.refs_1_, s32[1]{0:T(128)} %get-tuple-element.113.refs_2_), custom_call_target="tpu_custom_call" | custom-call | flops 20000000000 | tf_op jit(solution)/shard_map/fold/pallas_call | solution.py:260
  130.8 1.6 %collective-permute-start.19 = (bf16[2,12,128,128]{3,2,1,0:T(8,128)(2,1)S(1)}, bf16[2,12,128,128]{3,2,1,0:T(8,128)(2,1)S(1)}, u32[]{:S(2)}, u32[]{:S(2)}) collective-permute-start(bf16[2,12,128,128]{3,2,1,0:T(8,128)(2,1)S(1)} %get-tuple-element.115), channel_id=1, source_target_pairs={{0,16},{4,12},{8,24},{12,4},{16,0},{20,28},{24,8},{28,20},{1,17},{... | collective-permute-start | bytes 2359304 | tf_op jit(solution)/shard_map/ppermute | solution.py:312
  132.5 2.7 %update.3 = (f32[3,12,128,128]{3,2,1,0:T(8,128)}, s32[1]{0:T(128)}) custom-call(s32[2]{0:T(128)S(1)} %pad_add_fusion.refs_0_, s32[3]{0:T(128)S(1)} %bitcast.11, bf16[1,12,128,128]{3,2,1,0:T(8,128)(2,1)S(1)} %get-tuple-element.118.refs_2_, bf16[1,12,128,128]{3,2,1,0:T(8,128)(2,1)S(1)} %collective-permute-done.21.refs_3_, f32[3,12,128,128]{3,2,1,0:T(8,128)S(1)} %copy-done, ...), custom_call_target="tpu_custom_call" | custom-call | flops 20000000000 | tf_op jit(solution)/shard_map/update/pallas_call | solution.py:260
  135.1 5.1 %collective-permute-done.20.refs_3_ = bf16[1,12,128,128]{3,2,1,0:T(8,128)(2,1)S(1)} collective-permute-done((bf16[1,12,128,128]{3,2,1,0:T(8,128)(2,1)S(1)}, bf16[1,12,128,128]{3,2,1,0:T(8,128)(2,1)S(1)}, u32[]{:S(2)}, u32[]{:S(2)}) %collective-permute-start.20) | collective-permute-done | bytes 393248 | tf_op jit(solution)/shard_map/ppermute | solution.py:312
  140.2 2.6 %update.4 = (f32[3,12,128,128]{3,2,1,0:T(8,128)}, s32[1]{0:T(128)}) custom-call(s32[2]{0:T(128)S(1)} %pad_add_fusion.refs_0_, s32[3]{0:T(128)S(1)} %bitcast.12, bf16[1,12,128,128]{3,2,1,0:T(8,128)(2,1)S(1)} %get-tuple-element.116.refs_2_, bf16[1,12,128,128]{3,2,1,0:T(8,128)(2,1)S(1)} %collective-permute-done.20.refs_3_, ...), custom_call_target="tpu_custom_call", output_to_operand_aliasing={{0}: (6, {})} | custom-call | flops 20000000000 | tf_op jit(solution)/shard_map/update/pallas_call | solution.py:260
  144.3 1.4 collective-permute-start.22
  145.7 1.7 %finish.3 = (bf16[128,2048]{1,0:T(8,128)(2,1)}, s32[1]{0:T(128)}) custom-call(bf16[128,2048]{1,0:T(8,128)(2,1)S(1)} %get-tuple-element.97.refs_0_, bf16[128,2048]{1,0:T(8,128)(2,1)S(1)} %collective-permute-done.15.refs_1_, bf16[128,2048]{1,0:T(8,128)(2,1)S(1)} %collective-permute-done.16.refs_2_, s32[1]{0:T(128)} %get-tuple-element.124.refs_3_), custom_call_target="tpu_custom_call" | custom-call | flops 20000000000 | tf_op jit(solution)/shard_map/finish/pallas_call | solution.py:260
  147.4 4.8 %collective-permute-done.22.refs_3_ = bf16[1,12,128,128]{3,2,1,0:T(8,128)(2,1)S(1)} collective-permute-done((bf16[1,12,128,128]{3,2,1,0:T(8,128)(2,1)S(1)}, bf16[1,12,128,128]{3,2,1,0:T(8,128)(2,1)S(1)}, u32[]{:S(2)}, u32[]{:S(2)}) %collective-permute-start.22) | collective-permute-done | bytes 393248 | tf_op jit(solution)/shard_map/ppermute | solution.py:312
  152.1 2.6 %update.5 = (f32[3,12,128,128]{3,2,1,0:T(8,128)}, s32[1]{0:T(128)}) custom-call(s32[2]{0:T(128)S(1)} %pad_add_fusion.refs_0_, s32[3]{0:T(128)S(1)} %bitcast.13, bf16[1,12,128,128]{3,2,1,0:T(8,128)(2,1)S(1)} %get-tuple-element.126.refs_2_, bf16[1,12,128,128]{3,2,1,0:T(8,128)(2,1)S(1)} %collective-permute-done.22.refs_3_, ...), custom_call_target="tpu_custom_call", output_to_operand_aliasing={{0}: (6, {})} | custom-call | flops 20000000000 | tf_op jit(solution)/shard_map/update/pallas_call | solution.py:260
  (55 shorter events, 16.6 us)
Async XLA Ops:
  0.6 27.6 %collective-permute-start.1 = (bf16[128,2048]{1,0:T(8,128)(2,1)}, bf16[128,2048]{1,0:T(8,128)(2,1)S(1)}, u32[]{:S(2)}, u32[]{:S(2)}) collective-permute-start(bf16[128,2048]{1,0:T(8,128)(2,1)} %refs_1_.1), channel_id=1, source_target_pairs={{0,2},{1,3},{2,0},{3,1},{4,6},{5,7},{6,4},{7,5},{8,10},{9,11},{10,... | collective-permute-start | bytes 1572872 | tf_op jit(solution)/shard_map/ppermute | solution.py:276
  4.7 35.0 %collective-permute-start = (bf16[128,2048]{1,0:T(8,128)(2,1)}, bf16[128,2048]{1,0:T(8,128)(2,1)S(1)}, u32[]{:S(2)}, u32[]{:S(2)}) collective-permute-start(bf16[128,2048]{1,0:T(8,128)(2,1)} %refs_1_.1), channel_id=1, source_target_pairs={{0,1},{1,0},{2,3},{3,2},{4,5},{5,4},{6,7},{7,6},{8,9},{9,8},{10,11... | collective-permute-start | bytes 1572872 | tf_op jit(solution)/shard_map/ppermute | solution.py:276
  7.3 45.2 %slice-start = ((s8[9437184]{0:T(1024)(128)(4,1)}), s8[4194304]{0:T(1024)(128)(4,1)S(1)}, s32[]{:S(2)}) async-start(s8[9437184]{0:T(1024)(128)(4,1)} %bitcast.3), calls=%async_computation | async-start | bytes 8388608
  7.3 45.1 %slice-start.1 = ((s8[9437184]{0:T(1024)(128)(4,1)}), s8[4194304]{0:T(1024)(128)(4,1)S(1)}, s32[]{:S(2)}) async-start(s8[9437184]{0:T(1024)(128)(4,1)} %bitcast.3), calls=%async_computation.1 | async-start | bytes 8388608
  7.4 45.1 %slice-start.2 = ((s8[9437184]{0:T(1024)(128)(4,1)}), s8[1048576]{0:T(1024)(128)(4,1)S(1)}, s32[]{:S(2)}) async-start(s8[9437184]{0:T(1024)(128)(4,1)} %bitcast.3), calls=%async_computation.2 | async-start | bytes 2097152
  28.2 24.2 %collective-permute-start.2 = (bf16[128,2048]{1,0:T(8,128)(2,1)S(1)}, bf16[128,2048]{1,0:T(8,128)(2,1)S(1)}, u32[]{:S(2)}, u32[]{:S(2)}) collective-permute-start(bf16[128,2048]{1,0:T(8,128)(2,1)S(1)} %collective-permute-done.1.refs_1_.refs_5_.refs_3_), channel_id=1, source_target_pairs={{0,1},{1,0},{2,3},{3,2},{4,5},{5,4},{6,7},{7,6},{8,9},{9,8},{10,11... | collective-permute-start | bytes 1572872 | tf_op jit(solution)/shard_map/ppermute | solution.py:276
  28.9 1.0 copy-start.2
  30.0 22.5 %copy-start.3 = (bf16[128,2048]{1,0:T(8,128)(2,1)S(1)}, bf16[128,2048]{1,0:T(8,128)(2,1)}, u32[]{:S(2)}) copy-start(bf16[128,2048]{1,0:T(8,128)(2,1)} %refs_1_.1) | copy-start | bytes 1572868
  30.0 22.5 %copy-start.4 = (s32[1,3]{1,0:T(1,128)S(1)}, s32[1,3]{1,0:T(1,128)}, u32[]{:S(2)}) copy-start(s32[1,3]{1,0:T(1,128)} %param.11) | copy-start | bytes 40
  30.5 32.2 %collective-permute-start.9 = (bf16[128,2048]{1,0:T(8,128)(2,1)S(1)}, bf16[128,2048]{1,0:T(8,128)(2,1)S(1)}, u32[]{:S(2)}, u32[]{:S(2)}) collective-permute-start(bf16[128,2048]{1,0:T(8,128)(2,1)S(1)} %get-tuple-element.78.refs_3_), channel_id=1, source_target_pairs={{0,2},{1,3},{2,0},{3,1},{4,6},{5,7},{6,4},{7,5},{8,10},{9,11},{10,... | collective-permute-start | bytes 1572872 | tf_op jit(solution)/shard_map/ppermute | solution.py:276
  33.9 48.5 %collective-permute-start.8 = (bf16[128,2048]{1,0:T(8,128)(2,1)S(1)}, bf16[128,2048]{1,0:T(8,128)(2,1)S(1)}, u32[]{:S(2)}, u32[]{:S(2)}) collective-permute-start(bf16[128,2048]{1,0:T(8,128)(2,1)S(1)} %get-tuple-element.78.refs_3_), channel_id=1, source_target_pairs={{1,0},{2,1},{3,2},{5,4},{6,5},{7,6},{9,8},{10,9},{11,10},{13,12},{... | collective-permute-start | bytes 1572872 | tf_op jit(solution)/shard_map/ppermute | solution.py:287
  35.2 47.2 %collective-permute-start.7 = (bf16[128,2048]{1,0:T(8,128)(2,1)S(1)}, bf16[128,2048]{1,0:T(8,128)(2,1)S(1)}, u32[]{:S(2)}, u32[]{:S(2)}) collective-permute-start(bf16[128,2048]{1,0:T(8,128)(2,1)S(1)} %get-tuple-element.78.refs_3_), channel_id=1, source_target_pairs={{0,1},{1,2},{2,3},{4,5},{5,6},{6,7},{8,9},{9,10},{10,11},{12,13},{... | collective-permute-start | bytes 1572872 | tf_op jit(solution)/shard_map/ppermute | solution.py:286
  60.7 13.3 %collective-permute-start.3 = (bf16[128,2048]{1,0:T(8,128)(2,1)S(1)}, bf16[128,2048]{1,0:T(8,128)(2,1)S(1)}, u32[]{:S(2)}, u32[]{:S(2)}) collective-permute-start(bf16[128,2048]{1,0:T(8,128)(2,1)S(1)} %get-tuple-element.70), channel_id=1, source_target_pairs={{0,1},{3,2},{4,5},{7,6},{8,9},{11,10},{12,13},{15,14},{16,17},{19,... | collective-permute-start | bytes 1572872 | tf_op jit(solution)/shard_map/ppermute | solution.py:295
  62.1 12.0 %collective-permute-start.4 = (bf16[128,2048]{1,0:T(8,128)(2,1)S(1)}, bf16[128,2048]{1,0:T(8,128)(2,1)S(1)}, u32[]{:S(2)}, u32[]{:S(2)}) collective-permute-start(bf16[128,2048]{1,0:T(8,128)(2,1)S(1)} %get-tuple-element.72), channel_id=1, source_target_pairs={{1,2},{2,1},{5,6},{6,5},{9,10},{10,9},{13,14},{14,13},{17,18},{18,... | collective-permute-start | bytes 1572872 | tf_op jit(solution)/shard_map/ppermute | solution.py:295
  62.8 19.6 %collective-permute-start.10 = (bf16[128,2048]{1,0:T(8,128)(2,1)S(1)}, bf16[128,2048]{1,0:T(8,128)(2,1)S(1)}, u32[]{:S(2)}, u32[]{:S(2)}) collective-permute-start(bf16[128,2048]{1,0:T(8,128)(2,1)S(1)} %collective-permute-done.9.refs_6_), channel_id=1, source_target_pairs={{2,3},{1,0},{6,7},{5,4},{10,11},{9,8},{14,15},{13,12},{18,19},{17,... | collective-permute-start | bytes 1572872 | tf_op jit(solution)/shard_map/ppermute | solution.py:288
  75.4 33.2 %collective-permute-start.5 = (bf16[128,2048]{1,0:T(8,128)(2,1)S(1)}, bf16[128,2048]{1,0:T(8,128)(2,1)S(1)}, u32[]{:S(2)}, u32[]{:S(2)}) collective-permute-start(bf16[128,2048]{1,0:T(8,128)(2,1)S(1)} %get-tuple-element.75), channel_id=1, source_target_pairs={{0,2},{1,3},{2,0},{3,1},{4,6},{5,7},{6,4},{7,5},{8,10},{9,11},{10,... | collective-permute-start | bytes 1572872 | tf_op jit(solution)/shard_map/ppermute | solution.py:276
  82.3 26.2 %collective-permute-start.6 = (bf16[128,2048]{1,0:T(8,128)(2,1)S(1)}, bf16[128,2048]{1,0:T(8,128)(2,1)S(1)}, u32[]{:S(2)}, u32[]{:S(2)}) collective-permute-start(bf16[128,2048]{1,0:T(8,128)(2,1)S(1)} %get-tuple-element.76), channel_id=1, source_target_pairs={{0,1},{1,0},{2,3},{3,2},{4,5},{5,4},{6,7},{7,6},{8,9},{9,8},{10,11... | collective-permute-start | bytes 1572872 | tf_op jit(solution)/shard_map/ppermute | solution.py:276
  86.3 4.5 %collective-permute-start.11 = (bf16[4,12,128,128]{3,2,1,0:T(8,128)(2,1)S(1)}, bf16[4,12,128,128]{3,2,1,0:T(8,128)(2,1)S(1)}, u32[]{:S(2)}, u32[]{:S(2)}) collective-permute-start(bf16[4,12,128,128]{3,2,1,0:T(8,128)(2,1)S(1)} %get-tuple-element.82), channel_id=1, source_target_pairs={{0,4},{4,0},{8,12},{12,8},{16,20},{20,16},{24,28},{28,24},{1,5},{5... | collective-permute-start | bytes 4718600 | tf_op jit(solution)/shard_map/ppermute | solution.py:306
  92.4 13.4 %collective-permute-start.12 = (bf16[2,12,128,128]{3,2,1,0:T(8,128)(2,1)S(1)}, bf16[2,12,128,128]{3,2,1,0:T(8,128)(2,1)S(1)}, u32[]{:S(2)}, u32[]{:S(2)}) collective-permute-start(bf16[2,12,128,128]{3,2,1,0:T(8,128)(2,1)S(1)} %get-tuple-element.88), channel_id=1, source_target_pairs={{0,16},{4,12},{8,24},{12,4},{16,0},{20,28},{24,8},{28,20},{1,17},{... | collective-permute-start | bytes 2359304 | tf_op jit(solution)/shard_map/ppermute | solution.py:312
  101.4 14.9 %collective-permute-start.13 = (bf16[128,2048]{1,0:T(8,128)(2,1)S(1)}, bf16[128,2048]{1,0:T(8,128)(2,1)S(1)}, u32[]{:S(2)}, u32[]{:S(2)}) collective-permute-start(bf16[128,2048]{1,0:T(8,128)(2,1)S(1)} %get-tuple-element.99), channel_id=1, source_target_pairs={{0,1},{1,0},{2,3},{3,2},{4,5},{5,4},{6,7},{7,6},{8,9},{9,8},{10,11... | collective-permute-start | bytes 1572872 | tf_op jit(solution)/shard_map/ppermute | solution.py:276
  105.5 4.7 %collective-permute-start.14 = (bf16[4,12,128,128]{3,2,1,0:T(8,128)(2,1)S(1)}, bf16[4,12,128,128]{3,2,1,0:T(8,128)(2,1)S(1)}, u32[]{:S(2)}, u32[]{:S(2)}) collective-permute-start(bf16[4,12,128,128]{3,2,1,0:T(8,128)(2,1)S(1)} %get-tuple-element.102), channel_id=1, source_target_pairs={{0,4},{4,0},{8,12},{12,8},{16,20},{20,16},{24,28},{28,24},{1,5},{5... | collective-permute-start | bytes 4718600 | tf_op jit(solution)/shard_map/ppermute | solution.py:306
  107.1 25.3 %collective-permute-start.21 = (bf16[1,12,128,128]{3,2,1,0:T(8,128)(2,1)S(1)}, bf16[1,12,128,128]{3,2,1,0:T(8,128)(2,1)S(1)}, u32[]{:S(2)}, u32[]{:S(2)}) collective-permute-start(bf16[1,12,128,128]{3,2,1,0:T(8,128)(2,1)S(1)} %get-tuple-element.119), channel_id=1, source_target_pairs={{0,8},{4,20},{8,0},{12,28},{16,24},{20,4},{24,16},{28,12},{1,9},{5... | collective-permute-start | bytes 1179656 | tf_op jit(solution)/shard_map/ppermute | solution.py:312
  114.9 12.1 %collective-permute-start.18 = (bf16[2,12,128,128]{3,2,1,0:T(8,128)(2,1)S(1)}, bf16[2,12,128,128]{3,2,1,0:T(8,128)(2,1)S(1)}, u32[]{:S(2)}, u32[]{:S(2)}) collective-permute-start(bf16[2,12,128,128]{3,2,1,0:T(8,128)(2,1)S(1)} %get-tuple-element.111), channel_id=1, source_target_pairs={{0,16},{4,12},{8,24},{12,4},{16,0},{20,28},{24,8},{28,20},{1,17},{... | collective-permute-start | bytes 2359304 | tf_op jit(solution)/shard_map/ppermute | solution.py:312
  117.6 28.2 %collective-permute-start.15 = (bf16[128,2048]{1,0:T(8,128)(2,1)S(1)}, bf16[128,2048]{1,0:T(8,128)(2,1)S(1)}, u32[]{:S(2)}, u32[]{:S(2)}) collective-permute-start(bf16[128,2048]{1,0:T(8,128)(2,1)S(1)} %get-tuple-element.106), channel_id=1, source_target_pairs={{0,2},{1,3},{2,0},{3,1},{4,6},{5,7},{6,4},{7,5},{8,10},{9,11},{10,... | collective-permute-start | bytes 1572872 | tf_op jit(solution)/shard_map/ppermute | solution.py:276
  119.1 26.6 %collective-permute-start.16 = (bf16[128,2048]{1,0:T(8,128)(2,1)S(1)}, bf16[128,2048]{1,0:T(8,128)(2,1)S(1)}, u32[]{:S(2)}, u32[]{:S(2)}) collective-permute-start(bf16[128,2048]{1,0:T(8,128)(2,1)S(1)} %get-tuple-element.107), channel_id=1, source_target_pairs={{0,1},{1,0},{2,3},{3,2},{4,5},{5,4},{6,7},{7,6},{8,9},{9,8},{10,11... | collective-permute-start | bytes 1572872 | tf_op jit(solution)/shard_map/ppermute | solution.py:276
  119.9 9.3 %collective-permute-start.17 = (bf16[4,12,128,128]{3,2,1,0:T(8,128)(2,1)S(1)}, bf16[4,12,128,128]{3,2,1,0:T(8,128)(2,1)S(1)}, u32[]{:S(2)}, u32[]{:S(2)}) collective-permute-start(bf16[4,12,128,128]{3,2,1,0:T(8,128)(2,1)S(1)} %get-tuple-element.109), channel_id=1, source_target_pairs={{0,4},{4,0},{8,12},{12,8},{16,20},{20,16},{24,28},{28,24},{1,5},{5... | collective-permute-start | bytes 4718600 | tf_op jit(solution)/shard_map/ppermute | solution.py:306
  128.4 11.8 %collective-permute-start.20 = (bf16[1,12,128,128]{3,2,1,0:T(8,128)(2,1)S(1)}, bf16[1,12,128,128]{3,2,1,0:T(8,128)(2,1)S(1)}, u32[]{:S(2)}, u32[]{:S(2)}) collective-permute-start(bf16[1,12,128,128]{3,2,1,0:T(8,128)(2,1)S(1)} %get-tuple-element.117), channel_id=1, source_target_pairs={{0,8},{4,20},{8,0},{12,28},{16,24},{20,4},{24,16},{28,12},{1,9},{5... | collective-permute-start | bytes 1179656 | tf_op jit(solution)/shard_map/ppermute | solution.py:312
  129.2 3.3 %copy-start = (f32[3,12,128,128]{3,2,1,0:T(8,128)S(1)}, f32[3,12,128,128]{3,2,1,0:T(8,128)}, u32[]{:S(2)}) copy-start(f32[3,12,128,128]{3,2,1,0:T(8,128)} %refs_4_.5) | copy-start | bytes 7077892
  129.2 3.3 %copy-start.1 = (f32[3,12,128,128]{3,2,1,0:T(8,128)S(1)}, f32[3,12,128,128]{3,2,1,0:T(8,128)}, u32[]{:S(2)}) copy-start(f32[3,12,128,128]{3,2,1,0:T(8,128)} %refs_5_.7) | copy-start | bytes 7077892
  130.8 12.1 %collective-permute-start.19 = (bf16[2,12,128,128]{3,2,1,0:T(8,128)(2,1)S(1)}, bf16[2,12,128,128]{3,2,1,0:T(8,128)(2,1)S(1)}, u32[]{:S(2)}, u32[]{:S(2)}) collective-permute-start(bf16[2,12,128,128]{3,2,1,0:T(8,128)(2,1)S(1)} %get-tuple-element.115), channel_id=1, source_target_pairs={{0,16},{4,12},{8,24},{12,4},{16,0},{20,28},{24,8},{28,20},{1,17},{... | collective-permute-start | bytes 2359304 | tf_op jit(solution)/shard_map/ppermute | solution.py:312
  144.3 7.8 %collective-permute-start.22 = (bf16[1,12,128,128]{3,2,1,0:T(8,128)(2,1)S(1)}, bf16[1,12,128,128]{3,2,1,0:T(8,128)(2,1)S(1)}, u32[]{:S(2)}, u32[]{:S(2)}) collective-permute-start(bf16[1,12,128,128]{3,2,1,0:T(8,128)(2,1)S(1)} %get-tuple-element.127), channel_id=1, source_target_pairs={{0,8},{4,20},{8,0},{12,28},{16,24},{20,4},{24,16},{28,12},{1,9},{5... | collective-permute-start | bytes 1179656 | tf_op jit(solution)/shard_map/ppermute | solution.py:312

commit v7 on v6

--- a/solution.py
+++ b/solution.py
@@ -16,7 +16,8 @@
 SMEM = pl.BlockSpec(memory_space=pltpu.SMEM)
 VMEM = pl.BlockSpec(memory_space=pltpu.VMEM)
 ANY = pl.BlockSpec(memory_space=pl.ANY)
-TOKEN = SHAPE((1,), jnp.int32)
+TOKEN = SHAPE((8, 128), F32)
+HEAD = 5
 
 
 def group_of(capacity):
@@ -29,9 +30,9 @@
     return ref.at[lax.div(block, per_shard), :, pl.ds(start, size)]
 
 
-def slot_pair(index_ref, matrix, slot, capacity):
-    at = (matrix * capacity + slot) * 2
-    return index_ref[at], index_ref[at + 1]
+def slot_pair(plan_ref, matrix, slot, capacity):
+    at = HEAD + (matrix * capacity + slot) * 2
+    return plan_ref[at], plan_ref[at + 1]
 
 
 def each_group(count, group, body):
@@ -46,13 +47,14 @@
     return lax.dot_general(a, b, (contract, ((), ())), preferred_element_type=F32)
 
 
-def accumulate(index_ref, matrix, count, capacity, acc, into, product):
+def accumulate(plan_ref, matrix, capacity, acc, into, product):
     trash = acc.shape[0] - 1
+    count = plan_ref[2 + matrix]
 
     def body(slots):
         products, targets = [], []
         for s in slots:
-            pair = slot_pair(index_ref, matrix, s, capacity)
+            pair = slot_pair(plan_ref, matrix, s, capacity)
             targets.append(jnp.where(s < count, pair[into], trash))
             products.append(product(s, *pair))
         for t, p in zip(targets, products):
@@ -103,11 +105,11 @@
             out[:, c * size : (c + 1) * size] = total[t * per_shard + c].astype(out.dtype)
 
 
-def forward_kernel(n_pieces, n_outs, me_ref, index_ref, count_ref, *refs):
+def forward_kernel(n_pieces, n_outs, plan_ref, *refs):
     pieces, refs = refs[:n_pieces], refs[n_pieces:]
     w_ref, hidden_ref, turned_ref, act_ref, slope_ref = refs[:5]
     outs, (held, gate, up, total) = refs[5 : 5 + n_outs], refs[5 + n_outs :]
-    me = me_ref[0]
+    me = plan_ref[0]
     x_ref = load_shards(pieces, held, me)
     capacity, size = w_ref.shape[1], w_ref.shape[2]
     gate[...] = jnp.zeros_like(gate)
@@ -115,7 +117,7 @@
     total[...] = jnp.zeros_like(total)
     for matrix, acc in ((0, gate), (1, up)):
         accumulate(
-            index_ref, matrix, count_ref[matrix], capacity, acc, 1,
+            plan_ref, matrix, capacity, acc, 1,
             lambda s, f, h, matrix=matrix: dot(feature_block(x_ref, f, size)[...], w_ref[matrix, s], ((1,), (0,))),
         )
     for h in range(hidden_ref.shape[0]):
@@ -128,15 +130,15 @@
         hidden_ref[h] = hidden
         turned_ref[h] = hidden.T
     accumulate(
-        index_ref, 2, count_ref[2], capacity, total, 0,
+        plan_ref, 2, capacity, total, 0,
         lambda s, f, h: dot(hidden_ref[h], w_ref[2, s], ((1,), (0,))),
     )
     store_shards(total, outs, me, x_ref.shape[2] // size, size)
 
 
-def turn_kernel(n_pieces, me_ref, *refs):
+def turn_kernel(n_pieces, plan_ref, *refs):
     pieces, (turned_ref, held) = refs[:n_pieces], refs[n_pieces:]
-    x_ref = load_shards(pieces, held, me_ref[0])
+    x_ref = load_shards(pieces, held, plan_ref[0])
     size = turned_ref.shape[1]
     per_shard = x_ref.shape[2] // size
     for f in range(turned_ref.shape[0]):
@@ -144,14 +146,14 @@
         turned_ref[f] = x_ref[f // per_shard, :, c * size : (c + 1) * size].T
 
 
-def rows_kernel(n_pieces, me_ref, index_ref, count_ref, *refs):
+def rows_kernel(n_pieces, plan_ref, *refs):
     pieces, refs = refs[:n_pieces], refs[n_pieces:]
     w_ref, act_ref, slope_ref, gate_rows_ref, up_rows_ref, held, acc = refs
-    og_ref = load_shards(pieces, held, me_ref[0])
+    og_ref = load_shards(pieces, held, plan_ref[0])
     capacity, size = w_ref.shape[1], w_ref.shape[2]
     acc[...] = jnp.zeros_like(acc)
     accumulate(
-        index_ref, 2, count_ref[2], capacity, acc, 1,
+        plan_ref, 2, capacity, acc, 1,
         lambda s, f, h: dot(feature_block(og_ref, f, size)[...], w_ref[2, s], ((1,), (1,))),
     )
     for h in range(act_ref.shape[0]):
@@ -165,15 +167,15 @@
     return 2 * jnp.where(core == 0, place, turned)
 
 
-def grads_kernel(matrix, n_pieces, me_ref, index_ref, count_ref, *refs):
+def grads_kernel(matrix, n_pieces, plan_ref, *refs):
     pieces, refs = refs[:n_pieces], refs[n_pieces:]
     turned_ref, keep_ref, send_ref, held = refs
     size, share = keep_ref.shape[2], keep_ref.shape[1]
     places = keep_ref.shape[0]
-    replica = me_ref[1]
-    right_ref = load_shards(pieces, held, me_ref[0])
+    replica = plan_ref[1]
+    right_ref = load_shards(pieces, held, plan_ref[0])
     capacity = 2 * places * share
-    count = count_ref[matrix]
+    count = plan_ref[2 + matrix]
     for out, bit in ((send_ref, 1), (keep_ref, 0)):
 
         def one_place(q, carry, out=out, bit=bit):
@@ -183,7 +185,7 @@
             @pl.when(first < count)
             def _():
                 for s in range(share):
-                    f, h = slot_pair(index_ref, matrix, first + s, capacity)
+                    f, h = slot_pair(plan_ref, matrix, first + s, capacity)
                     if matrix == 2:
                         left, right = turned_ref[h], feature_block(right_ref, f, size)[...]
                     else:
@@ -195,16 +197,16 @@
         lax.fori_loop(0, places, one_place, 0)
 
 
-def input_kernel(n_outs, me_ref, index_ref, count_ref, gate_rows_ref, up_rows_ref, w_ref, *refs):
+def input_kernel(n_outs, plan_ref, gate_rows_ref, up_rows_ref, w_ref, *refs):
     outs, (total,) = refs[:n_outs], refs[n_outs:]
     capacity, size = w_ref.shape[1], w_ref.shape[2]
     total[...] = jnp.zeros_like(total)
     for matrix, rows in ((0, gate_rows_ref), (1, up_rows_ref)):
         accumulate(
-            index_ref, matrix, count_ref[matrix], capacity, total, 0,
+            plan_ref, matrix, capacity, total, 0,
             lambda s, f, h, matrix=matrix, rows=rows: dot(rows[h], w_ref[matrix, s], ((1,), (1,))),
         )
-    store_shards(total, outs, me_ref[0], outs[0].shape[-1] // size, size)
+    store_shards(total, outs, plan_ref[0], outs[0].shape[-1] // size, size)
 
 
 def fold_kernel(keep_ref, got_ref, keep_out, send_out):
@@ -228,15 +230,15 @@
     out_ref[...] = total.astype(out_ref.dtype)
 
 
-def update_kernel(matrix, me_ref, count_ref, keep_ref, got_ref, m1_ref, m2_ref, *refs):
+def update_kernel(matrix, plan_ref, keep_ref, got_ref, m1_ref, m2_ref, *refs):
     out_ref = refs[-1]
     share = keep_ref.shape[1]
-    first = me_ref[1] * share
+    first = plan_ref[1] * share
     for s in range(share):
         g = keep_ref[0, s].astype(F32) + got_ref[0, s].astype(F32)
         first_new = 0.9 * m1_ref[0, s] + 0.1 * g
         second_new = 0.95 * m2_ref[0, s] + 0.05 * g * g
-        live = first + s < count_ref[matrix]
+        live = first + s < plan_ref[2 + matrix]
         out_ref[0, s] = jnp.where(live, first_new / (jnp.sqrt(second_new) + EPSILON), 0.0)
 
 
@@ -247,28 +249,28 @@
 class Line:
     token = None
 
-    def __call__(self, kernel, name, outs, scratch, operands, scalars=(), specs=None, out_specs=None, aliases=None, cost=COST, **more):
-        tokens = [] if self.token is None else [self.token]
+    def __call__(self, kernel, name, outs, scratch, operands, plan=None, after=(), specs=None, out_specs=None, **more):
+        scalars = [] if plan is None else [plan]
+        extra = [*after] if self.token is None else [*after, self.token]
         n_in, n_out = len(scalars) + len(operands), len(outs)
 
         def body(*refs):
-            ins, rest = refs[:n_in], refs[n_in + len(tokens) :]
+            ins, rest = refs[:n_in], refs[n_in + len(extra) :]
             results, token, scratches = rest[:n_out], rest[n_out], rest[n_out + 1 :]
-            token[0] = 0
+            token[...] = jnp.zeros_like(token)
             kernel(*ins, *results, *scratches)
 
         *results, self.token = pl.pallas_call(
             body,
             name=name,
             out_shape=[*outs, TOKEN],
-            in_specs=[SMEM] * len(scalars) + (specs or [VMEM] * len(operands)) + [SMEM] * len(tokens),
-            out_specs=[*(out_specs or [VMEM] * n_out), SMEM],
+            in_specs=[SMEM] * len(scalars) + (specs or [VMEM] * len(operands)) + [VMEM] * len(extra),
+            out_specs=[*(out_specs or [VMEM] * n_out), VMEM],
             scratch_shapes=scratch,
-            input_output_aliases=aliases or {},
             compiler_params=pltpu.CompilerParams(vmem_limit_bytes=VMEM_LIMIT),
-            cost_estimate=pl.CostEstimate(flops=cost, bytes_accessed=0, transcendentals=0),
+            cost_estimate=pl.CostEstimate(flops=COST, bytes_accessed=0, transcendentals=0),
             **more,
-        )(*scalars, *operands, *tokens)
+        )(*scalars, *operands, *extra)
         return results
 
 
@@ -298,8 +300,8 @@
 def scatter_second(line, parts, came):
     piece = SHAPE(parts[0].shape, parts[0].dtype)
     own, beside, across = parts[:3]
-    across, beside, *came = line(join_kernel, "join", [piece] * (1 + len(came)), [], [across, came[0], beside, *came[1:]])
-    return [own, flip(across, 4, 2), flip(beside, 4, 1), *came]
+    across, beside = line(join_kernel, "join", [piece] * 2, [], [across, came[0], beside])
+    return [own, flip(across, 4, 2), flip(beside, 4, 1), *came[1:]]
 
 
 def core_swap(v, replicas):
@@ -316,7 +318,7 @@
     capacity, size = weights.shape[1], weights.shape[2]
     rows, width = inputs.shape
     me = jnp.stack([lax.axis_index("tensor"), lax.axis_index("dp")]).astype(jnp.int32)
-    scalars = (me, block_index.reshape(-1), block_counts[0])
+    plan = jnp.concatenate([me, block_counts[0], block_index.reshape(-1)])
     features = shards * width // size
     places, share = replicas // 2, capacity // replicas
     levels = places.bit_length() - 1
@@ -336,11 +338,11 @@
     def parts_of(count):
         return [piece] * count if lined else [SHAPE((shards, rows, width), BF16)]
 
-    def grads(matrix, right, left):
+    def grads(matrix, right, left, after=()):
         half = SHAPE((places, share, size, size), BF16)
         name = ("gate_grads", "up_grads", "down_grads")[matrix]
         kernel = functools.partial(grads_kernel, matrix, len(right))
-        keep, send = line(kernel, name, [half, half], [held], [*right, left], scalars)
+        keep, send = line(kernel, name, [half, half], [held], [*right, left], plan, after)
         return keep, core_swap(send, replicas)
 
     def fold(keep, got, step):
@@ -357,10 +359,10 @@
             [SHAPE(first_moment.shape, F32)],
             [],
             [keep, got, first_moment, second_moment, *extra],
-            (me, scalars[2]),
+            plan,
             specs=[VMEM, VMEM, block, block] + [ANY] * len(extra),
             out_specs=[block],
-            aliases={6: 0} if extra else {},
+            input_output_aliases={5: 0} if extra else {},
             grid=(1,),
         )[0]
 
@@ -378,25 +380,25 @@
         [narrow, turned, wide, wide, *out_parts],
         [held, acc, acc, total],
         [*x, weights],
-        scalars,
+        plan,
     )
     if lined:
         out_far = scatter_first(out_parts)
     else:
         outputs = lax.psum_scatter(out_parts[0], "tensor", scatter_dimension=0)
     (x_turned,) = line(
-        functools.partial(turn_kernel, len(x)), "turn", [SHAPE((features, size, rows), BF16)], [held], x, (me,)
+        functools.partial(turn_kernel, len(x)), "turn", [SHAPE((features, size, rows), BF16)], [held], x, plan
     )
     if lined:
         out_sums = scatter_second(line, out_parts, out_far)
-    down = grads(2, og, hidden_turned)
+    down = grads(2, og, hidden_turned, out_far[1:] if lined else ())
     gate_rows, up_rows = line(
         functools.partial(rows_kernel, len(og)),
         "row_grads",
         [narrow, narrow],
         [held, acc],
         [*og, weights, act, slope],
-        scalars,
+        plan,
     )
     down = fold(*down, 0)
     in_parts = line(
@@ -405,7 +407,7 @@
         in_parts,
         [total],
         [gate_rows, up_rows, weights],
-        scalars,
+        plan,
     )
     if lined:
         in_came = scatter_first(in_parts)
@@ -418,10 +420,10 @@
         outputs = finish(out_sums)
     gate = fold(*gate, 0)
     up = grads(1, [up_rows], x_turned)
-    if lined:
-        in_sums = scatter_second(line, in_parts, in_came)
     for step in range(1, levels):
         gate = fold(*gate, step)
+    if lined:
+        in_sums = scatter_second(line, in_parts, in_came)
     up = fold(*up, 0)
     buffer = update(2, *down, None)
     buffer = update(0, *gate, buffer)

time: 157 us -> 157 us (level)
  Pallas kernels: 56.4 us -> 39.8 us
  waiting for transfers between devices: 59.1 us -> 68.3 us
  starting transfers between devices: 36.2 us -> 43.7 us
    pallas_call x21, Pallas kernels: 56.4 us -> 39.8 us  [__call__(): pl.pallas_call(body, name=name, out_shape=[*outs, TOKEN], in_specs=[SMEM]...]
    ppermute x9, waiting for transfers between devices: 34.1 us -> 45.9 us  [flip(): return lax.ppermute(v, 'tensor', [(a, a ^ bit) for a in range(shards)])]
    ppermute x9, starting transfers between devices: 19.2 us -> 26.4 us  [flip(): return lax.ppermute(v, 'tensor', [(a, a ^ bit) for a in range(shards)])]
    ppermute x6, waiting for transfers between devices: 17 us -> 13.9 us  [axis_swap(): return lax.ppermute(v, 'dp', pairs)]
  transfers between devices with their start and end apart: 23 -> 23, of which waited for: 7 -> 8; matrix products, arithmetic and copies ran while one was open for 1% -> 1% of each run, Pallas kernels for 35% -> 24%
where the time goes in v7:
time: 157 us; the launch traced here: 156 us
  waiting for transfers between devices  68.3 us (44%)
  starting transfers between devices  43.7 us (28%)
  Pallas kernels  39.8 us (25%)
  local copies, waits for them, and re-layouts  2.72 us (2%)
    ppermute x9, waiting for transfers between devices, flip(): return lax.ppermute(v, 'tensor', [(a, a ^ bit) for a in range(shards)])  45.9 us
    pallas_call x21, Pallas kernels, __call__(): pl.pallas_call(body, name=name, out_shape=[*outs, TOKEN], in_specs=[SMEM]...  39.8 us
    ppermute x9, starting transfers between devices, flip(): return lax.ppermute(v, 'tensor', [(a, a ^ bit) for a in range(shards)])  26.4 us
    ppermute x6, waiting for transfers between devices, axis_swap(): return lax.ppermute(v, 'dp', pairs)  13.9 us
    ppermute x1, waiting for transfers between devices, scatter_first(): lax.ppermute(parts[3], 'tensor', [(0, 1), (3, 2)])  7.92 us
    ppermute x6, starting transfers between devices, axis_swap(): return lax.ppermute(v, 'dp', pairs)  7.34 us
    ppermute x1, starting transfers between devices, gather_line(): below = lax.ppermute(v, 'tensor', [(a, a + 1) for a in range(3)])  4.58 us
  transfers between devices with their start and end apart: 23, of which 8 were waited for; matrix products, arithmetic and copies ran while one was open for 1% of the time, Pallas kernels for 24%

profile of v7, /device:TPU:0, one launch (start us, length us, event | category | flops | bytes accessed | tf_op | source)
XLA Modules:
  0.0 156.3 jit_solution(2906690701429522648)
XLA Ops:
  0.6 4.1 %collective-permute-start.1 = (bf16[128,2048]{1,0:T(8,128)(2,1)}, bf16[128,2048]{1,0:T(8,128)(2,1)S(1)}, u32[]{:S(2)}, u32[]{:S(2)}) collective-permute-start(bf16[128,2048]{1,0:T(8,128)(2,1)} %refs_1_.3), channel_id=1, source_target_pairs={{0,2},{1,3},{2,0},{3,1},{4,6},{5,7},{6,4},{7,5},{8,10},{9,11},{10,... | collective-permute-start | bytes 1572872 | tf_op jit(solution)/shard_map/ppermute | solution.py:278
  4.7 1.6 %collective-permute-start = (bf16[128,2048]{1,0:T(8,128)(2,1)}, bf16[128,2048]{1,0:T(8,128)(2,1)S(1)}, u32[]{:S(2)}, u32[]{:S(2)}) collective-permute-start(bf16[128,2048]{1,0:T(8,128)(2,1)} %refs_1_.3), channel_id=1, source_target_pairs={{0,1},{1,0},{2,3},{3,2},{4,5},{5,4},{6,7},{7,6},{8,9},{9,8},{10,11... | collective-permute-start | bytes 1572872 | tf_op jit(solution)/shard_map/ppermute | solution.py:278
  8.2 20.1 %collective-permute-done.1.refs_1_.refs_3_ = bf16[128,2048]{1,0:T(8,128)(2,1)S(1)} collective-permute-done((bf16[128,2048]{1,0:T(8,128)(2,1)}, bf16[128,2048]{1,0:T(8,128)(2,1)S(1)}, u32[]{:S(2)}, u32[]{:S(2)}) %collective-permute-start.1) | collective-permute-done | bytes 524320 | tf_op jit(solution)/shard_map/ppermute | solution.py:278
  30.0 3.3 %collective-permute-start.9 = (bf16[128,2048]{1,0:T(8,128)(2,1)S(1)}, bf16[128,2048]{1,0:T(8,128)(2,1)S(1)}, u32[]{:S(2)}, u32[]{:S(2)}) collective-permute-start(bf16[128,2048]{1,0:T(8,128)(2,1)S(1)} %get-tuple-element.76.refs_1_), channel_id=1, source_target_pairs={{0,2},{1,3},{2,0},{3,1},{4,6},{5,7},{6,4},{7,5},{8,10},{9,11},{10,... | collective-permute-start | bytes 1572872 | tf_op jit(solution)/shard_map/ppermute | solution.py:278
  33.4 1.3 collective-permute-start.8
  34.6 4.6 %collective-permute-start.7 = (bf16[128,2048]{1,0:T(8,128)(2,1)S(1)}, bf16[128,2048]{1,0:T(8,128)(2,1)S(1)}, u32[]{:S(2)}, u32[]{:S(2)}) collective-permute-start(bf16[128,2048]{1,0:T(8,128)(2,1)S(1)} %get-tuple-element.76.refs_1_), channel_id=1, source_target_pairs={{0,1},{1,2},{2,3},{4,5},{5,6},{6,7},{8,9},{9,10},{10,11},{12,13},{... | collective-permute-start | bytes 1572872 | tf_op jit(solution)/shard_map/ppermute | solution.py:288
  39.2 13.7 %collective-permute-done.2.refs_4_ = bf16[128,2048]{1,0:T(8,128)(2,1)S(1)} collective-permute-done((bf16[128,2048]{1,0:T(8,128)(2,1)S(1)}, bf16[128,2048]{1,0:T(8,128)(2,1)S(1)}, u32[]{:S(2)}, u32[]{:S(2)}) %collective-permute-start.2) | collective-permute-done | bytes 524320 | tf_op jit(solution)/shard_map/ppermute | solution.py:278
  53.0 8.5 %forward.1 = (bf16[14,128,128]{2,1,0:T(8,128)(2,1)}, bf16[14,128,128]{2,1,0:T(8,128)(2,1)S(1)}, f32[14,128,128]{2,1,0:T(8,128)S(1)}, f32[14,128,128]{2,1,0:T(8,1...) custom-call(s32[581]{0:T(1024)S(1)} %pad_add_fusion.refs_0_, ...), custom_call_target="tpu_custom_call" | custom-call | flops 20000000000 | tf_op jit(solution)/shard_map/forward/pallas_call | solution.py:263
  61.5 1.3 collective-permute-start.3
  63.5 1.3 collective-permute-start.10
  64.8 1.3 turn.1
  66.1 7.9 %collective-permute-done.3.refs_1_ = bf16[128,2048]{1,0:T(8,128)(2,1)S(1)} collective-permute-done((bf16[128,2048]{1,0:T(8,128)(2,1)S(1)}, bf16[128,2048]{1,0:T(8,128)(2,1)S(1)}, u32[]{:S(2)}, u32[]{:S(2)}) %collective-permute-start.3) | collective-permute-done | bytes 524320 | tf_op jit(solution)/shard_map/ppermute | solution.py:297
  74.2 4.1 %collective-permute-start.4 = (bf16[128,2048]{1,0:T(8,128)(2,1)S(1)}, bf16[128,2048]{1,0:T(8,128)(2,1)S(1)}, u32[]{:S(2)}, u32[]{:S(2)}) collective-permute-start(bf16[128,2048]{1,0:T(8,128)(2,1)S(1)} %get-tuple-element.73), channel_id=1, source_target_pairs={{0,2},{1,3},{2,0},{3,1},{4,6},{5,7},{6,4},{7,5},{8,10},{9,11},{10,... | collective-permute-start | bytes 1572872 | tf_op jit(solution)/shard_map/ppermute | solution.py:278
  78.3 3.1 %down_grads.1 = (bf16[4,12,128,128]{3,2,1,0:T(8,128)(2,1)S(1)}, bf16[4,12,128,128]{3,2,1,0:T(8,128)(2,1)S(1)}, f32[8,128]{1,0:T(8,128)S(1)}) custom-call(s32[581]{0:T(1024)S(1)} %pad_add_fusion.refs_0_, bf16[128,2048]{1,0:T(8,128)(2,1)S(1)} %get-tuple-element.76.refs_1_, bf16[128,2048]{1,0:T(8,128)(2,1)S(1)} %collective-permute-done.7.refs_2_, ...), custom_call_target="tpu_custom_call" | custom-call | flops 20000000000 | tf_op jit(solution)/shard_map/down_grads/pallas_call | solution.py:263
  81.4 3.9 %row_grads.1 = (bf16[14,128,128]{2,1,0:T(8,128)(2,1)S(1)}, bf16[14,128,128]{2,1,0:T(8,128)(2,1)S(1)}, f32[8,128]{1,0:T(8,128)S(1)}) custom-call(s32[581]{0:T(1024)S(1)} %pad_add_fusion.refs_0_, bf16[128,2048]{1,0:T(8,128)(2,1)S(1)} %get-tuple-element.76.refs_1_, bf16[128,2048]{1,0:T(8,128)(2,1)S(1)} %collective-permute-done.7.refs_2_, ...), custom_call_target="tpu_custom_call" | custom-call | flops 20000000000 | tf_op jit(solution)/shard_map/row_grads/pallas_call | solution.py:263
  85.7 1.6 %collective-permute-start.12 = (bf16[2,12,128,128]{3,2,1,0:T(8,128)(2,1)S(1)}, bf16[2,12,128,128]{3,2,1,0:T(8,128)(2,1)S(1)}, u32[]{:S(2)}, u32[]{:S(2)}) collective-permute-start(bf16[2,12,128,128]{3,2,1,0:T(8,128)(2,1)S(1)} %get-tuple-element.86), channel_id=1, source_target_pairs={{0,16},{4,12},{8,24},{12,4},{16,0},{20,28},{24,8},{28,20},{1,17},{... | collective-permute-start | bytes 2359304 | tf_op jit(solution)/shard_map/ppermute | solution.py:314
  87.3 7.4 %input_grads.1 = (bf16[128,2048]{1,0:T(8,128)(2,1)S(1)}, bf16[128,2048]{1,0:T(8,128)(2,1)S(1)}, bf16[128,2048]{1,0:T(8,128)(2,1)S(1)}, bf16[128,2048]{1,0:T(8,128)(2,1)S(1)}, f32[8,128]{1,0:T(8,128)S(1)}) custom-call(s32[581]{0:T(1024)S(1)} %pad_add_fusion.refs_0_, bf16[14,128,128]{2,1,0:T(8,128)(2,1)S(1)} %get-tuple-element.87.refs_1_, ...), custom_call_target="tpu_custom_call" | custom-call | flops 20000000000 | tf_op jit(solution)/shard_map/input_grads/pallas_call | solution.py:263
  94.7 8.1 %collective-permute-start.13 = (bf16[128,2048]{1,0:T(8,128)(2,1)S(1)}, bf16[128,2048]{1,0:T(8,128)(2,1)S(1)}, u32[]{:S(2)}, u32[]{:S(2)}) collective-permute-start(bf16[128,2048]{1,0:T(8,128)(2,1)S(1)} %get-tuple-element.97), channel_id=1, source_target_pairs={{0,1},{1,0},{2,3},{3,2},{4,5},{5,4},{6,7},{7,6},{8,9},{9,8},{10,11... | collective-permute-start | bytes 1572872 | tf_op jit(solution)/shard_map/ppermute | solution.py:278
  102.9 2.8 %gate_grads.1 = (bf16[4,12,128,128]{3,2,1,0:T(8,128)(2,1)S(1)}, bf16[4,12,128,128]{3,2,1,0:T(8,128)(2,1)S(1)}, f32[8,128]{1,0:T(8,128)S(1)}) custom-call(s32[581]{0:T(1024)S(1)} %pad_add_fusion.refs_0_, bf16[14,128,128]{2,1,0:T(8,128)(2,1)S(1)} %get-tuple-element.87.refs_1_, bf16[64,128,128]{2,1,0:T(8,128)(2,1)S(1)} %get-tuple-element.88.refs_2_, ...), custom_call_target="tpu_custom_call" | custom-call | flops 20000000000 | tf_op jit(solution)/shard_map/gate_grads/pallas_call | solution.py:263
  106.0 1.6 collective-permute-start.21
  107.5 1.1 finish.2
  110.3 2.9 %up_grads.1 = (bf16[4,12,128,128]{3,2,1,0:T(8,128)(2,1)S(1)}, bf16[4,12,128,128]{3,2,1,0:T(8,128)(2,1)S(1)}, f32[8,128]{1,0:T(8,128)S(1)}) custom-call(s32[581]{0:T(1024)S(1)} %pad_add_fusion.refs_0_, bf16[14,128,128]{2,1,0:T(8,128)(2,1)S(1)} %get-tuple-element.89.refs_2_.refs_1_, bf16[64,128,128]{2,1,0:T(8,128)(2,1)S(1)} %get-tuple-element.88.refs_2_, ...), custom_call_target="tpu_custom_call" | custom-call | flops 20000000000 | tf_op jit(solution)/shard_map/up_grads/pallas_call | solution.py:263
  113.9 7.9 %collective-permute-done.15.refs_1_ = bf16[2,12,128,128]{3,2,1,0:T(8,128)(2,1)S(1)} collective-permute-done((bf16[2,12,128,128]{3,2,1,0:T(8,128)(2,1)S(1)}, bf16[2,12,128,128]{3,2,1,0:T(8,128)(2,1)S(1)}, u32[]{:S(2)}, u32[]{:S(2)}) %collective-permute-start.15) | collective-permute-done | bytes 786464 | tf_op jit(solution)/shard_map/ppermute | solution.py:314
  121.9 1.6 collective-permute-start.20
  123.6 4.1 %collective-permute-start.16 = (bf16[128,2048]{1,0:T(8,128)(2,1)S(1)}, bf16[128,2048]{1,0:T(8,128)(2,1)S(1)}, u32[]{:S(2)}, u32[]{:S(2)}) collective-permute-start(bf16[128,2048]{1,0:T(8,128)(2,1)S(1)} %get-tuple-element.107), channel_id=1, source_target_pairs={{0,2},{1,3},{2,0},{3,1},{4,6},{5,7},{6,4},{7,5},{8,10},{9,11},{10,... | collective-permute-start | bytes 1572872 | tf_op jit(solution)/shard_map/ppermute | solution.py:278
  128.4 1.3 collective-permute-start.19
  130.4 2.0 %update.3 = (f32[3,12,128,128]{3,2,1,0:T(8,128)}, f32[8,128]{1,0:T(8,128)S(1)}) custom-call(s32[581]{0:T(1024)S(1)} %pad_add_fusion.refs_0_, bf16[1,12,128,128]{3,2,1,0:T(8,128)(2,1)S(1)} %get-tuple-element.116.refs_1_, bf16[1,12,128,128]{3,2,1,0:T(8,128)(2,1)S(1)} %collective-permute-done.21.refs_2_, f32[3,12,128,128]{3,2,1,0:T(8,128)S(1)} %copy-done, ...), custom_call_target="tpu_custom_call" | custom-call | flops 20000000000 | tf_op jit(solution)/shard_map/update/pallas_call | solution.py:263
  132.4 2.0 %update.4 = (f32[3,12,128,128]{3,2,1,0:T(8,128)}, f32[8,128]{1,0:T(8,128)S(1)}) custom-call(s32[581]{0:T(1024)S(1)} %pad_add_fusion.refs_0_, bf16[1,12,128,128]{3,2,1,0:T(8,128)(2,1)S(1)} %get-tuple-element.114.refs_1_, bf16[1,12,128,128]{3,2,1,0:T(8,128)(2,1)S(1)} %collective-permute-done.20.refs_2_, ...), custom_call_target="tpu_custom_call", output_to_operand_aliasing={{0}: (5, {})} | custom-call | flops 20000000000 | tf_op jit(solution)/shard_map/update/pallas_call | solution.py:263
  134.4 6.0 %collective-permute-done.19.refs_1_ = bf16[2,12,128,128]{3,2,1,0:T(8,128)(2,1)S(1)} collective-permute-done((bf16[2,12,128,128]{3,2,1,0:T(8,128)(2,1)S(1)}, bf16[2,12,128,128]{3,2,1,0:T(8,128)(2,1)S(1)}, u32[]{:S(2)}, u32[]{:S(2)}) %collective-permute-start.19) | collective-permute-done | bytes 786464 | tf_op jit(solution)/shard_map/ppermute | solution.py:314
  141.2 9.6 %collective-permute-done.16.refs_1_ = bf16[128,2048]{1,0:T(8,128)(2,1)S(1)} collective-permute-done((bf16[128,2048]{1,0:T(8,128)(2,1)S(1)}, bf16[128,2048]{1,0:T(8,128)(2,1)S(1)}, u32[]{:S(2)}, u32[]{:S(2)}) %collective-permute-start.16) | collective-permute-done | bytes 524320 | tf_op jit(solution)/shard_map/ppermute | solution.py:278
  150.8 2.5 %collective-permute-done.17.refs_2_ = bf16[128,2048]{1,0:T(8,128)(2,1)S(1)} collective-permute-done((bf16[128,2048]{1,0:T(8,128)(2,1)S(1)}, bf16[128,2048]{1,0:T(8,128)(2,1)S(1)}, u32[]{:S(2)}, u32[]{:S(2)}) %collective-permute-start.17) | collective-permute-done | bytes 524320 | tf_op jit(solution)/shard_map/ppermute | solution.py:278
  154.3 2.0 %update.5 = (f32[3,12,128,128]{3,2,1,0:T(8,128)}, f32[8,128]{1,0:T(8,128)}) custom-call(s32[581]{0:T(1024)S(1)} %pad_add_fusion.refs_0_, bf16[1,12,128,128]{3,2,1,0:T(8,128)(2,1)S(1)} %get-tuple-element.124.refs_1_, bf16[1,12,128,128]{3,2,1,0:T(8,128)(2,1)S(1)} %collective-permute-done.22.refs_2_, ...), custom_call_target="tpu_custom_call", output_to_operand_aliasing={{0}: (5, {})} | custom-call | flops 20000000000 | tf_op jit(solution)/shard_map/update/pallas_call | solution.py:263
  (53 shorter events, 10.9 us)
Async XLA Ops:
  0.6 27.6 %collective-permute-start.1 = (bf16[128,2048]{1,0:T(8,128)(2,1)}, bf16[128,2048]{1,0:T(8,128)(2,1)S(1)}, u32[]{:S(2)}, u32[]{:S(2)}) collective-permute-start(bf16[128,2048]{1,0:T(8,128)(2,1)} %refs_1_.3), channel_id=1, source_target_pairs={{0,2},{1,3},{2,0},{3,1},{4,6},{5,7},{6,4},{7,5},{8,10},{9,11},{10,... | collective-permute-start | bytes 1572872 | tf_op jit(solution)/shard_map/ppermute | solution.py:278
  4.7 34.5 %collective-permute-start = (bf16[128,2048]{1,0:T(8,128)(2,1)}, bf16[128,2048]{1,0:T(8,128)(2,1)S(1)}, u32[]{:S(2)}, u32[]{:S(2)}) collective-permute-start(bf16[128,2048]{1,0:T(8,128)(2,1)} %refs_1_.3), channel_id=1, source_target_pairs={{0,1},{1,0},{2,3},{3,2},{4,5},{5,4},{6,7},{7,6},{8,9},{9,8},{10,11... | collective-permute-start | bytes 1572872 | tf_op jit(solution)/shard_map/ppermute | solution.py:278
  7.3 45.7 %slice-start = ((s8[9437184]{0:T(1024)(128)(4,1)}), s8[4194304]{0:T(1024)(128)(4,1)S(1)}, s32[]{:S(2)}) async-start(s8[9437184]{0:T(1024)(128)(4,1)} %bitcast.3), calls=%async_computation | async-start | bytes 8388608
  8.2 44.8 %slice-start.1 = ((s8[9437184]{0:T(1024)(128)(4,1)}), s8[4194304]{0:T(1024)(128)(4,1)S(1)}, s32[]{:S(2)}) async-start(s8[9437184]{0:T(1024)(128)(4,1)} %bitcast.3), calls=%async_computation.1 | async-start | bytes 8388608
  8.2 44.8 %slice-start.2 = ((s8[9437184]{0:T(1024)(128)(4,1)}), s8[1048576]{0:T(1024)(128)(4,1)S(1)}, s32[]{:S(2)}) async-start(s8[9437184]{0:T(1024)(128)(4,1)} %bitcast.3), calls=%async_computation.2 | async-start | bytes 2097152
  28.2 24.7 %collective-permute-start.2 = (bf16[128,2048]{1,0:T(8,128)(2,1)S(1)}, bf16[128,2048]{1,0:T(8,128)(2,1)S(1)}, u32[]{:S(2)}, u32[]{:S(2)}) collective-permute-start(bf16[128,2048]{1,0:T(8,128)(2,1)S(1)} %collective-permute-done.1.refs_1_.refs_3_), channel_id=1, source_target_pairs={{0,1},{1,0},{2,3},{3,2},{4,5},{5,4},{6,7},{7,6},{8,9},{9,8},{10,11... | collective-permute-start | bytes 1572872 | tf_op jit(solution)/shard_map/ppermute | solution.py:278
  28.9 1.0 copy-start.2
  30.0 23.0 %copy-start.3 = (bf16[128,2048]{1,0:T(8,128)(2,1)S(1)}, bf16[128,2048]{1,0:T(8,128)(2,1)}, u32[]{:S(2)}) copy-start(bf16[128,2048]{1,0:T(8,128)(2,1)} %refs_1_.3) | copy-start | bytes 1572868
  30.0 33.5 %collective-permute-start.9 = (bf16[128,2048]{1,0:T(8,128)(2,1)S(1)}, bf16[128,2048]{1,0:T(8,128)(2,1)S(1)}, u32[]{:S(2)}, u32[]{:S(2)}) collective-permute-start(bf16[128,2048]{1,0:T(8,128)(2,1)S(1)} %get-tuple-element.76.refs_1_), channel_id=1, source_target_pairs={{0,2},{1,3},{2,0},{3,1},{4,6},{5,7},{6,4},{7,5},{8,10},{9,11},{10,... | collective-permute-start | bytes 1572872 | tf_op jit(solution)/shard_map/ppermute | solution.py:278
  33.4 44.9 %collective-permute-start.8 = (bf16[128,2048]{1,0:T(8,128)(2,1)S(1)}, bf16[128,2048]{1,0:T(8,128)(2,1)S(1)}, u32[]{:S(2)}, u32[]{:S(2)}) collective-permute-start(bf16[128,2048]{1,0:T(8,128)(2,1)S(1)} %get-tuple-element.76.refs_1_), channel_id=1, source_target_pairs={{1,0},{2,1},{3,2},{5,4},{6,5},{7,6},{9,8},{10,9},{11,10},{13,12},{... | collective-permute-start | bytes 1572872 | tf_op jit(solution)/shard_map/ppermute | solution.py:289
  34.6 43.6 %collective-permute-start.7 = (bf16[128,2048]{1,0:T(8,128)(2,1)S(1)}, bf16[128,2048]{1,0:T(8,128)(2,1)S(1)}, u32[]{:S(2)}, u32[]{:S(2)}) collective-permute-start(bf16[128,2048]{1,0:T(8,128)(2,1)S(1)} %get-tuple-element.76.refs_1_), channel_id=1, source_target_pairs={{0,1},{1,2},{2,3},{4,5},{5,6},{6,7},{8,9},{9,10},{10,11},{12,13},{... | collective-permute-start | bytes 1572872 | tf_op jit(solution)/shard_map/ppermute | solution.py:288
  61.5 12.6 %collective-permute-start.3 = (bf16[128,2048]{1,0:T(8,128)(2,1)S(1)}, bf16[128,2048]{1,0:T(8,128)(2,1)S(1)}, u32[]{:S(2)}, u32[]{:S(2)}) collective-permute-start(bf16[128,2048]{1,0:T(8,128)(2,1)S(1)} %get-tuple-element.69), channel_id=1, source_target_pairs={{0,1},{3,2},{4,5},{7,6},{8,9},{11,10},{12,13},{15,14},{16,17},{19,... | collective-permute-start | bytes 1572872 | tf_op jit(solution)/shard_map/ppermute | solution.py:297
  62.8 15.5 %collective-permute-start.6 = (bf16[128,2048]{1,0:T(8,128)(2,1)S(1)}, bf16[128,2048]{1,0:T(8,128)(2,1)S(1)}, u32[]{:S(2)}, u32[]{:S(2)}) collective-permute-start(bf16[128,2048]{1,0:T(8,128)(2,1)S(1)} %get-tuple-element.75), channel_id=1, source_target_pairs={{1,2},{2,1},{5,6},{6,5},{9,10},{10,9},{13,14},{14,13},{17,18},{18,... | collective-permute-start | bytes 1572872 | tf_op jit(solution)/shard_map/ppermute | solution.py:297
  63.5 14.7 %collective-permute-start.10 = (bf16[128,2048]{1,0:T(8,128)(2,1)S(1)}, bf16[128,2048]{1,0:T(8,128)(2,1)S(1)}, u32[]{:S(2)}, u32[]{:S(2)}) collective-permute-start(bf16[128,2048]{1,0:T(8,128)(2,1)S(1)} %collective-permute-done.9.refs_4_), channel_id=1, source_target_pairs={{2,3},{1,0},{6,7},{5,4},{10,11},{9,8},{14,15},{13,12},{18,19},{17,... | collective-permute-start | bytes 1572872 | tf_op jit(solution)/shard_map/ppermute | solution.py:290
  74.2 33.4 %collective-permute-start.4 = (bf16[128,2048]{1,0:T(8,128)(2,1)S(1)}, bf16[128,2048]{1,0:T(8,128)(2,1)S(1)}, u32[]{:S(2)}, u32[]{:S(2)}) collective-permute-start(bf16[128,2048]{1,0:T(8,128)(2,1)S(1)} %get-tuple-element.73), channel_id=1, source_target_pairs={{0,2},{1,3},{2,0},{3,1},{4,6},{5,7},{6,4},{7,5},{8,10},{9,11},{10,... | collective-permute-start | bytes 1572872 | tf_op jit(solution)/shard_map/ppermute | solution.py:278
  78.2 29.3 %collective-permute-start.5 = (bf16[128,2048]{1,0:T(8,128)(2,1)S(1)}, bf16[128,2048]{1,0:T(8,128)(2,1)S(1)}, u32[]{:S(2)}, u32[]{:S(2)}) collective-permute-start(bf16[128,2048]{1,0:T(8,128)(2,1)S(1)} %get-tuple-element.74), channel_id=1, source_target_pairs={{0,1},{1,0},{2,3},{3,2},{4,5},{5,4},{6,7},{7,6},{8,9},{9,8},{10,11... | collective-permute-start | bytes 1572872 | tf_op jit(solution)/shard_map/ppermute | solution.py:278
  81.4 4.0 %collective-permute-start.11 = (bf16[4,12,128,128]{3,2,1,0:T(8,128)(2,1)S(1)}, bf16[4,12,128,128]{3,2,1,0:T(8,128)(2,1)S(1)}, u32[]{:S(2)}, u32[]{:S(2)}) collective-permute-start(bf16[4,12,128,128]{3,2,1,0:T(8,128)(2,1)S(1)} %get-tuple-element.80), channel_id=1, source_target_pairs={{0,4},{4,0},{8,12},{12,8},{16,20},{20,16},{24,28},{28,24},{1,5},{5... | collective-permute-start | bytes 4718600 | tf_op jit(solution)/shard_map/ppermute | solution.py:308
  85.7 20.1 %collective-permute-start.12 = (bf16[2,12,128,128]{3,2,1,0:T(8,128)(2,1)S(1)}, bf16[2,12,128,128]{3,2,1,0:T(8,128)(2,1)S(1)}, u32[]{:S(2)}, u32[]{:S(2)}) collective-permute-start(bf16[2,12,128,128]{3,2,1,0:T(8,128)(2,1)S(1)} %get-tuple-element.86), channel_id=1, source_target_pairs={{0,16},{4,12},{8,24},{12,4},{16,0},{20,28},{24,8},{28,20},{1,17},{... | collective-permute-start | bytes 2359304 | tf_op jit(solution)/shard_map/ppermute | solution.py:314
  94.7 28.8 %collective-permute-start.13 = (bf16[128,2048]{1,0:T(8,128)(2,1)S(1)}, bf16[128,2048]{1,0:T(8,128)(2,1)S(1)}, u32[]{:S(2)}, u32[]{:S(2)}) collective-permute-start(bf16[128,2048]{1,0:T(8,128)(2,1)S(1)} %get-tuple-element.97), channel_id=1, source_target_pairs={{0,1},{1,0},{2,3},{3,2},{4,5},{5,4},{6,7},{7,6},{8,9},{9,8},{10,11... | collective-permute-start | bytes 1572872 | tf_op jit(solution)/shard_map/ppermute | solution.py:278
  105.7 3.5 %collective-permute-start.14 = (bf16[4,12,128,128]{3,2,1,0:T(8,128)(2,1)S(1)}, bf16[4,12,128,128]{3,2,1,0:T(8,128)(2,1)S(1)}, u32[]{:S(2)}, u32[]{:S(2)}) collective-permute-start(bf16[4,12,128,128]{3,2,1,0:T(8,128)(2,1)S(1)} %get-tuple-element.100), channel_id=1, source_target_pairs={{0,4},{4,0},{8,12},{12,8},{16,20},{20,16},{24,28},{28,24},{1,5},{5... | collective-permute-start | bytes 4718600 | tf_op jit(solution)/shard_map/ppermute | solution.py:308
  106.0 23.7 %collective-permute-start.21 = (bf16[1,12,128,128]{3,2,1,0:T(8,128)(2,1)S(1)}, bf16[1,12,128,128]{3,2,1,0:T(8,128)(2,1)S(1)}, u32[]{:S(2)}, u32[]{:S(2)}) collective-permute-start(bf16[1,12,128,128]{3,2,1,0:T(8,128)(2,1)S(1)} %get-tuple-element.117), channel_id=1, source_target_pairs={{0,8},{4,20},{8,0},{12,28},{16,24},{20,4},{24,16},{28,12},{1,9},{5... | collective-permute-start | bytes 1179656 | tf_op jit(solution)/shard_map/ppermute | solution.py:314
  109.5 12.2 %collective-permute-start.15 = (bf16[2,12,128,128]{3,2,1,0:T(8,128)(2,1)S(1)}, bf16[2,12,128,128]{3,2,1,0:T(8,128)(2,1)S(1)}, u32[]{:S(2)}, u32[]{:S(2)}) collective-permute-start(bf16[2,12,128,128]{3,2,1,0:T(8,128)(2,1)S(1)} %get-tuple-element.103), channel_id=1, source_target_pairs={{0,16},{4,12},{8,24},{12,4},{16,0},{20,28},{24,8},{28,20},{1,17},{... | collective-permute-start | bytes 2359304 | tf_op jit(solution)/shard_map/ppermute | solution.py:314
  113.2 14.9 %collective-permute-start.18 = (bf16[4,12,128,128]{3,2,1,0:T(8,128)(2,1)S(1)}, bf16[4,12,128,128]{3,2,1,0:T(8,128)(2,1)S(1)}, u32[]{:S(2)}, u32[]{:S(2)}) collective-permute-start(bf16[4,12,128,128]{3,2,1,0:T(8,128)(2,1)S(1)} %get-tuple-element.110), channel_id=1, source_target_pairs={{0,4},{4,0},{8,12},{12,8},{16,20},{20,16},{24,28},{28,24},{1,5},{5... | collective-permute-start | bytes 4718600 | tf_op jit(solution)/shard_map/ppermute | solution.py:308
  121.9 10.5 %collective-permute-start.20 = (bf16[1,12,128,128]{3,2,1,0:T(8,128)(2,1)S(1)}, bf16[1,12,128,128]{3,2,1,0:T(8,128)(2,1)S(1)}, u32[]{:S(2)}, u32[]{:S(2)}) collective-permute-start(bf16[1,12,128,128]{3,2,1,0:T(8,128)(2,1)S(1)} %get-tuple-element.115), channel_id=1, source_target_pairs={{0,8},{4,20},{8,0},{12,28},{16,24},{20,4},{24,16},{28,12},{1,9},{5... | collective-permute-start | bytes 1179656 | tf_op jit(solution)/shard_map/ppermute | solution.py:314
  123.6 27.2 %collective-permute-start.16 = (bf16[128,2048]{1,0:T(8,128)(2,1)S(1)}, bf16[128,2048]{1,0:T(8,128)(2,1)S(1)}, u32[]{:S(2)}, u32[]{:S(2)}) collective-permute-start(bf16[128,2048]{1,0:T(8,128)(2,1)S(1)} %get-tuple-element.107), channel_id=1, source_target_pairs={{0,2},{1,3},{2,0},{3,1},{4,6},{5,7},{6,4},{7,5},{8,10},{9,11},{10,... | collective-permute-start | bytes 1572872 | tf_op jit(solution)/shard_map/ppermute | solution.py:278
  127.7 25.6 %collective-permute-start.17 = (bf16[128,2048]{1,0:T(8,128)(2,1)S(1)}, bf16[128,2048]{1,0:T(8,128)(2,1)S(1)}, u32[]{:S(2)}, u32[]{:S(2)}) collective-permute-start(bf16[128,2048]{1,0:T(8,128)(2,1)S(1)} %get-tuple-element.108), channel_id=1, source_target_pairs={{0,1},{1,0},{2,3},{3,2},{4,5},{5,4},{6,7},{7,6},{8,9},{9,8},{10,11... | collective-permute-start | bytes 1572872 | tf_op jit(solution)/shard_map/ppermute | solution.py:278
  128.0 1.7 %copy-start = (f32[3,12,128,128]{3,2,1,0:T(8,128)S(1)}, f32[3,12,128,128]{3,2,1,0:T(8,128)}, u32[]{:S(2)}) copy-start(f32[3,12,128,128]{3,2,1,0:T(8,128)} %refs_3_.7) | copy-start | bytes 7077892
  128.0 2.4 %copy-start.1 = (f32[3,12,128,128]{3,2,1,0:T(8,128)S(1)}, f32[3,12,128,128]{3,2,1,0:T(8,128)}, u32[]{:S(2)}) copy-start(f32[3,12,128,128]{3,2,1,0:T(8,128)} %refs_4_.5) | copy-start | bytes 7077892
  128.4 12.1 %collective-permute-start.19 = (bf16[2,12,128,128]{3,2,1,0:T(8,128)(2,1)S(1)}, bf16[2,12,128,128]{3,2,1,0:T(8,128)(2,1)S(1)}, u32[]{:S(2)}, u32[]{:S(2)}) collective-permute-start(bf16[2,12,128,128]{3,2,1,0:T(8,128)(2,1)S(1)} %get-tuple-element.113), channel_id=1, source_target_pairs={{0,16},{4,12},{8,24},{12,4},{16,0},{20,28},{24,8},{28,20},{1,17},{... | collective-permute-start | bytes 2359304 | tf_op jit(solution)/shard_map/ppermute | solution.py:314
  140.6 13.7 %collective-permute-start.22 = (bf16[1,12,128,128]{3,2,1,0:T(8,128)(2,1)S(1)}, bf16[1,12,128,128]{3,2,1,0:T(8,128)(2,1)S(1)}, u32[]{:S(2)}, u32[]{:S(2)}) collective-permute-start(bf16[1,12,128,128]{3,2,1,0:T(8,128)(2,1)S(1)} %get-tuple-element.125), channel_id=1, source_target_pairs={{0,8},{4,20},{8,0},{12,28},{16,24},{20,4},{24,16},{28,12},{1,9},{5... | collective-permute-start | bytes 1179656 | tf_op jit(solution)/shard_map/ppermute | solution.py:314

commit v8 on v7

--- a/solution.py
+++ b/solution.py
@@ -35,32 +35,56 @@
     return plan_ref[at], plan_ref[at + 1]
 
 
-def each_group(count, group, body):
+def each_group(first, last, group, body):
     def step(i, carry):
-        body([i * group + u for u in range(group)])
+        body([first + i * group + u for u in range(group)])
         return carry
 
-    lax.fori_loop(0, lax.div(count + (group - 1), group), step, 0)
+    lax.fori_loop(0, lax.div(last - first + (group - 1), group), step, 0)
 
 
 def dot(a, b, contract):
     return lax.dot_general(a, b, (contract, ((), ())), preferred_element_type=F32)
 
 
-def accumulate(plan_ref, matrix, capacity, acc, into, product):
+def accumulate(plan_ref, matrix, capacity, acc, into, product, order=None, base=0):
     trash = acc.shape[0] - 1
-    count = plan_ref[2 + matrix]
-
-    def body(slots):
+    order_ref, first, last = order or (None, 0, plan_ref[2 + matrix])
+
+    def body(places):
         products, targets = [], []
-        for s in slots:
+        for p in places:
+            s = p if order is None else jnp.where(p < last, order_ref[p], 0)
             pair = slot_pair(plan_ref, matrix, s, capacity)
-            targets.append(jnp.where(s < count, pair[into], trash))
+            targets.append(jnp.where(p < last, pair[into] - base, trash))
             products.append(product(s, *pair))
         for t, p in zip(targets, products):
             acc[t] += p
 
-    each_group(count, group_of(capacity), body)
+    each_group(first, last, group_of(capacity), body)
+
+
+def order_kernel(per_shard, capacity, plan_ref, order_ref):
+    far = lax.bitwise_xor(plan_ref[0], 3)
+    for matrix in (0, 1):
+
+        def is_far(s, matrix=matrix):
+            return lax.div(slot_pair(plan_ref, matrix, s, capacity)[0], per_shard) == far
+
+        def count(s, total):
+            return total + is_far(s).astype(jnp.int32)
+
+        def put(s, at):
+            here, there = at
+            found = is_far(s)
+            order_ref[matrix * capacity + jnp.where(found, here, there)] = s
+            step = found.astype(jnp.int32)
+            return here + step, there + 1 - step
+
+        live = plan_ref[2 + matrix]
+        total = lax.fori_loop(0, live, count, 0)
+        order_ref[2 * capacity + matrix] = total
+        lax.fori_loop(0, live, put, (0, total))
 
 
 def load_shards(pieces, held, me):
@@ -209,6 +233,28 @@
     store_shards(total, outs, plan_ref[0], outs[0].shape[-1] // size, size)
 
 
+def input_part_kernel(is_far, plan_ref, order_ref, gate_rows_ref, up_rows_ref, w_ref, *refs):
+    *outs, total = refs
+    capacity, size = w_ref.shape[1], w_ref.shape[2]
+    per_shard = outs[0].shape[-1] // size
+    me = plan_ref[0]
+    base = lax.bitwise_xor(me, 3) * per_shard if is_far else 0
+    total[...] = jnp.zeros_like(total)
+    for matrix, rows in ((0, gate_rows_ref), (1, up_rows_ref)):
+        at = matrix * capacity
+        cut = at + order_ref[2 * capacity + matrix]
+        accumulate(
+            plan_ref, matrix, capacity, total, 0,
+            lambda s, f, h, matrix=matrix, rows=rows: dot(rows[h], w_ref[matrix, s], ((1,), (1,))),
+            (order_ref, at, cut) if is_far else (order_ref, cut, at + plan_ref[2 + matrix]),
+            base,
+        )
+    for offset, out in enumerate(outs):
+        first = 0 if is_far else lax.bitwise_xor(me, offset) * per_shard
+        for c in range(per_shard):
+            out[:, c * size : (c + 1) * size] = total[first + c].astype(out.dtype)
+
+
 def fold_kernel(keep_ref, got_ref, keep_out, send_out):
     half = keep_out.shape[0]
     keep_out[...] = keep_ref[:half] + got_ref[:half]
@@ -249,8 +295,8 @@
 class Line:
     token = None
 
-    def __call__(self, kernel, name, outs, scratch, operands, plan=None, after=(), specs=None, out_specs=None, **more):
-        scalars = [] if plan is None else [plan]
+    def __call__(self, kernel, name, outs, scratch, operands, plan=(), after=(), specs=None, out_specs=None, cost=COST, **more):
+        scalars = [*plan]
         extra = [*after] if self.token is None else [*after, self.token]
         n_in, n_out = len(scalars) + len(operands), len(outs)
 
@@ -268,7 +314,7 @@
             out_specs=[*(out_specs or [VMEM] * n_out), VMEM],
             scratch_shapes=scratch,
             compiler_params=pltpu.CompilerParams(vmem_limit_bytes=VMEM_LIMIT),
-            cost_estimate=pl.CostEstimate(flops=COST, bytes_accessed=0, transcendentals=0),
+            cost_estimate=pl.CostEstimate(flops=cost, bytes_accessed=0, transcendentals=0),
             **more,
         )(*scalars, *operands, *extra)
         return results
@@ -292,8 +338,6 @@
 
 
 def scatter_first(parts):
-    if len(parts) == 4:
-        return [flip(parts[3], 4, 1)]
     return [lax.ppermute(parts[3], "tensor", [(0, 1), (3, 2)]), lax.ppermute(parts[4], "tensor", [(1, 2), (2, 1)])]
 
 
@@ -318,7 +362,7 @@
     capacity, size = weights.shape[1], weights.shape[2]
     rows, width = inputs.shape
     me = jnp.stack([lax.axis_index("tensor"), lax.axis_index("dp")]).astype(jnp.int32)
-    plan = jnp.concatenate([me, block_counts[0], block_index.reshape(-1)])
+    plan = (jnp.concatenate([me, block_counts[0], block_index.reshape(-1)]),)
     features = shards * width // size
     places, share = replicas // 2, capacity // replicas
     levels = places.bit_length() - 1
@@ -371,6 +415,11 @@
 
     x = gather(inputs, gather_near)
     if lined:
+        (order,) = line(
+            functools.partial(order_kernel, width // size, capacity), "order",
+            [SHAPE((2 * capacity + 2,), jnp.int32)], [], [], plan, out_specs=[SMEM],
+        )
+    if lined:
         (out_grad,) = line(hold_kernel, "hold", [piece], [], [out_grad, x[2]])
     og = gather(out_grad, gather_line)
     out_parts, in_parts = parts_of(5), parts_of(4)
@@ -391,7 +440,7 @@
     )
     if lined:
         out_sums = scatter_second(line, out_parts, out_far)
-    down = grads(2, og, hidden_turned, out_far[1:] if lined else ())
+    down = grads(2, og, hidden_turned)
     gate_rows, up_rows = line(
         functools.partial(rows_kernel, len(og)),
         "row_grads",
@@ -401,17 +450,21 @@
         plan,
     )
     down = fold(*down, 0)
-    in_parts = line(
-        functools.partial(input_kernel, len(in_parts)),
-        "input_grads",
-        in_parts,
-        [total],
-        [gate_rows, up_rows, weights],
-        plan,
-    )
-    if lined:
-        in_came = scatter_first(in_parts)
+    if lined:
+        part_total = pltpu.VMEM((width // size + 1, rows, size), F32)
+        in_operands = [gate_rows, up_rows, weights]
+        (in_far,) = line(
+            functools.partial(input_part_kernel, True), "input_far", [piece], [part_total], in_operands, (*plan, order)
+        )
+        in_far = flip(in_far, 4, 1)
+    if lined:
+        in_parts = line(
+            functools.partial(input_part_kernel, False), "input_rest", [piece] * 3, [total], in_operands, (*plan, order)
+        )
     else:
+        in_parts = line(
+            functools.partial(input_kernel, 1), "input_grads", in_parts, [total], [gate_rows, up_rows, weights], plan
+        )
         input_grad = lax.psum_scatter(in_parts[0], "tensor", scatter_dimension=0)
     gate = grads(0, [gate_rows], x_turned)
     for step in range(1, levels):
@@ -419,16 +472,16 @@
     if lined:
         outputs = finish(out_sums)
     gate = fold(*gate, 0)
+    buffer = update(2, *down, None)
     up = grads(1, [up_rows], x_turned)
+    if lined:
+        in_sums = scatter_second(line, in_parts, [in_far])
+    up = fold(*up, 0)
     for step in range(1, levels):
         gate = fold(*gate, step)
-    if lined:
-        in_sums = scatter_second(line, in_parts, in_came)
-    up = fold(*up, 0)
-    buffer = update(2, *down, None)
-    buffer = update(0, *gate, buffer)
     for step in range(1, levels):
         up = fold(*up, step)
+    buffer = update(0, *gate, buffer)
     if lined:
         input_grad = finish(in_sums)
     buffer = update(1, *up, buffer)

time: 157 us -> 146 us (0.930)
  waiting for transfers between devices: 68.3 us -> 61.1 us
  starting transfers between devices: 43.7 us -> 39.5 us
  Pallas kernels: 39.8 us -> 42.7 us
  local copies, waits for them, and re-layouts: 2.72 us -> 0.96 us
    ppermute x9, waiting for transfers between devices: 45.9 us -> 35 us  [flip(): return lax.ppermute(v, 'tensor', [(a, a ^ bit) for a in range(shards)])]
    ppermute x9, starting transfers between devices: 26.4 us -> 19.9 us  [flip(): return lax.ppermute(v, 'tensor', [(a, a ^ bit) for a in range(shards)])]
    ppermute x6, waiting for transfers between devices: 13.9 us -> 18.6 us  [axis_swap(): return lax.ppermute(v, 'dp', pairs)]
    pallas_call x21 -> x23, Pallas kernels: 39.8 us -> 42.7 us  [__call__(): pl.pallas_call(body, name=name, out_shape=[*outs, TOKEN], in_specs=[SMEM]...]
    ppermute x6, starting transfers between devices: 7.34 us -> 9.56 us  [axis_swap(): return lax.ppermute(v, 'dp', pairs)]
    unnamed x15, local copies, waits for them, and re-layouts: 2.58 us -> 0.82 us
  transfers between devices with their start and end apart: 23 -> 23, of which waited for: 8 -> 9; matrix products, arithmetic and copies ran while one was open for 1% -> 1% of each run, Pallas kernels for 24% -> 28%
where the time goes in v8:
time: 146 us
  waiting for transfers between devices  61.1 us (42%)
  Pallas kernels  42.7 us (29%)
  starting transfers between devices  39.5 us (27%)
    pallas_call x23, Pallas kernels, __call__(): pl.pallas_call(body, name=name, out_shape=[*outs, TOKEN], in_specs=[SMEM]...  42.7 us
    ppermute x9, waiting for transfers between devices, flip(): return lax.ppermute(v, 'tensor', [(a, a ^ bit) for a in range(shards)])  35 us
    ppermute x9, starting transfers between devices, flip(): return lax.ppermute(v, 'tensor', [(a, a ^ bit) for a in range(shards)])  19.9 us
    ppermute x6, waiting for transfers between devices, axis_swap(): return lax.ppermute(v, 'dp', pairs)  18.6 us
    ppermute x6, starting transfers between devices, axis_swap(): return lax.ppermute(v, 'dp', pairs)  9.56 us
    ppermute x1, waiting for transfers between devices, scatter_first(): lax.ppermute(parts[3], 'tensor', [(0, 1), (3, 2)])  7.51 us
    ppermute x1, starting transfers between devices, gather_line(): below = lax.ppermute(v, 'tensor', [(a, a + 1) for a in range(3)])  4.58 us
  transfers between devices with their start and end apart: 23, of which 9 were waited for; matrix products, arithmetic and copies ran while one was open for 1% of the time, Pallas kernels for 28%

profile of v8, /device:TPU:0, one launch (start us, length us, event | category | flops | bytes accessed | tf_op | source)
XLA Modules:
  0.0 145.8 jit_solution(6194060072575588769)
XLA Ops:
  0.6 4.1 %collective-permute-start.1 = (bf16[128,2048]{1,0:T(8,128)(2,1)}, bf16[128,2048]{1,0:T(8,128)(2,1)S(1)}, u32[]{:S(2)}, u32[]{:S(2)}) collective-permute-start(bf16[128,2048]{1,0:T(8,128)(2,1)} %refs_1_.3), channel_id=1, source_target_pairs={{0,2},{1,3},{2,0},{3,1},{4,6},{5,7},{6,4},{7,5},{8,10},{9,11},{10,... | collective-permute-start | bytes 1572872 | tf_op jit(solution)/shard_map/ppermute | solution.py:324
  4.7 1.6 %collective-permute-start = (bf16[128,2048]{1,0:T(8,128)(2,1)}, bf16[128,2048]{1,0:T(8,128)(2,1)S(1)}, u32[]{:S(2)}, u32[]{:S(2)}) collective-permute-start(bf16[128,2048]{1,0:T(8,128)(2,1)} %refs_1_.3), channel_id=1, source_target_pairs={{0,1},{1,0},{2,3},{3,2},{4,5},{5,4},{6,7},{7,6},{8,9},{9,8},{10,11... | collective-permute-start | bytes 1572872 | tf_op jit(solution)/shard_map/ppermute | solution.py:324
  8.0 4.9 %order.1 = (s32[194]{0:T(256)S(1)}, f32[8,128]{1,0:T(8,128)S(1)}) custom-call(s32[581]{0:T(1024)S(1)} %pad_add_fusion.refs_0_), custom_call_target="tpu_custom_call" | custom-call | flops 20000000000 | tf_op jit(solution)/shard_map/order/pallas_call | solution.py:309
  12.9 15.3 %collective-permute-done.1.refs_1_.refs_3_ = bf16[128,2048]{1,0:T(8,128)(2,1)S(1)} collective-permute-done((bf16[128,2048]{1,0:T(8,128)(2,1)}, bf16[128,2048]{1,0:T(8,128)(2,1)S(1)}, u32[]{:S(2)}, u32[]{:S(2)}) %collective-permute-start.1) | collective-permute-done | bytes 524320 | tf_op jit(solution)/shard_map/ppermute | solution.py:324
  29.0 3.3 %collective-permute-start.9 = (bf16[128,2048]{1,0:T(8,128)(2,1)S(1)}, bf16[128,2048]{1,0:T(8,128)(2,1)S(1)}, u32[]{:S(2)}, u32[]{:S(2)}) collective-permute-start(bf16[128,2048]{1,0:T(8,128)(2,1)S(1)} %get-tuple-element.80.refs_1_), channel_id=1, source_target_pairs={{0,2},{1,3},{2,0},{3,1},{4,6},{5,7},{6,4},{7,5},{8,10},{9,11},{10,... | collective-permute-start | bytes 1572872 | tf_op jit(solution)/shard_map/ppermute | solution.py:324
  33.6 4.6 %collective-permute-start.7 = (bf16[128,2048]{1,0:T(8,128)(2,1)S(1)}, bf16[128,2048]{1,0:T(8,128)(2,1)S(1)}, u32[]{:S(2)}, u32[]{:S(2)}) collective-permute-start(bf16[128,2048]{1,0:T(8,128)(2,1)S(1)} %get-tuple-element.80.refs_1_), channel_id=1, source_target_pairs={{0,1},{1,2},{2,3},{4,5},{5,6},{6,7},{8,9},{9,10},{10,11},{12,13},{... | collective-permute-start | bytes 1572872 | tf_op jit(solution)/shard_map/ppermute | solution.py:334
  38.2 15.5 %collective-permute-done.2.refs_4_ = bf16[128,2048]{1,0:T(8,128)(2,1)S(1)} collective-permute-done((bf16[128,2048]{1,0:T(8,128)(2,1)S(1)}, bf16[128,2048]{1,0:T(8,128)(2,1)S(1)}, u32[]{:S(2)}, u32[]{:S(2)}) %collective-permute-start.2) | collective-permute-done | bytes 524320 | tf_op jit(solution)/shard_map/ppermute | solution.py:324
  53.7 7.5 %forward.1 = (bf16[14,128,128]{2,1,0:T(8,128)(2,1)}, bf16[14,128,128]{2,1,0:T(8,128)(2,1)S(1)}, f32[14,128,128]{2,1,0:T(8,128)S(1)}, f32[14,128,128]{2,1,0:T(8,1...) custom-call(s32[581]{0:T(1024)S(1)} %pad_add_fusion.refs_0_, ...), custom_call_target="tpu_custom_call" | custom-call | flops 20000000000 | tf_op jit(solution)/shard_map/forward/pallas_call | solution.py:309
  62.5 1.5 %collective-permute-start.6 = (bf16[128,2048]{1,0:T(8,128)(2,1)}, bf16[128,2048]{1,0:T(8,128)(2,1)}, u32[]{:S(2)}, u32[]{:S(2)}) collective-permute-start(bf16[128,2048]{1,0:T(8,128)(2,1)} %get-tuple-element.79), channel_id=1, source_target_pairs={{1,2},{2,1},{5,6},{6,5},{9,10},{10,9},{13,14},{14,13},{17,18},{18,... | collective-permute-start | bytes 1572872 | tf_op jit(solution)/shard_map/ppermute | solution.py:341
  66.5 7.5 %collective-permute-done.3.refs_1_ = bf16[128,2048]{1,0:T(8,128)(2,1)S(1)} collective-permute-done((bf16[128,2048]{1,0:T(8,128)(2,1)S(1)}, bf16[128,2048]{1,0:T(8,128)(2,1)S(1)}, u32[]{:S(2)}, u32[]{:S(2)}) %collective-permute-start.3) | collective-permute-done | bytes 524320 | tf_op jit(solution)/shard_map/ppermute | solution.py:341
  74.1 4.1 %collective-permute-start.4 = (bf16[128,2048]{1,0:T(8,128)(2,1)S(1)}, bf16[128,2048]{1,0:T(8,128)(2,1)S(1)}, u32[]{:S(2)}, u32[]{:S(2)}) collective-permute-start(bf16[128,2048]{1,0:T(8,128)(2,1)S(1)} %get-tuple-element.77), channel_id=1, source_target_pairs={{0,2},{1,3},{2,0},{3,1},{4,6},{5,7},{6,4},{7,5},{8,10},{9,11},{10,... | collective-permute-start | bytes 1572872 | tf_op jit(solution)/shard_map/ppermute | solution.py:324
  78.3 2.5 %down_grads.1 = (bf16[4,12,128,128]{3,2,1,0:T(8,128)(2,1)S(1)}, bf16[4,12,128,128]{3,2,1,0:T(8,128)(2,1)S(1)}, f32[8,128]{1,0:T(8,128)S(1)}) custom-call(s32[581]{0:T(1024)S(1)} %pad_add_fusion.refs_0_, bf16[128,2048]{1,0:T(8,128)(2,1)S(1)} %get-tuple-element.80.refs_1_, bf16[128,2048]{1,0:T(8,128)(2,1)S(1)} %collective-permute-done.7.refs_2_, ...), custom_call_target="tpu_custom_call" | custom-call | flops 20000000000 | tf_op jit(solution)/shard_map/down_grads/pallas_call | solution.py:309
  80.9 3.4 %row_grads.1 = (bf16[14,128,128]{2,1,0:T(8,128)(2,1)S(1)}, bf16[14,128,128]{2,1,0:T(8,128)(2,1)S(1)}, f32[8,128]{1,0:T(8,128)S(1)}) custom-call(s32[581]{0:T(1024)S(1)} %pad_add_fusion.refs_0_, bf16[128,2048]{1,0:T(8,128)(2,1)S(1)} %get-tuple-element.80.refs_1_, bf16[128,2048]{1,0:T(8,128)(2,1)S(1)} %collective-permute-done.7.refs_2_, ...), custom_call_target="tpu_custom_call" | custom-call | flops 20000000000 | tf_op jit(solution)/shard_map/row_grads/pallas_call | solution.py:309
  84.6 2.3 %input_far.1 = (bf16[128,2048]{1,0:T(8,128)(2,1)S(1)}, f32[8,128]{1,0:T(8,128)S(1)}) custom-call(s32[581]{0:T(1024)S(1)} %pad_add_fusion.refs_0_, s32[194]{0:T(256)S(1)} %get-tuple-element.93.refs_1_, bf16[14,128,128]{2,1,0:T(8,128)(2,1)S(1)} %get-tuple-element.91.refs_2_.refs_1_, bf16[14,128,128]{2,1,0:T(8,128)(2,1)S(1)} %get-tuple-element.94.refs_3_.refs_1_, ...), custom_call_target="tpu_custom_call" | custom-call | flops 20000000000 | tf_op jit(solution)/shard_map/input_far/pallas_call | solution.py:309
  86.9 1.5 %collective-permute-start.13 = (bf16[128,2048]{1,0:T(8,128)(2,1)S(1)}, bf16[128,2048]{1,0:T(8,128)(2,1)S(1)}, u32[]{:S(2)}, u32[]{:S(2)}) collective-permute-start(bf16[128,2048]{1,0:T(8,128)(2,1)S(1)} %get-tuple-element.103), channel_id=1, source_target_pairs={{0,1},{1,0},{2,3},{3,2},{4,5},{5,4},{6,7},{7,6},{8,9},{9,8},{10,11... | collective-permute-start | bytes 1572872 | tf_op jit(solution)/shard_map/ppermute | solution.py:324
  88.4 1.5 %collective-permute-start.12 = (bf16[2,12,128,128]{3,2,1,0:T(8,128)(2,1)S(1)}, bf16[2,12,128,128]{3,2,1,0:T(8,128)(2,1)S(1)}, u32[]{:S(2)}, u32[]{:S(2)}) collective-permute-start(bf16[2,12,128,128]{3,2,1,0:T(8,128)(2,1)S(1)} %get-tuple-element.90), channel_id=1, source_target_pairs={{0,16},{4,12},{8,24},{12,4},{16,0},{20,28},{24,8},{28,20},{1,17},{... | collective-permute-start | bytes 2359304 | tf_op jit(solution)/shard_map/ppermute | solution.py:358
  89.9 5.3 %input_rest.1 = (bf16[128,2048]{1,0:T(8,128)(2,1)S(1)}, bf16[128,2048]{1,0:T(8,128)(2,1)S(1)}, bf16[128,2048]{1,0:T(8,128)(2,1)S(1)}, f32[8,128]{1,0:T(8,128)S(1)}) custom-call(s32[581]{0:T(1024)S(1)} %pad_add_fusion.refs_0_, s32[194]{0:T(256)S(1)} %get-tuple-element.93.refs_1_, bf16[14,128,128]{2,1,0:T(8,128)(2,1)S(1)} %get-tuple-element.91.refs_2_.refs_1_, ...), custom_call_target="tpu_custom_call" | custom-call | flops 20000000000 | tf_op jit(solution)/shard_map/input_rest/pallas_call | solution.py:309
  95.2 1.8 %gate_grads.1 = (bf16[4,12,128,128]{3,2,1,0:T(8,128)(2,1)S(1)}, bf16[4,12,128,128]{3,2,1,0:T(8,128)(2,1)S(1)}, f32[8,128]{1,0:T(8,128)S(1)}) custom-call(s32[581]{0:T(1024)S(1)} %pad_add_fusion.refs_0_, bf16[14,128,128]{2,1,0:T(8,128)(2,1)S(1)} %get-tuple-element.91.refs_2_.refs_1_, bf16[64,128,128]{2,1,0:T(8,128)(2,1)S(1)} %get-tuple-element.92.refs_2_, ...), custom_call_target="tpu_custom_call" | custom-call | flops 20000000000 | tf_op jit(solution)/shard_map/gate_grads/pallas_call | solution.py:309
  97.0 3.4 %collective-permute-done.12.refs_1_ = bf16[2,12,128,128]{3,2,1,0:T(8,128)(2,1)S(1)} collective-permute-done((bf16[2,12,128,128]{3,2,1,0:T(8,128)(2,1)S(1)}, bf16[2,12,128,128]{3,2,1,0:T(8,128)(2,1)S(1)}, u32[]{:S(2)}, u32[]{:S(2)}) %collective-permute-start.12) | collective-permute-done | bytes 786464 | tf_op jit(solution)/shard_map/ppermute | solution.py:358
  100.6 1.6 %collective-permute-start.14 = (bf16[1,12,128,128]{3,2,1,0:T(8,128)(2,1)S(1)}, bf16[1,12,128,128]{3,2,1,0:T(8,128)(2,1)S(1)}, u32[]{:S(2)}, u32[]{:S(2)}) collective-permute-start(bf16[1,12,128,128]{3,2,1,0:T(8,128)(2,1)S(1)} %get-tuple-element.106), channel_id=1, source_target_pairs={{0,8},{4,20},{8,0},{12,28},{16,24},{20,4},{24,16},{28,12},{1,9},{5... | collective-permute-start | bytes 1179656 | tf_op jit(solution)/shard_map/ppermute | solution.py:358
  102.5 2.1 %finish.2 = (bf16[128,2048]{1,0:T(8,128)(2,1)}, f32[8,128]{1,0:T(8,128)S(1)}) custom-call(bf16[128,2048]{1,0:T(8,128)(2,1)S(1)} %get-tuple-element.71.refs_0_, bf16[128,2048]{1,0:T(8,128)(2,1)S(1)} %collective-permute-done.4.refs_1_, bf16[128,2048]{1,0:T(8,128)(2,1)S(1)} %collective-permute-done.5.refs_2_, bf16[128,2048]{1,0:T(8,128)(2,1)} %collective-permute-done.6.refs_3_, ...), custom_call_target="tpu_custom_call" | custom-call | flops 20000000000 | tf_op jit(solution)/shard_map/finish/pallas_call | solution.py:309
  104.9 1.6 %collective-permute-start.18 = (bf16[2,12,128,128]{3,2,1,0:T(8,128)(2,1)S(1)}, bf16[2,12,128,128]{3,2,1,0:T(8,128)(2,1)S(1)}, u32[]{:S(2)}, u32[]{:S(2)}) collective-permute-start(bf16[2,12,128,128]{3,2,1,0:T(8,128)(2,1)S(1)} %get-tuple-element.116), channel_id=1, source_target_pairs={{0,16},{4,12},{8,24},{12,4},{16,0},{20,28},{24,8},{28,20},{1,17},{... | collective-permute-start | bytes 2359304 | tf_op jit(solution)/shard_map/ppermute | solution.py:358
  106.5 2.8 %collective-permute-done.14.refs_2_ = bf16[1,12,128,128]{3,2,1,0:T(8,128)(2,1)S(1)} collective-permute-done((bf16[1,12,128,128]{3,2,1,0:T(8,128)(2,1)S(1)}, bf16[1,12,128,128]{3,2,1,0:T(8,128)(2,1)S(1)}, u32[]{:S(2)}, u32[]{:S(2)}) %collective-permute-start.14) | collective-permute-done | bytes 393248 | tf_op jit(solution)/shard_map/ppermute | solution.py:358
  109.3 2.0 %update.3 = (f32[3,12,128,128]{3,2,1,0:T(8,128)}, f32[8,128]{1,0:T(8,128)S(1)}) custom-call(s32[581]{0:T(1024)S(1)} %pad_add_fusion.refs_0_, bf16[1,12,128,128]{3,2,1,0:T(8,128)(2,1)S(1)} %get-tuple-element.105.refs_1_, bf16[1,12,128,128]{3,2,1,0:T(8,128)(2,1)S(1)} %collective-permute-done.14.refs_2_, f32[3,12,128,128]{3,2,1,0:T(8,128)S(1)} %copy-done, ...), custom_call_target="tpu_custom_call" | custom-call | flops 20000000000 | tf_op jit(solution)/shard_map/update/pallas_call | solution.py:309
  111.3 2.9 %up_grads.1 = (bf16[4,12,128,128]{3,2,1,0:T(8,128)(2,1)S(1)}, bf16[4,12,128,128]{3,2,1,0:T(8,128)(2,1)S(1)}, f32[8,128]{1,0:T(8,128)S(1)}) custom-call(s32[581]{0:T(1024)S(1)} %pad_add_fusion.refs_0_, bf16[14,128,128]{2,1,0:T(8,128)(2,1)S(1)} %get-tuple-element.94.refs_3_.refs_1_, bf16[64,128,128]{2,1,0:T(8,128)(2,1)S(1)} %get-tuple-element.92.refs_2_, ...), custom_call_target="tpu_custom_call" | custom-call | flops 20000000000 | tf_op jit(solution)/shard_map/up_grads/pallas_call | solution.py:309
  114.3 3.7 %collective-permute-start.16 = (bf16[128,2048]{1,0:T(8,128)(2,1)S(1)}, bf16[128,2048]{1,0:T(8,128)(2,1)S(1)}, u32[]{:S(2)}, u32[]{:S(2)}) collective-permute-start(bf16[128,2048]{1,0:T(8,128)(2,1)S(1)} %get-tuple-element.113), channel_id=1, source_target_pairs={{0,2},{1,3},{2,0},{3,1},{4,6},{5,7},{6,4},{7,5},{8,10},{9,11},{10,... | collective-permute-start | bytes 1572872 | tf_op jit(solution)/shard_map/ppermute | solution.py:324
  119.2 2.1 %collective-permute-start.21 = (bf16[2,12,128,128]{3,2,1,0:T(8,128)(2,1)S(1)}, bf16[2,12,128,128]{3,2,1,0:T(8,128)(2,1)S(1)}, u32[]{:S(2)}, u32[]{:S(2)}) collective-permute-start(bf16[2,12,128,128]{3,2,1,0:T(8,128)(2,1)S(1)} %get-tuple-element.125), channel_id=1, source_target_pairs={{0,16},{4,12},{8,24},{12,4},{16,0},{20,28},{24,8},{28,20},{1,17},{... | collective-permute-start | bytes 2359304 | tf_op jit(solution)/shard_map/ppermute | solution.py:358
  121.5 1.5 %collective-permute-start.20 = (bf16[1,12,128,128]{3,2,1,0:T(8,128)(2,1)S(1)}, bf16[1,12,128,128]{3,2,1,0:T(8,128)(2,1)S(1)}, u32[]{:S(2)}, u32[]{:S(2)}) collective-permute-start(bf16[1,12,128,128]{3,2,1,0:T(8,128)(2,1)S(1)} %get-tuple-element.122), channel_id=1, source_target_pairs={{0,8},{4,20},{8,0},{12,28},{16,24},{20,4},{24,16},{28,12},{1,9},{5... | collective-permute-start | bytes 1179656 | tf_op jit(solution)/shard_map/ppermute | solution.py:358
  123.0 12.5 %collective-permute-done.21.refs_1_ = bf16[2,12,128,128]{3,2,1,0:T(8,128)(2,1)S(1)} collective-permute-done((bf16[2,12,128,128]{3,2,1,0:T(8,128)(2,1)S(1)}, bf16[2,12,128,128]{3,2,1,0:T(8,128)(2,1)S(1)}, u32[]{:S(2)}, u32[]{:S(2)}) %collective-permute-start.21) | collective-permute-done | bytes 786464 | tf_op jit(solution)/shard_map/ppermute | solution.py:358
  137.0 2.0 %update.4 = (f32[3,12,128,128]{3,2,1,0:T(8,128)}, f32[8,128]{1,0:T(8,128)S(1)}) custom-call(s32[581]{0:T(1024)S(1)} %pad_add_fusion.refs_0_, bf16[1,12,128,128]{3,2,1,0:T(8,128)(2,1)S(1)} %get-tuple-element.121.refs_1_, bf16[1,12,128,128]{3,2,1,0:T(8,128)(2,1)S(1)} %collective-permute-done.20.refs_2_, ...), custom_call_target="tpu_custom_call", output_to_operand_aliasing={{0}: (5, {})} | custom-call | flops 20000000000 | tf_op jit(solution)/shard_map/update/pallas_call | solution.py:309
  139.0 2.9 %collective-permute-done.16.refs_1_ = bf16[128,2048]{1,0:T(8,128)(2,1)S(1)} collective-permute-done((bf16[128,2048]{1,0:T(8,128)(2,1)S(1)}, bf16[128,2048]{1,0:T(8,128)(2,1)S(1)}, u32[]{:S(2)}, u32[]{:S(2)}) %collective-permute-start.16) | collective-permute-done | bytes 524320 | tf_op jit(solution)/shard_map/ppermute | solution.py:324
  143.8 2.0 %update.5 = (f32[3,12,128,128]{3,2,1,0:T(8,128)}, f32[8,128]{1,0:T(8,128)}) custom-call(s32[581]{0:T(1024)S(1)} %pad_add_fusion.refs_0_, bf16[1,12,128,128]{3,2,1,0:T(8,128)(2,1)S(1)} %get-tuple-element.130.refs_1_, bf16[1,12,128,128]{3,2,1,0:T(8,128)(2,1)S(1)} %collective-permute-done.22.refs_2_, ...), custom_call_target="tpu_custom_call", output_to_operand_aliasing={{0}: (5, {})} | custom-call | flops 20000000000 | tf_op jit(solution)/shard_map/update/pallas_call | solution.py:309
  (55 shorter events, 14.0 us)
Async XLA Ops:
  0.6 27.6 %collective-permute-start.1 = (bf16[128,2048]{1,0:T(8,128)(2,1)}, bf16[128,2048]{1,0:T(8,128)(2,1)S(1)}, u32[]{:S(2)}, u32[]{:S(2)}) collective-permute-start(bf16[128,2048]{1,0:T(8,128)(2,1)} %refs_1_.3), channel_id=1, source_target_pairs={{0,2},{1,3},{2,0},{3,1},{4,6},{5,7},{6,4},{7,5},{8,10},{9,11},{10,... | collective-permute-start | bytes 1572872 | tf_op jit(solution)/shard_map/ppermute | solution.py:324
  4.7 33.5 %collective-permute-start = (bf16[128,2048]{1,0:T(8,128)(2,1)}, bf16[128,2048]{1,0:T(8,128)(2,1)S(1)}, u32[]{:S(2)}, u32[]{:S(2)}) collective-permute-start(bf16[128,2048]{1,0:T(8,128)(2,1)} %refs_1_.3), channel_id=1, source_target_pairs={{0,1},{1,0},{2,3},{3,2},{4,5},{5,4},{6,7},{7,6},{8,9},{9,8},{10,11... | collective-permute-start | bytes 1572872 | tf_op jit(solution)/shard_map/ppermute | solution.py:324
  8.0 20.9 %copy-start.2 = (bf16[128,2048]{1,0:T(8,128)(2,1)S(1)}, bf16[128,2048]{1,0:T(8,128)(2,1)}, u32[]{:S(2)}) copy-start(bf16[128,2048]{1,0:T(8,128)(2,1)} %refs_0_.1) | copy-start | bytes 1572868
  8.0 45.7 %slice-start = ((s8[9437184]{0:T(1024)(128)(4,1)}), s8[4194304]{0:T(1024)(128)(4,1)S(1)}, s32[]{:S(2)}) async-start(s8[9437184]{0:T(1024)(128)(4,1)} %bitcast.3), calls=%async_computation | async-start | bytes 8388608
  8.0 45.7 %slice-start.1 = ((s8[9437184]{0:T(1024)(128)(4,1)}), s8[4194304]{0:T(1024)(128)(4,1)S(1)}, s32[]{:S(2)}) async-start(s8[9437184]{0:T(1024)(128)(4,1)} %bitcast.3), calls=%async_computation.1 | async-start | bytes 8388608
  28.2 25.5 %collective-permute-start.2 = (bf16[128,2048]{1,0:T(8,128)(2,1)S(1)}, bf16[128,2048]{1,0:T(8,128)(2,1)S(1)}, u32[]{:S(2)}, u32[]{:S(2)}) collective-permute-start(bf16[128,2048]{1,0:T(8,128)(2,1)S(1)} %collective-permute-done.1.refs_1_.refs_3_), channel_id=1, source_target_pairs={{0,1},{1,0},{2,3},{3,2},{4,5},{5,4},{6,7},{7,6},{8,9},{9,8},{10,11... | collective-permute-start | bytes 1572872 | tf_op jit(solution)/shard_map/ppermute | solution.py:324
  28.9 24.7 %slice-start.2 = ((s8[9437184]{0:T(1024)(128)(4,1)}), s8[1048576]{0:T(1024)(128)(4,1)S(1)}, s32[]{:S(2)}) async-start(s8[9437184]{0:T(1024)(128)(4,1)} %bitcast.3), calls=%async_computation.2 | async-start | bytes 2097152
  28.9 24.7 %copy-start.3 = (bf16[128,2048]{1,0:T(8,128)(2,1)S(1)}, bf16[128,2048]{1,0:T(8,128)(2,1)}, u32[]{:S(2)}) copy-start(bf16[128,2048]{1,0:T(8,128)(2,1)} %refs_1_.3) | copy-start | bytes 1572868
  29.0 35.0 %collective-permute-start.9 = (bf16[128,2048]{1,0:T(8,128)(2,1)S(1)}, bf16[128,2048]{1,0:T(8,128)(2,1)S(1)}, u32[]{:S(2)}, u32[]{:S(2)}) collective-permute-start(bf16[128,2048]{1,0:T(8,128)(2,1)S(1)} %get-tuple-element.80.refs_1_), channel_id=1, source_target_pairs={{0,2},{1,3},{2,0},{3,1},{4,6},{5,7},{6,4},{7,5},{8,10},{9,11},{10,... | collective-permute-start | bytes 1572872 | tf_op jit(solution)/shard_map/ppermute | solution.py:324
  32.3 45.9 %collective-permute-start.8 = (bf16[128,2048]{1,0:T(8,128)(2,1)S(1)}, bf16[128,2048]{1,0:T(8,128)(2,1)S(1)}, u32[]{:S(2)}, u32[]{:S(2)}) collective-permute-start(bf16[128,2048]{1,0:T(8,128)(2,1)S(1)} %get-tuple-element.80.refs_1_), channel_id=1, source_target_pairs={{1,0},{2,1},{3,2},{5,4},{6,5},{7,6},{9,8},{10,9},{11,10},{13,12},{... | collective-permute-start | bytes 1572872 | tf_op jit(solution)/shard_map/ppermute | solution.py:335
  33.6 44.6 %collective-permute-start.7 = (bf16[128,2048]{1,0:T(8,128)(2,1)S(1)}, bf16[128,2048]{1,0:T(8,128)(2,1)S(1)}, u32[]{:S(2)}, u32[]{:S(2)}) collective-permute-start(bf16[128,2048]{1,0:T(8,128)(2,1)S(1)} %get-tuple-element.80.refs_1_), channel_id=1, source_target_pairs={{0,1},{1,2},{2,3},{4,5},{5,6},{6,7},{8,9},{9,10},{10,11},{12,13},{... | collective-permute-start | bytes 1572872 | tf_op jit(solution)/shard_map/ppermute | solution.py:334
  61.2 12.9 %collective-permute-start.3 = (bf16[128,2048]{1,0:T(8,128)(2,1)S(1)}, bf16[128,2048]{1,0:T(8,128)(2,1)S(1)}, u32[]{:S(2)}, u32[]{:S(2)}) collective-permute-start(bf16[128,2048]{1,0:T(8,128)(2,1)S(1)} %get-tuple-element.73), channel_id=1, source_target_pairs={{0,1},{3,2},{4,5},{7,6},{8,9},{11,10},{12,13},{15,14},{16,17},{19,... | collective-permute-start | bytes 1572872 | tf_op jit(solution)/shard_map/ppermute | solution.py:341
  62.5 38.1 %collective-permute-start.6 = (bf16[128,2048]{1,0:T(8,128)(2,1)}, bf16[128,2048]{1,0:T(8,128)(2,1)}, u32[]{:S(2)}, u32[]{:S(2)}) collective-permute-start(bf16[128,2048]{1,0:T(8,128)(2,1)} %get-tuple-element.79), channel_id=1, source_target_pairs={{1,2},{2,1},{5,6},{6,5},{9,10},{10,9},{13,14},{14,13},{17,18},{18,... | collective-permute-start | bytes 1572872 | tf_op jit(solution)/shard_map/ppermute | solution.py:341
  63.9 14.3 %collective-permute-start.10 = (bf16[128,2048]{1,0:T(8,128)(2,1)S(1)}, bf16[128,2048]{1,0:T(8,128)(2,1)S(1)}, u32[]{:S(2)}, u32[]{:S(2)}) collective-permute-start(bf16[128,2048]{1,0:T(8,128)(2,1)S(1)} %collective-permute-done.9.refs_4_), channel_id=1, source_target_pairs={{2,3},{1,0},{6,7},{5,4},{10,11},{9,8},{14,15},{13,12},{18,19},{17,... | collective-permute-start | bytes 1572872 | tf_op jit(solution)/shard_map/ppermute | solution.py:336
  74.1 28.0 %collective-permute-start.4 = (bf16[128,2048]{1,0:T(8,128)(2,1)S(1)}, bf16[128,2048]{1,0:T(8,128)(2,1)S(1)}, u32[]{:S(2)}, u32[]{:S(2)}) collective-permute-start(bf16[128,2048]{1,0:T(8,128)(2,1)S(1)} %get-tuple-element.77), channel_id=1, source_target_pairs={{0,2},{1,3},{2,0},{3,1},{4,6},{5,7},{6,4},{7,5},{8,10},{9,11},{10,... | collective-permute-start | bytes 1572872 | tf_op jit(solution)/shard_map/ppermute | solution.py:324
  78.2 24.2 %collective-permute-start.5 = (bf16[128,2048]{1,0:T(8,128)(2,1)S(1)}, bf16[128,2048]{1,0:T(8,128)(2,1)S(1)}, u32[]{:S(2)}, u32[]{:S(2)}) collective-permute-start(bf16[128,2048]{1,0:T(8,128)(2,1)S(1)} %get-tuple-element.78), channel_id=1, source_target_pairs={{0,1},{1,0},{2,3},{3,2},{4,5},{5,4},{6,7},{7,6},{8,9},{9,8},{10,11... | collective-permute-start | bytes 1572872 | tf_op jit(solution)/shard_map/ppermute | solution.py:324
  80.8 3.5 %collective-permute-start.11 = (bf16[4,12,128,128]{3,2,1,0:T(8,128)(2,1)S(1)}, bf16[4,12,128,128]{3,2,1,0:T(8,128)(2,1)S(1)}, u32[]{:S(2)}, u32[]{:S(2)}) collective-permute-start(bf16[4,12,128,128]{3,2,1,0:T(8,128)(2,1)S(1)} %get-tuple-element.84), channel_id=1, source_target_pairs={{0,4},{4,0},{8,12},{12,8},{16,20},{20,16},{24,28},{28,24},{1,5},{5... | collective-permute-start | bytes 4718600 | tf_op jit(solution)/shard_map/ppermute | solution.py:352
  86.9 27.4 %collective-permute-start.13 = (bf16[128,2048]{1,0:T(8,128)(2,1)S(1)}, bf16[128,2048]{1,0:T(8,128)(2,1)S(1)}, u32[]{:S(2)}, u32[]{:S(2)}) collective-permute-start(bf16[128,2048]{1,0:T(8,128)(2,1)S(1)} %get-tuple-element.103), channel_id=1, source_target_pairs={{0,1},{1,0},{2,3},{3,2},{4,5},{5,4},{6,7},{7,6},{8,9},{9,8},{10,11... | collective-permute-start | bytes 1572872 | tf_op jit(solution)/shard_map/ppermute | solution.py:324
  88.4 12.0 %collective-permute-start.12 = (bf16[2,12,128,128]{3,2,1,0:T(8,128)(2,1)S(1)}, bf16[2,12,128,128]{3,2,1,0:T(8,128)(2,1)S(1)}, u32[]{:S(2)}, u32[]{:S(2)}) collective-permute-start(bf16[2,12,128,128]{3,2,1,0:T(8,128)(2,1)S(1)} %get-tuple-element.90), channel_id=1, source_target_pairs={{0,16},{4,12},{8,24},{12,4},{16,0},{20,28},{24,8},{28,20},{1,17},{... | collective-permute-start | bytes 2359304 | tf_op jit(solution)/shard_map/ppermute | solution.py:358
  100.4 4.2 %collective-permute-start.15 = (bf16[4,12,128,128]{3,2,1,0:T(8,128)(2,1)S(1)}, bf16[4,12,128,128]{3,2,1,0:T(8,128)(2,1)S(1)}, u32[]{:S(2)}, u32[]{:S(2)}) collective-permute-start(bf16[4,12,128,128]{3,2,1,0:T(8,128)(2,1)S(1)} %get-tuple-element.108), channel_id=1, source_target_pairs={{0,4},{4,0},{8,12},{12,8},{16,20},{20,16},{24,28},{28,24},{1,5},{5... | collective-permute-start | bytes 4718600 | tf_op jit(solution)/shard_map/ppermute | solution.py:352
  100.6 8.7 %collective-permute-start.14 = (bf16[1,12,128,128]{3,2,1,0:T(8,128)(2,1)S(1)}, bf16[1,12,128,128]{3,2,1,0:T(8,128)(2,1)S(1)}, u32[]{:S(2)}, u32[]{:S(2)}) collective-permute-start(bf16[1,12,128,128]{3,2,1,0:T(8,128)(2,1)S(1)} %get-tuple-element.106), channel_id=1, source_target_pairs={{0,8},{4,20},{8,0},{12,28},{16,24},{20,4},{24,16},{28,12},{1,9},{5... | collective-permute-start | bytes 1179656 | tf_op jit(solution)/shard_map/ppermute | solution.py:358
  104.6 4.7 %copy-start = (f32[3,12,128,128]{3,2,1,0:T(8,128)S(1)}, f32[3,12,128,128]{3,2,1,0:T(8,128)}, u32[]{:S(2)}) copy-start(f32[3,12,128,128]{3,2,1,0:T(8,128)} %refs_3_.5) | copy-start | bytes 7077892
  104.6 4.7 %copy-start.1 = (f32[3,12,128,128]{3,2,1,0:T(8,128)S(1)}, f32[3,12,128,128]{3,2,1,0:T(8,128)}, u32[]{:S(2)}) copy-start(f32[3,12,128,128]{3,2,1,0:T(8,128)} %refs_4_.9) | copy-start | bytes 7077892
  104.9 16.4 %collective-permute-start.18 = (bf16[2,12,128,128]{3,2,1,0:T(8,128)(2,1)S(1)}, bf16[2,12,128,128]{3,2,1,0:T(8,128)(2,1)S(1)}, u32[]{:S(2)}, u32[]{:S(2)}) collective-permute-start(bf16[2,12,128,128]{3,2,1,0:T(8,128)(2,1)S(1)} %get-tuple-element.116), channel_id=1, source_target_pairs={{0,16},{4,12},{8,24},{12,4},{16,0},{20,28},{24,8},{28,20},{1,17},{... | collective-permute-start | bytes 2359304 | tf_op jit(solution)/shard_map/ppermute | solution.py:358
  114.1 4.7 %collective-permute-start.19 = (bf16[4,12,128,128]{3,2,1,0:T(8,128)(2,1)S(1)}, bf16[4,12,128,128]{3,2,1,0:T(8,128)(2,1)S(1)}, u32[]{:S(2)}, u32[]{:S(2)}) collective-permute-start(bf16[4,12,128,128]{3,2,1,0:T(8,128)(2,1)S(1)} %get-tuple-element.118), channel_id=1, source_target_pairs={{0,4},{4,0},{8,12},{12,8},{16,20},{20,16},{24,28},{28,24},{1,5},{5... | collective-permute-start | bytes 4718600 | tf_op jit(solution)/shard_map/ppermute | solution.py:352
  114.3 27.6 %collective-permute-start.16 = (bf16[128,2048]{1,0:T(8,128)(2,1)S(1)}, bf16[128,2048]{1,0:T(8,128)(2,1)S(1)}, u32[]{:S(2)}, u32[]{:S(2)}) collective-permute-start(bf16[128,2048]{1,0:T(8,128)(2,1)S(1)} %get-tuple-element.113), channel_id=1, source_target_pairs={{0,2},{1,3},{2,0},{3,1},{4,6},{5,7},{6,4},{7,5},{8,10},{9,11},{10,... | collective-permute-start | bytes 1572872 | tf_op jit(solution)/shard_map/ppermute | solution.py:324
  118.0 24.8 %collective-permute-start.17 = (bf16[128,2048]{1,0:T(8,128)(2,1)S(1)}, bf16[128,2048]{1,0:T(8,128)(2,1)S(1)}, u32[]{:S(2)}, u32[]{:S(2)}) collective-permute-start(bf16[128,2048]{1,0:T(8,128)(2,1)S(1)} %get-tuple-element.114), channel_id=1, source_target_pairs={{0,1},{1,0},{2,3},{3,2},{4,5},{5,4},{6,7},{7,6},{8,9},{9,8},{10,11... | collective-permute-start | bytes 1572872 | tf_op jit(solution)/shard_map/ppermute | solution.py:324
  119.2 16.3 %collective-permute-start.21 = (bf16[2,12,128,128]{3,2,1,0:T(8,128)(2,1)S(1)}, bf16[2,12,128,128]{3,2,1,0:T(8,128)(2,1)S(1)}, u32[]{:S(2)}, u32[]{:S(2)}) collective-permute-start(bf16[2,12,128,128]{3,2,1,0:T(8,128)(2,1)S(1)} %get-tuple-element.125), channel_id=1, source_target_pairs={{0,16},{4,12},{8,24},{12,4},{16,0},{20,28},{24,8},{28,20},{1,17},{... | collective-permute-start | bytes 2359304 | tf_op jit(solution)/shard_map/ppermute | solution.py:358
  121.5 15.5 %collective-permute-start.20 = (bf16[1,12,128,128]{3,2,1,0:T(8,128)(2,1)S(1)}, bf16[1,12,128,128]{3,2,1,0:T(8,128)(2,1)S(1)}, u32[]{:S(2)}, u32[]{:S(2)}) collective-permute-start(bf16[1,12,128,128]{3,2,1,0:T(8,128)(2,1)S(1)} %get-tuple-element.122), channel_id=1, source_target_pairs={{0,8},{4,20},{8,0},{12,28},{16,24},{20,4},{24,16},{28,12},{1,9},{5... | collective-permute-start | bytes 1179656 | tf_op jit(solution)/shard_map/ppermute | solution.py:358
  135.7 8.1 %collective-permute-start.22 = (bf16[1,12,128,128]{3,2,1,0:T(8,128)(2,1)S(1)}, bf16[1,12,128,128]{3,2,1,0:T(8,128)(2,1)S(1)}, u32[]{:S(2)}, u32[]{:S(2)}) collective-permute-start(bf16[1,12,128,128]{3,2,1,0:T(8,128)(2,1)S(1)} %get-tuple-element.131), channel_id=1, source_target_pairs={{0,8},{4,20},{8,0},{12,28},{16,24},{20,4},{24,16},{28,12},{1,9},{5... | collective-permute-start | bytes 1179656 | tf_op jit(solution)/shard_map/ppermute | solution.py:358

commit v9 on v8

--- a/solution.py
+++ b/solution.py
@@ -8,7 +8,7 @@
 
 HB_DEV = 14
 EPSILON = 1e-08
-GROUP = 16
+GROUPS = (32, 8)
 COST = 2 * 10**10
 VMEM_LIMIT = 32 * 1024 * 1024
 F32, BF16 = jnp.float32, jnp.bfloat16
@@ -20,10 +20,6 @@
 HEAD = 5
 
 
-def group_of(capacity):
-    return next(g for g in (GROUP, 8, 4, 2, 1) if capacity % g == 0)
-
-
 def feature_block(ref, block, size):
     per_shard = ref.shape[2] // size
     start = pl.multiple_of(lax.rem(block, per_shard) * size, size)
@@ -35,12 +31,20 @@
     return plan_ref[at], plan_ref[at + 1]
 
 
-def each_group(first, last, group, body):
-    def step(i, carry):
-        body([first + i * group + u for u in range(group)])
-        return carry
-
-    lax.fori_loop(0, lax.div(last - first + (group - 1), group), step, 0)
+def each_group(first, last, body):
+    large, small = GROUPS
+
+    def run(at, size, count, whole):
+        def step(i, carry):
+            body([at + i * size + u for u in range(size)], whole)
+            return carry
+
+        lax.fori_loop(0, count, step, 0)
+
+    full = lax.div(last - first, large)
+    rest = first + full * large
+    run(first, large, full, True)
+    run(rest, small, lax.div(last - rest + (small - 1), small), False)
 
 
 def dot(a, b, contract):
@@ -51,17 +55,19 @@
     trash = acc.shape[0] - 1
     order_ref, first, last = order or (None, 0, plan_ref[2 + matrix])
 
-    def body(places):
+    def body(places, whole):
         products, targets = [], []
         for p in places:
-            s = p if order is None else jnp.where(p < last, order_ref[p], 0)
+            here = p if whole else jnp.minimum(p, last - 1)
+            s = here if order is None else order_ref[here]
             pair = slot_pair(plan_ref, matrix, s, capacity)
-            targets.append(jnp.where(p < last, pair[into] - base, trash))
+            target = pair[into] - base
+            targets.append(target if whole else jnp.where(p < last, target, trash))
             products.append(product(s, *pair))
         for t, p in zip(targets, products):
             acc[t] += p
 
-    each_group(first, last, group_of(capacity), body)
+    each_group(first, last, body)
 
 
 def order_kernel(per_shard, capacity, plan_ref, order_ref):
@@ -200,14 +206,16 @@
     right_ref = load_shards(pieces, held, plan_ref[0])
     capacity = 2 * places * share
     count = plan_ref[2 + matrix]
-    for out, bit in ((send_ref, 1), (keep_ref, 0)):
-
-        def one_place(q, carry, out=out, bit=bit):
+
+    def one_place(q, carry):
+        todo = []
+        for out, bit in ((send_ref, 1), (keep_ref, 0)):
             owner = lax.bitwise_xor(replica, bit)
-            first = lax.bitwise_xor(owner, spread(q, lax.bitwise_and(owner, 1), places)) * share
-
-            @pl.when(first < count)
-            def _():
+            todo.append((out, lax.bitwise_xor(owner, spread(q, lax.bitwise_and(owner, 1), places)) * share))
+
+        @pl.when(jnp.minimum(todo[0][1], todo[1][1]) < count)
+        def _():
+            for out, first in todo:
                 for s in range(share):
                     f, h = slot_pair(plan_ref, matrix, first + s, capacity)
                     if matrix == 2:
@@ -216,9 +224,9 @@
                         left, right = turned_ref[f], right_ref[h]
                     out[q, s] = dot(left, right, ((1,), (0,))).astype(out.dtype)
 
-            return carry
-
-        lax.fori_loop(0, places, one_place, 0)
+        return carry
+
+    lax.fori_loop(0, places, one_place, 0)
 
 
 def input_kernel(n_outs, plan_ref, gate_rows_ref, up_rows_ref, w_ref, *refs):
@@ -278,10 +286,11 @@
 
 def update_kernel(matrix, plan_ref, keep_ref, got_ref, m1_ref, m2_ref, *refs):
     out_ref = refs[-1]
-    share = keep_ref.shape[1]
-    first = plan_ref[1] * share
-    for s in range(share):
-        g = keep_ref[0, s].astype(F32) + got_ref[0, s].astype(F32)
+    share, part = keep_ref.shape[1], out_ref.shape[1]
+    skip = pl.program_id(0) * part
+    first = plan_ref[1] * share + skip
+    for s in range(part):
+        g = keep_ref[0, skip + s].astype(F32) + got_ref[0, skip + s].astype(F32)
         first_new = 0.9 * m1_ref[0, s] + 0.1 * g
         second_new = 0.95 * m2_ref[0, s] + 0.05 * g * g
         live = first + s < plan_ref[2 + matrix]
@@ -395,7 +404,8 @@
         return keep, axis_swap(send, replicas, step)
 
     def update(matrix, keep, got, buffer):
-        block = pl.BlockSpec((1, share, size, size), lambda i: (matrix, 0, 0, 0))
+        steps = 3 if share % 3 == 0 else 1
+        block = pl.BlockSpec((1, share // steps, size, size), lambda i: (matrix, i, 0, 0))
         extra = [] if buffer is None else [buffer]
         return line(
             functools.partial(update_kernel, matrix),
@@ -407,7 +417,7 @@
             specs=[VMEM, VMEM, block, block] + [ANY] * len(extra),
             out_specs=[block],
             input_output_aliases={5: 0} if extra else {},
-            grid=(1,),
+            grid=(steps,),
         )[0]
 
     def finish(held_parts):

time: 146 us -> 145 us (level)
  Pallas kernels: 42.7 us -> 46.2 us
  starting transfers between devices: 39.5 us -> 36.2 us
    ppermute x9, starting transfers between devices: 19.9 us -> 16.2 us  [flip(): return lax.ppermute(v, 'tensor', [(a, a ^ bit) for a in range(shards)])]
    pallas_call x23, Pallas kernels: 42.7 us -> 46.2 us  [__call__(): pl.pallas_call(body, name=name, out_shape=[*outs, TOKEN], in_specs=[SMEM]...]
    ppermute x3, waiting for transfers between devices: 0.01 us -> 1.97 us  [core_swap(): return lax.ppermute(v, 'dp', [(a, a ^ 1) for a in range(replicas)])]
  transfers between devices with their start and end apart: 23 -> 23, of which waited for: 9 -> 10; matrix products, arithmetic and copies ran while one was open for 1% -> 1% of each run, Pallas kernels for 28% -> 30%
where the time goes in v9:
time: 145 us
  waiting for transfers between devices  60.1 us (41%)
  Pallas kernels  46.2 us (32%)
  starting transfers between devices  36.2 us (25%)
    pallas_call x23, Pallas kernels, __call__(): pl.pallas_call(body, name=name, out_shape=[*outs, TOKEN], in_specs=[SMEM]...  46.2 us
    ppermute x9, waiting for transfers between devices, flip(): return lax.ppermute(v, 'tensor', [(a, a ^ bit) for a in range(shards)])  33.7 us
    ppermute x6, waiting for transfers between devices, axis_swap(): return lax.ppermute(v, 'dp', pairs)  17.6 us
    ppermute x9, starting transfers between devices, flip(): return lax.ppermute(v, 'tensor', [(a, a ^ bit) for a in range(shards)])  16.2 us
    ppermute x6, starting transfers between devices, axis_swap(): return lax.ppermute(v, 'dp', pairs)  9.97 us
    ppermute x1, waiting for transfers between devices, scatter_first(): lax.ppermute(parts[3], 'tensor', [(0, 1), (3, 2)])  6.88 us
    ppermute x1, starting transfers between devices, gather_line(): below = lax.ppermute(v, 'tensor', [(a, a + 1) for a in range(3)])  4.58 us
  transfers between devices with their start and end apart: 23, of which 10 were waited for; matrix products, arithmetic and copies ran while one was open for 1% of the time, Pallas kernels for 30%

profile of v9, /device:TPU:0, one launch (start us, length us, event | category | flops | bytes accessed | tf_op | source)
XLA Modules:
  0.0 145.1 jit_solution(4954622709902984427)
XLA Ops:
  0.6 4.1 %collective-permute-start.1 = (bf16[128,2048]{1,0:T(8,128)(2,1)}, bf16[128,2048]{1,0:T(8,128)(2,1)S(1)}, u32[]{:S(2)}, u32[]{:S(2)}) collective-permute-start(bf16[128,2048]{1,0:T(8,128)(2,1)} %refs_1_.3), channel_id=1, source_target_pairs={{0,2},{1,3},{2,0},{3,1},{4,6},{5,7},{6,4},{7,5},{8,10},{9,11},{10,... | collective-permute-start | bytes 1572872 | tf_op jit(solution)/shard_map/ppermute | solution.py:333
  4.7 1.6 %collective-permute-start = (bf16[128,2048]{1,0:T(8,128)(2,1)}, bf16[128,2048]{1,0:T(8,128)(2,1)S(1)}, u32[]{:S(2)}, u32[]{:S(2)}) collective-permute-start(bf16[128,2048]{1,0:T(8,128)(2,1)} %refs_1_.3), channel_id=1, source_target_pairs={{0,1},{1,0},{2,3},{3,2},{4,5},{5,4},{6,7},{7,6},{8,9},{9,8},{10,11... | collective-permute-start | bytes 1572872 | tf_op jit(solution)/shard_map/ppermute | solution.py:333
  8.0 5.7 %order.1 = (s32[194]{0:T(256)S(1)}, f32[8,128]{1,0:T(8,128)S(1)}) custom-call(s32[581]{0:T(1024)S(1)} %pad_add_fusion.refs_0_), custom_call_target="tpu_custom_call" | custom-call | flops 20000000000 | tf_op jit(solution)/shard_map/order/pallas_call | solution.py:318
  13.7 14.5 %collective-permute-done.1.refs_1_.refs_3_ = bf16[128,2048]{1,0:T(8,128)(2,1)S(1)} collective-permute-done((bf16[128,2048]{1,0:T(8,128)(2,1)}, bf16[128,2048]{1,0:T(8,128)(2,1)S(1)}, u32[]{:S(2)}, u32[]{:S(2)}) %collective-permute-start.1) | collective-permute-done | bytes 524320 | tf_op jit(solution)/shard_map/ppermute | solution.py:333
  29.0 3.3 %collective-permute-start.9 = (bf16[128,2048]{1,0:T(8,128)(2,1)S(1)}, bf16[128,2048]{1,0:T(8,128)(2,1)S(1)}, u32[]{:S(2)}, u32[]{:S(2)}) collective-permute-start(bf16[128,2048]{1,0:T(8,128)(2,1)S(1)} %get-tuple-element.80.refs_1_), channel_id=1, source_target_pairs={{0,2},{1,3},{2,0},{3,1},{4,6},{5,7},{6,4},{7,5},{8,10},{9,11},{10,... | collective-permute-start | bytes 1572872 | tf_op jit(solution)/shard_map/ppermute | solution.py:333
  33.6 4.6 %collective-permute-start.7 = (bf16[128,2048]{1,0:T(8,128)(2,1)S(1)}, bf16[128,2048]{1,0:T(8,128)(2,1)S(1)}, u32[]{:S(2)}, u32[]{:S(2)}) collective-permute-start(bf16[128,2048]{1,0:T(8,128)(2,1)S(1)} %get-tuple-element.80.refs_1_), channel_id=1, source_target_pairs={{0,1},{1,2},{2,3},{4,5},{5,6},{6,7},{8,9},{9,10},{10,11},{12,13},{... | collective-permute-start | bytes 1572872 | tf_op jit(solution)/shard_map/ppermute | solution.py:343
  38.2 15.5 %collective-permute-done.2.refs_4_ = bf16[128,2048]{1,0:T(8,128)(2,1)S(1)} collective-permute-done((bf16[128,2048]{1,0:T(8,128)(2,1)S(1)}, bf16[128,2048]{1,0:T(8,128)(2,1)S(1)}, u32[]{:S(2)}, u32[]{:S(2)}) %collective-permute-start.2) | collective-permute-done | bytes 524320 | tf_op jit(solution)/shard_map/ppermute | solution.py:333
  53.7 8.1 %forward.1 = (bf16[14,128,128]{2,1,0:T(8,128)(2,1)}, bf16[14,128,128]{2,1,0:T(8,128)(2,1)S(1)}, f32[14,128,128]{2,1,0:T(8,128)S(1)}, f32[14,128,128]{2,1,0:T(8,1...) custom-call(s32[581]{0:T(1024)S(1)} %pad_add_fusion.refs_0_, ...), custom_call_target="tpu_custom_call" | custom-call | flops 20000000000 | tf_op jit(solution)/shard_map/forward/pallas_call | solution.py:318
  63.1 1.5 %collective-permute-start.6 = (bf16[128,2048]{1,0:T(8,128)(2,1)}, bf16[128,2048]{1,0:T(8,128)(2,1)}, u32[]{:S(2)}, u32[]{:S(2)}) collective-permute-start(bf16[128,2048]{1,0:T(8,128)(2,1)} %get-tuple-element.79), channel_id=1, source_target_pairs={{1,2},{2,1},{5,6},{6,5},{9,10},{10,9},{13,14},{14,13},{17,18},{18,... | collective-permute-start | bytes 1572872 | tf_op jit(solution)/shard_map/ppermute | solution.py:350
  67.2 6.9 %collective-permute-done.3.refs_1_ = bf16[128,2048]{1,0:T(8,128)(2,1)S(1)} collective-permute-done((bf16[128,2048]{1,0:T(8,128)(2,1)S(1)}, bf16[128,2048]{1,0:T(8,128)(2,1)S(1)}, u32[]{:S(2)}, u32[]{:S(2)}) %collective-permute-start.3) | collective-permute-done | bytes 524320 | tf_op jit(solution)/shard_map/ppermute | solution.py:350
  74.1 4.1 %collective-permute-start.4 = (bf16[128,2048]{1,0:T(8,128)(2,1)S(1)}, bf16[128,2048]{1,0:T(8,128)(2,1)S(1)}, u32[]{:S(2)}, u32[]{:S(2)}) collective-permute-start(bf16[128,2048]{1,0:T(8,128)(2,1)S(1)} %get-tuple-element.77), channel_id=1, source_target_pairs={{0,2},{1,3},{2,0},{3,1},{4,6},{5,7},{6,4},{7,5},{8,10},{9,11},{10,... | collective-permute-start | bytes 1572872 | tf_op jit(solution)/shard_map/ppermute | solution.py:333
  78.3 2.4 %down_grads.1 = (bf16[4,12,128,128]{3,2,1,0:T(8,128)(2,1)S(1)}, bf16[4,12,128,128]{3,2,1,0:T(8,128)(2,1)S(1)}, f32[8,128]{1,0:T(8,128)S(1)}) custom-call(s32[581]{0:T(1024)S(1)} %pad_add_fusion.refs_0_, bf16[128,2048]{1,0:T(8,128)(2,1)S(1)} %get-tuple-element.80.refs_1_, bf16[128,2048]{1,0:T(8,128)(2,1)S(1)} %collective-permute-done.7.refs_2_, ...), custom_call_target="tpu_custom_call" | custom-call | flops 20000000000 | tf_op jit(solution)/shard_map/down_grads/pallas_call | solution.py:318
  80.7 3.9 %row_grads.1 = (bf16[14,128,128]{2,1,0:T(8,128)(2,1)S(1)}, bf16[14,128,128]{2,1,0:T(8,128)(2,1)S(1)}, f32[8,128]{1,0:T(8,128)S(1)}) custom-call(s32[581]{0:T(1024)S(1)} %pad_add_fusion.refs_0_, bf16[128,2048]{1,0:T(8,128)(2,1)S(1)} %get-tuple-element.80.refs_1_, bf16[128,2048]{1,0:T(8,128)(2,1)S(1)} %collective-permute-done.7.refs_2_, ...), custom_call_target="tpu_custom_call" | custom-call | flops 20000000000 | tf_op jit(solution)/shard_map/row_grads/pallas_call | solution.py:318
  85.0 3.0 %input_far.1 = (bf16[128,2048]{1,0:T(8,128)(2,1)S(1)}, f32[8,128]{1,0:T(8,128)S(1)}) custom-call(s32[581]{0:T(1024)S(1)} %pad_add_fusion.refs_0_, s32[194]{0:T(256)S(1)} %get-tuple-element.93.refs_1_, bf16[14,128,128]{2,1,0:T(8,128)(2,1)S(1)} %get-tuple-element.91.refs_2_.refs_1_, bf16[14,128,128]{2,1,0:T(8,128)(2,1)S(1)} %get-tuple-element.94.refs_3_.refs_1_, ...), custom_call_target="tpu_custom_call" | custom-call | flops 20000000000 | tf_op jit(solution)/shard_map/input_far/pallas_call | solution.py:318
  89.1 1.5 %collective-permute-start.12 = (bf16[2,12,128,128]{3,2,1,0:T(8,128)(2,1)S(1)}, bf16[2,12,128,128]{3,2,1,0:T(8,128)(2,1)S(1)}, u32[]{:S(2)}, u32[]{:S(2)}) collective-permute-start(bf16[2,12,128,128]{3,2,1,0:T(8,128)(2,1)S(1)} %get-tuple-element.90), channel_id=1, source_target_pairs={{0,16},{4,12},{8,24},{12,4},{16,0},{20,28},{24,8},{28,20},{1,17},{... | collective-permute-start | bytes 2359304 | tf_op jit(solution)/shard_map/ppermute | solution.py:367
  90.6 5.5 %input_rest.1 = (bf16[128,2048]{1,0:T(8,128)(2,1)S(1)}, bf16[128,2048]{1,0:T(8,128)(2,1)S(1)}, bf16[128,2048]{1,0:T(8,128)(2,1)S(1)}, f32[8,128]{1,0:T(8,128)S(1)}) custom-call(s32[581]{0:T(1024)S(1)} %pad_add_fusion.refs_0_, s32[194]{0:T(256)S(1)} %get-tuple-element.93.refs_1_, bf16[14,128,128]{2,1,0:T(8,128)(2,1)S(1)} %get-tuple-element.91.refs_2_.refs_1_, ...), custom_call_target="tpu_custom_call" | custom-call | flops 20000000000 | tf_op jit(solution)/shard_map/input_rest/pallas_call | solution.py:318
  96.2 2.2 %gate_grads.1 = (bf16[4,12,128,128]{3,2,1,0:T(8,128)(2,1)S(1)}, bf16[4,12,128,128]{3,2,1,0:T(8,128)(2,1)S(1)}, f32[8,128]{1,0:T(8,128)S(1)}) custom-call(s32[581]{0:T(1024)S(1)} %pad_add_fusion.refs_0_, bf16[14,128,128]{2,1,0:T(8,128)(2,1)S(1)} %get-tuple-element.91.refs_2_.refs_1_, bf16[64,128,128]{2,1,0:T(8,128)(2,1)S(1)} %get-tuple-element.92.refs_2_, ...), custom_call_target="tpu_custom_call" | custom-call | flops 20000000000 | tf_op jit(solution)/shard_map/gate_grads/pallas_call | solution.py:318
  98.3 2.8 %collective-permute-done.12.refs_1_ = bf16[2,12,128,128]{3,2,1,0:T(8,128)(2,1)S(1)} collective-permute-done((bf16[2,12,128,128]{3,2,1,0:T(8,128)(2,1)S(1)}, bf16[2,12,128,128]{3,2,1,0:T(8,128)(2,1)S(1)}, u32[]{:S(2)}, u32[]{:S(2)}) %collective-permute-start.12) | collective-permute-done | bytes 786464 | tf_op jit(solution)/shard_map/ppermute | solution.py:367
  101.3 1.6 %collective-permute-start.14 = (bf16[1,12,128,128]{3,2,1,0:T(8,128)(2,1)S(1)}, bf16[1,12,128,128]{3,2,1,0:T(8,128)(2,1)S(1)}, u32[]{:S(2)}, u32[]{:S(2)}) collective-permute-start(bf16[1,12,128,128]{3,2,1,0:T(8,128)(2,1)S(1)} %get-tuple-element.106), channel_id=1, source_target_pairs={{0,8},{4,20},{8,0},{12,28},{16,24},{20,4},{24,16},{28,12},{1,9},{5... | collective-permute-start | bytes 1179656 | tf_op jit(solution)/shard_map/ppermute | solution.py:367
  104.0 2.1 %finish.2 = (bf16[128,2048]{1,0:T(8,128)(2,1)}, f32[8,128]{1,0:T(8,128)S(1)}) custom-call(bf16[128,2048]{1,0:T(8,128)(2,1)S(1)} %get-tuple-element.71.refs_0_, bf16[128,2048]{1,0:T(8,128)(2,1)S(1)} %collective-permute-done.4.refs_1_, bf16[128,2048]{1,0:T(8,128)(2,1)S(1)} %collective-permute-done.5.refs_2_, bf16[128,2048]{1,0:T(8,128)(2,1)} %collective-permute-done.6.refs_3_, ...), custom_call_target="tpu_custom_call" | custom-call | flops 20000000000 | tf_op jit(solution)/shard_map/finish/pallas_call | solution.py:318
  106.5 1.6 %collective-permute-start.18 = (bf16[2,12,128,128]{3,2,1,0:T(8,128)(2,1)S(1)}, bf16[2,12,128,128]{3,2,1,0:T(8,128)(2,1)S(1)}, u32[]{:S(2)}, u32[]{:S(2)}) collective-permute-start(bf16[2,12,128,128]{3,2,1,0:T(8,128)(2,1)S(1)} %get-tuple-element.116), channel_id=1, source_target_pairs={{0,16},{4,12},{8,24},{12,4},{16,0},{20,28},{24,8},{28,20},{1,17},{... | collective-permute-start | bytes 2359304 | tf_op jit(solution)/shard_map/ppermute | solution.py:367
  108.1 1.8 %collective-permute-done.14.refs_2_ = bf16[1,12,128,128]{3,2,1,0:T(8,128)(2,1)S(1)} collective-permute-done((bf16[1,12,128,128]{3,2,1,0:T(8,128)(2,1)S(1)}, bf16[1,12,128,128]{3,2,1,0:T(8,128)(2,1)S(1)}, u32[]{:S(2)}, u32[]{:S(2)}) %collective-permute-start.14) | collective-permute-done | bytes 393248 | tf_op jit(solution)/shard_map/ppermute | solution.py:367
  110.0 2.4 %update.3 = (f32[3,12,128,128]{3,2,1,0:T(8,128)}, f32[8,128]{1,0:T(8,128)S(1)}) custom-call(s32[581]{0:T(1024)S(1)} %pad_add_fusion.refs_0_, bf16[1,12,128,128]{3,2,1,0:T(8,128)(2,1)S(1)} %get-tuple-element.105.refs_1_, bf16[1,12,128,128]{3,2,1,0:T(8,128)(2,1)S(1)} %collective-permute-done.14.refs_2_, f32[3,12,128,128]{3,2,1,0:T(8,128)S(1)} %copy-done, ...), custom_call_target="tpu_custom_call" | custom-call | flops 20000000000 | tf_op jit(solution)/shard_map/update/pallas_call | solution.py:318
  112.3 2.2 %up_grads.1 = (bf16[4,12,128,128]{3,2,1,0:T(8,128)(2,1)S(1)}, bf16[4,12,128,128]{3,2,1,0:T(8,128)(2,1)S(1)}, f32[8,128]{1,0:T(8,128)S(1)}) custom-call(s32[581]{0:T(1024)S(1)} %pad_add_fusion.refs_0_, bf16[14,128,128]{2,1,0:T(8,128)(2,1)S(1)} %get-tuple-element.94.refs_3_.refs_1_, bf16[64,128,128]{2,1,0:T(8,128)(2,1)S(1)} %get-tuple-element.92.refs_2_, ...), custom_call_target="tpu_custom_call" | custom-call | flops 20000000000 | tf_op jit(solution)/shard_map/up_grads/pallas_call | solution.py:318
  116.0 2.0 %collective-permute-done.19.refs_1_ = bf16[4,12,128,128]{3,2,1,0:T(8,128)(2,1)S(1)} collective-permute-done((bf16[4,12,128,128]{3,2,1,0:T(8,128)(2,1)S(1)}, bf16[4,12,128,128]{3,2,1,0:T(8,128)(2,1)S(1)}, u32[]{:S(2)}, u32[]{:S(2)}) %collective-permute-start.19) | collective-permute-done | bytes 1572896 | tf_op jit(solution)/shard_map/ppermute | solution.py:361
  118.3 2.2 %collective-permute-start.21 = (bf16[2,12,128,128]{3,2,1,0:T(8,128)(2,1)S(1)}, bf16[2,12,128,128]{3,2,1,0:T(8,128)(2,1)S(1)}, u32[]{:S(2)}, u32[]{:S(2)}) collective-permute-start(bf16[2,12,128,128]{3,2,1,0:T(8,128)(2,1)S(1)} %get-tuple-element.125), channel_id=1, source_target_pairs={{0,16},{4,12},{8,24},{12,4},{16,0},{20,28},{24,8},{28,20},{1,17},{... | collective-permute-start | bytes 2359304 | tf_op jit(solution)/shard_map/ppermute | solution.py:367
  120.7 1.6 %collective-permute-start.20 = (bf16[1,12,128,128]{3,2,1,0:T(8,128)(2,1)S(1)}, bf16[1,12,128,128]{3,2,1,0:T(8,128)(2,1)S(1)}, u32[]{:S(2)}, u32[]{:S(2)}) collective-permute-start(bf16[1,12,128,128]{3,2,1,0:T(8,128)(2,1)S(1)} %get-tuple-element.122), channel_id=1, source_target_pairs={{0,8},{4,20},{8,0},{12,28},{16,24},{20,4},{24,16},{28,12},{1,9},{5... | collective-permute-start | bytes 1179656 | tf_op jit(solution)/shard_map/ppermute | solution.py:367
  122.2 12.4 %collective-permute-done.21.refs_1_ = bf16[2,12,128,128]{3,2,1,0:T(8,128)(2,1)S(1)} collective-permute-done((bf16[2,12,128,128]{3,2,1,0:T(8,128)(2,1)S(1)}, bf16[2,12,128,128]{3,2,1,0:T(8,128)(2,1)S(1)}, u32[]{:S(2)}, u32[]{:S(2)}) %collective-permute-start.21) | collective-permute-done | bytes 786464 | tf_op jit(solution)/shard_map/ppermute | solution.py:367
  134.9 1.5 %collective-permute-start.22 = (bf16[1,12,128,128]{3,2,1,0:T(8,128)(2,1)S(1)}, bf16[1,12,128,128]{3,2,1,0:T(8,128)(2,1)S(1)}, u32[]{:S(2)}, u32[]{:S(2)}) collective-permute-start(bf16[1,12,128,128]{3,2,1,0:T(8,128)(2,1)S(1)} %get-tuple-element.131), channel_id=1, source_target_pairs={{0,8},{4,20},{8,0},{12,28},{16,24},{20,4},{24,16},{28,12},{1,9},{5... | collective-permute-start | bytes 1179656 | tf_op jit(solution)/shard_map/ppermute | solution.py:367
  136.4 2.4 %update.4 = (f32[3,12,128,128]{3,2,1,0:T(8,128)}, f32[8,128]{1,0:T(8,128)S(1)}) custom-call(s32[581]{0:T(1024)S(1)} %pad_add_fusion.refs_0_, bf16[1,12,128,128]{3,2,1,0:T(8,128)(2,1)S(1)} %get-tuple-element.121.refs_1_, bf16[1,12,128,128]{3,2,1,0:T(8,128)(2,1)S(1)} %collective-permute-done.20.refs_2_, ...), custom_call_target="tpu_custom_call", output_to_operand_aliasing={{0}: (5, {})} | custom-call | flops 20000000000 | tf_op jit(solution)/shard_map/update/pallas_call | solution.py:318
  138.7 2.5 %collective-permute-done.16.refs_1_ = bf16[128,2048]{1,0:T(8,128)(2,1)S(1)} collective-permute-done((bf16[128,2048]{1,0:T(8,128)(2,1)S(1)}, bf16[128,2048]{1,0:T(8,128)(2,1)S(1)}, u32[]{:S(2)}, u32[]{:S(2)}) %collective-permute-start.16) | collective-permute-done | bytes 524320 | tf_op jit(solution)/shard_map/ppermute | solution.py:333
  142.7 2.4 %update.5 = (f32[3,12,128,128]{3,2,1,0:T(8,128)}, f32[8,128]{1,0:T(8,128)}) custom-call(s32[581]{0:T(1024)S(1)} %pad_add_fusion.refs_0_, bf16[1,12,128,128]{3,2,1,0:T(8,128)(2,1)S(1)} %get-tuple-element.130.refs_1_, bf16[1,12,128,128]{3,2,1,0:T(8,128)(2,1)S(1)} %collective-permute-done.22.refs_2_, ...), custom_call_target="tpu_custom_call", output_to_operand_aliasing={{0}: (5, {})} | custom-call | flops 20000000000 | tf_op jit(solution)/shard_map/update/pallas_call | solution.py:318
  (55 shorter events, 14.6 us)
Async XLA Ops:
  0.6 27.6 %collective-permute-start.1 = (bf16[128,2048]{1,0:T(8,128)(2,1)}, bf16[128,2048]{1,0:T(8,128)(2,1)S(1)}, u32[]{:S(2)}, u32[]{:S(2)}) collective-permute-start(bf16[128,2048]{1,0:T(8,128)(2,1)} %refs_1_.3), channel_id=1, source_target_pairs={{0,2},{1,3},{2,0},{3,1},{4,6},{5,7},{6,4},{7,5},{8,10},{9,11},{10,... | collective-permute-start | bytes 1572872 | tf_op jit(solution)/shard_map/ppermute | solution.py:333
  4.7 33.5 %collective-permute-start = (bf16[128,2048]{1,0:T(8,128)(2,1)}, bf16[128,2048]{1,0:T(8,128)(2,1)S(1)}, u32[]{:S(2)}, u32[]{:S(2)}) collective-permute-start(bf16[128,2048]{1,0:T(8,128)(2,1)} %refs_1_.3), channel_id=1, source_target_pairs={{0,1},{1,0},{2,3},{3,2},{4,5},{5,4},{6,7},{7,6},{8,9},{9,8},{10,11... | collective-permute-start | bytes 1572872 | tf_op jit(solution)/shard_map/ppermute | solution.py:333
  8.0 20.9 %copy-start.2 = (bf16[128,2048]{1,0:T(8,128)(2,1)S(1)}, bf16[128,2048]{1,0:T(8,128)(2,1)}, u32[]{:S(2)}) copy-start(bf16[128,2048]{1,0:T(8,128)(2,1)} %refs_0_.1) | copy-start | bytes 1572868
  8.0 45.7 %slice-start = ((s8[9437184]{0:T(1024)(128)(4,1)}), s8[4194304]{0:T(1024)(128)(4,1)S(1)}, s32[]{:S(2)}) async-start(s8[9437184]{0:T(1024)(128)(4,1)} %bitcast.3), calls=%async_computation | async-start | bytes 8388608
  8.0 45.7 %slice-start.1 = ((s8[9437184]{0:T(1024)(128)(4,1)}), s8[4194304]{0:T(1024)(128)(4,1)S(1)}, s32[]{:S(2)}) async-start(s8[9437184]{0:T(1024)(128)(4,1)} %bitcast.3), calls=%async_computation.1 | async-start | bytes 8388608
  28.2 25.5 %collective-permute-start.2 = (bf16[128,2048]{1,0:T(8,128)(2,1)S(1)}, bf16[128,2048]{1,0:T(8,128)(2,1)S(1)}, u32[]{:S(2)}, u32[]{:S(2)}) collective-permute-start(bf16[128,2048]{1,0:T(8,128)(2,1)S(1)} %collective-permute-done.1.refs_1_.refs_3_), channel_id=1, source_target_pairs={{0,1},{1,0},{2,3},{3,2},{4,5},{5,4},{6,7},{7,6},{8,9},{9,8},{10,11... | collective-permute-start | bytes 1572872 | tf_op jit(solution)/shard_map/ppermute | solution.py:333
  28.9 24.7 %slice-start.2 = ((s8[9437184]{0:T(1024)(128)(4,1)}), s8[1048576]{0:T(1024)(128)(4,1)S(1)}, s32[]{:S(2)}) async-start(s8[9437184]{0:T(1024)(128)(4,1)} %bitcast.3), calls=%async_computation.2 | async-start | bytes 2097152
  28.9 24.7 %copy-start.3 = (bf16[128,2048]{1,0:T(8,128)(2,1)S(1)}, bf16[128,2048]{1,0:T(8,128)(2,1)}, u32[]{:S(2)}) copy-start(bf16[128,2048]{1,0:T(8,128)(2,1)} %refs_1_.3) | copy-start | bytes 1572868
  29.0 35.6 %collective-permute-start.9 = (bf16[128,2048]{1,0:T(8,128)(2,1)S(1)}, bf16[128,2048]{1,0:T(8,128)(2,1)S(1)}, u32[]{:S(2)}, u32[]{:S(2)}) collective-permute-start(bf16[128,2048]{1,0:T(8,128)(2,1)S(1)} %get-tuple-element.80.refs_1_), channel_id=1, source_target_pairs={{0,2},{1,3},{2,0},{3,1},{4,6},{5,7},{6,4},{7,5},{8,10},{9,11},{10,... | collective-permute-start | bytes 1572872 | tf_op jit(solution)/shard_map/ppermute | solution.py:333
  32.3 45.9 %collective-permute-start.8 = (bf16[128,2048]{1,0:T(8,128)(2,1)S(1)}, bf16[128,2048]{1,0:T(8,128)(2,1)S(1)}, u32[]{:S(2)}, u32[]{:S(2)}) collective-permute-start(bf16[128,2048]{1,0:T(8,128)(2,1)S(1)} %get-tuple-element.80.refs_1_), channel_id=1, source_target_pairs={{1,0},{2,1},{3,2},{5,4},{6,5},{7,6},{9,8},{10,9},{11,10},{13,12},{... | collective-permute-start | bytes 1572872 | tf_op jit(solution)/shard_map/ppermute | solution.py:344
  33.6 44.6 %collective-permute-start.7 = (bf16[128,2048]{1,0:T(8,128)(2,1)S(1)}, bf16[128,2048]{1,0:T(8,128)(2,1)S(1)}, u32[]{:S(2)}, u32[]{:S(2)}) collective-permute-start(bf16[128,2048]{1,0:T(8,128)(2,1)S(1)} %get-tuple-element.80.refs_1_), channel_id=1, source_target_pairs={{0,1},{1,2},{2,3},{4,5},{5,6},{6,7},{8,9},{9,10},{10,11},{12,13},{... | collective-permute-start | bytes 1572872 | tf_op jit(solution)/shard_map/ppermute | solution.py:343
  61.8 12.3 %collective-permute-start.3 = (bf16[128,2048]{1,0:T(8,128)(2,1)S(1)}, bf16[128,2048]{1,0:T(8,128)(2,1)S(1)}, u32[]{:S(2)}, u32[]{:S(2)}) collective-permute-start(bf16[128,2048]{1,0:T(8,128)(2,1)S(1)} %get-tuple-element.73), channel_id=1, source_target_pairs={{0,1},{3,2},{4,5},{7,6},{8,9},{11,10},{12,13},{15,14},{16,17},{19,... | collective-permute-start | bytes 1572872 | tf_op jit(solution)/shard_map/ppermute | solution.py:350
  63.1 38.2 %collective-permute-start.6 = (bf16[128,2048]{1,0:T(8,128)(2,1)}, bf16[128,2048]{1,0:T(8,128)(2,1)}, u32[]{:S(2)}, u32[]{:S(2)}) collective-permute-start(bf16[128,2048]{1,0:T(8,128)(2,1)} %get-tuple-element.79), channel_id=1, source_target_pairs={{1,2},{2,1},{5,6},{6,5},{9,10},{10,9},{13,14},{14,13},{17,18},{18,... | collective-permute-start | bytes 1572872 | tf_op jit(solution)/shard_map/ppermute | solution.py:350
  64.6 13.7 %collective-permute-start.10 = (bf16[128,2048]{1,0:T(8,128)(2,1)S(1)}, bf16[128,2048]{1,0:T(8,128)(2,1)S(1)}, u32[]{:S(2)}, u32[]{:S(2)}) collective-permute-start(bf16[128,2048]{1,0:T(8,128)(2,1)S(1)} %collective-permute-done.9.refs_4_), channel_id=1, source_target_pairs={{2,3},{1,0},{6,7},{5,4},{10,11},{9,8},{14,15},{13,12},{18,19},{17,... | collective-permute-start | bytes 1572872 | tf_op jit(solution)/shard_map/ppermute | solution.py:345
  74.1 28.7 %collective-permute-start.4 = (bf16[128,2048]{1,0:T(8,128)(2,1)S(1)}, bf16[128,2048]{1,0:T(8,128)(2,1)S(1)}, u32[]{:S(2)}, u32[]{:S(2)}) collective-permute-start(bf16[128,2048]{1,0:T(8,128)(2,1)S(1)} %get-tuple-element.77), channel_id=1, source_target_pairs={{0,2},{1,3},{2,0},{3,1},{4,6},{5,7},{6,4},{7,5},{8,10},{9,11},{10,... | collective-permute-start | bytes 1572872 | tf_op jit(solution)/shard_map/ppermute | solution.py:333
  78.2 25.8 %collective-permute-start.5 = (bf16[128,2048]{1,0:T(8,128)(2,1)S(1)}, bf16[128,2048]{1,0:T(8,128)(2,1)S(1)}, u32[]{:S(2)}, u32[]{:S(2)}) collective-permute-start(bf16[128,2048]{1,0:T(8,128)(2,1)S(1)} %get-tuple-element.78), channel_id=1, source_target_pairs={{0,1},{1,0},{2,3},{3,2},{4,5},{5,4},{6,7},{7,6},{8,9},{9,8},{10,11... | collective-permute-start | bytes 1572872 | tf_op jit(solution)/shard_map/ppermute | solution.py:333
  80.7 4.0 %collective-permute-start.11 = (bf16[4,12,128,128]{3,2,1,0:T(8,128)(2,1)S(1)}, bf16[4,12,128,128]{3,2,1,0:T(8,128)(2,1)S(1)}, u32[]{:S(2)}, u32[]{:S(2)}) collective-permute-start(bf16[4,12,128,128]{3,2,1,0:T(8,128)(2,1)S(1)} %get-tuple-element.84), channel_id=1, source_target_pairs={{0,4},{4,0},{8,12},{12,8},{16,20},{20,16},{24,28},{28,24},{1,5},{5... | collective-permute-start | bytes 4718600 | tf_op jit(solution)/shard_map/ppermute | solution.py:361
  88.0 26.6 %collective-permute-start.13 = (bf16[128,2048]{1,0:T(8,128)(2,1)S(1)}, bf16[128,2048]{1,0:T(8,128)(2,1)S(1)}, u32[]{:S(2)}, u32[]{:S(2)}) collective-permute-start(bf16[128,2048]{1,0:T(8,128)(2,1)S(1)} %get-tuple-element.103), channel_id=1, source_target_pairs={{0,1},{1,0},{2,3},{3,2},{4,5},{5,4},{6,7},{7,6},{8,9},{9,8},{10,11... | collective-permute-start | bytes 1572872 | tf_op jit(solution)/shard_map/ppermute | solution.py:333
  89.1 12.0 %collective-permute-start.12 = (bf16[2,12,128,128]{3,2,1,0:T(8,128)(2,1)S(1)}, bf16[2,12,128,128]{3,2,1,0:T(8,128)(2,1)S(1)}, u32[]{:S(2)}, u32[]{:S(2)}) collective-permute-start(bf16[2,12,128,128]{3,2,1,0:T(8,128)(2,1)S(1)} %get-tuple-element.90), channel_id=1, source_target_pairs={{0,16},{4,12},{8,24},{12,4},{16,0},{20,28},{24,8},{28,20},{1,17},{... | collective-permute-start | bytes 2359304 | tf_op jit(solution)/shard_map/ppermute | solution.py:367
  101.1 5.1 %collective-permute-start.15 = (bf16[4,12,128,128]{3,2,1,0:T(8,128)(2,1)S(1)}, bf16[4,12,128,128]{3,2,1,0:T(8,128)(2,1)S(1)}, u32[]{:S(2)}, u32[]{:S(2)}) collective-permute-start(bf16[4,12,128,128]{3,2,1,0:T(8,128)(2,1)S(1)} %get-tuple-element.108), channel_id=1, source_target_pairs={{0,4},{4,0},{8,12},{12,8},{16,20},{20,16},{24,28},{28,24},{1,5},{5... | collective-permute-start | bytes 4718600 | tf_op jit(solution)/shard_map/ppermute | solution.py:361
  101.3 8.7 %collective-permute-start.14 = (bf16[1,12,128,128]{3,2,1,0:T(8,128)(2,1)S(1)}, bf16[1,12,128,128]{3,2,1,0:T(8,128)(2,1)S(1)}, u32[]{:S(2)}, u32[]{:S(2)}) collective-permute-start(bf16[1,12,128,128]{3,2,1,0:T(8,128)(2,1)S(1)} %get-tuple-element.106), channel_id=1, source_target_pairs={{0,8},{4,20},{8,0},{12,28},{16,24},{20,4},{24,16},{28,12},{1,9},{5... | collective-permute-start | bytes 1179656 | tf_op jit(solution)/shard_map/ppermute | solution.py:367
  106.1 3.8 %copy-start = (f32[3,12,128,128]{3,2,1,0:T(8,128)S(1)}, f32[3,12,128,128]{3,2,1,0:T(8,128)}, u32[]{:S(2)}) copy-start(f32[3,12,128,128]{3,2,1,0:T(8,128)} %refs_3_.5) | copy-start | bytes 7077892
  106.1 3.8 %copy-start.1 = (f32[3,12,128,128]{3,2,1,0:T(8,128)S(1)}, f32[3,12,128,128]{3,2,1,0:T(8,128)}, u32[]{:S(2)}) copy-start(f32[3,12,128,128]{3,2,1,0:T(8,128)} %refs_4_.9) | copy-start | bytes 7077892
  106.5 14.0 %collective-permute-start.18 = (bf16[2,12,128,128]{3,2,1,0:T(8,128)(2,1)S(1)}, bf16[2,12,128,128]{3,2,1,0:T(8,128)(2,1)S(1)}, u32[]{:S(2)}, u32[]{:S(2)}) collective-permute-start(bf16[2,12,128,128]{3,2,1,0:T(8,128)(2,1)S(1)} %get-tuple-element.116), channel_id=1, source_target_pairs={{0,16},{4,12},{8,24},{12,4},{16,0},{20,28},{24,8},{28,20},{1,17},{... | collective-permute-start | bytes 2359304 | tf_op jit(solution)/shard_map/ppermute | solution.py:367
  114.5 3.5 %collective-permute-start.19 = (bf16[4,12,128,128]{3,2,1,0:T(8,128)(2,1)S(1)}, bf16[4,12,128,128]{3,2,1,0:T(8,128)(2,1)S(1)}, u32[]{:S(2)}, u32[]{:S(2)}) collective-permute-start(bf16[4,12,128,128]{3,2,1,0:T(8,128)(2,1)S(1)} %get-tuple-element.118), channel_id=1, source_target_pairs={{0,4},{4,0},{8,12},{12,8},{16,20},{20,16},{24,28},{28,24},{1,5},{5... | collective-permute-start | bytes 4718600 | tf_op jit(solution)/shard_map/ppermute | solution.py:361
  114.7 26.5 %collective-permute-start.16 = (bf16[128,2048]{1,0:T(8,128)(2,1)S(1)}, bf16[128,2048]{1,0:T(8,128)(2,1)S(1)}, u32[]{:S(2)}, u32[]{:S(2)}) collective-permute-start(bf16[128,2048]{1,0:T(8,128)(2,1)S(1)} %get-tuple-element.113), channel_id=1, source_target_pairs={{0,2},{1,3},{2,0},{3,1},{4,6},{5,7},{6,4},{7,5},{8,10},{9,11},{10,... | collective-permute-start | bytes 1572872 | tf_op jit(solution)/shard_map/ppermute | solution.py:333
  115.4 25.8 %collective-permute-start.17 = (bf16[128,2048]{1,0:T(8,128)(2,1)S(1)}, bf16[128,2048]{1,0:T(8,128)(2,1)S(1)}, u32[]{:S(2)}, u32[]{:S(2)}) collective-permute-start(bf16[128,2048]{1,0:T(8,128)(2,1)S(1)} %get-tuple-element.114), channel_id=1, source_target_pairs={{0,1},{1,0},{2,3},{3,2},{4,5},{5,4},{6,7},{7,6},{8,9},{9,8},{10,11... | collective-permute-start | bytes 1572872 | tf_op jit(solution)/shard_map/ppermute | solution.py:333
  118.3 16.4 %collective-permute-start.21 = (bf16[2,12,128,128]{3,2,1,0:T(8,128)(2,1)S(1)}, bf16[2,12,128,128]{3,2,1,0:T(8,128)(2,1)S(1)}, u32[]{:S(2)}, u32[]{:S(2)}) collective-permute-start(bf16[2,12,128,128]{3,2,1,0:T(8,128)(2,1)S(1)} %get-tuple-element.125), channel_id=1, source_target_pairs={{0,16},{4,12},{8,24},{12,4},{16,0},{20,28},{24,8},{28,20},{1,17},{... | collective-permute-start | bytes 2359304 | tf_op jit(solution)/shard_map/ppermute | solution.py:367
  120.7 15.7 %collective-permute-start.20 = (bf16[1,12,128,128]{3,2,1,0:T(8,128)(2,1)S(1)}, bf16[1,12,128,128]{3,2,1,0:T(8,128)(2,1)S(1)}, u32[]{:S(2)}, u32[]{:S(2)}) collective-permute-start(bf16[1,12,128,128]{3,2,1,0:T(8,128)(2,1)S(1)} %get-tuple-element.122), channel_id=1, source_target_pairs={{0,8},{4,20},{8,0},{12,28},{16,24},{20,4},{24,16},{28,12},{1,9},{5... | collective-permute-start | bytes 1179656 | tf_op jit(solution)/shard_map/ppermute | solution.py:367
  134.9 7.8 %collective-permute-start.22 = (bf16[1,12,128,128]{3,2,1,0:T(8,128)(2,1)S(1)}, bf16[1,12,128,128]{3,2,1,0:T(8,128)(2,1)S(1)}, u32[]{:S(2)}, u32[]{:S(2)}) collective-permute-start(bf16[1,12,128,128]{3,2,1,0:T(8,128)(2,1)S(1)} %get-tuple-element.131), channel_id=1, source_target_pairs={{0,8},{4,20},{8,0},{12,28},{16,24},{20,4},{24,16},{28,12},{1,9},{5... | collective-permute-start | bytes 1179656 | tf_op jit(solution)/shard_map/ppermute | solution.py:367

commit v10 on v9

--- a/solution.py
+++ b/solution.py
@@ -286,11 +286,10 @@
 
 def update_kernel(matrix, plan_ref, keep_ref, got_ref, m1_ref, m2_ref, *refs):
     out_ref = refs[-1]
-    share, part = keep_ref.shape[1], out_ref.shape[1]
-    skip = pl.program_id(0) * part
-    first = plan_ref[1] * share + skip
-    for s in range(part):
-        g = keep_ref[0, skip + s].astype(F32) + got_ref[0, skip + s].astype(F32)
+    share = keep_ref.shape[1]
+    first = plan_ref[1] * share
+    for s in range(share):
+        g = keep_ref[0, s].astype(F32) + got_ref[0, s].astype(F32)
         first_new = 0.9 * m1_ref[0, s] + 0.1 * g
         second_new = 0.95 * m2_ref[0, s] + 0.05 * g * g
         live = first + s < plan_ref[2 + matrix]
@@ -350,10 +349,10 @@
     return [lax.ppermute(parts[3], "tensor", [(0, 1), (3, 2)]), lax.ppermute(parts[4], "tensor", [(1, 2), (2, 1)])]
 
 
-def scatter_second(line, parts, came):
+def scatter_second(line, parts, came, after=()):
     piece = SHAPE(parts[0].shape, parts[0].dtype)
     own, beside, across = parts[:3]
-    across, beside = line(join_kernel, "join", [piece] * 2, [], [across, came[0], beside])
+    across, beside = line(join_kernel, "join", [piece] * 2, [], [across, came[0], beside], (), after)
     return [own, flip(across, 4, 2), flip(beside, 4, 1), *came[1:]]
 
 
@@ -398,14 +397,13 @@
         keep, send = line(kernel, name, [half, half], [held], [*right, left], plan, after)
         return keep, core_swap(send, replicas)
 
-    def fold(keep, got, step):
+    def fold(keep, got, step, after=()):
         half = SHAPE((keep.shape[0] // 2, *keep.shape[1:]), BF16)
-        keep, send = line(fold_kernel, "fold", [half, half], [], [keep, got])
+        keep, send = line(fold_kernel, "fold", [half, half], [], [keep, got], (), after)
         return keep, axis_swap(send, replicas, step)
 
     def update(matrix, keep, got, buffer):
-        steps = 3 if share % 3 == 0 else 1
-        block = pl.BlockSpec((1, share // steps, size, size), lambda i: (matrix, i, 0, 0))
+        block = pl.BlockSpec((1, share, size, size), lambda i: (matrix, 0, 0, 0))
         extra = [] if buffer is None else [buffer]
         return line(
             functools.partial(update_kernel, matrix),
@@ -417,11 +415,14 @@
             specs=[VMEM, VMEM, block, block] + [ANY] * len(extra),
             out_specs=[block],
             input_output_aliases={5: 0} if extra else {},
-            grid=(steps,),
+            grid=(1,),
         )[0]
 
     def finish(held_parts):
         return line(sum_kernel, "finish", [piece], [], held_parts)[0]
+
+    def touch(*arrived):
+        line(lambda: None, "touch", [], [], [], (), arrived)
 
     x = gather(inputs, gather_near)
     if lined:
@@ -448,6 +449,7 @@
     (x_turned,) = line(
         functools.partial(turn_kernel, len(x)), "turn", [SHAPE((features, size, rows), BF16)], [held], x, plan
     )
+    buffer = None
     if lined:
         out_sums = scatter_second(line, out_parts, out_far)
     down = grads(2, og, hidden_turned)
@@ -467,6 +469,7 @@
             functools.partial(input_part_kernel, True), "input_far", [piece], [part_total], in_operands, (*plan, order)
         )
         in_far = flip(in_far, 4, 1)
+    gate = grads(0, [gate_rows], x_turned, out_far[1:] if lined else ())
     if lined:
         in_parts = line(
             functools.partial(input_part_kernel, False), "input_rest", [piece] * 3, [total], in_operands, (*plan, order)
@@ -476,13 +479,12 @@
             functools.partial(input_kernel, 1), "input_grads", in_parts, [total], [gate_rows, up_rows, weights], plan
         )
         input_grad = lax.psum_scatter(in_parts[0], "tensor", scatter_dimension=0)
-    gate = grads(0, [gate_rows], x_turned)
     for step in range(1, levels):
         down = fold(*down, step)
     if lined:
         outputs = finish(out_sums)
     gate = fold(*gate, 0)
-    buffer = update(2, *down, None)
+    buffer = update(2, *down, buffer)
     up = grads(1, [up_rows], x_turned)
     if lined:
         in_sums = scatter_second(line, in_parts, [in_far])

time: 145 us -> 147 us (1.014)
  waiting for transfers between devices: 60.1 us -> 68.2 us
  Pallas kernels: 46.2 us -> 38.7 us
    pallas_call x23, Pallas kernels: 46.2 us -> 38.7 us  [__call__(): pl.pallas_call(body, name=name, out_shape=[*outs, TOKEN], in_specs=[SMEM]...]
    ppermute x6, waiting for transfers between devices: 17.6 us -> 22.8 us  [axis_swap(): return lax.ppermute(v, 'dp', pairs)]
    ppermute x1, waiting for transfers between devices: 6.88 us -> 8.81 us  [scatter_first(): lax.ppermute(parts[3], 'tensor', [(0, 1), (3, 2)])]
    ppermute x9, waiting for transfers between devices: 33.7 us -> 35.4 us  [flip(): return lax.ppermute(v, 'tensor', [(a, a ^ bit) for a in range(shards)])]
  transfers between devices with their start and end apart: 23 -> 23, of which waited for: 10 -> 10; matrix products, arithmetic and copies ran while one was open for 1% -> 1% of each run, Pallas kernels for 30% -> 25%
where the time goes in v10:
time: 147 us; the launch traced here: 146 us
  waiting for transfers between devices  68.2 us (46%)
  Pallas kernels  38.7 us (26%)
  starting transfers between devices  36.8 us (25%)
    pallas_call x23, Pallas kernels, __call__(): pl.pallas_call(body, name=name, out_shape=[*outs, TOKEN], in_specs=[SMEM]...  38.7 us
    ppermute x9, waiting for transfers between devices, flip(): return lax.ppermute(v, 'tensor', [(a, a ^ bit) for a in range(shards)])  35.4 us
    ppermute x6, waiting for transfers between devices, axis_swap(): return lax.ppermute(v, 'dp', pairs)  22.8 us
    ppermute x9, starting transfers between devices, flip(): return lax.ppermute(v, 'tensor', [(a, a ^ bit) for a in range(shards)])  17.2 us
    ppermute x6, starting transfers between devices, axis_swap(): return lax.ppermute(v, 'dp', pairs)  10.2 us
    ppermute x1, waiting for transfers between devices, scatter_first(): lax.ppermute(parts[3], 'tensor', [(0, 1), (3, 2)])  8.81 us
    ppermute x1, starting transfers between devices, gather_line(): below = lax.ppermute(v, 'tensor', [(a, a + 1) for a in range(3)])  4.58 us
  transfers between devices with their start and end apart: 23, of which 10 were waited for; matrix products, arithmetic and copies ran while one was open for 1% of the time, Pallas kernels for 25%

profile of v10, /device:TPU:0, one launch (start us, length us, event | category | flops | bytes accessed | tf_op | source)
XLA Modules:
  0.0 146.2 jit_solution(80624568453959454)
XLA Ops:
  0.6 4.1 %collective-permute-start.1 = (bf16[128,2048]{1,0:T(8,128)(2,1)}, bf16[128,2048]{1,0:T(8,128)(2,1)S(1)}, u32[]{:S(2)}, u32[]{:S(2)}) collective-permute-start(bf16[128,2048]{1,0:T(8,128)(2,1)} %refs_1_.3), channel_id=1, source_target_pairs={{0,2},{1,3},{2,0},{3,1},{4,6},{5,7},{6,4},{7,5},{8,10},{9,11},{10,... | collective-permute-start | bytes 1572872 | tf_op jit(solution)/shard_map/ppermute | solution.py:332
  4.7 1.6 %collective-permute-start = (bf16[128,2048]{1,0:T(8,128)(2,1)}, bf16[128,2048]{1,0:T(8,128)(2,1)S(1)}, u32[]{:S(2)}, u32[]{:S(2)}) collective-permute-start(bf16[128,2048]{1,0:T(8,128)(2,1)} %refs_1_.3), channel_id=1, source_target_pairs={{0,1},{1,0},{2,3},{3,2},{4,5},{5,4},{6,7},{7,6},{8,9},{9,8},{10,11... | collective-permute-start | bytes 1572872 | tf_op jit(solution)/shard_map/ppermute | solution.py:332
  8.0 4.3 %order.1 = (s32[194]{0:T(256)S(1)}, f32[8,128]{1,0:T(8,128)S(1)}) custom-call(s32[581]{0:T(1024)S(1)} %pad_add_fusion.refs_0_), custom_call_target="tpu_custom_call" | custom-call | flops 20000000000 | tf_op jit(solution)/shard_map/order/pallas_call | solution.py:317
  12.3 15.9 %collective-permute-done.1.refs_1_.refs_3_ = bf16[128,2048]{1,0:T(8,128)(2,1)S(1)} collective-permute-done((bf16[128,2048]{1,0:T(8,128)(2,1)}, bf16[128,2048]{1,0:T(8,128)(2,1)S(1)}, u32[]{:S(2)}, u32[]{:S(2)}) %collective-permute-start.1) | collective-permute-done | bytes 524320 | tf_op jit(solution)/shard_map/ppermute | solution.py:332
  29.0 3.3 %collective-permute-start.9 = (bf16[128,2048]{1,0:T(8,128)(2,1)S(1)}, bf16[128,2048]{1,0:T(8,128)(2,1)S(1)}, u32[]{:S(2)}, u32[]{:S(2)}) collective-permute-start(bf16[128,2048]{1,0:T(8,128)(2,1)S(1)} %get-tuple-element.80.refs_1_), channel_id=1, source_target_pairs={{0,2},{1,3},{2,0},{3,1},{4,6},{5,7},{6,4},{7,5},{8,10},{9,11},{10,... | collective-permute-start | bytes 1572872 | tf_op jit(solution)/shard_map/ppermute | solution.py:332
  33.6 4.6 %collective-permute-start.7 = (bf16[128,2048]{1,0:T(8,128)(2,1)S(1)}, bf16[128,2048]{1,0:T(8,128)(2,1)S(1)}, u32[]{:S(2)}, u32[]{:S(2)}) collective-permute-start(bf16[128,2048]{1,0:T(8,128)(2,1)S(1)} %get-tuple-element.80.refs_1_), channel_id=1, source_target_pairs={{0,1},{1,2},{2,3},{4,5},{5,6},{6,7},{8,9},{9,10},{10,11},{12,13},{... | collective-permute-start | bytes 1572872 | tf_op jit(solution)/shard_map/ppermute | solution.py:342
  38.2 15.5 %collective-permute-done.2.refs_4_ = bf16[128,2048]{1,0:T(8,128)(2,1)S(1)} collective-permute-done((bf16[128,2048]{1,0:T(8,128)(2,1)S(1)}, bf16[128,2048]{1,0:T(8,128)(2,1)S(1)}, u32[]{:S(2)}, u32[]{:S(2)}) %collective-permute-start.2) | collective-permute-done | bytes 524320 | tf_op jit(solution)/shard_map/ppermute | solution.py:332
  53.7 6.9 %forward.1 = (bf16[14,128,128]{2,1,0:T(8,128)(2,1)}, bf16[14,128,128]{2,1,0:T(8,128)(2,1)S(1)}, f32[14,128,128]{2,1,0:T(8,128)S(1)}, f32[14,128,128]{2,1,0:T(8,1...) custom-call(s32[581]{0:T(1024)S(1)} %pad_add_fusion.refs_0_, ...), custom_call_target="tpu_custom_call" | custom-call | flops 20000000000 | tf_op jit(solution)/shard_map/forward/pallas_call | solution.py:317
  60.6 1.3 collective-permute-start.3
  63.9 1.3 turn.1
  65.2 8.8 %collective-permute-done.3.refs_1_ = bf16[128,2048]{1,0:T(8,128)(2,1)S(1)} collective-permute-done((bf16[128,2048]{1,0:T(8,128)(2,1)S(1)}, bf16[128,2048]{1,0:T(8,128)(2,1)S(1)}, u32[]{:S(2)}, u32[]{:S(2)}) %collective-permute-start.3) | collective-permute-done | bytes 524320 | tf_op jit(solution)/shard_map/ppermute | solution.py:349
  74.1 4.1 %collective-permute-start.4 = (bf16[128,2048]{1,0:T(8,128)(2,1)S(1)}, bf16[128,2048]{1,0:T(8,128)(2,1)S(1)}, u32[]{:S(2)}, u32[]{:S(2)}) collective-permute-start(bf16[128,2048]{1,0:T(8,128)(2,1)S(1)} %get-tuple-element.77), channel_id=1, source_target_pairs={{0,2},{1,3},{2,0},{3,1},{4,6},{5,7},{6,4},{7,5},{8,10},{9,11},{10,... | collective-permute-start | bytes 1572872 | tf_op jit(solution)/shard_map/ppermute | solution.py:332
  78.3 2.4 %down_grads.1 = (bf16[4,12,128,128]{3,2,1,0:T(8,128)(2,1)S(1)}, bf16[4,12,128,128]{3,2,1,0:T(8,128)(2,1)S(1)}, f32[8,128]{1,0:T(8,128)S(1)}) custom-call(s32[581]{0:T(1024)S(1)} %pad_add_fusion.refs_0_, bf16[128,2048]{1,0:T(8,128)(2,1)S(1)} %get-tuple-element.80.refs_1_, bf16[128,2048]{1,0:T(8,128)(2,1)S(1)} %collective-permute-done.7.refs_2_, ...), custom_call_target="tpu_custom_call" | custom-call | flops 20000000000 | tf_op jit(solution)/shard_map/down_grads/pallas_call | solution.py:317
  80.7 3.6 %row_grads.1 = (bf16[14,128,128]{2,1,0:T(8,128)(2,1)S(1)}, bf16[14,128,128]{2,1,0:T(8,128)(2,1)S(1)}, f32[8,128]{1,0:T(8,128)S(1)}) custom-call(s32[581]{0:T(1024)S(1)} %pad_add_fusion.refs_0_, bf16[128,2048]{1,0:T(8,128)(2,1)S(1)} %get-tuple-element.80.refs_1_, bf16[128,2048]{1,0:T(8,128)(2,1)S(1)} %collective-permute-done.7.refs_2_, ...), custom_call_target="tpu_custom_call" | custom-call | flops 20000000000 | tf_op jit(solution)/shard_map/row_grads/pallas_call | solution.py:317
  84.7 2.4 %input_far.1 = (bf16[128,2048]{1,0:T(8,128)(2,1)S(1)}, f32[8,128]{1,0:T(8,128)S(1)}) custom-call(s32[581]{0:T(1024)S(1)} %pad_add_fusion.refs_0_, s32[194]{0:T(256)S(1)} %get-tuple-element.91.refs_1_, bf16[14,128,128]{2,1,0:T(8,128)(2,1)S(1)} %get-tuple-element.92.refs_2_.refs_1_, bf16[14,128,128]{2,1,0:T(8,128)(2,1)S(1)} %get-tuple-element.93.refs_3_.refs_1_, ...), custom_call_target="tpu_custom_call" | custom-call | flops 20000000000 | tf_op jit(solution)/shard_map/input_far/pallas_call | solution.py:317
  88.2 1.9 %collective-permute-start.12 = (bf16[2,12,128,128]{3,2,1,0:T(8,128)(2,1)S(1)}, bf16[2,12,128,128]{3,2,1,0:T(8,128)(2,1)S(1)}, u32[]{:S(2)}, u32[]{:S(2)}) collective-permute-start(bf16[2,12,128,128]{3,2,1,0:T(8,128)(2,1)S(1)} %get-tuple-element.90), channel_id=1, source_target_pairs={{0,16},{4,12},{8,24},{12,4},{16,0},{20,28},{24,8},{28,20},{1,17},{... | collective-permute-start | bytes 2359304 | tf_op jit(solution)/shard_map/ppermute | solution.py:366
  90.2 1.8 %gate_grads.1 = (bf16[4,12,128,128]{3,2,1,0:T(8,128)(2,1)S(1)}, bf16[4,12,128,128]{3,2,1,0:T(8,128)(2,1)S(1)}, f32[8,128]{1,0:T(8,128)S(1)}) custom-call(s32[581]{0:T(1024)S(1)} %pad_add_fusion.refs_0_, bf16[14,128,128]{2,1,0:T(8,128)(2,1)S(1)} %get-tuple-element.92.refs_2_.refs_1_, bf16[64,128,128]{2,1,0:T(8,128)(2,1)S(1)} %get-tuple-element.94.refs_2_, ...), custom_call_target="tpu_custom_call" | custom-call | flops 20000000000 | tf_op jit(solution)/shard_map/gate_grads/pallas_call | solution.py:317
  91.9 4.1 %input_rest.1 = (bf16[128,2048]{1,0:T(8,128)(2,1)S(1)}, bf16[128,2048]{1,0:T(8,128)(2,1)S(1)}, bf16[128,2048]{1,0:T(8,128)(2,1)S(1)}, f32[8,128]{1,0:T(8,128)S(1)}) custom-call(s32[581]{0:T(1024)S(1)} %pad_add_fusion.refs_0_, s32[194]{0:T(256)S(1)} %get-tuple-element.91.refs_1_, bf16[14,128,128]{2,1,0:T(8,128)(2,1)S(1)} %get-tuple-element.92.refs_2_.refs_1_, ...), custom_call_target="tpu_custom_call" | custom-call | flops 20000000000 | tf_op jit(solution)/shard_map/input_rest/pallas_call | solution.py:317
  96.1 4.1 %collective-permute-done.12.refs_1_ = bf16[2,12,128,128]{3,2,1,0:T(8,128)(2,1)S(1)} collective-permute-done((bf16[2,12,128,128]{3,2,1,0:T(8,128)(2,1)S(1)}, bf16[2,12,128,128]{3,2,1,0:T(8,128)(2,1)S(1)}, u32[]{:S(2)}, u32[]{:S(2)}) %collective-permute-start.12) | collective-permute-done | bytes 786464 | tf_op jit(solution)/shard_map/ppermute | solution.py:366
  100.4 1.9 %collective-permute-start.14 = (bf16[1,12,128,128]{3,2,1,0:T(8,128)(2,1)S(1)}, bf16[1,12,128,128]{3,2,1,0:T(8,128)(2,1)S(1)}, u32[]{:S(2)}, u32[]{:S(2)}) collective-permute-start(bf16[1,12,128,128]{3,2,1,0:T(8,128)(2,1)S(1)} %get-tuple-element.106), channel_id=1, source_target_pairs={{0,8},{4,20},{8,0},{12,28},{16,24},{20,4},{24,16},{28,12},{1,9},{5... | collective-permute-start | bytes 1179656 | tf_op jit(solution)/shard_map/ppermute | solution.py:366
  102.4 1.7 %collective-permute-done.5.refs_2_ = bf16[128,2048]{1,0:T(8,128)(2,1)S(1)} collective-permute-done((bf16[128,2048]{1,0:T(8,128)(2,1)S(1)}, bf16[128,2048]{1,0:T(8,128)(2,1)S(1)}, u32[]{:S(2)}, u32[]{:S(2)}) %collective-permute-start.5) | collective-permute-done | bytes 524320 | tf_op jit(solution)/shard_map/ppermute | solution.py:332
  105.4 1.6 %collective-permute-start.18 = (bf16[2,12,128,128]{3,2,1,0:T(8,128)(2,1)S(1)}, bf16[2,12,128,128]{3,2,1,0:T(8,128)(2,1)S(1)}, u32[]{:S(2)}, u32[]{:S(2)}) collective-permute-start(bf16[2,12,128,128]{3,2,1,0:T(8,128)(2,1)S(1)} %get-tuple-element.116), channel_id=1, source_target_pairs={{0,16},{4,12},{8,24},{12,4},{16,0},{20,28},{24,8},{28,20},{1,17},{... | collective-permute-start | bytes 2359304 | tf_op jit(solution)/shard_map/ppermute | solution.py:366
  107.0 4.4 %collective-permute-done.14.refs_2_ = bf16[1,12,128,128]{3,2,1,0:T(8,128)(2,1)S(1)} collective-permute-done((bf16[1,12,128,128]{3,2,1,0:T(8,128)(2,1)S(1)}, bf16[1,12,128,128]{3,2,1,0:T(8,128)(2,1)S(1)}, u32[]{:S(2)}, u32[]{:S(2)}) %collective-permute-start.14) | collective-permute-done | bytes 393248 | tf_op jit(solution)/shard_map/ppermute | solution.py:366
  111.4 2.0 %update.3 = (f32[3,12,128,128]{3,2,1,0:T(8,128)}, f32[8,128]{1,0:T(8,128)S(1)}) custom-call(s32[581]{0:T(1024)S(1)} %pad_add_fusion.refs_0_, bf16[1,12,128,128]{3,2,1,0:T(8,128)(2,1)S(1)} %get-tuple-element.105.refs_1_, bf16[1,12,128,128]{3,2,1,0:T(8,128)(2,1)S(1)} %collective-permute-done.14.refs_2_, f32[3,12,128,128]{3,2,1,0:T(8,128)S(1)} %copy-done, ...), custom_call_target="tpu_custom_call" | custom-call | flops 20000000000 | tf_op jit(solution)/shard_map/update/pallas_call | solution.py:317
  113.4 2.2 %up_grads.1 = (bf16[4,12,128,128]{3,2,1,0:T(8,128)(2,1)S(1)}, bf16[4,12,128,128]{3,2,1,0:T(8,128)(2,1)S(1)}, f32[8,128]{1,0:T(8,128)S(1)}) custom-call(s32[581]{0:T(1024)S(1)} %pad_add_fusion.refs_0_, bf16[14,128,128]{2,1,0:T(8,128)(2,1)S(1)} %get-tuple-element.93.refs_3_.refs_1_, bf16[64,128,128]{2,1,0:T(8,128)(2,1)S(1)} %get-tuple-element.94.refs_2_, ...), custom_call_target="tpu_custom_call" | custom-call | flops 20000000000 | tf_op jit(solution)/shard_map/up_grads/pallas_call | solution.py:317
  116.7 1.3 collective-permute-start.17
  119.4 2.6 %collective-permute-start.21 = (bf16[2,12,128,128]{3,2,1,0:T(8,128)(2,1)S(1)}, bf16[2,12,128,128]{3,2,1,0:T(8,128)(2,1)S(1)}, u32[]{:S(2)}, u32[]{:S(2)}) collective-permute-start(bf16[2,12,128,128]{3,2,1,0:T(8,128)(2,1)S(1)} %get-tuple-element.125), channel_id=1, source_target_pairs={{0,16},{4,12},{8,24},{12,4},{16,0},{20,28},{24,8},{28,20},{1,17},{... | collective-permute-start | bytes 2359304 | tf_op jit(solution)/shard_map/ppermute | solution.py:366
  122.9 13.3 %collective-permute-done.21.refs_1_ = bf16[2,12,128,128]{3,2,1,0:T(8,128)(2,1)S(1)} collective-permute-done((bf16[2,12,128,128]{3,2,1,0:T(8,128)(2,1)S(1)}, bf16[2,12,128,128]{3,2,1,0:T(8,128)(2,1)S(1)}, u32[]{:S(2)}, u32[]{:S(2)}) %collective-permute-start.21) | collective-permute-done | bytes 786464 | tf_op jit(solution)/shard_map/ppermute | solution.py:366
  136.4 1.5 %collective-permute-start.22 = (bf16[1,12,128,128]{3,2,1,0:T(8,128)(2,1)S(1)}, bf16[1,12,128,128]{3,2,1,0:T(8,128)(2,1)S(1)}, u32[]{:S(2)}, u32[]{:S(2)}) collective-permute-start(bf16[1,12,128,128]{3,2,1,0:T(8,128)(2,1)S(1)} %get-tuple-element.131), channel_id=1, source_target_pairs={{0,8},{4,20},{8,0},{12,28},{16,24},{20,4},{24,16},{28,12},{1,9},{5... | collective-permute-start | bytes 1179656 | tf_op jit(solution)/shard_map/ppermute | solution.py:366
  137.9 2.0 %update.4 = (f32[3,12,128,128]{3,2,1,0:T(8,128)}, f32[8,128]{1,0:T(8,128)S(1)}) custom-call(s32[581]{0:T(1024)S(1)} %pad_add_fusion.refs_0_, bf16[1,12,128,128]{3,2,1,0:T(8,128)(2,1)S(1)} %get-tuple-element.121.refs_1_, bf16[1,12,128,128]{3,2,1,0:T(8,128)(2,1)S(1)} %collective-permute-done.20.refs_2_, ...), custom_call_target="tpu_custom_call", output_to_operand_aliasing={{0}: (5, {})} | custom-call | flops 20000000000 | tf_op jit(solution)/shard_map/update/pallas_call | solution.py:317
  139.9 2.4 %collective-permute-done.16.refs_1_ = bf16[128,2048]{1,0:T(8,128)(2,1)S(1)} collective-permute-done((bf16[128,2048]{1,0:T(8,128)(2,1)S(1)}, bf16[128,2048]{1,0:T(8,128)(2,1)S(1)}, u32[]{:S(2)}, u32[]{:S(2)}) %collective-permute-start.16) | collective-permute-done | bytes 524320 | tf_op jit(solution)/shard_map/ppermute | solution.py:332
  144.2 2.0 %update.5 = (f32[3,12,128,128]{3,2,1,0:T(8,128)}, f32[8,128]{1,0:T(8,128)}) custom-call(s32[581]{0:T(1024)S(1)} %pad_add_fusion.refs_0_, bf16[1,12,128,128]{3,2,1,0:T(8,128)(2,1)S(1)} %get-tuple-element.130.refs_1_, bf16[1,12,128,128]{3,2,1,0:T(8,128)(2,1)S(1)} %collective-permute-done.22.refs_2_, ...), custom_call_target="tpu_custom_call", output_to_operand_aliasing={{0}: (5, {})} | custom-call | flops 20000000000 | tf_op jit(solution)/shard_map/update/pallas_call | solution.py:317
  (55 shorter events, 14.5 us)
Async XLA Ops:
  0.6 27.6 %collective-permute-start.1 = (bf16[128,2048]{1,0:T(8,128)(2,1)}, bf16[128,2048]{1,0:T(8,128)(2,1)S(1)}, u32[]{:S(2)}, u32[]{:S(2)}) collective-permute-start(bf16[128,2048]{1,0:T(8,128)(2,1)} %refs_1_.3), channel_id=1, source_target_pairs={{0,2},{1,3},{2,0},{3,1},{4,6},{5,7},{6,4},{7,5},{8,10},{9,11},{10,... | collective-permute-start | bytes 1572872 | tf_op jit(solution)/shard_map/ppermute | solution.py:332
  4.7 33.5 %collective-permute-start = (bf16[128,2048]{1,0:T(8,128)(2,1)}, bf16[128,2048]{1,0:T(8,128)(2,1)S(1)}, u32[]{:S(2)}, u32[]{:S(2)}) collective-permute-start(bf16[128,2048]{1,0:T(8,128)(2,1)} %refs_1_.3), channel_id=1, source_target_pairs={{0,1},{1,0},{2,3},{3,2},{4,5},{5,4},{6,7},{7,6},{8,9},{9,8},{10,11... | collective-permute-start | bytes 1572872 | tf_op jit(solution)/shard_map/ppermute | solution.py:332
  8.0 20.9 %copy-start.2 = (bf16[128,2048]{1,0:T(8,128)(2,1)S(1)}, bf16[128,2048]{1,0:T(8,128)(2,1)}, u32[]{:S(2)}) copy-start(bf16[128,2048]{1,0:T(8,128)(2,1)} %refs_0_.1) | copy-start | bytes 1572868
  8.0 45.7 %slice-start = ((s8[9437184]{0:T(1024)(128)(4,1)}), s8[4194304]{0:T(1024)(128)(4,1)S(1)}, s32[]{:S(2)}) async-start(s8[9437184]{0:T(1024)(128)(4,1)} %bitcast.3), calls=%async_computation | async-start | bytes 8388608
  8.0 45.7 %slice-start.1 = ((s8[9437184]{0:T(1024)(128)(4,1)}), s8[4194304]{0:T(1024)(128)(4,1)S(1)}, s32[]{:S(2)}) async-start(s8[9437184]{0:T(1024)(128)(4,1)} %bitcast.3), calls=%async_computation.1 | async-start | bytes 8388608
  28.2 25.5 %collective-permute-start.2 = (bf16[128,2048]{1,0:T(8,128)(2,1)S(1)}, bf16[128,2048]{1,0:T(8,128)(2,1)S(1)}, u32[]{:S(2)}, u32[]{:S(2)}) collective-permute-start(bf16[128,2048]{1,0:T(8,128)(2,1)S(1)} %collective-permute-done.1.refs_1_.refs_3_), channel_id=1, source_target_pairs={{0,1},{1,0},{2,3},{3,2},{4,5},{5,4},{6,7},{7,6},{8,9},{9,8},{10,11... | collective-permute-start | bytes 1572872 | tf_op jit(solution)/shard_map/ppermute | solution.py:332
  28.9 24.7 %slice-start.2 = ((s8[9437184]{0:T(1024)(128)(4,1)}), s8[1048576]{0:T(1024)(128)(4,1)S(1)}, s32[]{:S(2)}) async-start(s8[9437184]{0:T(1024)(128)(4,1)} %bitcast.3), calls=%async_computation.2 | async-start | bytes 2097152
  28.9 24.7 %copy-start.3 = (bf16[128,2048]{1,0:T(8,128)(2,1)S(1)}, bf16[128,2048]{1,0:T(8,128)(2,1)}, u32[]{:S(2)}) copy-start(bf16[128,2048]{1,0:T(8,128)(2,1)} %refs_1_.3) | copy-start | bytes 1572868
  29.0 33.6 %collective-permute-start.9 = (bf16[128,2048]{1,0:T(8,128)(2,1)S(1)}, bf16[128,2048]{1,0:T(8,128)(2,1)S(1)}, u32[]{:S(2)}, u32[]{:S(2)}) collective-permute-start(bf16[128,2048]{1,0:T(8,128)(2,1)S(1)} %get-tuple-element.80.refs_1_), channel_id=1, source_target_pairs={{0,2},{1,3},{2,0},{3,1},{4,6},{5,7},{6,4},{7,5},{8,10},{9,11},{10,... | collective-permute-start | bytes 1572872 | tf_op jit(solution)/shard_map/ppermute | solution.py:332
  32.3 45.9 %collective-permute-start.8 = (bf16[128,2048]{1,0:T(8,128)(2,1)S(1)}, bf16[128,2048]{1,0:T(8,128)(2,1)S(1)}, u32[]{:S(2)}, u32[]{:S(2)}) collective-permute-start(bf16[128,2048]{1,0:T(8,128)(2,1)S(1)} %get-tuple-element.80.refs_1_), channel_id=1, source_target_pairs={{1,0},{2,1},{3,2},{5,4},{6,5},{7,6},{9,8},{10,9},{11,10},{13,12},{... | collective-permute-start | bytes 1572872 | tf_op jit(solution)/shard_map/ppermute | solution.py:343
  33.6 44.6 %collective-permute-start.7 = (bf16[128,2048]{1,0:T(8,128)(2,1)S(1)}, bf16[128,2048]{1,0:T(8,128)(2,1)S(1)}, u32[]{:S(2)}, u32[]{:S(2)}) collective-permute-start(bf16[128,2048]{1,0:T(8,128)(2,1)S(1)} %get-tuple-element.80.refs_1_), channel_id=1, source_target_pairs={{0,1},{1,2},{2,3},{4,5},{5,6},{6,7},{8,9},{9,10},{10,11},{12,13},{... | collective-permute-start | bytes 1572872 | tf_op jit(solution)/shard_map/ppermute | solution.py:342
  60.6 13.5 %collective-permute-start.3 = (bf16[128,2048]{1,0:T(8,128)(2,1)S(1)}, bf16[128,2048]{1,0:T(8,128)(2,1)S(1)}, u32[]{:S(2)}, u32[]{:S(2)}) collective-permute-start(bf16[128,2048]{1,0:T(8,128)(2,1)S(1)} %get-tuple-element.73), channel_id=1, source_target_pairs={{0,1},{3,2},{4,5},{7,6},{8,9},{11,10},{12,13},{15,14},{16,17},{19,... | collective-permute-start | bytes 1572872 | tf_op jit(solution)/shard_map/ppermute | solution.py:349
  61.9 28.2 %collective-permute-start.6 = (bf16[128,2048]{1,0:T(8,128)(2,1)S(1)}, bf16[128,2048]{1,0:T(8,128)(2,1)S(1)}, u32[]{:S(2)}, u32[]{:S(2)}) collective-permute-start(bf16[128,2048]{1,0:T(8,128)(2,1)S(1)} %get-tuple-element.79), channel_id=1, source_target_pairs={{1,2},{2,1},{5,6},{6,5},{9,10},{10,9},{13,14},{14,13},{17,18},{18,... | collective-permute-start | bytes 1572872 | tf_op jit(solution)/shard_map/ppermute | solution.py:349
  62.6 15.6 %collective-permute-start.10 = (bf16[128,2048]{1,0:T(8,128)(2,1)S(1)}, bf16[128,2048]{1,0:T(8,128)(2,1)S(1)}, u32[]{:S(2)}, u32[]{:S(2)}) collective-permute-start(bf16[128,2048]{1,0:T(8,128)(2,1)S(1)} %collective-permute-done.9.refs_4_), channel_id=1, source_target_pairs={{2,3},{1,0},{6,7},{5,4},{10,11},{9,8},{14,15},{13,12},{18,19},{17,... | collective-permute-start | bytes 1572872 | tf_op jit(solution)/shard_map/ppermute | solution.py:344
  74.1 28.2 %collective-permute-start.4 = (bf16[128,2048]{1,0:T(8,128)(2,1)S(1)}, bf16[128,2048]{1,0:T(8,128)(2,1)S(1)}, u32[]{:S(2)}, u32[]{:S(2)}) collective-permute-start(bf16[128,2048]{1,0:T(8,128)(2,1)S(1)} %get-tuple-element.77), channel_id=1, source_target_pairs={{0,2},{1,3},{2,0},{3,1},{4,6},{5,7},{6,4},{7,5},{8,10},{9,11},{10,... | collective-permute-start | bytes 1572872 | tf_op jit(solution)/shard_map/ppermute | solution.py:332
  78.2 25.8 %collective-permute-start.5 = (bf16[128,2048]{1,0:T(8,128)(2,1)S(1)}, bf16[128,2048]{1,0:T(8,128)(2,1)S(1)}, u32[]{:S(2)}, u32[]{:S(2)}) collective-permute-start(bf16[128,2048]{1,0:T(8,128)(2,1)S(1)} %get-tuple-element.78), channel_id=1, source_target_pairs={{0,1},{1,0},{2,3},{3,2},{4,5},{5,4},{6,7},{7,6},{8,9},{9,8},{10,11... | collective-permute-start | bytes 1572872 | tf_op jit(solution)/shard_map/ppermute | solution.py:332
  80.7 3.7 %collective-permute-start.11 = (bf16[4,12,128,128]{3,2,1,0:T(8,128)(2,1)S(1)}, bf16[4,12,128,128]{3,2,1,0:T(8,128)(2,1)S(1)}, u32[]{:S(2)}, u32[]{:S(2)}) collective-permute-start(bf16[4,12,128,128]{3,2,1,0:T(8,128)(2,1)S(1)} %get-tuple-element.84), channel_id=1, source_target_pairs={{0,4},{4,0},{8,12},{12,8},{16,20},{20,16},{24,28},{28,24},{1,5},{5... | collective-permute-start | bytes 4718600 | tf_op jit(solution)/shard_map/ppermute | solution.py:360
  87.1 28.6 %collective-permute-start.13 = (bf16[128,2048]{1,0:T(8,128)(2,1)S(1)}, bf16[128,2048]{1,0:T(8,128)(2,1)S(1)}, u32[]{:S(2)}, u32[]{:S(2)}) collective-permute-start(bf16[128,2048]{1,0:T(8,128)(2,1)S(1)} %get-tuple-element.103), channel_id=1, source_target_pairs={{0,1},{1,0},{2,3},{3,2},{4,5},{5,4},{6,7},{7,6},{8,9},{9,8},{10,11... | collective-permute-start | bytes 1572872 | tf_op jit(solution)/shard_map/ppermute | solution.py:332
  88.2 12.0 %collective-permute-start.12 = (bf16[2,12,128,128]{3,2,1,0:T(8,128)(2,1)S(1)}, bf16[2,12,128,128]{3,2,1,0:T(8,128)(2,1)S(1)}, u32[]{:S(2)}, u32[]{:S(2)}) collective-permute-start(bf16[2,12,128,128]{3,2,1,0:T(8,128)(2,1)S(1)} %get-tuple-element.90), channel_id=1, source_target_pairs={{0,16},{4,12},{8,24},{12,4},{16,0},{20,28},{24,8},{28,20},{1,17},{... | collective-permute-start | bytes 2359304 | tf_op jit(solution)/shard_map/ppermute | solution.py:366
  96.0 9.1 %collective-permute-start.15 = (bf16[4,12,128,128]{3,2,1,0:T(8,128)(2,1)S(1)}, bf16[4,12,128,128]{3,2,1,0:T(8,128)(2,1)S(1)}, u32[]{:S(2)}, u32[]{:S(2)}) collective-permute-start(bf16[4,12,128,128]{3,2,1,0:T(8,128)(2,1)S(1)} %get-tuple-element.108), channel_id=1, source_target_pairs={{0,4},{4,0},{8,12},{12,8},{16,20},{20,16},{24,28},{28,24},{1,5},{5... | collective-permute-start | bytes 4718600 | tf_op jit(solution)/shard_map/ppermute | solution.py:360
  100.4 11.0 %collective-permute-start.14 = (bf16[1,12,128,128]{3,2,1,0:T(8,128)(2,1)S(1)}, bf16[1,12,128,128]{3,2,1,0:T(8,128)(2,1)S(1)}, u32[]{:S(2)}, u32[]{:S(2)}) collective-permute-start(bf16[1,12,128,128]{3,2,1,0:T(8,128)(2,1)S(1)} %get-tuple-element.106), channel_id=1, source_target_pairs={{0,8},{4,20},{8,0},{12,28},{16,24},{20,4},{24,16},{28,12},{1,9},{5... | collective-permute-start | bytes 1179656 | tf_op jit(solution)/shard_map/ppermute | solution.py:366
  105.1 6.3 %copy-start = (f32[3,12,128,128]{3,2,1,0:T(8,128)S(1)}, f32[3,12,128,128]{3,2,1,0:T(8,128)}, u32[]{:S(2)}) copy-start(f32[3,12,128,128]{3,2,1,0:T(8,128)} %refs_3_.5) | copy-start | bytes 7077892
  105.1 6.3 %copy-start.1 = (f32[3,12,128,128]{3,2,1,0:T(8,128)S(1)}, f32[3,12,128,128]{3,2,1,0:T(8,128)}, u32[]{:S(2)}) copy-start(f32[3,12,128,128]{3,2,1,0:T(8,128)} %refs_4_.9) | copy-start | bytes 7077892
  105.4 16.6 %collective-permute-start.18 = (bf16[2,12,128,128]{3,2,1,0:T(8,128)(2,1)S(1)}, bf16[2,12,128,128]{3,2,1,0:T(8,128)(2,1)S(1)}, u32[]{:S(2)}, u32[]{:S(2)}) collective-permute-start(bf16[2,12,128,128]{3,2,1,0:T(8,128)(2,1)S(1)} %get-tuple-element.116), channel_id=1, source_target_pairs={{0,16},{4,12},{8,24},{12,4},{16,0},{20,28},{24,8},{28,20},{1,17},{... | collective-permute-start | bytes 2359304 | tf_op jit(solution)/shard_map/ppermute | solution.py:366
  115.6 3.5 %collective-permute-start.19 = (bf16[4,12,128,128]{3,2,1,0:T(8,128)(2,1)S(1)}, bf16[4,12,128,128]{3,2,1,0:T(8,128)(2,1)S(1)}, u32[]{:S(2)}, u32[]{:S(2)}) collective-permute-start(bf16[4,12,128,128]{3,2,1,0:T(8,128)(2,1)S(1)} %get-tuple-element.118), channel_id=1, source_target_pairs={{0,4},{4,0},{8,12},{12,8},{16,20},{20,16},{24,28},{28,24},{1,5},{5... | collective-permute-start | bytes 4718600 | tf_op jit(solution)/shard_map/ppermute | solution.py:360
  115.8 26.5 %collective-permute-start.16 = (bf16[128,2048]{1,0:T(8,128)(2,1)S(1)}, bf16[128,2048]{1,0:T(8,128)(2,1)S(1)}, u32[]{:S(2)}, u32[]{:S(2)}) collective-permute-start(bf16[128,2048]{1,0:T(8,128)(2,1)S(1)} %get-tuple-element.113), channel_id=1, source_target_pairs={{0,2},{1,3},{2,0},{3,1},{4,6},{5,7},{6,4},{7,5},{8,10},{9,11},{10,... | collective-permute-start | bytes 1572872 | tf_op jit(solution)/shard_map/ppermute | solution.py:332
  116.7 25.6 %collective-permute-start.17 = (bf16[128,2048]{1,0:T(8,128)(2,1)S(1)}, bf16[128,2048]{1,0:T(8,128)(2,1)S(1)}, u32[]{:S(2)}, u32[]{:S(2)}) collective-permute-start(bf16[128,2048]{1,0:T(8,128)(2,1)S(1)} %get-tuple-element.114), channel_id=1, source_target_pairs={{0,1},{1,0},{2,3},{3,2},{4,5},{5,4},{6,7},{7,6},{8,9},{9,8},{10,11... | collective-permute-start | bytes 1572872 | tf_op jit(solution)/shard_map/ppermute | solution.py:332
  119.4 16.8 %collective-permute-start.21 = (bf16[2,12,128,128]{3,2,1,0:T(8,128)(2,1)S(1)}, bf16[2,12,128,128]{3,2,1,0:T(8,128)(2,1)S(1)}, u32[]{:S(2)}, u32[]{:S(2)}) collective-permute-start(bf16[2,12,128,128]{3,2,1,0:T(8,128)(2,1)S(1)} %get-tuple-element.125), channel_id=1, source_target_pairs={{0,16},{4,12},{8,24},{12,4},{16,0},{20,28},{24,8},{28,20},{1,17},{... | collective-permute-start | bytes 2359304 | tf_op jit(solution)/shard_map/ppermute | solution.py:366
  122.2 15.7 %collective-permute-start.20 = (bf16[1,12,128,128]{3,2,1,0:T(8,128)(2,1)S(1)}, bf16[1,12,128,128]{3,2,1,0:T(8,128)(2,1)S(1)}, u32[]{:S(2)}, u32[]{:S(2)}) collective-permute-start(bf16[1,12,128,128]{3,2,1,0:T(8,128)(2,1)S(1)} %get-tuple-element.122), channel_id=1, source_target_pairs={{0,8},{4,20},{8,0},{12,28},{16,24},{20,4},{24,16},{28,12},{1,9},{5... | collective-permute-start | bytes 1179656 | tf_op jit(solution)/shard_map/ppermute | solution.py:366
  136.4 7.8 %collective-permute-start.22 = (bf16[1,12,128,128]{3,2,1,0:T(8,128)(2,1)S(1)}, bf16[1,12,128,128]{3,2,1,0:T(8,128)(2,1)S(1)}, u32[]{:S(2)}, u32[]{:S(2)}) collective-permute-start(bf16[1,12,128,128]{3,2,1,0:T(8,128)(2,1)S(1)} %get-tuple-element.131), channel_id=1, source_target_pairs={{0,8},{4,20},{8,0},{12,28},{16,24},{20,4},{24,16},{28,12},{1,9},{5... | collective-permute-start | bytes 1179656 | tf_op jit(solution)/shard_map/ppermute | solution.py:366

commit v11 on v10

--- a/solution.py
+++ b/solution.py
@@ -469,7 +469,6 @@
             functools.partial(input_part_kernel, True), "input_far", [piece], [part_total], in_operands, (*plan, order)
         )
         in_far = flip(in_far, 4, 1)
-    gate = grads(0, [gate_rows], x_turned, out_far[1:] if lined else ())
     if lined:
         in_parts = line(
             functools.partial(input_part_kernel, False), "input_rest", [piece] * 3, [total], in_operands, (*plan, order)
@@ -479,13 +478,14 @@
             functools.partial(input_kernel, 1), "input_grads", in_parts, [total], [gate_rows, up_rows, weights], plan
         )
         input_grad = lax.psum_scatter(in_parts[0], "tensor", scatter_dimension=0)
+    gate = grads(0, [gate_rows], x_turned, out_far[1:] if lined else ())
     for step in range(1, levels):
         down = fold(*down, step)
     if lined:
         outputs = finish(out_sums)
     gate = fold(*gate, 0)
+    up = grads(1, [up_rows], x_turned)
     buffer = update(2, *down, buffer)
-    up = grads(1, [up_rows], x_turned)
     if lined:
         in_sums = scatter_second(line, in_parts, [in_far])
     up = fold(*up, 0)

time: 147 us -> 143 us (0.973)
  waiting for transfers between devices: 68.2 us -> 59.4 us
  Pallas kernels: 38.7 us -> 42 us
    ppermute x6, waiting for transfers between devices: 22.8 us -> 19.1 us  [axis_swap(): return lax.ppermute(v, 'dp', pairs)]
    pallas_call x23, Pallas kernels: 38.7 us -> 42 us  [__call__(): pl.pallas_call(body, name=name, out_shape=[*outs, TOKEN], in_specs=[SMEM]...]
    ppermute x9, waiting for transfers between devices: 35.4 us -> 32.6 us  [flip(): return lax.ppermute(v, 'tensor', [(a, a ^ bit) for a in range(shards)])]
  transfers between devices with their start and end apart: 23 -> 23, of which waited for: 10 -> 11; matrix products, arithmetic and copies ran while one was open for 1% -> 1% of each run, Pallas kernels for 25% -> 28%
where the time goes in v11:
time: 143 us; the launch traced here: 142 us
  waiting for transfers between devices  59.4 us (42%)
  Pallas kernels  42 us (29%)
  starting transfers between devices  36.8 us (26%)
  local copies, waits for them, and re-layouts  1.77 us (1%)
    pallas_call x23, Pallas kernels, __call__(): pl.pallas_call(body, name=name, out_shape=[*outs, TOKEN], in_specs=[SMEM]...  42 us
    ppermute x9, waiting for transfers between devices, flip(): return lax.ppermute(v, 'tensor', [(a, a ^ bit) for a in range(shards)])  32.6 us
    ppermute x6, waiting for transfers between devices, axis_swap(): return lax.ppermute(v, 'dp', pairs)  19.1 us
    ppermute x9, starting transfers between devices, flip(): return lax.ppermute(v, 'tensor', [(a, a ^ bit) for a in range(shards)])  18.4 us
    ppermute x6, starting transfers between devices, axis_swap(): return lax.ppermute(v, 'dp', pairs)  9.03 us
    ppermute x1, waiting for transfers between devices, scatter_first(): lax.ppermute(parts[3], 'tensor', [(0, 1), (3, 2)])  7.42 us
    ppermute x1, starting transfers between devices, gather_line(): below = lax.ppermute(v, 'tensor', [(a, a + 1) for a in range(3)])  4.58 us
  transfers between devices with their start and end apart: 23, of which 11 were waited for; matrix products, arithmetic and copies ran while one was open for 1% of the time, Pallas kernels for 28%

profile of v11, /device:TPU:0, one launch (start us, length us, event | category | flops | bytes accessed | tf_op | source)
XLA Modules:
  0.0 141.5 jit_solution(3306999506684285751)
XLA Ops:
  0.6 4.1 %collective-permute-start.1 = (bf16[128,2048]{1,0:T(8,128)(2,1)}, bf16[128,2048]{1,0:T(8,128)(2,1)S(1)}, u32[]{:S(2)}, u32[]{:S(2)}) collective-permute-start(bf16[128,2048]{1,0:T(8,128)(2,1)} %refs_1_.3), channel_id=1, source_target_pairs={{0,2},{1,3},{2,0},{3,1},{4,6},{5,7},{6,4},{7,5},{8,10},{9,11},{10,... | collective-permute-start | bytes 1572872 | tf_op jit(solution)/shard_map/ppermute | solution.py:332
  4.7 1.6 %collective-permute-start = (bf16[128,2048]{1,0:T(8,128)(2,1)}, bf16[128,2048]{1,0:T(8,128)(2,1)S(1)}, u32[]{:S(2)}, u32[]{:S(2)}) collective-permute-start(bf16[128,2048]{1,0:T(8,128)(2,1)} %refs_1_.3), channel_id=1, source_target_pairs={{0,1},{1,0},{2,3},{3,2},{4,5},{5,4},{6,7},{7,6},{8,9},{9,8},{10,11... | collective-permute-start | bytes 1572872 | tf_op jit(solution)/shard_map/ppermute | solution.py:332
  8.0 5.8 %order.1 = (s32[194]{0:T(256)S(1)}, f32[8,128]{1,0:T(8,128)S(1)}) custom-call(s32[581]{0:T(1024)S(1)} %pad_add_fusion.refs_0_), custom_call_target="tpu_custom_call" | custom-call | flops 20000000000 | tf_op jit(solution)/shard_map/order/pallas_call | solution.py:317
  13.8 14.4 %collective-permute-done.1.refs_1_.refs_3_ = bf16[128,2048]{1,0:T(8,128)(2,1)S(1)} collective-permute-done((bf16[128,2048]{1,0:T(8,128)(2,1)}, bf16[128,2048]{1,0:T(8,128)(2,1)S(1)}, u32[]{:S(2)}, u32[]{:S(2)}) %collective-permute-start.1) | collective-permute-done | bytes 524320 | tf_op jit(solution)/shard_map/ppermute | solution.py:332
  29.0 3.3 %collective-permute-start.9 = (bf16[128,2048]{1,0:T(8,128)(2,1)S(1)}, bf16[128,2048]{1,0:T(8,128)(2,1)S(1)}, u32[]{:S(2)}, u32[]{:S(2)}) collective-permute-start(bf16[128,2048]{1,0:T(8,128)(2,1)S(1)} %get-tuple-element.80.refs_1_), channel_id=1, source_target_pairs={{0,2},{1,3},{2,0},{3,1},{4,6},{5,7},{6,4},{7,5},{8,10},{9,11},{10,... | collective-permute-start | bytes 1572872 | tf_op jit(solution)/shard_map/ppermute | solution.py:332
  33.6 4.6 %collective-permute-start.7 = (bf16[128,2048]{1,0:T(8,128)(2,1)S(1)}, bf16[128,2048]{1,0:T(8,128)(2,1)S(1)}, u32[]{:S(2)}, u32[]{:S(2)}) collective-permute-start(bf16[128,2048]{1,0:T(8,128)(2,1)S(1)} %get-tuple-element.80.refs_1_), channel_id=1, source_target_pairs={{0,1},{1,2},{2,3},{4,5},{5,6},{6,7},{8,9},{9,10},{10,11},{12,13},{... | collective-permute-start | bytes 1572872 | tf_op jit(solution)/shard_map/ppermute | solution.py:342
  38.2 15.5 %collective-permute-done.2.refs_4_ = bf16[128,2048]{1,0:T(8,128)(2,1)S(1)} collective-permute-done((bf16[128,2048]{1,0:T(8,128)(2,1)S(1)}, bf16[128,2048]{1,0:T(8,128)(2,1)S(1)}, u32[]{:S(2)}, u32[]{:S(2)}) %collective-permute-start.2) | collective-permute-done | bytes 524320 | tf_op jit(solution)/shard_map/ppermute | solution.py:332
  53.7 7.4 %forward.1 = (bf16[14,128,128]{2,1,0:T(8,128)(2,1)}, bf16[14,128,128]{2,1,0:T(8,128)(2,1)S(1)}, f32[14,128,128]{2,1,0:T(8,128)S(1)}, f32[14,128,128]{2,1,0:T(8,1...) custom-call(s32[581]{0:T(1024)S(1)} %pad_add_fusion.refs_0_, ...), custom_call_target="tpu_custom_call" | custom-call | flops 20000000000 | tf_op jit(solution)/shard_map/forward/pallas_call | solution.py:317
  61.9 1.4 collective-permute-start.3
  65.3 1.3 turn.1
  66.6 7.4 %collective-permute-done.3.refs_1_ = bf16[128,2048]{1,0:T(8,128)(2,1)S(1)} collective-permute-done((bf16[128,2048]{1,0:T(8,128)(2,1)S(1)}, bf16[128,2048]{1,0:T(8,128)(2,1)S(1)}, u32[]{:S(2)}, u32[]{:S(2)}) %collective-permute-start.3) | collective-permute-done | bytes 524320 | tf_op jit(solution)/shard_map/ppermute | solution.py:349
  74.2 4.1 %collective-permute-start.4 = (bf16[128,2048]{1,0:T(8,128)(2,1)S(1)}, bf16[128,2048]{1,0:T(8,128)(2,1)S(1)}, u32[]{:S(2)}, u32[]{:S(2)}) collective-permute-start(bf16[128,2048]{1,0:T(8,128)(2,1)S(1)} %get-tuple-element.77), channel_id=1, source_target_pairs={{0,2},{1,3},{2,0},{3,1},{4,6},{5,7},{6,4},{7,5},{8,10},{9,11},{10,... | collective-permute-start | bytes 1572872 | tf_op jit(solution)/shard_map/ppermute | solution.py:332
  78.3 2.0 %down_grads.1 = (bf16[4,12,128,128]{3,2,1,0:T(8,128)(2,1)S(1)}, bf16[4,12,128,128]{3,2,1,0:T(8,128)(2,1)S(1)}, f32[8,128]{1,0:T(8,128)S(1)}) custom-call(s32[581]{0:T(1024)S(1)} %pad_add_fusion.refs_0_, bf16[128,2048]{1,0:T(8,128)(2,1)S(1)} %get-tuple-element.80.refs_1_, bf16[128,2048]{1,0:T(8,128)(2,1)S(1)} %collective-permute-done.7.refs_2_, ...), custom_call_target="tpu_custom_call" | custom-call | flops 20000000000 | tf_op jit(solution)/shard_map/down_grads/pallas_call | solution.py:317
  80.3 3.1 %row_grads.1 = (bf16[14,128,128]{2,1,0:T(8,128)(2,1)S(1)}, bf16[14,128,128]{2,1,0:T(8,128)(2,1)S(1)}, f32[8,128]{1,0:T(8,128)S(1)}) custom-call(s32[581]{0:T(1024)S(1)} %pad_add_fusion.refs_0_, bf16[128,2048]{1,0:T(8,128)(2,1)S(1)} %get-tuple-element.80.refs_1_, bf16[128,2048]{1,0:T(8,128)(2,1)S(1)} %collective-permute-done.7.refs_2_, ...), custom_call_target="tpu_custom_call" | custom-call | flops 20000000000 | tf_op jit(solution)/shard_map/row_grads/pallas_call | solution.py:317
  84.1 2.7 %input_far.1 = (bf16[128,2048]{1,0:T(8,128)(2,1)S(1)}, f32[8,128]{1,0:T(8,128)S(1)}) custom-call(s32[581]{0:T(1024)S(1)} %pad_add_fusion.refs_0_, s32[194]{0:T(256)S(1)} %get-tuple-element.93.refs_1_, bf16[14,128,128]{2,1,0:T(8,128)(2,1)S(1)} %get-tuple-element.91.refs_2_.refs_1_, bf16[14,128,128]{2,1,0:T(8,128)(2,1)S(1)} %get-tuple-element.94.refs_3_.refs_1_, ...), custom_call_target="tpu_custom_call" | custom-call | flops 20000000000 | tf_op jit(solution)/shard_map/input_far/pallas_call | solution.py:317
  86.8 2.7 %collective-permute-start.13 = (bf16[128,2048]{1,0:T(8,128)(2,1)S(1)}, bf16[128,2048]{1,0:T(8,128)(2,1)S(1)}, u32[]{:S(2)}, u32[]{:S(2)}) collective-permute-start(bf16[128,2048]{1,0:T(8,128)(2,1)S(1)} %get-tuple-element.103), channel_id=1, source_target_pairs={{0,1},{1,0},{2,3},{3,2},{4,5},{5,4},{6,7},{7,6},{8,9},{9,8},{10,11... | collective-permute-start | bytes 1572872 | tf_op jit(solution)/shard_map/ppermute | solution.py:332
  89.5 1.5 %collective-permute-start.12 = (bf16[2,12,128,128]{3,2,1,0:T(8,128)(2,1)S(1)}, bf16[2,12,128,128]{3,2,1,0:T(8,128)(2,1)S(1)}, u32[]{:S(2)}, u32[]{:S(2)}) collective-permute-start(bf16[2,12,128,128]{3,2,1,0:T(8,128)(2,1)S(1)} %get-tuple-element.90), channel_id=1, source_target_pairs={{0,16},{4,12},{8,24},{12,4},{16,0},{20,28},{24,8},{28,20},{1,17},{... | collective-permute-start | bytes 2359304 | tf_op jit(solution)/shard_map/ppermute | solution.py:366
  91.0 5.5 %input_rest.1 = (bf16[128,2048]{1,0:T(8,128)(2,1)S(1)}, bf16[128,2048]{1,0:T(8,128)(2,1)S(1)}, bf16[128,2048]{1,0:T(8,128)(2,1)S(1)}, f32[8,128]{1,0:T(8,128)S(1)}) custom-call(s32[581]{0:T(1024)S(1)} %pad_add_fusion.refs_0_, s32[194]{0:T(256)S(1)} %get-tuple-element.93.refs_1_, bf16[14,128,128]{2,1,0:T(8,128)(2,1)S(1)} %get-tuple-element.91.refs_2_.refs_1_, ...), custom_call_target="tpu_custom_call" | custom-call | flops 20000000000 | tf_op jit(solution)/shard_map/input_rest/pallas_call | solution.py:317
  96.5 2.2 %gate_grads.1 = (bf16[4,12,128,128]{3,2,1,0:T(8,128)(2,1)S(1)}, bf16[4,12,128,128]{3,2,1,0:T(8,128)(2,1)S(1)}, f32[8,128]{1,0:T(8,128)S(1)}) custom-call(s32[581]{0:T(1024)S(1)} %pad_add_fusion.refs_0_, bf16[14,128,128]{2,1,0:T(8,128)(2,1)S(1)} %get-tuple-element.91.refs_2_.refs_1_, bf16[64,128,128]{2,1,0:T(8,128)(2,1)S(1)} %get-tuple-element.92.refs_2_, ...), custom_call_target="tpu_custom_call" | custom-call | flops 20000000000 | tf_op jit(solution)/shard_map/gate_grads/pallas_call | solution.py:317
  98.8 2.7 %collective-permute-done.12.refs_1_ = bf16[2,12,128,128]{3,2,1,0:T(8,128)(2,1)S(1)} collective-permute-done((bf16[2,12,128,128]{3,2,1,0:T(8,128)(2,1)S(1)}, bf16[2,12,128,128]{3,2,1,0:T(8,128)(2,1)S(1)}, u32[]{:S(2)}, u32[]{:S(2)}) %collective-permute-start.12) | collective-permute-done | bytes 786464 | tf_op jit(solution)/shard_map/ppermute | solution.py:366
  101.6 1.6 %collective-permute-start.14 = (bf16[1,12,128,128]{3,2,1,0:T(8,128)(2,1)S(1)}, bf16[1,12,128,128]{3,2,1,0:T(8,128)(2,1)S(1)}, u32[]{:S(2)}, u32[]{:S(2)}) collective-permute-start(bf16[1,12,128,128]{3,2,1,0:T(8,128)(2,1)S(1)} %get-tuple-element.106), channel_id=1, source_target_pairs={{0,8},{4,20},{8,0},{12,28},{16,24},{20,4},{24,16},{28,12},{1,9},{5... | collective-permute-start | bytes 1179656 | tf_op jit(solution)/shard_map/ppermute | solution.py:366
  104.6 2.2 %up_grads.1 = (bf16[4,12,128,128]{3,2,1,0:T(8,128)(2,1)S(1)}, bf16[4,12,128,128]{3,2,1,0:T(8,128)(2,1)S(1)}, f32[8,128]{1,0:T(8,128)S(1)}) custom-call(s32[581]{0:T(1024)S(1)} %pad_add_fusion.refs_0_, bf16[14,128,128]{2,1,0:T(8,128)(2,1)S(1)} %get-tuple-element.94.refs_3_.refs_1_, bf16[64,128,128]{2,1,0:T(8,128)(2,1)S(1)} %get-tuple-element.92.refs_2_, ...), custom_call_target="tpu_custom_call" | custom-call | flops 20000000000 | tf_op jit(solution)/shard_map/up_grads/pallas_call | solution.py:317
  106.8 1.6 %collective-permute-start.18 = (bf16[2,12,128,128]{3,2,1,0:T(8,128)(2,1)S(1)}, bf16[2,12,128,128]{3,2,1,0:T(8,128)(2,1)S(1)}, u32[]{:S(2)}, u32[]{:S(2)}) collective-permute-start(bf16[2,12,128,128]{3,2,1,0:T(8,128)(2,1)S(1)} %get-tuple-element.116), channel_id=1, source_target_pairs={{0,16},{4,12},{8,24},{12,4},{16,0},{20,28},{24,8},{28,20},{1,17},{... | collective-permute-start | bytes 2359304 | tf_op jit(solution)/shard_map/ppermute | solution.py:366
  108.4 1.9 %collective-permute-done.14.refs_2_ = bf16[1,12,128,128]{3,2,1,0:T(8,128)(2,1)S(1)} collective-permute-done((bf16[1,12,128,128]{3,2,1,0:T(8,128)(2,1)S(1)}, bf16[1,12,128,128]{3,2,1,0:T(8,128)(2,1)S(1)}, u32[]{:S(2)}, u32[]{:S(2)}) %collective-permute-start.14) | collective-permute-done | bytes 393248 | tf_op jit(solution)/shard_map/ppermute | solution.py:366
  110.3 2.0 %update.3 = (f32[3,12,128,128]{3,2,1,0:T(8,128)}, f32[8,128]{1,0:T(8,128)S(1)}) custom-call(s32[581]{0:T(1024)S(1)} %pad_add_fusion.refs_0_, bf16[1,12,128,128]{3,2,1,0:T(8,128)(2,1)S(1)} %get-tuple-element.105.refs_1_, bf16[1,12,128,128]{3,2,1,0:T(8,128)(2,1)S(1)} %collective-permute-done.14.refs_2_, f32[3,12,128,128]{3,2,1,0:T(8,128)S(1)} %copy-done, ...), custom_call_target="tpu_custom_call" | custom-call | flops 20000000000 | tf_op jit(solution)/shard_map/update/pallas_call | solution.py:317
  112.7 1.8 %collective-permute-start.16 = (bf16[128,2048]{1,0:T(8,128)(2,1)S(1)}, bf16[128,2048]{1,0:T(8,128)(2,1)S(1)}, u32[]{:S(2)}, u32[]{:S(2)}) collective-permute-start(bf16[128,2048]{1,0:T(8,128)(2,1)S(1)} %get-tuple-element.113), channel_id=1, source_target_pairs={{0,2},{1,3},{2,0},{3,1},{4,6},{5,7},{6,4},{7,5},{8,10},{9,11},{10,... | collective-permute-start | bytes 1572872 | tf_op jit(solution)/shard_map/ppermute | solution.py:332
  114.9 1.8 %collective-permute-start.21 = (bf16[2,12,128,128]{3,2,1,0:T(8,128)(2,1)S(1)}, bf16[2,12,128,128]{3,2,1,0:T(8,128)(2,1)S(1)}, u32[]{:S(2)}, u32[]{:S(2)}) collective-permute-start(bf16[2,12,128,128]{3,2,1,0:T(8,128)(2,1)S(1)} %get-tuple-element.125), channel_id=1, source_target_pairs={{0,16},{4,12},{8,24},{12,4},{16,0},{20,28},{24,8},{28,20},{1,17},{... | collective-permute-start | bytes 2359304 | tf_op jit(solution)/shard_map/ppermute | solution.py:366
  116.7 2.2 %collective-permute-done.18.refs_1_ = bf16[2,12,128,128]{3,2,1,0:T(8,128)(2,1)S(1)} collective-permute-done((bf16[2,12,128,128]{3,2,1,0:T(8,128)(2,1)S(1)}, bf16[2,12,128,128]{3,2,1,0:T(8,128)(2,1)S(1)}, u32[]{:S(2)}, u32[]{:S(2)}) %collective-permute-start.18) | collective-permute-done | bytes 786464 | tf_op jit(solution)/shard_map/ppermute | solution.py:366
  120.3 11.2 %collective-permute-done.21.refs_1_ = bf16[2,12,128,128]{3,2,1,0:T(8,128)(2,1)S(1)} collective-permute-done((bf16[2,12,128,128]{3,2,1,0:T(8,128)(2,1)S(1)}, bf16[2,12,128,128]{3,2,1,0:T(8,128)(2,1)S(1)}, u32[]{:S(2)}, u32[]{:S(2)}) %collective-permute-start.21) | collective-permute-done | bytes 786464 | tf_op jit(solution)/shard_map/ppermute | solution.py:366
  133.0 2.0 %update.4 = (f32[3,12,128,128]{3,2,1,0:T(8,128)}, f32[8,128]{1,0:T(8,128)S(1)}) custom-call(s32[581]{0:T(1024)S(1)} %pad_add_fusion.refs_0_, bf16[1,12,128,128]{3,2,1,0:T(8,128)(2,1)S(1)} %get-tuple-element.121.refs_1_, bf16[1,12,128,128]{3,2,1,0:T(8,128)(2,1)S(1)} %collective-permute-done.20.refs_2_, ...), custom_call_target="tpu_custom_call", output_to_operand_aliasing={{0}: (5, {})} | custom-call | flops 20000000000 | tf_op jit(solution)/shard_map/update/pallas_call | solution.py:317
  135.0 2.4 %collective-permute-done.16.refs_1_ = bf16[128,2048]{1,0:T(8,128)(2,1)S(1)} collective-permute-done((bf16[128,2048]{1,0:T(8,128)(2,1)S(1)}, bf16[128,2048]{1,0:T(8,128)(2,1)S(1)}, u32[]{:S(2)}, u32[]{:S(2)}) %collective-permute-start.16) | collective-permute-done | bytes 524320 | tf_op jit(solution)/shard_map/ppermute | solution.py:332
  139.5 2.0 %update.5 = (f32[3,12,128,128]{3,2,1,0:T(8,128)}, f32[8,128]{1,0:T(8,128)}) custom-call(s32[581]{0:T(1024)S(1)} %pad_add_fusion.refs_0_, bf16[1,12,128,128]{3,2,1,0:T(8,128)(2,1)S(1)} %get-tuple-element.130.refs_1_, bf16[1,12,128,128]{3,2,1,0:T(8,128)(2,1)S(1)} %collective-permute-done.22.refs_2_, ...), custom_call_target="tpu_custom_call", output_to_operand_aliasing={{0}: (5, {})} | custom-call | flops 20000000000 | tf_op jit(solution)/shard_map/update/pallas_call | solution.py:317
  (63 shorter events, 14.8 us)
Async XLA Ops:
  0.6 27.6 %collective-permute-start.1 = (bf16[128,2048]{1,0:T(8,128)(2,1)}, bf16[128,2048]{1,0:T(8,128)(2,1)S(1)}, u32[]{:S(2)}, u32[]{:S(2)}) collective-permute-start(bf16[128,2048]{1,0:T(8,128)(2,1)} %refs_1_.3), channel_id=1, source_target_pairs={{0,2},{1,3},{2,0},{3,1},{4,6},{5,7},{6,4},{7,5},{8,10},{9,11},{10,... | collective-permute-start | bytes 1572872 | tf_op jit(solution)/shard_map/ppermute | solution.py:332
  4.7 33.5 %collective-permute-start = (bf16[128,2048]{1,0:T(8,128)(2,1)}, bf16[128,2048]{1,0:T(8,128)(2,1)S(1)}, u32[]{:S(2)}, u32[]{:S(2)}) collective-permute-start(bf16[128,2048]{1,0:T(8,128)(2,1)} %refs_1_.3), channel_id=1, source_target_pairs={{0,1},{1,0},{2,3},{3,2},{4,5},{5,4},{6,7},{7,6},{8,9},{9,8},{10,11... | collective-permute-start | bytes 1572872 | tf_op jit(solution)/shard_map/ppermute | solution.py:332
  8.0 20.9 %copy-start.2 = (bf16[128,2048]{1,0:T(8,128)(2,1)S(1)}, bf16[128,2048]{1,0:T(8,128)(2,1)}, u32[]{:S(2)}) copy-start(bf16[128,2048]{1,0:T(8,128)(2,1)} %refs_0_.1) | copy-start | bytes 1572868
  8.0 45.7 %slice-start = ((s8[9437184]{0:T(1024)(128)(4,1)}), s8[4194304]{0:T(1024)(128)(4,1)S(1)}, s32[]{:S(2)}) async-start(s8[9437184]{0:T(1024)(128)(4,1)} %bitcast.3), calls=%async_computation | async-start | bytes 8388608
  8.0 45.7 %slice-start.1 = ((s8[9437184]{0:T(1024)(128)(4,1)}), s8[4194304]{0:T(1024)(128)(4,1)S(1)}, s32[]{:S(2)}) async-start(s8[9437184]{0:T(1024)(128)(4,1)} %bitcast.3), calls=%async_computation.1 | async-start | bytes 8388608
  28.2 25.5 %collective-permute-start.2 = (bf16[128,2048]{1,0:T(8,128)(2,1)S(1)}, bf16[128,2048]{1,0:T(8,128)(2,1)S(1)}, u32[]{:S(2)}, u32[]{:S(2)}) collective-permute-start(bf16[128,2048]{1,0:T(8,128)(2,1)S(1)} %collective-permute-done.1.refs_1_.refs_3_), channel_id=1, source_target_pairs={{0,1},{1,0},{2,3},{3,2},{4,5},{5,4},{6,7},{7,6},{8,9},{9,8},{10,11... | collective-permute-start | bytes 1572872 | tf_op jit(solution)/shard_map/ppermute | solution.py:332
  28.9 24.7 %slice-start.2 = ((s8[9437184]{0:T(1024)(128)(4,1)}), s8[1048576]{0:T(1024)(128)(4,1)S(1)}, s32[]{:S(2)}) async-start(s8[9437184]{0:T(1024)(128)(4,1)} %bitcast.3), calls=%async_computation.2 | async-start | bytes 2097152
  28.9 24.7 %copy-start.3 = (bf16[128,2048]{1,0:T(8,128)(2,1)S(1)}, bf16[128,2048]{1,0:T(8,128)(2,1)}, u32[]{:S(2)}) copy-start(bf16[128,2048]{1,0:T(8,128)(2,1)} %refs_1_.3) | copy-start | bytes 1572868
  29.0 35.0 %collective-permute-start.9 = (bf16[128,2048]{1,0:T(8,128)(2,1)S(1)}, bf16[128,2048]{1,0:T(8,128)(2,1)S(1)}, u32[]{:S(2)}, u32[]{:S(2)}) collective-permute-start(bf16[128,2048]{1,0:T(8,128)(2,1)S(1)} %get-tuple-element.80.refs_1_), channel_id=1, source_target_pairs={{0,2},{1,3},{2,0},{3,1},{4,6},{5,7},{6,4},{7,5},{8,10},{9,11},{10,... | collective-permute-start | bytes 1572872 | tf_op jit(solution)/shard_map/ppermute | solution.py:332
  32.3 45.9 %collective-permute-start.8 = (bf16[128,2048]{1,0:T(8,128)(2,1)S(1)}, bf16[128,2048]{1,0:T(8,128)(2,1)S(1)}, u32[]{:S(2)}, u32[]{:S(2)}) collective-permute-start(bf16[128,2048]{1,0:T(8,128)(2,1)S(1)} %get-tuple-element.80.refs_1_), channel_id=1, source_target_pairs={{1,0},{2,1},{3,2},{5,4},{6,5},{7,6},{9,8},{10,9},{11,10},{13,12},{... | collective-permute-start | bytes 1572872 | tf_op jit(solution)/shard_map/ppermute | solution.py:343
  33.6 44.6 %collective-permute-start.7 = (bf16[128,2048]{1,0:T(8,128)(2,1)S(1)}, bf16[128,2048]{1,0:T(8,128)(2,1)S(1)}, u32[]{:S(2)}, u32[]{:S(2)}) collective-permute-start(bf16[128,2048]{1,0:T(8,128)(2,1)S(1)} %get-tuple-element.80.refs_1_), channel_id=1, source_target_pairs={{0,1},{1,2},{2,3},{4,5},{5,6},{6,7},{8,9},{9,10},{10,11},{12,13},{... | collective-permute-start | bytes 1572872 | tf_op jit(solution)/shard_map/ppermute | solution.py:342
  61.9 12.1 %collective-permute-start.3 = (bf16[128,2048]{1,0:T(8,128)(2,1)S(1)}, bf16[128,2048]{1,0:T(8,128)(2,1)S(1)}, u32[]{:S(2)}, u32[]{:S(2)}) collective-permute-start(bf16[128,2048]{1,0:T(8,128)(2,1)S(1)} %get-tuple-element.73), channel_id=1, source_target_pairs={{0,1},{3,2},{4,5},{7,6},{8,9},{11,10},{12,13},{15,14},{16,17},{19,... | collective-permute-start | bytes 1572872 | tf_op jit(solution)/shard_map/ppermute | solution.py:349
  63.3 33.2 %collective-permute-start.6 = (bf16[128,2048]{1,0:T(8,128)(2,1)S(1)}, bf16[128,2048]{1,0:T(8,128)(2,1)S(1)}, u32[]{:S(2)}, u32[]{:S(2)}) collective-permute-start(bf16[128,2048]{1,0:T(8,128)(2,1)S(1)} %get-tuple-element.79), channel_id=1, source_target_pairs={{1,2},{2,1},{5,6},{6,5},{9,10},{10,9},{13,14},{14,13},{17,18},{18,... | collective-permute-start | bytes 1572872 | tf_op jit(solution)/shard_map/ppermute | solution.py:349
  64.0 14.2 %collective-permute-start.10 = (bf16[128,2048]{1,0:T(8,128)(2,1)S(1)}, bf16[128,2048]{1,0:T(8,128)(2,1)S(1)}, u32[]{:S(2)}, u32[]{:S(2)}) collective-permute-start(bf16[128,2048]{1,0:T(8,128)(2,1)S(1)} %collective-permute-done.9.refs_4_), channel_id=1, source_target_pairs={{2,3},{1,0},{6,7},{5,4},{10,11},{9,8},{14,15},{13,12},{18,19},{17,... | collective-permute-start | bytes 1572872 | tf_op jit(solution)/shard_map/ppermute | solution.py:344
  74.2 29.0 %collective-permute-start.4 = (bf16[128,2048]{1,0:T(8,128)(2,1)S(1)}, bf16[128,2048]{1,0:T(8,128)(2,1)S(1)}, u32[]{:S(2)}, u32[]{:S(2)}) collective-permute-start(bf16[128,2048]{1,0:T(8,128)(2,1)S(1)} %get-tuple-element.77), channel_id=1, source_target_pairs={{0,2},{1,3},{2,0},{3,1},{4,6},{5,7},{6,4},{7,5},{8,10},{9,11},{10,... | collective-permute-start | bytes 1572872 | tf_op jit(solution)/shard_map/ppermute | solution.py:332
  78.2 25.0 %collective-permute-start.5 = (bf16[128,2048]{1,0:T(8,128)(2,1)S(1)}, bf16[128,2048]{1,0:T(8,128)(2,1)S(1)}, u32[]{:S(2)}, u32[]{:S(2)}) collective-permute-start(bf16[128,2048]{1,0:T(8,128)(2,1)S(1)} %get-tuple-element.78), channel_id=1, source_target_pairs={{0,1},{1,0},{2,3},{3,2},{4,5},{5,4},{6,7},{7,6},{8,9},{9,8},{10,11... | collective-permute-start | bytes 1572872 | tf_op jit(solution)/shard_map/ppermute | solution.py:332
  80.3 3.5 %collective-permute-start.11 = (bf16[4,12,128,128]{3,2,1,0:T(8,128)(2,1)S(1)}, bf16[4,12,128,128]{3,2,1,0:T(8,128)(2,1)S(1)}, u32[]{:S(2)}, u32[]{:S(2)}) collective-permute-start(bf16[4,12,128,128]{3,2,1,0:T(8,128)(2,1)S(1)} %get-tuple-element.84), channel_id=1, source_target_pairs={{0,4},{4,0},{8,12},{12,8},{16,20},{20,16},{24,28},{28,24},{1,5},{5... | collective-permute-start | bytes 4718600 | tf_op jit(solution)/shard_map/ppermute | solution.py:360
  86.8 25.8 %collective-permute-start.13 = (bf16[128,2048]{1,0:T(8,128)(2,1)S(1)}, bf16[128,2048]{1,0:T(8,128)(2,1)S(1)}, u32[]{:S(2)}, u32[]{:S(2)}) collective-permute-start(bf16[128,2048]{1,0:T(8,128)(2,1)S(1)} %get-tuple-element.103), channel_id=1, source_target_pairs={{0,1},{1,0},{2,3},{3,2},{4,5},{5,4},{6,7},{7,6},{8,9},{9,8},{10,11... | collective-permute-start | bytes 1572872 | tf_op jit(solution)/shard_map/ppermute | solution.py:332
  89.5 12.0 %collective-permute-start.12 = (bf16[2,12,128,128]{3,2,1,0:T(8,128)(2,1)S(1)}, bf16[2,12,128,128]{3,2,1,0:T(8,128)(2,1)S(1)}, u32[]{:S(2)}, u32[]{:S(2)}) collective-permute-start(bf16[2,12,128,128]{3,2,1,0:T(8,128)(2,1)S(1)} %get-tuple-element.90), channel_id=1, source_target_pairs={{0,16},{4,12},{8,24},{12,4},{16,0},{20,28},{24,8},{28,20},{1,17},{... | collective-permute-start | bytes 2359304 | tf_op jit(solution)/shard_map/ppermute | solution.py:366
  96.5 2.2 %copy-start.6 = (bf16[128,2048]{1,0:T(8,128)(2,1)}, bf16[128,2048]{1,0:T(8,128)(2,1)S(1)}, u32[]{:S(2)}) copy-start(bf16[128,2048]{1,0:T(8,128)(2,1)S(1)} %get-tuple-element.101.refs_0_) | copy-start | bytes 1572868
  98.7 5.5 %collective-permute-start.15 = (bf16[4,12,128,128]{3,2,1,0:T(8,128)(2,1)S(1)}, bf16[4,12,128,128]{3,2,1,0:T(8,128)(2,1)S(1)}, u32[]{:S(2)}, u32[]{:S(2)}) collective-permute-start(bf16[4,12,128,128]{3,2,1,0:T(8,128)(2,1)S(1)} %get-tuple-element.108), channel_id=1, source_target_pairs={{0,4},{4,0},{8,12},{12,8},{16,20},{20,16},{24,28},{28,24},{1,5},{5... | collective-permute-start | bytes 4718600 | tf_op jit(solution)/shard_map/ppermute | solution.py:360
  101.6 8.7 %collective-permute-start.14 = (bf16[1,12,128,128]{3,2,1,0:T(8,128)(2,1)S(1)}, bf16[1,12,128,128]{3,2,1,0:T(8,128)(2,1)S(1)}, u32[]{:S(2)}, u32[]{:S(2)}) collective-permute-start(bf16[1,12,128,128]{3,2,1,0:T(8,128)(2,1)S(1)} %get-tuple-element.106), channel_id=1, source_target_pairs={{0,8},{4,20},{8,0},{12,28},{16,24},{20,4},{24,16},{28,12},{1,9},{5... | collective-permute-start | bytes 1179656 | tf_op jit(solution)/shard_map/ppermute | solution.py:366
  104.6 5.7 %copy-start = (f32[3,12,128,128]{3,2,1,0:T(8,128)S(1)}, f32[3,12,128,128]{3,2,1,0:T(8,128)}, u32[]{:S(2)}) copy-start(f32[3,12,128,128]{3,2,1,0:T(8,128)} %refs_3_.5) | copy-start | bytes 7077892
  104.6 5.7 %copy-start.1 = (f32[3,12,128,128]{3,2,1,0:T(8,128)S(1)}, f32[3,12,128,128]{3,2,1,0:T(8,128)}, u32[]{:S(2)}) copy-start(f32[3,12,128,128]{3,2,1,0:T(8,128)} %refs_4_.9) | copy-start | bytes 7077892
  106.8 12.1 %collective-permute-start.18 = (bf16[2,12,128,128]{3,2,1,0:T(8,128)(2,1)S(1)}, bf16[2,12,128,128]{3,2,1,0:T(8,128)(2,1)S(1)}, u32[]{:S(2)}, u32[]{:S(2)}) collective-permute-start(bf16[2,12,128,128]{3,2,1,0:T(8,128)(2,1)S(1)} %get-tuple-element.116), channel_id=1, source_target_pairs={{0,16},{4,12},{8,24},{12,4},{16,0},{20,28},{24,8},{28,20},{1,17},{... | collective-permute-start | bytes 2359304 | tf_op jit(solution)/shard_map/ppermute | solution.py:366
  108.4 6.2 %collective-permute-start.19 = (bf16[4,12,128,128]{3,2,1,0:T(8,128)(2,1)S(1)}, bf16[4,12,128,128]{3,2,1,0:T(8,128)(2,1)S(1)}, u32[]{:S(2)}, u32[]{:S(2)}) collective-permute-start(bf16[4,12,128,128]{3,2,1,0:T(8,128)(2,1)S(1)} %get-tuple-element.118), channel_id=1, source_target_pairs={{0,4},{4,0},{8,12},{12,8},{16,20},{20,16},{24,28},{28,24},{1,5},{5... | collective-permute-start | bytes 4718600 | tf_op jit(solution)/shard_map/ppermute | solution.py:360
  112.7 24.7 %collective-permute-start.16 = (bf16[128,2048]{1,0:T(8,128)(2,1)S(1)}, bf16[128,2048]{1,0:T(8,128)(2,1)S(1)}, u32[]{:S(2)}, u32[]{:S(2)}) collective-permute-start(bf16[128,2048]{1,0:T(8,128)(2,1)S(1)} %get-tuple-element.113), channel_id=1, source_target_pairs={{0,2},{1,3},{2,0},{3,1},{4,6},{5,7},{6,4},{7,5},{8,10},{9,11},{10,... | collective-permute-start | bytes 1572872 | tf_op jit(solution)/shard_map/ppermute | solution.py:332
  114.5 22.8 %collective-permute-start.17 = (bf16[128,2048]{1,0:T(8,128)(2,1)S(1)}, bf16[128,2048]{1,0:T(8,128)(2,1)S(1)}, u32[]{:S(2)}, u32[]{:S(2)}) collective-permute-start(bf16[128,2048]{1,0:T(8,128)(2,1)S(1)} %get-tuple-element.114), channel_id=1, source_target_pairs={{0,1},{1,0},{2,3},{3,2},{4,5},{5,4},{6,7},{7,6},{8,9},{9,8},{10,11... | collective-permute-start | bytes 1572872 | tf_op jit(solution)/shard_map/ppermute | solution.py:332
  114.9 16.6 %collective-permute-start.21 = (bf16[2,12,128,128]{3,2,1,0:T(8,128)(2,1)S(1)}, bf16[2,12,128,128]{3,2,1,0:T(8,128)(2,1)S(1)}, u32[]{:S(2)}, u32[]{:S(2)}) collective-permute-start(bf16[2,12,128,128]{3,2,1,0:T(8,128)(2,1)S(1)} %get-tuple-element.125), channel_id=1, source_target_pairs={{0,16},{4,12},{8,24},{12,4},{16,0},{20,28},{24,8},{28,20},{1,17},{... | collective-permute-start | bytes 2359304 | tf_op jit(solution)/shard_map/ppermute | solution.py:366
  119.0 13.9 %collective-permute-start.20 = (bf16[1,12,128,128]{3,2,1,0:T(8,128)(2,1)S(1)}, bf16[1,12,128,128]{3,2,1,0:T(8,128)(2,1)S(1)}, u32[]{:S(2)}, u32[]{:S(2)}) collective-permute-start(bf16[1,12,128,128]{3,2,1,0:T(8,128)(2,1)S(1)} %get-tuple-element.122), channel_id=1, source_target_pairs={{0,8},{4,20},{8,0},{12,28},{16,24},{20,4},{24,16},{28,12},{1,9},{5... | collective-permute-start | bytes 1179656 | tf_op jit(solution)/shard_map/ppermute | solution.py:366
  131.7 7.8 %collective-permute-start.22 = (bf16[1,12,128,128]{3,2,1,0:T(8,128)(2,1)S(1)}, bf16[1,12,128,128]{3,2,1,0:T(8,128)(2,1)S(1)}, u32[]{:S(2)}, u32[]{:S(2)}) collective-permute-start(bf16[1,12,128,128]{3,2,1,0:T(8,128)(2,1)S(1)} %get-tuple-element.131), channel_id=1, source_target_pairs={{0,8},{4,20},{8,0},{12,28},{16,24},{20,4},{24,16},{28,12},{1,9},{5... | collective-permute-start | bytes 1179656 | tf_op jit(solution)/shard_map/ppermute | solution.py:366
  133.0 4.4 %copy-start.7 = (bf16[128,2048]{1,0:T(8,128)(2,1)S(1)}, bf16[128,2048]{1,0:T(8,128)(2,1)}, u32[]{:S(2)}) copy-start(bf16[128,2048]{1,0:T(8,128)(2,1)} %copy-done.6) | copy-start | bytes 1572868
  (2 other events, 2.5 us)

commit v12 on v11

--- a/solution.py
+++ b/solution.py
@@ -8,7 +8,7 @@
 
 HB_DEV = 14
 EPSILON = 1e-08
-GROUPS = (32, 8)
+GROUPS = (32, 16)
 COST = 2 * 10**10
 VMEM_LIMIT = 32 * 1024 * 1024
 F32, BF16 = jnp.float32, jnp.bfloat16

time: 143 us -> 142 us (level)
  Pallas kernels: 42 us -> 40.5 us
    pallas_call x23, Pallas kernels: 42 us -> 40.5 us  [__call__(): pl.pallas_call(body, name=name, out_shape=[*outs, TOKEN], in_specs=[SMEM]...]
  transfers between devices with their start and end apart: 23 -> 23, of which waited for: 11 -> 12; matrix products, arithmetic and copies ran while one was open for 1% -> 1% of each run, Pallas kernels for 28% -> 27%
where the time goes in v12:
time: 142 us
  waiting for transfers between devices  60.7 us (43%)
  Pallas kernels  40.5 us (29%)
  starting transfers between devices  37.1 us (26%)
  local copies, waits for them, and re-layouts  1.77 us (1%)
    pallas_call x23, Pallas kernels, __call__(): pl.pallas_call(body, name=name, out_shape=[*outs, TOKEN], in_specs=[SMEM]...  40.5 us
    ppermute x9, waiting for transfers between devices, flip(): return lax.ppermute(v, 'tensor', [(a, a ^ bit) for a in range(shards)])  33.1 us
    ppermute x6, waiting for transfers between devices, axis_swap(): return lax.ppermute(v, 'dp', pairs)  19 us
    ppermute x9, starting transfers between devices, flip(): return lax.ppermute(v, 'tensor', [(a, a ^ bit) for a in range(shards)])  17.4 us
    ppermute x6, starting transfers between devices, axis_swap(): return lax.ppermute(v, 'dp', pairs)  9.64 us
    ppermute x1, waiting for transfers between devices, scatter_first(): lax.ppermute(parts[3], 'tensor', [(0, 1), (3, 2)])  7.54 us
    ppermute x1, starting transfers between devices, gather_line(): below = lax.ppermute(v, 'tensor', [(a, a + 1) for a in range(3)])  4.58 us
  transfers between devices with their start and end apart: 23, of which 12 were waited for; matrix products, arithmetic and copies ran while one was open for 1% of the time, Pallas kernels for 27%

profile of v12, /device:TPU:0, one launch (start us, length us, event | category | flops | bytes accessed | tf_op | source)
XLA Modules:
  0.0 141.6 jit_solution(13541079685500706845)
XLA Ops:
  0.6 4.1 %collective-permute-start.1 = (bf16[128,2048]{1,0:T(8,128)(2,1)}, bf16[128,2048]{1,0:T(8,128)(2,1)S(1)}, u32[]{:S(2)}, u32[]{:S(2)}) collective-permute-start(bf16[128,2048]{1,0:T(8,128)(2,1)} %refs_1_.3), channel_id=1, source_target_pairs={{0,2},{1,3},{2,0},{3,1},{4,6},{5,7},{6,4},{7,5},{8,10},{9,11},{10,... | collective-permute-start | bytes 1572872 | tf_op jit(solution)/shard_map/ppermute | solution.py:332
  4.7 1.6 %collective-permute-start = (bf16[128,2048]{1,0:T(8,128)(2,1)}, bf16[128,2048]{1,0:T(8,128)(2,1)S(1)}, u32[]{:S(2)}, u32[]{:S(2)}) collective-permute-start(bf16[128,2048]{1,0:T(8,128)(2,1)} %refs_1_.3), channel_id=1, source_target_pairs={{0,1},{1,0},{2,3},{3,2},{4,5},{5,4},{6,7},{7,6},{8,9},{9,8},{10,11... | collective-permute-start | bytes 1572872 | tf_op jit(solution)/shard_map/ppermute | solution.py:332
  8.0 5.7 %order.1 = (s32[194]{0:T(256)S(1)}, f32[8,128]{1,0:T(8,128)S(1)}) custom-call(s32[581]{0:T(1024)S(1)} %pad_add_fusion.refs_0_), custom_call_target="tpu_custom_call" | custom-call | flops 20000000000 | tf_op jit(solution)/shard_map/order/pallas_call | solution.py:317
  13.7 14.5 %collective-permute-done.1.refs_1_.refs_3_ = bf16[128,2048]{1,0:T(8,128)(2,1)S(1)} collective-permute-done((bf16[128,2048]{1,0:T(8,128)(2,1)}, bf16[128,2048]{1,0:T(8,128)(2,1)S(1)}, u32[]{:S(2)}, u32[]{:S(2)}) %collective-permute-start.1) | collective-permute-done | bytes 524320 | tf_op jit(solution)/shard_map/ppermute | solution.py:332
  29.0 3.3 %collective-permute-start.9 = (bf16[128,2048]{1,0:T(8,128)(2,1)S(1)}, bf16[128,2048]{1,0:T(8,128)(2,1)S(1)}, u32[]{:S(2)}, u32[]{:S(2)}) collective-permute-start(bf16[128,2048]{1,0:T(8,128)(2,1)S(1)} %get-tuple-element.80.refs_1_), channel_id=1, source_target_pairs={{0,2},{1,3},{2,0},{3,1},{4,6},{5,7},{6,4},{7,5},{8,10},{9,11},{10,... | collective-permute-start | bytes 1572872 | tf_op jit(solution)/shard_map/ppermute | solution.py:332
  33.6 4.6 %collective-permute-start.7 = (bf16[128,2048]{1,0:T(8,128)(2,1)S(1)}, bf16[128,2048]{1,0:T(8,128)(2,1)S(1)}, u32[]{:S(2)}, u32[]{:S(2)}) collective-permute-start(bf16[128,2048]{1,0:T(8,128)(2,1)S(1)} %get-tuple-element.80.refs_1_), channel_id=1, source_target_pairs={{0,1},{1,2},{2,3},{4,5},{5,6},{6,7},{8,9},{9,10},{10,11},{12,13},{... | collective-permute-start | bytes 1572872 | tf_op jit(solution)/shard_map/ppermute | solution.py:342
  38.2 15.5 %collective-permute-done.2.refs_4_ = bf16[128,2048]{1,0:T(8,128)(2,1)S(1)} collective-permute-done((bf16[128,2048]{1,0:T(8,128)(2,1)S(1)}, bf16[128,2048]{1,0:T(8,128)(2,1)S(1)}, u32[]{:S(2)}, u32[]{:S(2)}) %collective-permute-start.2) | collective-permute-done | bytes 524320 | tf_op jit(solution)/shard_map/ppermute | solution.py:332
  53.7 6.7 %forward.1 = (bf16[14,128,128]{2,1,0:T(8,128)(2,1)}, bf16[14,128,128]{2,1,0:T(8,128)(2,1)S(1)}, f32[14,128,128]{2,1,0:T(8,128)S(1)}, f32[14,128,128]{2,1,0:T(8,1...) custom-call(s32[581]{0:T(1024)S(1)} %pad_add_fusion.refs_0_, ...), custom_call_target="tpu_custom_call" | custom-call | flops 20000000000 | tf_op jit(solution)/shard_map/forward/pallas_call | solution.py:317
  61.2 2.0 %collective-permute-start.3 = (bf16[128,2048]{1,0:T(8,128)(2,1)S(1)}, bf16[128,2048]{1,0:T(8,128)(2,1)S(1)}, u32[]{:S(2)}, u32[]{:S(2)}) collective-permute-start(bf16[128,2048]{1,0:T(8,128)(2,1)S(1)} %get-tuple-element.73), channel_id=1, source_target_pairs={{0,1},{3,2},{4,5},{7,6},{8,9},{11,10},{12,13},{15,14},{16,17},{19,... | collective-permute-start | bytes 1572872 | tf_op jit(solution)/shard_map/ppermute | solution.py:349
  66.5 7.5 %collective-permute-done.3.refs_1_ = bf16[128,2048]{1,0:T(8,128)(2,1)S(1)} collective-permute-done((bf16[128,2048]{1,0:T(8,128)(2,1)S(1)}, bf16[128,2048]{1,0:T(8,128)(2,1)S(1)}, u32[]{:S(2)}, u32[]{:S(2)}) %collective-permute-start.3) | collective-permute-done | bytes 524320 | tf_op jit(solution)/shard_map/ppermute | solution.py:349
  74.2 4.1 %collective-permute-start.4 = (bf16[128,2048]{1,0:T(8,128)(2,1)S(1)}, bf16[128,2048]{1,0:T(8,128)(2,1)S(1)}, u32[]{:S(2)}, u32[]{:S(2)}) collective-permute-start(bf16[128,2048]{1,0:T(8,128)(2,1)S(1)} %get-tuple-element.77), channel_id=1, source_target_pairs={{0,2},{1,3},{2,0},{3,1},{4,6},{5,7},{6,4},{7,5},{8,10},{9,11},{10,... | collective-permute-start | bytes 1572872 | tf_op jit(solution)/shard_map/ppermute | solution.py:332
  78.3 2.0 %down_grads.1 = (bf16[4,12,128,128]{3,2,1,0:T(8,128)(2,1)S(1)}, bf16[4,12,128,128]{3,2,1,0:T(8,128)(2,1)S(1)}, f32[8,128]{1,0:T(8,128)S(1)}) custom-call(s32[581]{0:T(1024)S(1)} %pad_add_fusion.refs_0_, bf16[128,2048]{1,0:T(8,128)(2,1)S(1)} %get-tuple-element.80.refs_1_, bf16[128,2048]{1,0:T(8,128)(2,1)S(1)} %collective-permute-done.7.refs_2_, ...), custom_call_target="tpu_custom_call" | custom-call | flops 20000000000 | tf_op jit(solution)/shard_map/down_grads/pallas_call | solution.py:317
  80.4 2.4 %row_grads.1 = (bf16[14,128,128]{2,1,0:T(8,128)(2,1)S(1)}, bf16[14,128,128]{2,1,0:T(8,128)(2,1)S(1)}, f32[8,128]{1,0:T(8,128)S(1)}) custom-call(s32[581]{0:T(1024)S(1)} %pad_add_fusion.refs_0_, bf16[128,2048]{1,0:T(8,128)(2,1)S(1)} %get-tuple-element.80.refs_1_, bf16[128,2048]{1,0:T(8,128)(2,1)S(1)} %collective-permute-done.7.refs_2_, ...), custom_call_target="tpu_custom_call" | custom-call | flops 20000000000 | tf_op jit(solution)/shard_map/row_grads/pallas_call | solution.py:317
  84.1 2.8 %input_far.1 = (bf16[128,2048]{1,0:T(8,128)(2,1)S(1)}, f32[8,128]{1,0:T(8,128)S(1)}) custom-call(s32[581]{0:T(1024)S(1)} %pad_add_fusion.refs_0_, s32[194]{0:T(256)S(1)} %get-tuple-element.93.refs_1_, bf16[14,128,128]{2,1,0:T(8,128)(2,1)S(1)} %get-tuple-element.91.refs_2_.refs_1_, bf16[14,128,128]{2,1,0:T(8,128)(2,1)S(1)} %get-tuple-element.94.refs_3_.refs_1_, ...), custom_call_target="tpu_custom_call" | custom-call | flops 20000000000 | tf_op jit(solution)/shard_map/input_far/pallas_call | solution.py:317
  86.9 2.2 %collective-permute-start.13 = (bf16[128,2048]{1,0:T(8,128)(2,1)S(1)}, bf16[128,2048]{1,0:T(8,128)(2,1)S(1)}, u32[]{:S(2)}, u32[]{:S(2)}) collective-permute-start(bf16[128,2048]{1,0:T(8,128)(2,1)S(1)} %get-tuple-element.103), channel_id=1, source_target_pairs={{0,1},{1,0},{2,3},{3,2},{4,5},{5,4},{6,7},{7,6},{8,9},{9,8},{10,11... | collective-permute-start | bytes 1572872 | tf_op jit(solution)/shard_map/ppermute | solution.py:332
  89.1 1.5 %collective-permute-start.12 = (bf16[2,12,128,128]{3,2,1,0:T(8,128)(2,1)S(1)}, bf16[2,12,128,128]{3,2,1,0:T(8,128)(2,1)S(1)}, u32[]{:S(2)}, u32[]{:S(2)}) collective-permute-start(bf16[2,12,128,128]{3,2,1,0:T(8,128)(2,1)S(1)} %get-tuple-element.90), channel_id=1, source_target_pairs={{0,16},{4,12},{8,24},{12,4},{16,0},{20,28},{24,8},{28,20},{1,17},{... | collective-permute-start | bytes 2359304 | tf_op jit(solution)/shard_map/ppermute | solution.py:366
  90.6 5.4 %input_rest.1 = (bf16[128,2048]{1,0:T(8,128)(2,1)S(1)}, bf16[128,2048]{1,0:T(8,128)(2,1)S(1)}, bf16[128,2048]{1,0:T(8,128)(2,1)S(1)}, f32[8,128]{1,0:T(8,128)S(1)}) custom-call(s32[581]{0:T(1024)S(1)} %pad_add_fusion.refs_0_, s32[194]{0:T(256)S(1)} %get-tuple-element.93.refs_1_, bf16[14,128,128]{2,1,0:T(8,128)(2,1)S(1)} %get-tuple-element.91.refs_2_.refs_1_, ...), custom_call_target="tpu_custom_call" | custom-call | flops 20000000000 | tf_op jit(solution)/shard_map/input_rest/pallas_call | solution.py:317
  96.1 2.2 %gate_grads.1 = (bf16[4,12,128,128]{3,2,1,0:T(8,128)(2,1)S(1)}, bf16[4,12,128,128]{3,2,1,0:T(8,128)(2,1)S(1)}, f32[8,128]{1,0:T(8,128)S(1)}) custom-call(s32[581]{0:T(1024)S(1)} %pad_add_fusion.refs_0_, bf16[14,128,128]{2,1,0:T(8,128)(2,1)S(1)} %get-tuple-element.91.refs_2_.refs_1_, bf16[64,128,128]{2,1,0:T(8,128)(2,1)S(1)} %get-tuple-element.92.refs_2_, ...), custom_call_target="tpu_custom_call" | custom-call | flops 20000000000 | tf_op jit(solution)/shard_map/gate_grads/pallas_call | solution.py:317
  98.3 2.7 %collective-permute-done.12.refs_1_ = bf16[2,12,128,128]{3,2,1,0:T(8,128)(2,1)S(1)} collective-permute-done((bf16[2,12,128,128]{3,2,1,0:T(8,128)(2,1)S(1)}, bf16[2,12,128,128]{3,2,1,0:T(8,128)(2,1)S(1)}, u32[]{:S(2)}, u32[]{:S(2)}) %collective-permute-start.12) | collective-permute-done | bytes 786464 | tf_op jit(solution)/shard_map/ppermute | solution.py:366
  101.3 1.6 %collective-permute-start.14 = (bf16[1,12,128,128]{3,2,1,0:T(8,128)(2,1)S(1)}, bf16[1,12,128,128]{3,2,1,0:T(8,128)(2,1)S(1)}, u32[]{:S(2)}, u32[]{:S(2)}) collective-permute-start(bf16[1,12,128,128]{3,2,1,0:T(8,128)(2,1)S(1)} %get-tuple-element.106), channel_id=1, source_target_pairs={{0,8},{4,20},{8,0},{12,28},{16,24},{20,4},{24,16},{28,12},{1,9},{5... | collective-permute-start | bytes 1179656 | tf_op jit(solution)/shard_map/ppermute | solution.py:366
  104.7 2.2 %up_grads.1 = (bf16[4,12,128,128]{3,2,1,0:T(8,128)(2,1)S(1)}, bf16[4,12,128,128]{3,2,1,0:T(8,128)(2,1)S(1)}, f32[8,128]{1,0:T(8,128)S(1)}) custom-call(s32[581]{0:T(1024)S(1)} %pad_add_fusion.refs_0_, bf16[14,128,128]{2,1,0:T(8,128)(2,1)S(1)} %get-tuple-element.94.refs_3_.refs_1_, bf16[64,128,128]{2,1,0:T(8,128)(2,1)S(1)} %get-tuple-element.92.refs_2_, ...), custom_call_target="tpu_custom_call" | custom-call | flops 20000000000 | tf_op jit(solution)/shard_map/up_grads/pallas_call | solution.py:317
  106.9 1.7 %collective-permute-start.18 = (bf16[2,12,128,128]{3,2,1,0:T(8,128)(2,1)S(1)}, bf16[2,12,128,128]{3,2,1,0:T(8,128)(2,1)S(1)}, u32[]{:S(2)}, u32[]{:S(2)}) collective-permute-start(bf16[2,12,128,128]{3,2,1,0:T(8,128)(2,1)S(1)} %get-tuple-element.116), channel_id=1, source_target_pairs={{0,16},{4,12},{8,24},{12,4},{16,0},{20,28},{24,8},{28,20},{1,17},{... | collective-permute-start | bytes 2359304 | tf_op jit(solution)/shard_map/ppermute | solution.py:366
  108.6 1.4 collective-permute-done.14.refs_2_
  110.0 2.0 %update.3 = (f32[3,12,128,128]{3,2,1,0:T(8,128)}, f32[8,128]{1,0:T(8,128)S(1)}) custom-call(s32[581]{0:T(1024)S(1)} %pad_add_fusion.refs_0_, bf16[1,12,128,128]{3,2,1,0:T(8,128)(2,1)S(1)} %get-tuple-element.105.refs_1_, bf16[1,12,128,128]{3,2,1,0:T(8,128)(2,1)S(1)} %collective-permute-done.14.refs_2_, f32[3,12,128,128]{3,2,1,0:T(8,128)S(1)} %copy-done, ...), custom_call_target="tpu_custom_call" | custom-call | flops 20000000000 | tf_op jit(solution)/shard_map/update/pallas_call | solution.py:317
  114.7 1.6 %collective-permute-start.21 = (bf16[2,12,128,128]{3,2,1,0:T(8,128)(2,1)S(1)}, bf16[2,12,128,128]{3,2,1,0:T(8,128)(2,1)S(1)}, u32[]{:S(2)}, u32[]{:S(2)}) collective-permute-start(bf16[2,12,128,128]{3,2,1,0:T(8,128)(2,1)S(1)} %get-tuple-element.125), channel_id=1, source_target_pairs={{0,16},{4,12},{8,24},{12,4},{16,0},{20,28},{24,8},{28,20},{1,17},{... | collective-permute-start | bytes 2359304 | tf_op jit(solution)/shard_map/ppermute | solution.py:366
  116.2 2.7 %collective-permute-done.18.refs_1_ = bf16[2,12,128,128]{3,2,1,0:T(8,128)(2,1)S(1)} collective-permute-done((bf16[2,12,128,128]{3,2,1,0:T(8,128)(2,1)S(1)}, bf16[2,12,128,128]{3,2,1,0:T(8,128)(2,1)S(1)}, u32[]{:S(2)}, u32[]{:S(2)}) %collective-permute-start.18) | collective-permute-done | bytes 786464 | tf_op jit(solution)/shard_map/ppermute | solution.py:366
  119.1 1.6 %collective-permute-start.20 = (bf16[1,12,128,128]{3,2,1,0:T(8,128)(2,1)S(1)}, bf16[1,12,128,128]{3,2,1,0:T(8,128)(2,1)S(1)}, u32[]{:S(2)}, u32[]{:S(2)}) collective-permute-start(bf16[1,12,128,128]{3,2,1,0:T(8,128)(2,1)S(1)} %get-tuple-element.122), channel_id=1, source_target_pairs={{0,8},{4,20},{8,0},{12,28},{16,24},{20,4},{24,16},{28,12},{1,9},{5... | collective-permute-start | bytes 1179656 | tf_op jit(solution)/shard_map/ppermute | solution.py:366
  120.7 10.8 %collective-permute-done.21.refs_1_ = bf16[2,12,128,128]{3,2,1,0:T(8,128)(2,1)S(1)} collective-permute-done((bf16[2,12,128,128]{3,2,1,0:T(8,128)(2,1)S(1)}, bf16[2,12,128,128]{3,2,1,0:T(8,128)(2,1)S(1)}, u32[]{:S(2)}, u32[]{:S(2)}) %collective-permute-start.21) | collective-permute-done | bytes 786464 | tf_op jit(solution)/shard_map/ppermute | solution.py:366
  131.7 1.6 %collective-permute-start.22 = (bf16[1,12,128,128]{3,2,1,0:T(8,128)(2,1)S(1)}, bf16[1,12,128,128]{3,2,1,0:T(8,128)(2,1)S(1)}, u32[]{:S(2)}, u32[]{:S(2)}) collective-permute-start(bf16[1,12,128,128]{3,2,1,0:T(8,128)(2,1)S(1)} %get-tuple-element.131), channel_id=1, source_target_pairs={{0,8},{4,20},{8,0},{12,28},{16,24},{20,4},{24,16},{28,12},{1,9},{5... | collective-permute-start | bytes 1179656 | tf_op jit(solution)/shard_map/ppermute | solution.py:366
  133.4 2.0 %update.4 = (f32[3,12,128,128]{3,2,1,0:T(8,128)}, f32[8,128]{1,0:T(8,128)S(1)}) custom-call(s32[581]{0:T(1024)S(1)} %pad_add_fusion.refs_0_, bf16[1,12,128,128]{3,2,1,0:T(8,128)(2,1)S(1)} %get-tuple-element.121.refs_1_, bf16[1,12,128,128]{3,2,1,0:T(8,128)(2,1)S(1)} %collective-permute-done.20.refs_2_, ...), custom_call_target="tpu_custom_call", output_to_operand_aliasing={{0}: (5, {})} | custom-call | flops 20000000000 | tf_op jit(solution)/shard_map/update/pallas_call | solution.py:317
  135.4 1.9 %collective-permute-done.16.refs_1_ = bf16[128,2048]{1,0:T(8,128)(2,1)S(1)} collective-permute-done((bf16[128,2048]{1,0:T(8,128)(2,1)S(1)}, bf16[128,2048]{1,0:T(8,128)(2,1)S(1)}, u32[]{:S(2)}, u32[]{:S(2)}) %collective-permute-start.16) | collective-permute-done | bytes 524320 | tf_op jit(solution)/shard_map/ppermute | solution.py:332
  139.6 2.0 %update.5 = (f32[3,12,128,128]{3,2,1,0:T(8,128)}, f32[8,128]{1,0:T(8,128)}) custom-call(s32[581]{0:T(1024)S(1)} %pad_add_fusion.refs_0_, bf16[1,12,128,128]{3,2,1,0:T(8,128)(2,1)S(1)} %get-tuple-element.130.refs_1_, bf16[1,12,128,128]{3,2,1,0:T(8,128)(2,1)S(1)} %collective-permute-done.22.refs_2_, ...), custom_call_target="tpu_custom_call", output_to_operand_aliasing={{0}: (5, {})} | custom-call | flops 20000000000 | tf_op jit(solution)/shard_map/update/pallas_call | solution.py:317
  (63 shorter events, 16.8 us)
Async XLA Ops:
  0.6 27.6 %collective-permute-start.1 = (bf16[128,2048]{1,0:T(8,128)(2,1)}, bf16[128,2048]{1,0:T(8,128)(2,1)S(1)}, u32[]{:S(2)}, u32[]{:S(2)}) collective-permute-start(bf16[128,2048]{1,0:T(8,128)(2,1)} %refs_1_.3), channel_id=1, source_target_pairs={{0,2},{1,3},{2,0},{3,1},{4,6},{5,7},{6,4},{7,5},{8,10},{9,11},{10,... | collective-permute-start | bytes 1572872 | tf_op jit(solution)/shard_map/ppermute | solution.py:332
  4.7 33.5 %collective-permute-start = (bf16[128,2048]{1,0:T(8,128)(2,1)}, bf16[128,2048]{1,0:T(8,128)(2,1)S(1)}, u32[]{:S(2)}, u32[]{:S(2)}) collective-permute-start(bf16[128,2048]{1,0:T(8,128)(2,1)} %refs_1_.3), channel_id=1, source_target_pairs={{0,1},{1,0},{2,3},{3,2},{4,5},{5,4},{6,7},{7,6},{8,9},{9,8},{10,11... | collective-permute-start | bytes 1572872 | tf_op jit(solution)/shard_map/ppermute | solution.py:332
  8.0 20.9 %copy-start.2 = (bf16[128,2048]{1,0:T(8,128)(2,1)S(1)}, bf16[128,2048]{1,0:T(8,128)(2,1)}, u32[]{:S(2)}) copy-start(bf16[128,2048]{1,0:T(8,128)(2,1)} %refs_0_.1) | copy-start | bytes 1572868
  8.0 45.7 %slice-start = ((s8[9437184]{0:T(1024)(128)(4,1)}), s8[4194304]{0:T(1024)(128)(4,1)S(1)}, s32[]{:S(2)}) async-start(s8[9437184]{0:T(1024)(128)(4,1)} %bitcast.3), calls=%async_computation | async-start | bytes 8388608
  8.0 45.7 %slice-start.1 = ((s8[9437184]{0:T(1024)(128)(4,1)}), s8[4194304]{0:T(1024)(128)(4,1)S(1)}, s32[]{:S(2)}) async-start(s8[9437184]{0:T(1024)(128)(4,1)} %bitcast.3), calls=%async_computation.1 | async-start | bytes 8388608
  28.2 25.5 %collective-permute-start.2 = (bf16[128,2048]{1,0:T(8,128)(2,1)S(1)}, bf16[128,2048]{1,0:T(8,128)(2,1)S(1)}, u32[]{:S(2)}, u32[]{:S(2)}) collective-permute-start(bf16[128,2048]{1,0:T(8,128)(2,1)S(1)} %collective-permute-done.1.refs_1_.refs_3_), channel_id=1, source_target_pairs={{0,1},{1,0},{2,3},{3,2},{4,5},{5,4},{6,7},{7,6},{8,9},{9,8},{10,11... | collective-permute-start | bytes 1572872 | tf_op jit(solution)/shard_map/ppermute | solution.py:332
  28.9 24.7 %slice-start.2 = ((s8[9437184]{0:T(1024)(128)(4,1)}), s8[1048576]{0:T(1024)(128)(4,1)S(1)}, s32[]{:S(2)}) async-start(s8[9437184]{0:T(1024)(128)(4,1)} %bitcast.3), calls=%async_computation.2 | async-start | bytes 2097152
  28.9 24.7 %copy-start.3 = (bf16[128,2048]{1,0:T(8,128)(2,1)S(1)}, bf16[128,2048]{1,0:T(8,128)(2,1)}, u32[]{:S(2)}) copy-start(bf16[128,2048]{1,0:T(8,128)(2,1)} %refs_1_.3) | copy-start | bytes 1572868
  29.0 34.9 %collective-permute-start.9 = (bf16[128,2048]{1,0:T(8,128)(2,1)S(1)}, bf16[128,2048]{1,0:T(8,128)(2,1)S(1)}, u32[]{:S(2)}, u32[]{:S(2)}) collective-permute-start(bf16[128,2048]{1,0:T(8,128)(2,1)S(1)} %get-tuple-element.80.refs_1_), channel_id=1, source_target_pairs={{0,2},{1,3},{2,0},{3,1},{4,6},{5,7},{6,4},{7,5},{8,10},{9,11},{10,... | collective-permute-start | bytes 1572872 | tf_op jit(solution)/shard_map/ppermute | solution.py:332
  32.3 45.9 %collective-permute-start.8 = (bf16[128,2048]{1,0:T(8,128)(2,1)S(1)}, bf16[128,2048]{1,0:T(8,128)(2,1)S(1)}, u32[]{:S(2)}, u32[]{:S(2)}) collective-permute-start(bf16[128,2048]{1,0:T(8,128)(2,1)S(1)} %get-tuple-element.80.refs_1_), channel_id=1, source_target_pairs={{1,0},{2,1},{3,2},{5,4},{6,5},{7,6},{9,8},{10,9},{11,10},{13,12},{... | collective-permute-start | bytes 1572872 | tf_op jit(solution)/shard_map/ppermute | solution.py:343
  33.6 44.6 %collective-permute-start.7 = (bf16[128,2048]{1,0:T(8,128)(2,1)S(1)}, bf16[128,2048]{1,0:T(8,128)(2,1)S(1)}, u32[]{:S(2)}, u32[]{:S(2)}) collective-permute-start(bf16[128,2048]{1,0:T(8,128)(2,1)S(1)} %get-tuple-element.80.refs_1_), channel_id=1, source_target_pairs={{0,1},{1,2},{2,3},{4,5},{5,6},{6,7},{8,9},{9,10},{10,11},{12,13},{... | collective-permute-start | bytes 1572872 | tf_op jit(solution)/shard_map/ppermute | solution.py:342
  61.2 12.9 %collective-permute-start.3 = (bf16[128,2048]{1,0:T(8,128)(2,1)S(1)}, bf16[128,2048]{1,0:T(8,128)(2,1)S(1)}, u32[]{:S(2)}, u32[]{:S(2)}) collective-permute-start(bf16[128,2048]{1,0:T(8,128)(2,1)S(1)} %get-tuple-element.73), channel_id=1, source_target_pairs={{0,1},{3,2},{4,5},{7,6},{8,9},{11,10},{12,13},{15,14},{16,17},{19,... | collective-permute-start | bytes 1572872 | tf_op jit(solution)/shard_map/ppermute | solution.py:349
  63.2 32.9 %collective-permute-start.6 = (bf16[128,2048]{1,0:T(8,128)(2,1)S(1)}, bf16[128,2048]{1,0:T(8,128)(2,1)S(1)}, u32[]{:S(2)}, u32[]{:S(2)}) collective-permute-start(bf16[128,2048]{1,0:T(8,128)(2,1)S(1)} %get-tuple-element.79), channel_id=1, source_target_pairs={{1,2},{2,1},{5,6},{6,5},{9,10},{10,9},{13,14},{14,13},{17,18},{18,... | collective-permute-start | bytes 1572872 | tf_op jit(solution)/shard_map/ppermute | solution.py:349
  63.9 14.4 %collective-permute-start.10 = (bf16[128,2048]{1,0:T(8,128)(2,1)S(1)}, bf16[128,2048]{1,0:T(8,128)(2,1)S(1)}, u32[]{:S(2)}, u32[]{:S(2)}) collective-permute-start(bf16[128,2048]{1,0:T(8,128)(2,1)S(1)} %collective-permute-done.9.refs_4_), channel_id=1, source_target_pairs={{2,3},{1,0},{6,7},{5,4},{10,11},{9,8},{14,15},{13,12},{18,19},{17,... | collective-permute-start | bytes 1572872 | tf_op jit(solution)/shard_map/ppermute | solution.py:344
  74.2 28.7 %collective-permute-start.4 = (bf16[128,2048]{1,0:T(8,128)(2,1)S(1)}, bf16[128,2048]{1,0:T(8,128)(2,1)S(1)}, u32[]{:S(2)}, u32[]{:S(2)}) collective-permute-start(bf16[128,2048]{1,0:T(8,128)(2,1)S(1)} %get-tuple-element.77), channel_id=1, source_target_pairs={{0,2},{1,3},{2,0},{3,1},{4,6},{5,7},{6,4},{7,5},{8,10},{9,11},{10,... | collective-permute-start | bytes 1572872 | tf_op jit(solution)/shard_map/ppermute | solution.py:332
  78.2 25.0 %collective-permute-start.5 = (bf16[128,2048]{1,0:T(8,128)(2,1)S(1)}, bf16[128,2048]{1,0:T(8,128)(2,1)S(1)}, u32[]{:S(2)}, u32[]{:S(2)}) collective-permute-start(bf16[128,2048]{1,0:T(8,128)(2,1)S(1)} %get-tuple-element.78), channel_id=1, source_target_pairs={{0,1},{1,0},{2,3},{3,2},{4,5},{5,4},{6,7},{7,6},{8,9},{9,8},{10,11... | collective-permute-start | bytes 1572872 | tf_op jit(solution)/shard_map/ppermute | solution.py:332
  80.3 3.5 %collective-permute-start.11 = (bf16[4,12,128,128]{3,2,1,0:T(8,128)(2,1)S(1)}, bf16[4,12,128,128]{3,2,1,0:T(8,128)(2,1)S(1)}, u32[]{:S(2)}, u32[]{:S(2)}) collective-permute-start(bf16[4,12,128,128]{3,2,1,0:T(8,128)(2,1)S(1)} %get-tuple-element.84), channel_id=1, source_target_pairs={{0,4},{4,0},{8,12},{12,8},{16,20},{20,16},{24,28},{28,24},{1,5},{5... | collective-permute-start | bytes 4718600 | tf_op jit(solution)/shard_map/ppermute | solution.py:360
  86.9 25.9 %collective-permute-start.13 = (bf16[128,2048]{1,0:T(8,128)(2,1)S(1)}, bf16[128,2048]{1,0:T(8,128)(2,1)S(1)}, u32[]{:S(2)}, u32[]{:S(2)}) collective-permute-start(bf16[128,2048]{1,0:T(8,128)(2,1)S(1)} %get-tuple-element.103), channel_id=1, source_target_pairs={{0,1},{1,0},{2,3},{3,2},{4,5},{5,4},{6,7},{7,6},{8,9},{9,8},{10,11... | collective-permute-start | bytes 1572872 | tf_op jit(solution)/shard_map/ppermute | solution.py:332
  89.1 12.0 %collective-permute-start.12 = (bf16[2,12,128,128]{3,2,1,0:T(8,128)(2,1)S(1)}, bf16[2,12,128,128]{3,2,1,0:T(8,128)(2,1)S(1)}, u32[]{:S(2)}, u32[]{:S(2)}) collective-permute-start(bf16[2,12,128,128]{3,2,1,0:T(8,128)(2,1)S(1)} %get-tuple-element.90), channel_id=1, source_target_pairs={{0,16},{4,12},{8,24},{12,4},{16,0},{20,28},{24,8},{28,20},{1,17},{... | collective-permute-start | bytes 2359304 | tf_op jit(solution)/shard_map/ppermute | solution.py:366
  98.3 6.1 %collective-permute-start.15 = (bf16[4,12,128,128]{3,2,1,0:T(8,128)(2,1)S(1)}, bf16[4,12,128,128]{3,2,1,0:T(8,128)(2,1)S(1)}, u32[]{:S(2)}, u32[]{:S(2)}) collective-permute-start(bf16[4,12,128,128]{3,2,1,0:T(8,128)(2,1)S(1)} %get-tuple-element.108), channel_id=1, source_target_pairs={{0,4},{4,0},{8,12},{12,8},{16,20},{20,16},{24,28},{28,24},{1,5},{5... | collective-permute-start | bytes 4718600 | tf_op jit(solution)/shard_map/ppermute | solution.py:360
  101.1 2.2 %copy-start.5 = (bf16[128,2048]{1,0:T(8,128)(2,1)S(1)}, bf16[128,2048]{1,0:T(8,128)(2,1)}, u32[]{:S(2)}) copy-start(bf16[128,2048]{1,0:T(8,128)(2,1)} %copy-done.4) | copy-start | bytes 1572868
  101.3 8.7 %collective-permute-start.14 = (bf16[1,12,128,128]{3,2,1,0:T(8,128)(2,1)S(1)}, bf16[1,12,128,128]{3,2,1,0:T(8,128)(2,1)S(1)}, u32[]{:S(2)}, u32[]{:S(2)}) collective-permute-start(bf16[1,12,128,128]{3,2,1,0:T(8,128)(2,1)S(1)} %get-tuple-element.106), channel_id=1, source_target_pairs={{0,8},{4,20},{8,0},{12,28},{16,24},{20,4},{24,16},{28,12},{1,9},{5... | collective-permute-start | bytes 1179656 | tf_op jit(solution)/shard_map/ppermute | solution.py:366
  104.7 5.3 %copy-start = (f32[3,12,128,128]{3,2,1,0:T(8,128)S(1)}, f32[3,12,128,128]{3,2,1,0:T(8,128)}, u32[]{:S(2)}) copy-start(f32[3,12,128,128]{3,2,1,0:T(8,128)} %refs_3_.5) | copy-start | bytes 7077892
  104.7 5.3 %copy-start.1 = (f32[3,12,128,128]{3,2,1,0:T(8,128)S(1)}, f32[3,12,128,128]{3,2,1,0:T(8,128)}, u32[]{:S(2)}) copy-start(f32[3,12,128,128]{3,2,1,0:T(8,128)} %refs_4_.9) | copy-start | bytes 7077892
  106.9 12.1 %collective-permute-start.18 = (bf16[2,12,128,128]{3,2,1,0:T(8,128)(2,1)S(1)}, bf16[2,12,128,128]{3,2,1,0:T(8,128)(2,1)S(1)}, u32[]{:S(2)}, u32[]{:S(2)}) collective-permute-start(bf16[2,12,128,128]{3,2,1,0:T(8,128)(2,1)S(1)} %get-tuple-element.116), channel_id=1, source_target_pairs={{0,16},{4,12},{8,24},{12,4},{16,0},{20,28},{24,8},{28,20},{1,17},{... | collective-permute-start | bytes 2359304 | tf_op jit(solution)/shard_map/ppermute | solution.py:366
  108.5 5.8 %collective-permute-start.19 = (bf16[4,12,128,128]{3,2,1,0:T(8,128)(2,1)S(1)}, bf16[4,12,128,128]{3,2,1,0:T(8,128)(2,1)S(1)}, u32[]{:S(2)}, u32[]{:S(2)}) collective-permute-start(bf16[4,12,128,128]{3,2,1,0:T(8,128)(2,1)S(1)} %get-tuple-element.118), channel_id=1, source_target_pairs={{0,4},{4,0},{8,12},{12,8},{16,20},{20,16},{24,28},{28,24},{1,5},{5... | collective-permute-start | bytes 4718600 | tf_op jit(solution)/shard_map/ppermute | solution.py:360
  112.9 24.4 %collective-permute-start.16 = (bf16[128,2048]{1,0:T(8,128)(2,1)S(1)}, bf16[128,2048]{1,0:T(8,128)(2,1)S(1)}, u32[]{:S(2)}, u32[]{:S(2)}) collective-permute-start(bf16[128,2048]{1,0:T(8,128)(2,1)S(1)} %get-tuple-element.113), channel_id=1, source_target_pairs={{0,2},{1,3},{2,0},{3,1},{4,6},{5,7},{6,4},{7,5},{8,10},{9,11},{10,... | collective-permute-start | bytes 1572872 | tf_op jit(solution)/shard_map/ppermute | solution.py:332
  113.0 24.3 %collective-permute-start.17 = (bf16[128,2048]{1,0:T(8,128)(2,1)S(1)}, bf16[128,2048]{1,0:T(8,128)(2,1)S(1)}, u32[]{:S(2)}, u32[]{:S(2)}) collective-permute-start(bf16[128,2048]{1,0:T(8,128)(2,1)S(1)} %get-tuple-element.114), channel_id=1, source_target_pairs={{0,1},{1,0},{2,3},{3,2},{4,5},{5,4},{6,7},{7,6},{8,9},{9,8},{10,11... | collective-permute-start | bytes 1572872 | tf_op jit(solution)/shard_map/ppermute | solution.py:332
  114.7 16.9 %collective-permute-start.21 = (bf16[2,12,128,128]{3,2,1,0:T(8,128)(2,1)S(1)}, bf16[2,12,128,128]{3,2,1,0:T(8,128)(2,1)S(1)}, u32[]{:S(2)}, u32[]{:S(2)}) collective-permute-start(bf16[2,12,128,128]{3,2,1,0:T(8,128)(2,1)S(1)} %get-tuple-element.125), channel_id=1, source_target_pairs={{0,16},{4,12},{8,24},{12,4},{16,0},{20,28},{24,8},{28,20},{1,17},{... | collective-permute-start | bytes 2359304 | tf_op jit(solution)/shard_map/ppermute | solution.py:366
  119.1 14.3 %collective-permute-start.20 = (bf16[1,12,128,128]{3,2,1,0:T(8,128)(2,1)S(1)}, bf16[1,12,128,128]{3,2,1,0:T(8,128)(2,1)S(1)}, u32[]{:S(2)}, u32[]{:S(2)}) collective-permute-start(bf16[1,12,128,128]{3,2,1,0:T(8,128)(2,1)S(1)} %get-tuple-element.122), channel_id=1, source_target_pairs={{0,8},{4,20},{8,0},{12,28},{16,24},{20,4},{24,16},{28,12},{1,9},{5... | collective-permute-start | bytes 1179656 | tf_op jit(solution)/shard_map/ppermute | solution.py:366
  131.7 7.8 %collective-permute-start.22 = (bf16[1,12,128,128]{3,2,1,0:T(8,128)(2,1)S(1)}, bf16[1,12,128,128]{3,2,1,0:T(8,128)(2,1)S(1)}, u32[]{:S(2)}, u32[]{:S(2)}) collective-permute-start(bf16[1,12,128,128]{3,2,1,0:T(8,128)(2,1)S(1)} %get-tuple-element.131), channel_id=1, source_target_pairs={{0,8},{4,20},{8,0},{12,28},{16,24},{20,4},{24,16},{28,12},{1,9},{5... | collective-permute-start | bytes 1179656 | tf_op jit(solution)/shard_map/ppermute | solution.py:366
  133.4 3.9 %copy-start.7 = (bf16[128,2048]{1,0:T(8,128)(2,1)S(1)}, bf16[128,2048]{1,0:T(8,128)(2,1)}, u32[]{:S(2)}) copy-start(bf16[128,2048]{1,0:T(8,128)(2,1)} %copy-done.6) | copy-start | bytes 1572868
  (2 other events, 3.0 us)

commit v13 on v11

--- a/solution.py
+++ b/solution.py
@@ -469,6 +469,7 @@
             functools.partial(input_part_kernel, True), "input_far", [piece], [part_total], in_operands, (*plan, order)
         )
         in_far = flip(in_far, 4, 1)
+    gate = grads(0, [gate_rows], x_turned, out_far[1:] if lined else ())
     if lined:
         in_parts = line(
             functools.partial(input_part_kernel, False), "input_rest", [piece] * 3, [total], in_operands, (*plan, order)
@@ -478,7 +479,6 @@
             functools.partial(input_kernel, 1), "input_grads", in_parts, [total], [gate_rows, up_rows, weights], plan
         )
         input_grad = lax.psum_scatter(in_parts[0], "tensor", scatter_dimension=0)
-    gate = grads(0, [gate_rows], x_turned, out_far[1:] if lined else ())
     for step in range(1, levels):
         down = fold(*down, step)
     if lined:

time: 143 us -> 142 us (level); the launches traced: 142 us -> 143 us
  Pallas kernels: 42 us -> 38.8 us
  waiting for transfers between devices: 59.4 us -> 62.5 us
  starting transfers between devices: 36.8 us -> 38.7 us
    pallas_call x23, Pallas kernels: 42 us -> 38.8 us  [__call__(): pl.pallas_call(body, name=name, out_shape=[*outs, TOKEN], in_specs=[SMEM]...]
    ppermute x1, starting transfers between devices: 1.37 us -> 3.08 us  [scatter_first(): lax.ppermute(parts[3], 'tensor', [(0, 1), (3, 2)])]
  transfers between devices with their start and end apart: 23 -> 23, of which waited for: 11 -> 12; matrix products, arithmetic and copies ran while one was open for 1% -> 1% of each run, Pallas kernels for 28% -> 26%
where the time goes in v13:
time: 142 us; the launch traced here: 143 us
  waiting for transfers between devices  62.5 us (44%)
  Pallas kernels  38.8 us (27%)
  starting transfers between devices  38.7 us (27%)
    pallas_call x23, Pallas kernels, __call__(): pl.pallas_call(body, name=name, out_shape=[*outs, TOKEN], in_specs=[SMEM]...  38.8 us
    ppermute x9, waiting for transfers between devices, flip(): return lax.ppermute(v, 'tensor', [(a, a ^ bit) for a in range(shards)])  33.8 us
    ppermute x6, waiting for transfers between devices, axis_swap(): return lax.ppermute(v, 'dp', pairs)  20.2 us
    ppermute x9, starting transfers between devices, flip(): return lax.ppermute(v, 'tensor', [(a, a ^ bit) for a in range(shards)])  18 us
    ppermute x6, starting transfers between devices, axis_swap(): return lax.ppermute(v, 'dp', pairs)  9.6 us
    ppermute x1, waiting for transfers between devices, scatter_first(): lax.ppermute(parts[3], 'tensor', [(0, 1), (3, 2)])  7.21 us
    ppermute x1, starting transfers between devices, gather_line(): below = lax.ppermute(v, 'tensor', [(a, a + 1) for a in range(3)])  4.58 us
    ppermute x1, starting transfers between devices, scatter_first(): lax.ppermute(parts[3], 'tensor', [(0, 1), (3, 2)])  3.08 us
  transfers between devices with their start and end apart: 23, of which 12 were waited for; matrix products, arithmetic and copies ran while one was open for 1% of the time, Pallas kernels for 26%

profile of v13, /device:TPU:0, one launch (start us, length us, event | category | flops | bytes accessed | tf_op | source)
XLA Modules:
  0.0 142.6 jit_solution(8714586328195100843)
XLA Ops:
  0.6 4.1 %collective-permute-start.1 = (bf16[128,2048]{1,0:T(8,128)(2,1)}, bf16[128,2048]{1,0:T(8,128)(2,1)S(1)}, u32[]{:S(2)}, u32[]{:S(2)}) collective-permute-start(bf16[128,2048]{1,0:T(8,128)(2,1)} %refs_1_.3), channel_id=1, source_target_pairs={{0,2},{1,3},{2,0},{3,1},{4,6},{5,7},{6,4},{7,5},{8,10},{9,11},{10,... | collective-permute-start | bytes 1572872 | tf_op jit(solution)/shard_map/ppermute | solution.py:332
  4.7 1.6 %collective-permute-start = (bf16[128,2048]{1,0:T(8,128)(2,1)}, bf16[128,2048]{1,0:T(8,128)(2,1)S(1)}, u32[]{:S(2)}, u32[]{:S(2)}) collective-permute-start(bf16[128,2048]{1,0:T(8,128)(2,1)} %refs_1_.3), channel_id=1, source_target_pairs={{0,1},{1,0},{2,3},{3,2},{4,5},{5,4},{6,7},{7,6},{8,9},{9,8},{10,11... | collective-permute-start | bytes 1572872 | tf_op jit(solution)/shard_map/ppermute | solution.py:332
  8.0 5.2 %order.1 = (s32[194]{0:T(256)S(1)}, f32[8,128]{1,0:T(8,128)S(1)}) custom-call(s32[581]{0:T(1024)S(1)} %pad_add_fusion.refs_0_), custom_call_target="tpu_custom_call" | custom-call | flops 20000000000 | tf_op jit(solution)/shard_map/order/pallas_call | solution.py:317
  13.2 15.0 %collective-permute-done.1.refs_1_.refs_3_ = bf16[128,2048]{1,0:T(8,128)(2,1)S(1)} collective-permute-done((bf16[128,2048]{1,0:T(8,128)(2,1)}, bf16[128,2048]{1,0:T(8,128)(2,1)S(1)}, u32[]{:S(2)}, u32[]{:S(2)}) %collective-permute-start.1) | collective-permute-done | bytes 524320 | tf_op jit(solution)/shard_map/ppermute | solution.py:332
  29.0 3.3 %collective-permute-start.9 = (bf16[128,2048]{1,0:T(8,128)(2,1)S(1)}, bf16[128,2048]{1,0:T(8,128)(2,1)S(1)}, u32[]{:S(2)}, u32[]{:S(2)}) collective-permute-start(bf16[128,2048]{1,0:T(8,128)(2,1)S(1)} %get-tuple-element.80.refs_1_), channel_id=1, source_target_pairs={{0,2},{1,3},{2,0},{3,1},{4,6},{5,7},{6,4},{7,5},{8,10},{9,11},{10,... | collective-permute-start | bytes 1572872 | tf_op jit(solution)/shard_map/ppermute | solution.py:332
  33.6 4.6 %collective-permute-start.7 = (bf16[128,2048]{1,0:T(8,128)(2,1)S(1)}, bf16[128,2048]{1,0:T(8,128)(2,1)S(1)}, u32[]{:S(2)}, u32[]{:S(2)}) collective-permute-start(bf16[128,2048]{1,0:T(8,128)(2,1)S(1)} %get-tuple-element.80.refs_1_), channel_id=1, source_target_pairs={{0,1},{1,2},{2,3},{4,5},{5,6},{6,7},{8,9},{9,10},{10,11},{12,13},{... | collective-permute-start | bytes 1572872 | tf_op jit(solution)/shard_map/ppermute | solution.py:342
  38.2 15.5 %collective-permute-done.2.refs_4_ = bf16[128,2048]{1,0:T(8,128)(2,1)S(1)} collective-permute-done((bf16[128,2048]{1,0:T(8,128)(2,1)S(1)}, bf16[128,2048]{1,0:T(8,128)(2,1)S(1)}, u32[]{:S(2)}, u32[]{:S(2)}) %collective-permute-start.2) | collective-permute-done | bytes 524320 | tf_op jit(solution)/shard_map/ppermute | solution.py:332
  53.7 6.7 %forward.1 = (bf16[14,128,128]{2,1,0:T(8,128)(2,1)}, bf16[14,128,128]{2,1,0:T(8,128)(2,1)S(1)}, f32[14,128,128]{2,1,0:T(8,128)S(1)}, f32[14,128,128]{2,1,0:T(8,1...) custom-call(s32[581]{0:T(1024)S(1)} %pad_add_fusion.refs_0_, ...), custom_call_target="tpu_custom_call" | custom-call | flops 20000000000 | tf_op jit(solution)/shard_map/forward/pallas_call | solution.py:317
  60.4 3.1 %collective-permute-start.3 = (bf16[128,2048]{1,0:T(8,128)(2,1)S(1)}, bf16[128,2048]{1,0:T(8,128)(2,1)S(1)}, u32[]{:S(2)}, u32[]{:S(2)}) collective-permute-start(bf16[128,2048]{1,0:T(8,128)(2,1)S(1)} %get-tuple-element.73), channel_id=1, source_target_pairs={{0,1},{3,2},{4,5},{7,6},{8,9},{11,10},{12,13},{15,14},{16,17},{19,... | collective-permute-start | bytes 1572872 | tf_op jit(solution)/shard_map/ppermute | solution.py:349
  66.8 7.2 %collective-permute-done.3.refs_1_ = bf16[128,2048]{1,0:T(8,128)(2,1)S(1)} collective-permute-done((bf16[128,2048]{1,0:T(8,128)(2,1)S(1)}, bf16[128,2048]{1,0:T(8,128)(2,1)S(1)}, u32[]{:S(2)}, u32[]{:S(2)}) %collective-permute-start.3) | collective-permute-done | bytes 524320 | tf_op jit(solution)/shard_map/ppermute | solution.py:349
  74.2 4.1 %collective-permute-start.4 = (bf16[128,2048]{1,0:T(8,128)(2,1)S(1)}, bf16[128,2048]{1,0:T(8,128)(2,1)S(1)}, u32[]{:S(2)}, u32[]{:S(2)}) collective-permute-start(bf16[128,2048]{1,0:T(8,128)(2,1)S(1)} %get-tuple-element.77), channel_id=1, source_target_pairs={{0,2},{1,3},{2,0},{3,1},{4,6},{5,7},{6,4},{7,5},{8,10},{9,11},{10,... | collective-permute-start | bytes 1572872 | tf_op jit(solution)/shard_map/ppermute | solution.py:332
  78.3 2.0 %down_grads.1 = (bf16[4,12,128,128]{3,2,1,0:T(8,128)(2,1)S(1)}, bf16[4,12,128,128]{3,2,1,0:T(8,128)(2,1)S(1)}, f32[8,128]{1,0:T(8,128)S(1)}) custom-call(s32[581]{0:T(1024)S(1)} %pad_add_fusion.refs_0_, bf16[128,2048]{1,0:T(8,128)(2,1)S(1)} %get-tuple-element.80.refs_1_, bf16[128,2048]{1,0:T(8,128)(2,1)S(1)} %collective-permute-done.7.refs_2_, ...), custom_call_target="tpu_custom_call" | custom-call | flops 20000000000 | tf_op jit(solution)/shard_map/down_grads/pallas_call | solution.py:317
  80.4 2.2 %row_grads.1 = (bf16[14,128,128]{2,1,0:T(8,128)(2,1)S(1)}, bf16[14,128,128]{2,1,0:T(8,128)(2,1)S(1)}, f32[8,128]{1,0:T(8,128)S(1)}) custom-call(s32[581]{0:T(1024)S(1)} %pad_add_fusion.refs_0_, bf16[128,2048]{1,0:T(8,128)(2,1)S(1)} %get-tuple-element.80.refs_1_, bf16[128,2048]{1,0:T(8,128)(2,1)S(1)} %collective-permute-done.7.refs_2_, ...), custom_call_target="tpu_custom_call" | custom-call | flops 20000000000 | tf_op jit(solution)/shard_map/row_grads/pallas_call | solution.py:317
  84.1 2.4 %input_far.1 = (bf16[128,2048]{1,0:T(8,128)(2,1)S(1)}, f32[8,128]{1,0:T(8,128)S(1)}) custom-call(s32[581]{0:T(1024)S(1)} %pad_add_fusion.refs_0_, s32[194]{0:T(256)S(1)} %get-tuple-element.91.refs_1_, bf16[14,128,128]{2,1,0:T(8,128)(2,1)S(1)} %get-tuple-element.92.refs_2_.refs_1_, bf16[14,128,128]{2,1,0:T(8,128)(2,1)S(1)} %get-tuple-element.93.refs_3_.refs_1_, ...), custom_call_target="tpu_custom_call" | custom-call | flops 20000000000 | tf_op jit(solution)/shard_map/input_far/pallas_call | solution.py:317
  86.5 3.4 %collective-permute-start.13 = (bf16[128,2048]{1,0:T(8,128)(2,1)S(1)}, bf16[128,2048]{1,0:T(8,128)(2,1)S(1)}, u32[]{:S(2)}, u32[]{:S(2)}) collective-permute-start(bf16[128,2048]{1,0:T(8,128)(2,1)S(1)} %get-tuple-element.103), channel_id=1, source_target_pairs={{0,1},{1,0},{2,3},{3,2},{4,5},{5,4},{6,7},{7,6},{8,9},{9,8},{10,11... | collective-permute-start | bytes 1572872 | tf_op jit(solution)/shard_map/ppermute | solution.py:332
  89.9 1.5 %collective-permute-start.12 = (bf16[2,12,128,128]{3,2,1,0:T(8,128)(2,1)S(1)}, bf16[2,12,128,128]{3,2,1,0:T(8,128)(2,1)S(1)}, u32[]{:S(2)}, u32[]{:S(2)}) collective-permute-start(bf16[2,12,128,128]{3,2,1,0:T(8,128)(2,1)S(1)} %get-tuple-element.90), channel_id=1, source_target_pairs={{0,16},{4,12},{8,24},{12,4},{16,0},{20,28},{24,8},{28,20},{1,17},{... | collective-permute-start | bytes 2359304 | tf_op jit(solution)/shard_map/ppermute | solution.py:366
  91.4 1.8 %gate_grads.1 = (bf16[4,12,128,128]{3,2,1,0:T(8,128)(2,1)S(1)}, bf16[4,12,128,128]{3,2,1,0:T(8,128)(2,1)S(1)}, f32[8,128]{1,0:T(8,128)S(1)}) custom-call(s32[581]{0:T(1024)S(1)} %pad_add_fusion.refs_0_, bf16[14,128,128]{2,1,0:T(8,128)(2,1)S(1)} %get-tuple-element.92.refs_2_.refs_1_, bf16[64,128,128]{2,1,0:T(8,128)(2,1)S(1)} %get-tuple-element.94.refs_2_, ...), custom_call_target="tpu_custom_call" | custom-call | flops 20000000000 | tf_op jit(solution)/shard_map/gate_grads/pallas_call | solution.py:317
  93.2 5.2 %input_rest.1 = (bf16[128,2048]{1,0:T(8,128)(2,1)S(1)}, bf16[128,2048]{1,0:T(8,128)(2,1)S(1)}, bf16[128,2048]{1,0:T(8,128)(2,1)S(1)}, f32[8,128]{1,0:T(8,128)S(1)}) custom-call(s32[581]{0:T(1024)S(1)} %pad_add_fusion.refs_0_, s32[194]{0:T(256)S(1)} %get-tuple-element.91.refs_1_, bf16[14,128,128]{2,1,0:T(8,128)(2,1)S(1)} %get-tuple-element.92.refs_2_.refs_1_, ...), custom_call_target="tpu_custom_call" | custom-call | flops 20000000000 | tf_op jit(solution)/shard_map/input_rest/pallas_call | solution.py:317
  98.5 3.4 %collective-permute-done.12.refs_1_ = bf16[2,12,128,128]{3,2,1,0:T(8,128)(2,1)S(1)} collective-permute-done((bf16[2,12,128,128]{3,2,1,0:T(8,128)(2,1)S(1)}, bf16[2,12,128,128]{3,2,1,0:T(8,128)(2,1)S(1)}, u32[]{:S(2)}, u32[]{:S(2)}) %collective-permute-start.12) | collective-permute-done | bytes 786464 | tf_op jit(solution)/shard_map/ppermute | solution.py:366
  102.0 1.6 %collective-permute-start.14 = (bf16[1,12,128,128]{3,2,1,0:T(8,128)(2,1)S(1)}, bf16[1,12,128,128]{3,2,1,0:T(8,128)(2,1)S(1)}, u32[]{:S(2)}, u32[]{:S(2)}) collective-permute-start(bf16[1,12,128,128]{3,2,1,0:T(8,128)(2,1)S(1)} %get-tuple-element.106), channel_id=1, source_target_pairs={{0,8},{4,20},{8,0},{12,28},{16,24},{20,4},{24,16},{28,12},{1,9},{5... | collective-permute-start | bytes 1179656 | tf_op jit(solution)/shard_map/ppermute | solution.py:366
  105.7 2.2 %up_grads.1 = (bf16[4,12,128,128]{3,2,1,0:T(8,128)(2,1)S(1)}, bf16[4,12,128,128]{3,2,1,0:T(8,128)(2,1)S(1)}, f32[8,128]{1,0:T(8,128)S(1)}) custom-call(s32[581]{0:T(1024)S(1)} %pad_add_fusion.refs_0_, bf16[14,128,128]{2,1,0:T(8,128)(2,1)S(1)} %get-tuple-element.93.refs_3_.refs_1_, bf16[64,128,128]{2,1,0:T(8,128)(2,1)S(1)} %get-tuple-element.94.refs_2_, ...), custom_call_target="tpu_custom_call" | custom-call | flops 20000000000 | tf_op jit(solution)/shard_map/up_grads/pallas_call | solution.py:317
  107.8 1.6 %collective-permute-start.18 = (bf16[2,12,128,128]{3,2,1,0:T(8,128)(2,1)S(1)}, bf16[2,12,128,128]{3,2,1,0:T(8,128)(2,1)S(1)}, u32[]{:S(2)}, u32[]{:S(2)}) collective-permute-start(bf16[2,12,128,128]{3,2,1,0:T(8,128)(2,1)S(1)} %get-tuple-element.116), channel_id=1, source_target_pairs={{0,16},{4,12},{8,24},{12,4},{16,0},{20,28},{24,8},{28,20},{1,17},{... | collective-permute-start | bytes 2359304 | tf_op jit(solution)/shard_map/ppermute | solution.py:366
  110.7 2.0 %update.3 = (f32[3,12,128,128]{3,2,1,0:T(8,128)}, f32[8,128]{1,0:T(8,128)S(1)}) custom-call(s32[581]{0:T(1024)S(1)} %pad_add_fusion.refs_0_, bf16[1,12,128,128]{3,2,1,0:T(8,128)(2,1)S(1)} %get-tuple-element.105.refs_1_, bf16[1,12,128,128]{3,2,1,0:T(8,128)(2,1)S(1)} %collective-permute-done.14.refs_2_, f32[3,12,128,128]{3,2,1,0:T(8,128)S(1)} %copy-done, ...), custom_call_target="tpu_custom_call" | custom-call | flops 20000000000 | tf_op jit(solution)/shard_map/update/pallas_call | solution.py:317
  114.9 1.8 %collective-permute-start.21 = (bf16[2,12,128,128]{3,2,1,0:T(8,128)(2,1)S(1)}, bf16[2,12,128,128]{3,2,1,0:T(8,128)(2,1)S(1)}, u32[]{:S(2)}, u32[]{:S(2)}) collective-permute-start(bf16[2,12,128,128]{3,2,1,0:T(8,128)(2,1)S(1)} %get-tuple-element.125), channel_id=1, source_target_pairs={{0,16},{4,12},{8,24},{12,4},{16,0},{20,28},{24,8},{28,20},{1,17},{... | collective-permute-start | bytes 2359304 | tf_op jit(solution)/shard_map/ppermute | solution.py:366
  116.7 3.2 %collective-permute-done.18.refs_1_ = bf16[2,12,128,128]{3,2,1,0:T(8,128)(2,1)S(1)} collective-permute-done((bf16[2,12,128,128]{3,2,1,0:T(8,128)(2,1)S(1)}, bf16[2,12,128,128]{3,2,1,0:T(8,128)(2,1)S(1)}, u32[]{:S(2)}, u32[]{:S(2)}) %collective-permute-start.18) | collective-permute-done | bytes 786464 | tf_op jit(solution)/shard_map/ppermute | solution.py:366
  120.1 1.6 %collective-permute-start.20 = (bf16[1,12,128,128]{3,2,1,0:T(8,128)(2,1)S(1)}, bf16[1,12,128,128]{3,2,1,0:T(8,128)(2,1)S(1)}, u32[]{:S(2)}, u32[]{:S(2)}) collective-permute-start(bf16[1,12,128,128]{3,2,1,0:T(8,128)(2,1)S(1)} %get-tuple-element.122), channel_id=1, source_target_pairs={{0,8},{4,20},{8,0},{12,28},{16,24},{20,4},{24,16},{28,12},{1,9},{5... | collective-permute-start | bytes 1179656 | tf_op jit(solution)/shard_map/ppermute | solution.py:366
  121.6 10.9 %collective-permute-done.21.refs_1_ = bf16[2,12,128,128]{3,2,1,0:T(8,128)(2,1)S(1)} collective-permute-done((bf16[2,12,128,128]{3,2,1,0:T(8,128)(2,1)S(1)}, bf16[2,12,128,128]{3,2,1,0:T(8,128)(2,1)S(1)}, u32[]{:S(2)}, u32[]{:S(2)}) %collective-permute-start.21) | collective-permute-done | bytes 786464 | tf_op jit(solution)/shard_map/ppermute | solution.py:366
  132.7 1.6 %collective-permute-start.22 = (bf16[1,12,128,128]{3,2,1,0:T(8,128)(2,1)S(1)}, bf16[1,12,128,128]{3,2,1,0:T(8,128)(2,1)S(1)}, u32[]{:S(2)}, u32[]{:S(2)}) collective-permute-start(bf16[1,12,128,128]{3,2,1,0:T(8,128)(2,1)S(1)} %get-tuple-element.131), channel_id=1, source_target_pairs={{0,8},{4,20},{8,0},{12,28},{16,24},{20,4},{24,16},{28,12},{1,9},{5... | collective-permute-start | bytes 1179656 | tf_op jit(solution)/shard_map/ppermute | solution.py:366
  134.3 2.0 %update.4 = (f32[3,12,128,128]{3,2,1,0:T(8,128)}, f32[8,128]{1,0:T(8,128)S(1)}) custom-call(s32[581]{0:T(1024)S(1)} %pad_add_fusion.refs_0_, bf16[1,12,128,128]{3,2,1,0:T(8,128)(2,1)S(1)} %get-tuple-element.121.refs_1_, bf16[1,12,128,128]{3,2,1,0:T(8,128)(2,1)S(1)} %collective-permute-done.20.refs_2_, ...), custom_call_target="tpu_custom_call", output_to_operand_aliasing={{0}: (5, {})} | custom-call | flops 20000000000 | tf_op jit(solution)/shard_map/update/pallas_call | solution.py:317
  136.3 1.8 %collective-permute-done.16.refs_1_ = bf16[128,2048]{1,0:T(8,128)(2,1)S(1)} collective-permute-done((bf16[128,2048]{1,0:T(8,128)(2,1)S(1)}, bf16[128,2048]{1,0:T(8,128)(2,1)S(1)}, u32[]{:S(2)}, u32[]{:S(2)}) %collective-permute-start.16) | collective-permute-done | bytes 524320 | tf_op jit(solution)/shard_map/ppermute | solution.py:332
  139.1 1.5 %collective-permute-done.22.refs_2_ = bf16[1,12,128,128]{3,2,1,0:T(8,128)(2,1)S(1)} collective-permute-done((bf16[1,12,128,128]{3,2,1,0:T(8,128)(2,1)S(1)}, bf16[1,12,128,128]{3,2,1,0:T(8,128)(2,1)S(1)}, u32[]{:S(2)}, u32[]{:S(2)}) %collective-permute-start.22) | collective-permute-done | bytes 393248 | tf_op jit(solution)/shard_map/ppermute | solution.py:366
  140.6 2.0 %update.5 = (f32[3,12,128,128]{3,2,1,0:T(8,128)}, f32[8,128]{1,0:T(8,128)}) custom-call(s32[581]{0:T(1024)S(1)} %pad_add_fusion.refs_0_, bf16[1,12,128,128]{3,2,1,0:T(8,128)(2,1)S(1)} %get-tuple-element.130.refs_1_, bf16[1,12,128,128]{3,2,1,0:T(8,128)(2,1)S(1)} %collective-permute-done.22.refs_2_, ...), custom_call_target="tpu_custom_call", output_to_operand_aliasing={{0}: (5, {})} | custom-call | flops 20000000000 | tf_op jit(solution)/shard_map/update/pallas_call | solution.py:317
  (55 shorter events, 15.8 us)
Async XLA Ops:
  0.6 27.6 %collective-permute-start.1 = (bf16[128,2048]{1,0:T(8,128)(2,1)}, bf16[128,2048]{1,0:T(8,128)(2,1)S(1)}, u32[]{:S(2)}, u32[]{:S(2)}) collective-permute-start(bf16[128,2048]{1,0:T(8,128)(2,1)} %refs_1_.3), channel_id=1, source_target_pairs={{0,2},{1,3},{2,0},{3,1},{4,6},{5,7},{6,4},{7,5},{8,10},{9,11},{10,... | collective-permute-start | bytes 1572872 | tf_op jit(solution)/shard_map/ppermute | solution.py:332
  4.7 33.5 %collective-permute-start = (bf16[128,2048]{1,0:T(8,128)(2,1)}, bf16[128,2048]{1,0:T(8,128)(2,1)S(1)}, u32[]{:S(2)}, u32[]{:S(2)}) collective-permute-start(bf16[128,2048]{1,0:T(8,128)(2,1)} %refs_1_.3), channel_id=1, source_target_pairs={{0,1},{1,0},{2,3},{3,2},{4,5},{5,4},{6,7},{7,6},{8,9},{9,8},{10,11... | collective-permute-start | bytes 1572872 | tf_op jit(solution)/shard_map/ppermute | solution.py:332
  8.0 20.9 %copy-start.2 = (bf16[128,2048]{1,0:T(8,128)(2,1)S(1)}, bf16[128,2048]{1,0:T(8,128)(2,1)}, u32[]{:S(2)}) copy-start(bf16[128,2048]{1,0:T(8,128)(2,1)} %refs_0_.1) | copy-start | bytes 1572868
  8.0 45.7 %slice-start = ((s8[9437184]{0:T(1024)(128)(4,1)}), s8[4194304]{0:T(1024)(128)(4,1)S(1)}, s32[]{:S(2)}) async-start(s8[9437184]{0:T(1024)(128)(4,1)} %bitcast.3), calls=%async_computation | async-start | bytes 8388608
  8.0 45.7 %slice-start.1 = ((s8[9437184]{0:T(1024)(128)(4,1)}), s8[4194304]{0:T(1024)(128)(4,1)S(1)}, s32[]{:S(2)}) async-start(s8[9437184]{0:T(1024)(128)(4,1)} %bitcast.3), calls=%async_computation.1 | async-start | bytes 8388608
  28.2 25.5 %collective-permute-start.2 = (bf16[128,2048]{1,0:T(8,128)(2,1)S(1)}, bf16[128,2048]{1,0:T(8,128)(2,1)S(1)}, u32[]{:S(2)}, u32[]{:S(2)}) collective-permute-start(bf16[128,2048]{1,0:T(8,128)(2,1)S(1)} %collective-permute-done.1.refs_1_.refs_3_), channel_id=1, source_target_pairs={{0,1},{1,0},{2,3},{3,2},{4,5},{5,4},{6,7},{7,6},{8,9},{9,8},{10,11... | collective-permute-start | bytes 1572872 | tf_op jit(solution)/shard_map/ppermute | solution.py:332
  28.9 24.7 %slice-start.2 = ((s8[9437184]{0:T(1024)(128)(4,1)}), s8[1048576]{0:T(1024)(128)(4,1)S(1)}, s32[]{:S(2)}) async-start(s8[9437184]{0:T(1024)(128)(4,1)} %bitcast.3), calls=%async_computation.2 | async-start | bytes 2097152
  28.9 24.7 %copy-start.3 = (bf16[128,2048]{1,0:T(8,128)(2,1)S(1)}, bf16[128,2048]{1,0:T(8,128)(2,1)}, u32[]{:S(2)}) copy-start(bf16[128,2048]{1,0:T(8,128)(2,1)} %refs_1_.3) | copy-start | bytes 1572868
  29.0 35.2 %collective-permute-start.9 = (bf16[128,2048]{1,0:T(8,128)(2,1)S(1)}, bf16[128,2048]{1,0:T(8,128)(2,1)S(1)}, u32[]{:S(2)}, u32[]{:S(2)}) collective-permute-start(bf16[128,2048]{1,0:T(8,128)(2,1)S(1)} %get-tuple-element.80.refs_1_), channel_id=1, source_target_pairs={{0,2},{1,3},{2,0},{3,1},{4,6},{5,7},{6,4},{7,5},{8,10},{9,11},{10,... | collective-permute-start | bytes 1572872 | tf_op jit(solution)/shard_map/ppermute | solution.py:332
  32.3 45.9 %collective-permute-start.8 = (bf16[128,2048]{1,0:T(8,128)(2,1)S(1)}, bf16[128,2048]{1,0:T(8,128)(2,1)S(1)}, u32[]{:S(2)}, u32[]{:S(2)}) collective-permute-start(bf16[128,2048]{1,0:T(8,128)(2,1)S(1)} %get-tuple-element.80.refs_1_), channel_id=1, source_target_pairs={{1,0},{2,1},{3,2},{5,4},{6,5},{7,6},{9,8},{10,9},{11,10},{13,12},{... | collective-permute-start | bytes 1572872 | tf_op jit(solution)/shard_map/ppermute | solution.py:343
  33.6 44.6 %collective-permute-start.7 = (bf16[128,2048]{1,0:T(8,128)(2,1)S(1)}, bf16[128,2048]{1,0:T(8,128)(2,1)S(1)}, u32[]{:S(2)}, u32[]{:S(2)}) collective-permute-start(bf16[128,2048]{1,0:T(8,128)(2,1)S(1)} %get-tuple-element.80.refs_1_), channel_id=1, source_target_pairs={{0,1},{1,2},{2,3},{4,5},{5,6},{6,7},{8,9},{9,10},{10,11},{12,13},{... | collective-permute-start | bytes 1572872 | tf_op jit(solution)/shard_map/ppermute | solution.py:342
  60.4 13.6 %collective-permute-start.3 = (bf16[128,2048]{1,0:T(8,128)(2,1)S(1)}, bf16[128,2048]{1,0:T(8,128)(2,1)S(1)}, u32[]{:S(2)}, u32[]{:S(2)}) collective-permute-start(bf16[128,2048]{1,0:T(8,128)(2,1)S(1)} %get-tuple-element.73), channel_id=1, source_target_pairs={{0,1},{3,2},{4,5},{7,6},{8,9},{11,10},{12,13},{15,14},{16,17},{19,... | collective-permute-start | bytes 1572872 | tf_op jit(solution)/shard_map/ppermute | solution.py:349
  63.5 27.9 %collective-permute-start.6 = (bf16[128,2048]{1,0:T(8,128)(2,1)S(1)}, bf16[128,2048]{1,0:T(8,128)(2,1)S(1)}, u32[]{:S(2)}, u32[]{:S(2)}) collective-permute-start(bf16[128,2048]{1,0:T(8,128)(2,1)S(1)} %get-tuple-element.79), channel_id=1, source_target_pairs={{1,2},{2,1},{5,6},{6,5},{9,10},{10,9},{13,14},{14,13},{17,18},{18,... | collective-permute-start | bytes 1572872 | tf_op jit(solution)/shard_map/ppermute | solution.py:349
  64.2 14.0 %collective-permute-start.10 = (bf16[128,2048]{1,0:T(8,128)(2,1)S(1)}, bf16[128,2048]{1,0:T(8,128)(2,1)S(1)}, u32[]{:S(2)}, u32[]{:S(2)}) collective-permute-start(bf16[128,2048]{1,0:T(8,128)(2,1)S(1)} %collective-permute-done.9.refs_4_), channel_id=1, source_target_pairs={{2,3},{1,0},{6,7},{5,4},{10,11},{9,8},{14,15},{13,12},{18,19},{17,... | collective-permute-start | bytes 1572872 | tf_op jit(solution)/shard_map/ppermute | solution.py:344
  74.2 29.4 %collective-permute-start.4 = (bf16[128,2048]{1,0:T(8,128)(2,1)S(1)}, bf16[128,2048]{1,0:T(8,128)(2,1)S(1)}, u32[]{:S(2)}, u32[]{:S(2)}) collective-permute-start(bf16[128,2048]{1,0:T(8,128)(2,1)S(1)} %get-tuple-element.77), channel_id=1, source_target_pairs={{0,2},{1,3},{2,0},{3,1},{4,6},{5,7},{6,4},{7,5},{8,10},{9,11},{10,... | collective-permute-start | bytes 1572872 | tf_op jit(solution)/shard_map/ppermute | solution.py:332
  78.2 26.0 %collective-permute-start.5 = (bf16[128,2048]{1,0:T(8,128)(2,1)S(1)}, bf16[128,2048]{1,0:T(8,128)(2,1)S(1)}, u32[]{:S(2)}, u32[]{:S(2)}) collective-permute-start(bf16[128,2048]{1,0:T(8,128)(2,1)S(1)} %get-tuple-element.78), channel_id=1, source_target_pairs={{0,1},{1,0},{2,3},{3,2},{4,5},{5,4},{6,7},{7,6},{8,9},{9,8},{10,11... | collective-permute-start | bytes 1572872 | tf_op jit(solution)/shard_map/ppermute | solution.py:332
  80.3 3.5 %collective-permute-start.11 = (bf16[4,12,128,128]{3,2,1,0:T(8,128)(2,1)S(1)}, bf16[4,12,128,128]{3,2,1,0:T(8,128)(2,1)S(1)}, u32[]{:S(2)}, u32[]{:S(2)}) collective-permute-start(bf16[4,12,128,128]{3,2,1,0:T(8,128)(2,1)S(1)} %get-tuple-element.84), channel_id=1, source_target_pairs={{0,4},{4,0},{8,12},{12,8},{16,20},{20,16},{24,28},{28,24},{1,5},{5... | collective-permute-start | bytes 4718600 | tf_op jit(solution)/shard_map/ppermute | solution.py:360
  86.5 27.2 %collective-permute-start.13 = (bf16[128,2048]{1,0:T(8,128)(2,1)S(1)}, bf16[128,2048]{1,0:T(8,128)(2,1)S(1)}, u32[]{:S(2)}, u32[]{:S(2)}) collective-permute-start(bf16[128,2048]{1,0:T(8,128)(2,1)S(1)} %get-tuple-element.103), channel_id=1, source_target_pairs={{0,1},{1,0},{2,3},{3,2},{4,5},{5,4},{6,7},{7,6},{8,9},{9,8},{10,11... | collective-permute-start | bytes 1572872 | tf_op jit(solution)/shard_map/ppermute | solution.py:332
  89.9 12.0 %collective-permute-start.12 = (bf16[2,12,128,128]{3,2,1,0:T(8,128)(2,1)S(1)}, bf16[2,12,128,128]{3,2,1,0:T(8,128)(2,1)S(1)}, u32[]{:S(2)}, u32[]{:S(2)}) collective-permute-start(bf16[2,12,128,128]{3,2,1,0:T(8,128)(2,1)S(1)} %get-tuple-element.90), channel_id=1, source_target_pairs={{0,16},{4,12},{8,24},{12,4},{16,0},{20,28},{24,8},{28,20},{1,17},{... | collective-permute-start | bytes 2359304 | tf_op jit(solution)/shard_map/ppermute | solution.py:366
  98.4 6.9 %collective-permute-start.15 = (bf16[4,12,128,128]{3,2,1,0:T(8,128)(2,1)S(1)}, bf16[4,12,128,128]{3,2,1,0:T(8,128)(2,1)S(1)}, u32[]{:S(2)}, u32[]{:S(2)}) collective-permute-start(bf16[4,12,128,128]{3,2,1,0:T(8,128)(2,1)S(1)} %get-tuple-element.108), channel_id=1, source_target_pairs={{0,4},{4,0},{8,12},{12,8},{16,20},{20,16},{24,28},{28,24},{1,5},{5... | collective-permute-start | bytes 4718600 | tf_op jit(solution)/shard_map/ppermute | solution.py:360
  102.0 8.7 %collective-permute-start.14 = (bf16[1,12,128,128]{3,2,1,0:T(8,128)(2,1)S(1)}, bf16[1,12,128,128]{3,2,1,0:T(8,128)(2,1)S(1)}, u32[]{:S(2)}, u32[]{:S(2)}) collective-permute-start(bf16[1,12,128,128]{3,2,1,0:T(8,128)(2,1)S(1)} %get-tuple-element.106), channel_id=1, source_target_pairs={{0,8},{4,20},{8,0},{12,28},{16,24},{20,4},{24,16},{28,12},{1,9},{5... | collective-permute-start | bytes 1179656 | tf_op jit(solution)/shard_map/ppermute | solution.py:366
  105.6 5.1 %copy-start = (f32[3,12,128,128]{3,2,1,0:T(8,128)S(1)}, f32[3,12,128,128]{3,2,1,0:T(8,128)}, u32[]{:S(2)}) copy-start(f32[3,12,128,128]{3,2,1,0:T(8,128)} %refs_3_.5) | copy-start | bytes 7077892
  105.6 5.1 %copy-start.1 = (f32[3,12,128,128]{3,2,1,0:T(8,128)S(1)}, f32[3,12,128,128]{3,2,1,0:T(8,128)}, u32[]{:S(2)}) copy-start(f32[3,12,128,128]{3,2,1,0:T(8,128)} %refs_4_.9) | copy-start | bytes 7077892
  107.8 12.1 %collective-permute-start.18 = (bf16[2,12,128,128]{3,2,1,0:T(8,128)(2,1)S(1)}, bf16[2,12,128,128]{3,2,1,0:T(8,128)(2,1)S(1)}, u32[]{:S(2)}, u32[]{:S(2)}) collective-permute-start(bf16[2,12,128,128]{3,2,1,0:T(8,128)(2,1)S(1)} %get-tuple-element.116), channel_id=1, source_target_pairs={{0,16},{4,12},{8,24},{12,4},{16,0},{20,28},{24,8},{28,20},{1,17},{... | collective-permute-start | bytes 2359304 | tf_op jit(solution)/shard_map/ppermute | solution.py:366
  109.4 5.1 %collective-permute-start.19 = (bf16[4,12,128,128]{3,2,1,0:T(8,128)(2,1)S(1)}, bf16[4,12,128,128]{3,2,1,0:T(8,128)(2,1)S(1)}, u32[]{:S(2)}, u32[]{:S(2)}) collective-permute-start(bf16[4,12,128,128]{3,2,1,0:T(8,128)(2,1)S(1)} %get-tuple-element.118), channel_id=1, source_target_pairs={{0,4},{4,0},{8,12},{12,8},{16,20},{20,16},{24,28},{28,24},{1,5},{5... | collective-permute-start | bytes 4718600 | tf_op jit(solution)/shard_map/ppermute | solution.py:360
  113.7 24.3 %collective-permute-start.16 = (bf16[128,2048]{1,0:T(8,128)(2,1)S(1)}, bf16[128,2048]{1,0:T(8,128)(2,1)S(1)}, u32[]{:S(2)}, u32[]{:S(2)}) collective-permute-start(bf16[128,2048]{1,0:T(8,128)(2,1)S(1)} %get-tuple-element.113), channel_id=1, source_target_pairs={{0,2},{1,3},{2,0},{3,1},{4,6},{5,7},{6,4},{7,5},{8,10},{9,11},{10,... | collective-permute-start | bytes 1572872 | tf_op jit(solution)/shard_map/ppermute | solution.py:332
  113.8 24.3 %collective-permute-start.17 = (bf16[128,2048]{1,0:T(8,128)(2,1)S(1)}, bf16[128,2048]{1,0:T(8,128)(2,1)S(1)}, u32[]{:S(2)}, u32[]{:S(2)}) collective-permute-start(bf16[128,2048]{1,0:T(8,128)(2,1)S(1)} %get-tuple-element.114), channel_id=1, source_target_pairs={{0,1},{1,0},{2,3},{3,2},{4,5},{5,4},{6,7},{7,6},{8,9},{9,8},{10,11... | collective-permute-start | bytes 1572872 | tf_op jit(solution)/shard_map/ppermute | solution.py:332
  114.9 17.6 %collective-permute-start.21 = (bf16[2,12,128,128]{3,2,1,0:T(8,128)(2,1)S(1)}, bf16[2,12,128,128]{3,2,1,0:T(8,128)(2,1)S(1)}, u32[]{:S(2)}, u32[]{:S(2)}) collective-permute-start(bf16[2,12,128,128]{3,2,1,0:T(8,128)(2,1)S(1)} %get-tuple-element.125), channel_id=1, source_target_pairs={{0,16},{4,12},{8,24},{12,4},{16,0},{20,28},{24,8},{28,20},{1,17},{... | collective-permute-start | bytes 2359304 | tf_op jit(solution)/shard_map/ppermute | solution.py:366
  120.1 14.2 %collective-permute-start.20 = (bf16[1,12,128,128]{3,2,1,0:T(8,128)(2,1)S(1)}, bf16[1,12,128,128]{3,2,1,0:T(8,128)(2,1)S(1)}, u32[]{:S(2)}, u32[]{:S(2)}) collective-permute-start(bf16[1,12,128,128]{3,2,1,0:T(8,128)(2,1)S(1)} %get-tuple-element.122), channel_id=1, source_target_pairs={{0,8},{4,20},{8,0},{12,28},{16,24},{20,4},{24,16},{28,12},{1,9},{5... | collective-permute-start | bytes 1179656 | tf_op jit(solution)/shard_map/ppermute | solution.py:366
  132.7 7.8 %collective-permute-start.22 = (bf16[1,12,128,128]{3,2,1,0:T(8,128)(2,1)S(1)}, bf16[1,12,128,128]{3,2,1,0:T(8,128)(2,1)S(1)}, u32[]{:S(2)}, u32[]{:S(2)}) collective-permute-start(bf16[1,12,128,128]{3,2,1,0:T(8,128)(2,1)S(1)} %get-tuple-element.131), channel_id=1, source_target_pairs={{0,8},{4,20},{8,0},{12,28},{16,24},{20,4},{24,16},{28,12},{1,9},{5... | collective-permute-start | bytes 1179656 | tf_op jit(solution)/shard_map/ppermute | solution.py:366
